TPU v7x, 32 devices: a whole 2x2x4 slice. The times are simulated.
32 devices in a mesh: dp: 8 (over z, core), tensor: 4 (over y, x).
Axes of the slice: x: 2, y: 2, z: 4, core: 2. Of those that a mesh axis runs over, the one named last changes fastest.
Arguments:
- tokens: bfloat16 [1024, 16, 2048], P('tensor', 'dp'), may hold values from -6 to 6
- cotangent: bfloat16 [1024, 16, 2048], P('tensor', 'dp'), may hold values from -8 to 8
- doc_lengths: int32 [16, 8], P('dp'), may hold values from 1 to 1017, as said below
- rel_bucket: int32 [2047], replicated, may hold values from 0 to 31
- gain_attn: bfloat16 [2048], P('dp'), may hold values from 0.5 to 1.5
- w_query: bfloat16 [2048, 2048], P('dp', 'tensor'), may hold values from -0.03125 to 0.03125
- w_key: bfloat16 [2048, 2048], P('dp', 'tensor'), may hold values from -0.125 to 0.125
- w_value: bfloat16 [2048, 2048], P('dp', 'tensor'), may hold values from -0.125 to 0.125
- w_out: bfloat16 [2048, 2048], P('tensor', 'dp'), may hold values from -0.5 to 0.5
- rel_table: bfloat16 [32, 32], P('dp', 'tensor'), may hold values from -4 to 4
- gain_ff: bfloat16 [2048], P('dp'), may hold values from 0.5 to 1.5
- w_gate: bfloat16 [2048, 5120], P('dp', 'tensor'), may hold values from -0.125 to 0.125
- w_up: bfloat16 [2048, 5120], P('dp', 'tensor'), may hold values from -0.125 to 0.125
- w_down: bfloat16 [5120, 2048], P('tensor', 'dp'), may hold values from -0.078125 to 0.078125
Outputs:
- output: bfloat16 [1024, 16, 2048], P('tensor', 'dp')
- grad_tokens: bfloat16 [1024, 16, 2048], P('tensor', 'dp')
- grad_gain_attn: float32 [2048], P('dp')
- grad_w_query: float32 [2048, 2048], P('dp', 'tensor')
- grad_w_key: float32 [2048, 2048], P('dp', 'tensor')
- grad_w_value: float32 [2048, 2048], P('dp', 'tensor')
- grad_w_out: float32 [2048, 2048], P('tensor', 'dp')
- grad_rel_table: float32 [32, 32], P('dp', 'tensor')
- grad_gain_ff: float32 [2048], P('dp')
- grad_w_gate: float32 [2048, 5120], P('dp', 'tensor')
- grad_w_up: float32 [2048, 5120], P('dp', 'tensor')
- grad_w_down: float32 [5120, 2048], P('tensor', 'dp')
Inputs may be any that keep to these rules, and one draw needn't show every extreme that they name: `doc_lengths`: each row gives 7 document lengths, each 1 or more, then a tail padding length of 1 to 128; each row sums to 1024. In one sequence of every 2 consecutive ones the first document holds 1017 slots.
All inputs are finite; a program needn't handle non-finite values.
Results may differ from a plain program's by a relative error of at most 0.024.
Values may be sent and summed in bfloat16 or wider, within the bound.
No kernel may reach another device: no remote copies, remote signals or barrier semaphores. Data moves between devices by JAX's collectives and lax.ppermute only.
A program may use at most 448 MiB of HBM per device.

v0:
```python
from functools import partial

import jax
import jax.numpy as jnp
from jax import lax
from jax.sharding import PartitionSpec as P

HEAD_DIM = 64
L = 1024
QBLOCK = 512
MICRO = 2
SEQS_MB = 1


EPSILON = 1e-06
NEGATIVE = -1e30
HIGH = lax.Precision.HIGHEST


def segment_ids(lengths, length):
    ends = jnp.cumsum(lengths, axis=1)
    slots = jnp.arange(length, dtype=jnp.int32)
    passed = jnp.sum((slots[None, :, None] >= ends[:, None, :]).astype(jnp.int32), axis=2)
    number = lengths.shape[1]
    return jnp.where(passed == number - 1, 0, passed + 1)


def norm_scale(rows):
    return lax.rsqrt(jnp.mean(rows * rows, axis=-1, keepdims=True) + EPSILON)


def norm_back(rows, scale, gain, grad_normed):
    scaled = gain * grad_normed
    inner = jnp.mean(scaled * rows, axis=-1, keepdims=True)
    grad_rows = scale * scaled - rows * scale * scale * scale * inner
    return (grad_rows, jnp.sum(grad_normed * rows * scale, axis=(0, 1)))


def contract(left, right, left_dim, right_dim):
    return lax.dot_general(
        left, right, (((left_dim,), (right_dim,)), ((), ())), preferred_element_type=jnp.float32
    )


def gather_rows(part):
    return lax.all_gather(part, "tensor", axis=0, tiled=True)


def reduce_rows(left, weight, right_dim):
    return lax.psum_scatter(
        contract(left, weight, 1, right_dim).astype(jnp.bfloat16),
        "tensor",
        scatter_dimension=0,
        tiled=True,
    ).astype(jnp.float32)


def toeplitz_tile(vector, length):
    padded = jnp.pad(vector, ((0, 0), (0, 1)))
    tiled = jnp.tile(padded, (1, length))
    window = tiled[:, length - 1 : length - 1 + length * (2 * length - 1)]
    return window.reshape(vector.shape[0], length, 2 * length - 1)[:, :, :length]


def fold_diagonals(grads):
    heads, rows, keys = grads.shape
    padded = jnp.pad(grads[:, ::-1, :], ((0, 0), (0, 0), (0, rows)))
    flat = padded.reshape(heads, rows * (keys + rows))[:, : rows * (keys + rows - 1)]
    return jnp.sum(flat.reshape(heads, rows, keys + rows - 1), axis=1)


def block_scores(block_queries, seq_keys, block_segments, seq_segments, bias_rows):
    scores = jnp.einsum("qhd,khd->hqk", block_queries, seq_keys, preferred_element_type=jnp.float32)
    scores = scores + bias_rows
    same = block_segments[:, None] == seq_segments[None, :]
    return jnp.where(same[None], scores, NEGATIVE)


def attend_forward(queries, keys, values, segments, bias_tile, block):
    length = queries.shape[1]

    def one_sequence(item):
        seq_queries, seq_keys, seq_values, seq_segments = item

        def one_block(start):
            block_queries = lax.dynamic_slice_in_dim(seq_queries, start, block, 0)
            block_segments = lax.dynamic_slice_in_dim(seq_segments, start, block, 0)
            bias_rows = lax.dynamic_slice_in_dim(bias_tile, start, block, 1)
            scores = block_scores(block_queries, seq_keys, block_segments, seq_segments, bias_rows)
            peak = jnp.max(scores, axis=2, keepdims=True)
            weights = jnp.exp(scores - peak)
            total = jnp.sum(weights, axis=2, keepdims=True)
            shares = (weights / total).astype(jnp.bfloat16)
            mixed = jnp.einsum(
                "hqk,khd->qhd", shares, seq_values, preferred_element_type=jnp.float32
            )
            return (mixed.astype(jnp.bfloat16), (peak + jnp.log(total))[:, :, 0])

        starts = jnp.arange(length // block, dtype=jnp.int32) * block
        mixed, logsum = lax.map(one_block, starts)
        return (mixed.reshape(seq_queries.shape), logsum)

    return lax.map(one_sequence, (queries, keys, values, segments))


def attend_backward(
    queries, keys, values, segments, logsum, grad_mixed, bias_tile, grad_diag, block
):
    length = queries.shape[1]

    def one_sequence(diag_total, item):
        seq_queries, seq_keys, seq_values, seq_segments, seq_logsum, seq_grad = item

        def one_block(carry, index):
            grad_keys, grad_values, diag_sum = carry
            start = index * block
            block_queries = lax.dynamic_slice_in_dim(seq_queries, start, block, 0)
            block_segments = lax.dynamic_slice_in_dim(seq_segments, start, block, 0)
            block_grad = lax.dynamic_slice_in_dim(seq_grad, start, block, 0)
            block_logsum = lax.dynamic_index_in_dim(seq_logsum, index, 0, keepdims=False)
            bias_rows = lax.dynamic_slice_in_dim(bias_tile, start, block, 1)
            scores = block_scores(block_queries, seq_keys, block_segments, seq_segments, bias_rows)
            probs_full = jnp.exp(scores - block_logsum[:, :, None])
            shares = probs_full.astype(jnp.bfloat16)
            grad_values = grad_values + jnp.einsum(
                "hqk,qhd->khd", shares, block_grad, preferred_element_type=jnp.float32
            )
            grad_shares = jnp.einsum(
                "qhd,khd->hqk", block_grad, seq_values, preferred_element_type=jnp.float32
            )
            inner = jnp.sum(probs_full * grad_shares, axis=2, keepdims=True)
            grad_scores = (probs_full * (grad_shares - inner)).astype(jnp.bfloat16)
            grad_queries = jnp.einsum(
                "hqk,khd->qhd", grad_scores, seq_keys, preferred_element_type=jnp.float32
            ).astype(jnp.bfloat16)
            grad_keys = grad_keys + jnp.einsum(
                "hqk,qhd->khd", grad_scores, block_queries, preferred_element_type=jnp.float32
            )
            folded = fold_diagonals(grad_scores.astype(jnp.float32))
            offset = length - block - start
            current = lax.dynamic_slice_in_dim(diag_sum, offset, length + block - 1, 1)
            diag_sum = lax.dynamic_update_slice_in_dim(diag_sum, current + folded, offset, 1)
            return ((grad_keys, grad_values, diag_sum), grad_queries)

        initial = (
            jnp.zeros(seq_keys.shape, jnp.float32),
            jnp.zeros(seq_keys.shape, jnp.float32),
            diag_total,
        )
        totals, grad_queries = lax.scan(
            one_block, initial, jnp.arange(length // block, dtype=jnp.int32)
        )
        return (
            totals[2],
            (
                grad_queries.reshape(seq_queries.shape),
                totals[0].astype(jnp.bfloat16),
                totals[1].astype(jnp.bfloat16),
            ),
        )

    grad_diag, results = lax.scan(
        one_sequence, grad_diag, (queries, keys, values, segments, logsum, grad_mixed)
    )
    return (results[0], results[1], results[2], grad_diag)


def local(
    tokens,
    cotangent,
    doc_lengths,
    rel_bucket,
    gain_attn,
    w_query,
    w_key,
    w_value,
    w_out,
    rel_table,
    gain_ff,
    w_gate,
    w_up,
    w_down,
):
    gathered = (
        lax.all_gather(w_query, "dp", axis=0, tiled=True),
        lax.all_gather(w_key, "dp", axis=0, tiled=True),
        lax.all_gather(w_value, "dp", axis=0, tiled=True),
        lax.all_gather(w_gate, "dp", axis=0, tiled=True),
        lax.all_gather(w_up, "dp", axis=0, tiled=True),
        lax.all_gather(gain_attn, "dp", axis=0, tiled=True),
        lax.all_gather(gain_ff, "dp", axis=0, tiled=True),
        lax.all_gather(rel_table, "dp", axis=0, tiled=True),
    )
    (
        full_query,
        full_key,
        full_value,
        full_gate,
        full_up,
        full_gain_attn,
        full_gain_ff,
        full_table,
    ) = gathered
    full_out, full_down = (
        lax.all_gather(w_out, "dp", axis=1, tiled=True),
        lax.all_gather(w_down, "dp", axis=1, tiled=True),
    )
    attn_weight = jnp.concatenate([full_query, full_key, full_value], axis=1)
    ff_weight = jnp.concatenate([full_gate, full_up], axis=1)
    gain_one = full_gain_attn.astype(jnp.float32)
    gain_two = full_gain_ff.astype(jnp.float32)
    width_heads = w_query.shape[1]
    heads_local = width_heads // HEAD_DIM
    width_ff = w_gate.shape[1]
    length = L
    bucket_onehot = (
        rel_bucket[:, None] == jnp.arange(full_table.shape[0], dtype=jnp.int32)[None, :]
    ).astype(jnp.float32)
    bias_offset = jnp.dot(bucket_onehot, full_table.astype(jnp.float32), precision=HIGH).T
    bias_tile = toeplitz_tile(bias_offset, length)
    grad_diag = jnp.zeros((heads_local, 2 * length - 1), jnp.float32)
    segments = segment_ids(doc_lengths, length)
    outputs = []
    grad_inputs = []
    totals_rows = None
    totals_cols = None
    for index in range(MICRO):
        first_seq = index * SEQS_MB
        rows_in = tokens[:, first_seq : first_seq + SEQS_MB].astype(jnp.float32)
        batch_segments = segments[first_seq : first_seq + SEQS_MB]
        scale_one = norm_scale(rows_in)
        normed_one = (rows_in * scale_one * gain_one).astype(jnp.bfloat16)
        whole_one = gather_rows(normed_one).reshape(length * SEQS_MB, -1)
        projected = jnp.dot(whole_one, attn_weight, preferred_element_type=jnp.float32).astype(
            jnp.bfloat16
        )
        heads_view = jnp.moveaxis(
            projected.reshape(length, SEQS_MB, 3, heads_local, HEAD_DIM), 1, 0
        )
        queries = heads_view[:, :, 0]
        keys = heads_view[:, :, 1]
        values = heads_view[:, :, 2]
        mixed, logsum = attend_forward(queries, keys, values, batch_segments, bias_tile, QBLOCK)
        mixed_flat = jnp.moveaxis(mixed, 0, 1).reshape(length * SEQS_MB, width_heads)
        attn_rows = reduce_rows(mixed_flat, full_out, 0).reshape(rows_in.shape)
        middle = rows_in + attn_rows
        scale_two = norm_scale(middle)
        normed_two = (middle * scale_two * gain_two).astype(jnp.bfloat16)
        whole_two = gather_rows(normed_two).reshape(length * SEQS_MB, -1)
        gate_up = jnp.dot(whole_two, ff_weight, preferred_element_type=jnp.float32)
        gate = gate_up[:, :width_ff]
        upward = gate_up[:, width_ff:]
        activated = jax.nn.gelu(gate, approximate=True)
        hidden = (activated * upward).astype(jnp.bfloat16)
        ff_rows = reduce_rows(hidden, full_down, 0).reshape(rows_in.shape)
        outputs.append((middle + ff_rows).astype(jnp.bfloat16))
        grad_final = cotangent[:, first_seq : first_seq + SEQS_MB].astype(jnp.float32)
        whole_grad = gather_rows(grad_final.astype(jnp.bfloat16)).reshape(length * SEQS_MB, -1)
        grad_down = contract(hidden, whole_grad, 0, 0)
        grad_hidden = contract(whole_grad, full_down, 1, 1)
        gelu_value, gelu_pull = jax.vjp(partial(jax.nn.gelu, approximate=True), gate)
        grad_gate = gelu_pull(grad_hidden * upward)[0]
        grad_ff_in = jnp.concatenate([grad_gate, grad_hidden * activated], axis=1).astype(
            jnp.bfloat16
        )
        grad_ff_weight = contract(whole_two, grad_ff_in, 0, 0)
        grad_normed_two = reduce_rows(grad_ff_in, ff_weight, 1).reshape(rows_in.shape)
        grad_mid_norm, grad_gain_two = norm_back(middle, scale_two, gain_two, grad_normed_two)
        grad_middle = grad_final + grad_mid_norm
        whole_mid = gather_rows(grad_middle.astype(jnp.bfloat16)).reshape(length * SEQS_MB, -1)
        grad_out_weight = contract(mixed_flat, whole_mid, 0, 0)
        grad_mixed = contract(whole_mid, full_out, 1, 1).astype(jnp.bfloat16)
        grad_heads = jnp.moveaxis(grad_mixed.reshape(length, SEQS_MB, heads_local, HEAD_DIM), 1, 0)
        grad_queries, grad_keys, grad_values, grad_diag = attend_backward(
            queries, keys, values, batch_segments, logsum, grad_heads, bias_tile, grad_diag, QBLOCK
        )
        grad_project = jnp.moveaxis(
            jnp.stack([grad_queries, grad_keys, grad_values], axis=2), 0, 1
        ).reshape(length * SEQS_MB, 3 * width_heads)
        grad_attn_weight = contract(whole_one, grad_project, 0, 0)
        grad_normed_one = reduce_rows(grad_project, attn_weight, 1).reshape(rows_in.shape)
        grad_in_norm, grad_gain_one = norm_back(rows_in, scale_one, gain_one, grad_normed_one)
        grad_inputs.append((grad_middle + grad_in_norm).astype(jnp.bfloat16))
        if index == MICRO - 1:
            grad_table = jnp.dot(bucket_onehot.T, grad_diag.T, precision=HIGH)
        else:
            grad_table = jnp.zeros((full_table.shape[0], heads_local), jnp.float32)
        batch_rows_grads = (
            grad_attn_weight,
            grad_ff_weight,
            grad_gain_one,
            grad_gain_two,
            grad_table,
        )
        batch_cols_grads = (grad_out_weight, grad_down)
        batch_rows_grads = (
            lax.psum_scatter(
                batch_rows_grads[0].astype(jnp.bfloat16), "dp", scatter_dimension=0, tiled=True
            ).astype(jnp.float32),
            lax.psum_scatter(
                batch_rows_grads[1].astype(jnp.bfloat16), "dp", scatter_dimension=0, tiled=True
            ).astype(jnp.float32),
            lax.psum_scatter(
                batch_rows_grads[2].astype(jnp.bfloat16), "dp", scatter_dimension=0, tiled=True
            ).astype(jnp.float32),
            lax.psum_scatter(
                batch_rows_grads[3].astype(jnp.bfloat16), "dp", scatter_dimension=0, tiled=True
            ).astype(jnp.float32),
            lax.psum_scatter(
                batch_rows_grads[4].astype(jnp.bfloat16), "dp", scatter_dimension=0, tiled=True
            ).astype(jnp.float32),
        )
        batch_cols_grads = (
            lax.psum_scatter(
                batch_cols_grads[0].astype(jnp.bfloat16), "dp", scatter_dimension=1, tiled=True
            ).astype(jnp.float32),
            lax.psum_scatter(
                batch_cols_grads[1].astype(jnp.bfloat16), "dp", scatter_dimension=1, tiled=True
            ).astype(jnp.float32),
        )
        totals_rows = (
            batch_rows_grads
            if totals_rows is None
            else jax.tree.map(jnp.add, totals_rows, batch_rows_grads)
        )
        totals_cols = (
            batch_cols_grads
            if totals_cols is None
            else jax.tree.map(jnp.add, totals_cols, batch_cols_grads)
        )
    gain_attn_grad, gain_ff_grad = lax.psum((totals_rows[2], totals_rows[3]), "tensor")
    attn_grads = totals_rows[0]
    ff_grads = totals_rows[1]
    output = jnp.concatenate(outputs, axis=1)
    grad_tokens = jnp.concatenate(grad_inputs, axis=1)
    return (
        output,
        grad_tokens,
        gain_attn_grad,
        attn_grads[:, :width_heads],
        attn_grads[:, width_heads : 2 * width_heads],
        attn_grads[:, 2 * width_heads :],
        totals_cols[0],
        totals_rows[4],
        gain_ff_grad,
        ff_grads[:, :width_ff],
        ff_grads[:, width_ff:],
        totals_cols[1],
    )


def solution(mesh):
    in_specs = (
        P("tensor", "dp", None),
        P("tensor", "dp", None),
        P("dp", None),
        P(),
        P("dp"),
        P("dp", "tensor"),
        P("dp", "tensor"),
        P("dp", "tensor"),
        P("tensor", "dp"),
        P("dp", "tensor"),
        P("dp"),
        P("dp", "tensor"),
        P("dp", "tensor"),
        P("tensor", "dp"),
    )
    out_specs = (
        P("tensor", "dp", None),
        P("tensor", "dp", None),
        P("dp"),
        P("dp", "tensor"),
        P("dp", "tensor"),
        P("dp", "tensor"),
        P("tensor", "dp"),
        P("dp", "tensor"),
        P("dp"),
        P("dp", "tensor"),
        P("dp", "tensor"),
        P("tensor", "dp"),
    )
    return jax.shard_map(local, mesh=mesh, in_specs=in_specs, out_specs=out_specs, check_vma=False)
```

profile of v0, /device:TPU:0, one launch (start us, length us, event | category | flops | bytes accessed | tf_op | source)
XLA Modules:
  0.0 3222.0 jit_solution(17448030830305395779)
XLA Ops:
  44.7 21.4 tile.4
  66.1 44.4 %slice.111 = f32[8,2096128]{1,0:T(8,128)} slice(f32[8,2097152]{1,0:T(8,128)} %bitcast.17), slice={[0:8], [1023:2097151]} | slice | bytes 134152192 | tf_op jit(solution)/shard_map/slice | solution.py:61
  110.5 214.9 %reshape.463 = f32[16769024]{0:T(1024)} reshape(f32[8,2096128]{1,0:T(8,128)} %slice.111) | data formatting | bytes 134152192
  325.5 98.5 %reshape.414 = f32[8,1024,2047]{2,1,0:T(8,128)} reshape(f32[16769024]{0:T(1024)} %reshape.463) | data formatting | bytes 134152192 | tf_op jit(solution)/shard_map/reshape | solution.py:62
  424.0 23.4 slice.112
  473.4 60.3 %while.106 = (s32[]{:T(128)}, bf16[2,512,8,64]{1,3,2,0:T(8,128)(2,1)}, f32[2,8,512]{2,1,0:T(8,128)S(1)}, s32[2]{0:T(128)S(1)}, s32[1024]{0:T(1024)S(1)}, /*index...) while((s32[]{:T(128)}, ...), condition=%wide.region_6.7_spmd, body=%wide.region_3.6_spmd.sunk | while | flops 1108078592 | bytes 146943248 | solution.py:100
  557.2 40.5 %reduce-scatter.17.cloned.1.call-done = bf16[256,2048]{1,0:T(8,128)(2,1)} async-done(((bf16[1024,2048]{1,0:T(8,128)(2,1)}), bf16[256,2048]{1,0:T(8,128)(2,1)}) %reduce-scatter.17.cloned.1.call-update) | async-done | bytes 1048592 | tf_op jit(solution)/shard_map/reduce_scatter | solution.py:50
  612.3 43.2 %all-gather.31.cloned.1.call-done = bf16[2048,1280]{1,0:T(8,128)(2,1)} async-done(((bf16[256,1280]{1,0:T(8,128)(2,1)}), bf16[2048,1280]{1,0:T(8,128)(2,1)}) %all-gather.31.cloned.1.call-update) | async-done | bytes 5242896 | tf_op jit(solution)/shard_map/all_gather | solution.py:188
  660.8 51.3 %all-gather.33.cloned.1.call-done = bf16[2048,1280]{1,0:T(8,128)(2,1)} async-done(((bf16[256,1280]{1,0:T(8,128)(2,1)}), bf16[2048,1280]{1,0:T(8,128)(2,1)}) %all-gather.33.cloned.1.call-update) | async-done | bytes 5242896 | tf_op jit(solution)/shard_map/all_gather | solution.py:189
  717.3 48.8 %all-gather.29.cloned.1.call-done = bf16[1024,1,2048]{2,0,1:T(8,128)(2,1)} async-done(((bf16[256,1,2048]{2,0,1:T(8,128)(2,1)}), bf16[1024,1,2048]{2,0,1:T(8,128)(2,1)}) %all-gather.29.cloned.1.call-update) | async-done | bytes 4194320 | tf_op jit(solution)/shard_map/all_gather | solution.py:46
  783.4 37.9 %all-gather.41.cloned.1.call-done = bf16[1024,1,2048]{2,0,1:T(8,128)(2,1)} async-done(((bf16[256,1,2048]{2,0,1:T(8,128)(2,1)}), bf16[1024,1,2048]{2,0,1:T(8,128)(2,1)}) %all-gather.41.cloned.1.call-update) | async-done | bytes 4194320 | tf_op jit(solution)/shard_map/all_gather | solution.py:46
  821.3 58.2 %all-gather.35.cloned.1.call-done = bf16[1280,2048]{1,0:T(8,128)(2,1)} async-done(((bf16[1280,256]{1,0:T(8,128)(2,1)}), bf16[1280,2048]{1,0:T(8,128)(2,1)}) %all-gather.35.cloned.1.call-update) | async-done | bytes 5242896 | tf_op jit(solution)/shard_map/all_gather | solution.py:206
  913.9 50.6 %reduce-scatter.25.cloned.1.call-done = bf16[256,2048]{1,0:T(8,128)(2,1)} async-done(((bf16[1024,2048]{1,0:T(8,128)(2,1)}), bf16[256,2048]{1,0:T(8,128)(2,1)}) %reduce-scatter.25.cloned.1.call-update) | async-done | bytes 1048592 | tf_op jit(solution)/shard_map/reduce_scatter | solution.py:50
  971.1 52.8 %all-gather.43.cloned.1.call-done = bf16[1024,1,2048]{2,0,1:T(8,128)(2,1)} async-done(((bf16[256,1,2048]{2,0,1:T(8,128)(2,1)}), bf16[1024,1,2048]{2,0,1:T(8,128)(2,1)}) %all-gather.43.cloned.1.call-update) | async-done | bytes 4194320 | tf_op jit(solution)/shard_map/all_gather | solution.py:46
  1031.1 628.5 %while.108 = (s32[]{:T(128)}, f32[1024,8,64]{0,2,1:T(8,128)S(1)}, f32[1024,8,64]{0,2,1:T(8,128)}, f32[8,2047]{1,0:T(8,128)S(1)}, bf16[2,512,8,64]{1,3,2,0:T(8,12...) while((s32[]{:T(128)}, f32[1024,8,64]{0,2,1:T(8,128)S(1)}, ...), condition=%wide.region_23.24_spmd.clone, body=%wide.region_20.23_spmd.clone.sunk | while | flops 2731270144 | bytes 535571648 | solution.py:150
  1045.3 19.5 multiply_reduce_fusion.6
  1092.8 121.1 %rev.16 = f32[8,512,1024]{2,1,0:T(8,128)} reverse(bf16[8,512,1024]{2,1,0:T(8,128)(2,1)} %multiply_convert_fusion.10), dimensions={1} | reverse | bytes 25165824 | tf_op jit(solution)/shard_map/while/body/eval_jaxpr/while/body/eval_jaxpr/rev | solution.py:67
  1222.2 32.2 copy.90
  1271.2 18.2 reshape.469
  1289.3 39.1 %reshape.470 = f32[8,512,1535]{2,1,0:T(8,128)} reshape(f32[6287360]{0:T(1024)} %reshape.469) | data formatting | bytes 50298880 | tf_op jit(solution)/shard_map/while/body/eval_jaxpr/while/body/eval_jaxpr/reshape | solution.py:69
  1359.3 19.5 multiply_reduce_fusion.6
  1406.8 121.1 %rev.16 = f32[8,512,1024]{2,1,0:T(8,128)} reverse(bf16[8,512,1024]{2,1,0:T(8,128)(2,1)} %multiply_convert_fusion.10), dimensions={1} | reverse | bytes 25165824 | tf_op jit(solution)/shard_map/while/body/eval_jaxpr/while/body/eval_jaxpr/rev | solution.py:67
  1536.1 32.2 copy.90
  1585.1 18.2 reshape.469
  1603.3 39.1 %reshape.470 = f32[8,512,1535]{2,1,0:T(8,128)} reshape(f32[6287360]{0:T(1024)} %reshape.469) | data formatting | bytes 50298880 | tf_op jit(solution)/shard_map/while/body/eval_jaxpr/while/body/eval_jaxpr/reshape | solution.py:69
  1681.2 50.3 %reduce-scatter.27.cloned.1.call-done = bf16[256,2048]{1,0:T(8,128)(2,1)} async-done(((bf16[1024,2048]{1,0:T(8,128)(2,1)}), bf16[256,2048]{1,0:T(8,128)(2,1)}) %reduce-scatter.27.cloned.1.call-update) | async-done | bytes 1048592 | tf_op jit(solution)/shard_map/reduce_scatter | solution.py:50
  1735.3 52.8 %all-gather.37.cloned.1.call-done = bf16[1024,1,2048]{2,0,1:T(8,128)(2,1)} async-done(((bf16[256,1,2048]{2,0,1:T(8,128)(2,1)}), bf16[1024,1,2048]{2,0,1:T(8,128)(2,1)}) %all-gather.37.cloned.1.call-update) | async-done | bytes 4194320 | tf_op jit(solution)/shard_map/all_gather | solution.py:46
  1807.5 60.3 %while.107 = (s32[]{:T(128)}, bf16[2,512,8,64]{1,3,2,0:T(8,128)(2,1)}, f32[2,8,512]{2,1,0:T(8,128)S(1)}, s32[2]{0:T(128)S(1)}, s32[1024]{0:T(1024)S(1)}, /*index...) while((s32[]{:T(128)}, ...), condition=%wide.region_14.15_spmd, body=%wide.region_11.14_spmd.sunk | while | flops 1108078592 | bytes 146943248 | solution.py:100
  1889.1 40.5 %reduce-scatter.21.cloned.1.call-done = bf16[256,2048]{1,0:T(8,128)(2,1)} async-done(((bf16[1024,2048]{1,0:T(8,128)(2,1)}), bf16[256,2048]{1,0:T(8,128)(2,1)}) %reduce-scatter.21.cloned.1.call-update) | async-done | bytes 1048592 | tf_op jit(solution)/shard_map/reduce_scatter | solution.py:50
  1931.3 53.9 %reduce-scatter.19.cloned.1.call-done = bf16[256,2048]{1,0:T(8,128)(2,1)} async-done(((bf16[1024,2048]{1,0:T(8,128)(2,1)}), bf16[256,2048]{1,0:T(8,128)(2,1)}) %reduce-scatter.19.cloned.1.call-update) | async-done | bytes 1048592 | tf_op jit(solution)/shard_map/reduce_scatter | solution.py:50
  1994.6 49.6 %all-gather.39.cloned.1.call-done = bf16[1024,1,2048]{2,0,1:T(8,128)(2,1)} async-done(((bf16[256,1,2048]{2,0,1:T(8,128)(2,1)}), bf16[1024,1,2048]{2,0,1:T(8,128)(2,1)}) %all-gather.39.cloned.1.call-update) | async-done | bytes 4194320 | tf_op jit(solution)/shard_map/all_gather | solution.py:46
  2061.4 38.0 %all-gather.45.cloned.1.call-done = bf16[1024,1,2048]{2,0,1:T(8,128)(2,1)} async-done(((bf16[256,1,2048]{2,0,1:T(8,128)(2,1)}), bf16[1024,1,2048]{2,0,1:T(8,128)(2,1)}) %all-gather.45.cloned.1.call-update) | async-done | bytes 4194320 | tf_op jit(solution)/shard_map/all_gather | solution.py:46
  2133.5 52.7 %reduce-scatter.29.cloned.1.call-done = bf16[256,2048]{1,0:T(8,128)(2,1)} async-done(((bf16[1024,2048]{1,0:T(8,128)(2,1)}), bf16[256,2048]{1,0:T(8,128)(2,1)}) %reduce-scatter.29.cloned.1.call-update) | async-done | bytes 1048592 | tf_op jit(solution)/shard_map/reduce_scatter | solution.py:50
  2221.5 24.4 all-gather.47.cloned.1.call-done
  2294.8 646.5 %while.109 = (s32[]{:T(128)}, f32[1024,8,64]{0,2,1:T(8,128)S(1)}, f32[1024,8,64]{0,2,1:T(8,128)}, f32[8,2047]{1,0:T(8,128)S(1)}, bf16[2,512,8,64]{1,3,2,0:T(8,12...) while((s32[]{:T(128)}, f32[1024,8,64]{0,2,1:T(8,128)S(1)}, ...), condition=%wide.region_31.32_spmd.clone, body=%wide.region_28.31_spmd.clone.sunk | while | flops 2731270144 | bytes 535604480 | solution.py:150
  2324.6 20.1 multiply_reduce_fusion.7
  2373.2 121.1 %rev.17 = f32[8,512,1024]{2,1,0:T(8,128)} reverse(bf16[8,512,1024]{2,1,0:T(8,128)(2,1)} %multiply_convert_fusion.11), dimensions={1} | reverse | bytes 25165824 | tf_op jit(solution)/shard_map/while/body/eval_jaxpr/while/body/eval_jaxpr/rev | solution.py:67
  2502.6 32.1 copy.91
  2551.6 19.2 reshape.471
  2570.8 39.4 %reshape.472 = f32[8,512,1535]{2,1,0:T(8,128)} reshape(f32[6287360]{0:T(1024)} %reshape.471) | data formatting | bytes 50298880 | tf_op jit(solution)/shard_map/while/body/eval_jaxpr/while/body/eval_jaxpr/reshape | solution.py:69
  2641.1 19.6 multiply_reduce_fusion.7
  2688.7 121.1 %rev.17 = f32[8,512,1024]{2,1,0:T(8,128)} reverse(bf16[8,512,1024]{2,1,0:T(8,128)(2,1)} %multiply_convert_fusion.11), dimensions={1} | reverse | bytes 25165824 | tf_op jit(solution)/shard_map/while/body/eval_jaxpr/while/body/eval_jaxpr/rev | solution.py:67
  2818.1 32.1 copy.91
  2885.0 39.1 %reshape.472 = f32[8,512,1535]{2,1,0:T(8,128)} reshape(f32[6287360]{0:T(1024)} %reshape.471) | data formatting | bytes 50298880 | tf_op jit(solution)/shard_map/while/body/eval_jaxpr/while/body/eval_jaxpr/reshape | solution.py:69
  3015.0 54.1 %reduce-scatter.23.cloned.1.call-done = bf16[256,2048]{1,0:T(8,128)(2,1)} async-done(((bf16[1024,2048]{1,0:T(8,128)(2,1)}), bf16[256,2048]{1,0:T(8,128)(2,1)}) %reduce-scatter.23.cloned.1.call-update) | async-done | bytes 1048592 | tf_op jit(solution)/shard_map/reduce_scatter | solution.py:50
  3080.8 30.6 all-reduce.9
  3121.4 20.2 reduce-scatter.33.cloned.1.call-done
  3141.7 70.5 %reduce-scatter.35.cloned.1.call-done = bf16[256,1536]{1,0:T(8,128)(2,1)} async-done(((bf16[2048,1536]{1,0:T(8,128)(2,1)}), bf16[256,1536]{1,0:T(8,128)(2,1)}) %reduce-scatter.35.cloned.1.call-update) | async-done | bytes 786448 | tf_op jit(solution)/shard_map/reduce_scatter | solution.py:297
  (484 shorter events, 942.3 us)
Async XLA Ops:
  7.2 440.2 %all-gather.21.cloned.1.call-start = ((), (), s32[]{:S(2)}) async-start(), calls=%async_computation.17 | async-start | bytes 2359296 | tf_op jit(solution)/shard_map/all_gather | solution.py:185
  7.9 442.6 %all-gather.23.cloned.1.call-start = ((), (), s32[]{:S(2)}) async-start(), calls=%async_computation.18 | async-start | bytes 2359296 | tf_op jit(solution)/shard_map/all_gather | solution.py:186
  8.7 445.0 %all-gather.25.cloned.1.call-start = ((), (), s32[]{:S(2)}) async-start(), calls=%async_computation.19 | async-start | bytes 2359296 | tf_op jit(solution)/shard_map/all_gather | solution.py:187
  9.4 447.3 %all-gather.19.cloned.1.call-start = ((), (), s32[]{:S(2)}) async-start(), calls=%async_computation.16 | async-start | bytes 5242880 | tf_op jit(solution)/shard_map/all_gather | solution.py:46
  33.1 504.9 %all-gather.27.cloned.1.call-start = ((), (), s32[]{:S(2)}) async-start(), calls=%async_computation.20 | async-start | bytes 2359296 | tf_op jit(solution)/shard_map/all_gather | solution.py:205
  33.7 564.0 %reduce-scatter.17.cloned.1.call-start = ((), (), s32[]{:S(2)}) async-start(), calls=%async_computation.21 | async-start | bytes 5242880 | tf_op jit(solution)/shard_map/reduce_scatter | solution.py:50
  544.4 111.0 %all-gather.31.cloned.1.call-start = ((), (), s32[]{:S(2)}) async-start(), calls=%async_computation.23 | async-start | bytes 5898240 | tf_op jit(solution)/shard_map/all_gather | solution.py:188
  545.2 166.9 %all-gather.33.cloned.1.call-start = ((), (), s32[]{:S(2)}) async-start(), calls=%async_computation.24 | async-start | bytes 5898240 | tf_op jit(solution)/shard_map/all_gather | solution.py:189
  545.9 220.2 %all-gather.29.cloned.1.call-start = ((), (), s32[]{:S(2)}) async-start(), calls=%async_computation.22 | async-start | bytes 5242880 | tf_op jit(solution)/shard_map/all_gather | solution.py:46
  557.2 410.0 %copy-start.48 = (f32[8,1,256]{2,1,0:T(1,128)}, f32[8,1,256]{2,1,0:T(1,128)S(1)}, u32[]{:S(2)}) copy-start(f32[8,1,256]{2,1,0:T(1,128)S(1)} %convert_element_type.359) | copy-start | bytes 24580
  599.4 367.8 %copy-start.59 = (f32[256]{0:T(256)}, f32[256]{0:T(256)S(1)}, u32[]{:S(2)}) copy-start(f32[256]{0:T(256)S(1)} %add_rsqrt_fusion.2) | copy-start | bytes 3076
  602.0 219.3 %all-gather.41.cloned.1.call-start = ((), (), s32[]{:S(2)}) async-start(), calls=%async_computation.31 | async-start | bytes 5242880 | tf_op jit(solution)/shard_map/all_gather | solution.py:46
  611.5 268.0 %all-gather.35.cloned.1.call-start = ((), (), s32[]{:S(2)}) async-start(), calls=%async_computation.25 | async-start | bytes 5898240 | tf_op jit(solution)/shard_map/all_gather | solution.py:206
  612.2 352.3 %reduce-scatter.25.cloned.1.call-start = ((), (), s32[]{:S(2)}) async-start(), calls=%async_computation.32 | async-start | bytes 5242880 | tf_op jit(solution)/shard_map/reduce_scatter | solution.py:50
  913.4 110.4 %all-gather.43.cloned.1.call-start = ((), (), s32[]{:S(2)}) async-start(), calls=%async_computation.33 | async-start | bytes 5242880 | tf_op jit(solution)/shard_map/all_gather | solution.py:46
  967.2 62.8 %copy-start.71 = (f32[256]{0:T(256)}, f32[256]{0:T(256)S(1)}, u32[]{:S(2)}) copy-start(f32[256]{0:T(256)S(1)} %broadcast_multiply_fusion.3) | copy-start | bytes 3076
  971.0 760.5 %reduce-scatter.27.cloned.1.call-start = ((), (), s32[]{:S(2)}) async-start(), calls=%async_computation.34 | async-start | bytes 5242880 | tf_op jit(solution)/shard_map/reduce_scatter | solution.py:50
  1678.6 109.4 %all-gather.37.cloned.1.call-start = ((), (), s32[]{:S(2)}) async-start(), calls=%async_computation.27 | async-start | bytes 5242880 | tf_op jit(solution)/shard_map/all_gather | solution.py:46
  1681.2 118.2 %copy-start.14 = (bf16[256,1,2048]{2,0,1:T(8,128)(2,1)}, bf16[256,1,2048]{2,0,1:T(8,128)(2,1)S(1)}, u32[]{:S(2)}) copy-start(bf16[256,1,2048]{2,0,1:T(8,128)(2,1)S(1)} %get-tuple-element.808) | copy-start | bytes 3145732
  1681.2 118.2 %copy-start.61 = (f32[256]{0:T(256)}, f32[256]{0:T(256)S(1)}, u32[]{:S(2)}) copy-start(f32[256]{0:T(256)S(1)} %add_rsqrt_fusion.1) | copy-start | bytes 3076
  1735.2 194.4 %reduce-scatter.21.cloned.1.call-start = ((), (), s32[]{:S(2)}) async-start(), calls=%async_computation.28 | async-start | bytes 5242880 | tf_op jit(solution)/shard_map/reduce_scatter | solution.py:50
  1876.8 108.4 %reduce-scatter.19.cloned.1.call-start = ((), (), s32[]{:S(2)}) async-start(), calls=%async_computation.26 | async-start | bytes 5242880 | tf_op jit(solution)/shard_map/reduce_scatter | solution.py:50
  1888.4 96.7 %copy-start.20 = (bf16[256,1,2048]{2,0,1:T(8,128)(2,1)S(1)}, bf16[256,1,2048]{2,0,1:T(8,128)(2,1)}, u32[]{:S(2)}) copy-start(bf16[256,1,2048]{2,0,1:T(8,128)(2,1)} %copy-done.17) | copy-start | bytes 3145732
  1888.4 96.7 %copy-start.26 = (bf16[256,2048]{1,0:T(8,128)(2,1)S(1)}, bf16[256,2048]{1,0:T(8,128)(2,1)}, u32[]{:S(2)}) copy-start(bf16[256,2048]{1,0:T(8,128)(2,1)} %reduce-scatter.17.cloned.1.call-done) | copy-start | bytes 3145732
  1888.4 96.7 %copy-start.49 = (f32[8,1,256]{2,1,0:T(1,128)S(1)}, f32[8,1,256]{2,1,0:T(1,128)}, u32[]{:S(2)}) copy-start(f32[8,1,256]{2,1,0:T(1,128)} %copy-done.48) | copy-start | bytes 24580
  1888.4 96.7 %copy-start.55 = (f32[8,1,256]{2,1,0:T(1,128)S(1)}, f32[8,1,256]{2,1,0:T(1,128)}, u32[]{:S(2)}) copy-start(f32[8,1,256]{2,1,0:T(1,128)} %copy-done.53) | copy-start | bytes 24580
  1888.4 96.7 %copy-start.60 = (f32[256]{0:T(256)S(1)}, f32[256]{0:T(256)}, u32[]{:S(2)}) copy-start(f32[256]{0:T(256)} %copy-done.59) | copy-start | bytes 3076
  1888.5 96.7 %copy-start.65 = (f32[256]{0:T(256)S(1)}, f32[256]{0:T(256)}, u32[]{:S(2)}) copy-start(f32[256]{0:T(256)} %copy-done.63) | copy-start | bytes 3076
  1888.5 96.7 %copy-start.72 = (f32[256]{0:T(256)S(1)}, f32[256]{0:T(256)}, u32[]{:S(2)}) copy-start(f32[256]{0:T(256)} %copy-done.71) | copy-start | bytes 3076
  1888.5 155.7 %all-gather.39.cloned.1.call-start = ((), (), s32[]{:S(2)}) async-start(), calls=%async_computation.29 | async-start | bytes 5242880 | tf_op jit(solution)/shard_map/all_gather | solution.py:46
  1931.3 257.8 %copy-start.57 = (f32[256]{0:T(256)}, f32[256]{0:T(256)S(1)}, u32[]{:S(2)}) copy-start(f32[256]{0:T(256)S(1)} %add_rsqrt_fusion) | copy-start | bytes 3076
  1991.3 108.2 %all-gather.45.cloned.1.call-start = ((), (), s32[]{:S(2)}) async-start(), calls=%async_computation.35 | async-start | bytes 5242880 | tf_op jit(solution)/shard_map/all_gather | solution.py:46
  1994.6 191.6 %reduce-scatter.29.cloned.1.call-start = ((), (), s32[]{:S(2)}) async-start(), calls=%async_computation.36 | async-start | bytes 5242880 | tf_op jit(solution)/shard_map/reduce_scatter | solution.py:50
  2133.3 112.6 %all-gather.47.cloned.1.call-start = ((), (), s32[]{:S(2)}) async-start(), calls=%async_computation.37 | async-start | bytes 5242880 | tf_op jit(solution)/shard_map/all_gather | solution.py:46
  2193.0 807.4 %reduce-scatter.45.cloned.1.call-start = ((), (), s32[]{:S(2)}) async-start(), calls=%async_computation.45 | async-start | bytes 5898240 | tf_op jit(solution)/shard_map/reduce_scatter | solution.py:317
  2203.1 797.4 %reduce-scatter.47.cloned.1.call-start = ((), (), s32[]{:S(2)}) async-start(), calls=%async_computation.46 | async-start | bytes 5898240 | tf_op jit(solution)/shard_map/reduce_scatter | solution.py:317
  2214.4 789.6 %reduce-scatter.37.cloned.1.call-start = ((), (), s32[]{:S(2)}) async-start(), calls=%async_computation.41 | async-start | bytes 2359296 | tf_op jit(solution)/shard_map/reduce_scatter | solution.py:314
  2221.5 782.5 %reduce-scatter.39.cloned.1.call-start = ((), (), s32[]{:S(2)}) async-start(), calls=%async_computation.42 | async-start | bytes 2359296 | tf_op jit(solution)/shard_map/reduce_scatter | solution.py:314
  2251.8 754.2 %reduce-scatter.41.cloned.1.call-start = ((), (), s32[]{:S(2)}) async-start(), calls=%async_computation.43 | async-start | bytes 11796480 | tf_op jit(solution)/shard_map/reduce_scatter | solution.py:300
  2269.4 736.6 %reduce-scatter.43.cloned.1.call-start = ((), (), s32[]{:S(2)}) async-start(), calls=%async_computation.44 | async-start | bytes 11796480 | tf_op jit(solution)/shard_map/reduce_scatter | solution.py:300
  2287.3 725.8 %reduce-scatter.31.cloned.1.call-start = ((), (), s32[]{:S(2)}) async-start(), calls=%async_computation.38 | async-start | bytes 5242880 | tf_op jit(solution)/shard_map/reduce_scatter | solution.py:50
  2960.3 108.7 %reduce-scatter.23.cloned.1.call-start = ((), (), s32[]{:S(2)}) async-start(), calls=%async_computation.30 | async-start | bytes 5242880 | tf_op jit(solution)/shard_map/reduce_scatter | solution.py:50
  2971.7 170.0 %reduce-scatter.33.cloned.1.call-start = ((), (), s32[]{:S(2)}) async-start(), calls=%async_computation.39 | async-start | bytes 7077888 | tf_op jit(solution)/shard_map/reduce_scatter | solution.py:297
  2984.6 227.5 %reduce-scatter.35.cloned.1.call-start = ((), (), s32[]{:S(2)}) async-start(), calls=%async_computation.40 | async-start | bytes 7077888 | tf_op jit(solution)/shard_map/reduce_scatter | solution.py:297
  3008.2 60.9 %copy-start.22 = (bf16[256,1,2048]{2,1,0:T(2,128)(2,1)S(1)}, bf16[256,1,2048]{2,1,0:T(2,128)(2,1)}, u32[]{:S(2)}) copy-start(bf16[256,1,2048]{2,1,0:T(2,128)(2,1)} %get-tuple-element.835) | copy-start | bytes 3145732
  3008.2 60.9 %copy-start.50 = (f32[8,1,256]{2,1,0:T(1,128)S(1)}, f32[8,1,256]{2,1,0:T(1,128)}, u32[]{:S(2)}) copy-start(f32[8,1,256]{2,1,0:T(1,128)} %copy-done.48) | copy-start | bytes 24580
  3008.2 60.9 %copy-start.58 = (f32[256]{0:T(256)S(1)}, f32[256]{0:T(256)}, u32[]{:S(2)}) copy-start(f32[256]{0:T(256)} %copy-done.57) | copy-start | bytes 3076
  3008.2 60.9 %copy-start.70 = (f32[256]{0:T(256)S(1)}, f32[256]{0:T(256)}, u32[]{:S(2)}) copy-start(f32[256]{0:T(256)} %copy-done.69) | copy-start | bytes 3076
  (88 other events, 861.0 us)
Sparse Core Ops, SparseCore 0:
  9.6 31.8 all-gather.20
  43.1 28.6 all-gather.22
  73.4 28.5 all-gather.24
  104.3 52.1 all-gather.18
  157.9 30.8 all-gather.26
  544.6 53.0 reduce-scatter.16
  599.4 56.0 all-gather.30
  657.2 54.8 all-gather.32
  714.6 51.4 all-gather.28
  768.6 52.6 all-gather.40
  823.0 56.4 all-gather.34
  913.6 50.9 reduce-scatter.24
  971.1 52.6 all-gather.42
  1678.8 52.6 reduce-scatter.26
  1735.3 52.6 all-gather.36
  1876.9 52.6 reduce-scatter.20
  1932.4 52.6 reduce-scatter.18
  1991.4 52.6 all-gather.38
  2046.7 52.6 all-gather.44
  2133.4 52.7 reduce-scatter.28
  2193.2 52.6 all-gather.46
  2248.2 59.8 reduce-scatter.44
  2310.4 58.2 reduce-scatter.46
  2370.9 34.1 reduce-scatter.36
  2408.0 34.3 reduce-scatter.38
  2444.5 107.9 reduce-scatter.40
  2554.6 107.7 reduce-scatter.42
  2960.5 52.5 reduce-scatter.30
  3016.3 52.6 reduce-scatter.22
  3071.2 70.4 reduce-scatter.32
  3144.0 68.1 reduce-scatter.34
where the time goes:
time: 3290 us; the launch traced here: 3220 us
  local copies, waits for them, and re-layouts  1490 us (45%)
  waiting for transfers between devices  899 us (27%)
  matrix products  513 us (16%)
  other arithmetic  190 us (6%)
  blocking collectives  73.2 us (2%)
  loops' own time  35.5 us (1%)
    rev x4, local copies, waits for them, and re-layouts, fold_diagonals(): padded = jnp.pad(grads[:, ::-1, :], ((0, 0), (0, 0), (0, rows)))  484 us
    reduce_scatter x8, waiting for transfers between devices, reduce_rows(): lax.psum_scatter(contract(left, weight, 1, right_dim).astype(jnp.bfloat16...  346 us
    all_gather x8, waiting for transfers between devices, gather_rows(): return lax.all_gather(part, 'tensor', axis=0, tiled=True)  304 us
    while x68, local copies, waits for them, and re-layouts  269 us
    unnamed x167, local copies, waits for them, and re-layouts  265 us
    dot_general x20, matrix products, contract(): lax.dot_general(left, right, (((left_dim,), (right_dim,)), ((), ())), pre...  215 us
    reshape x4, local copies, waits for them, and re-layouts, fold_diagonals(): return jnp.sum(flat.reshape(heads, rows, keys + rows - 1), axis=1)  157 us
    dot_general x8, matrix products, block_scores(): jnp.einsum('qhd,khd->hqk', block_queries, seq_keys, preferred_element_typ...  126 us
  transfers between devices with their start and end apart: 31, of which 20 were waited for; matrix products, arithmetic and copies ran while one was open for 41% of the time, Pallas kernels for 0%

commit v1 on v0

v1 whole, which is shorter than its diff:
```python
import functools
import jax
import jax.numpy as jnp
from jax import lax
from jax.experimental import pallas as pl
from jax.experimental.pallas import tpu as pltpu
from jax.sharding import PartitionSpec as P

HD=64
B=256
BIG=1e30
F32=jnp.float32; BF=jnp.bfloat16

def nt(a,b): return lax.dot_general(a,b,(((1,),(1,)),((),())),preferred_element_type=F32)
def nn(a,b): return lax.dot_general(a,b,(((1,),(0,)),((),())),preferred_element_type=F32)

def strips_kernel(w_ref, out_ref):
    nrb=w_ref.shape[1]
    def body(i,_):
        w=w_ref[0,pl.ds(i,1),:]
        t=pltpu.roll(jnp.broadcast_to(w,(B,2*B)),0,1,stride=1,stride_axis=0)
        out_ref[0,pl.ds(pl.multiple_of(i*B,B),B),:]=t[:,:B]
        return 0
    lax.fori_loop(0,nrb,body,0)

def strips_call(w,n):
    heads=w.shape[0]
    return pl.pallas_call(strips_kernel,grid=(heads,),
        in_specs=[pl.BlockSpec((1,2*n-1,2*B),lambda h:(h,0,0))],
        out_specs=pl.BlockSpec((1,(2*n-1)*B,B),lambda h:(h,0,0)),
        out_shape=jax.ShapeDtypeStruct((heads,(2*n-1)*B,B),F32),
        compiler_params=pltpu.CompilerParams(vmem_limit_bytes=32<<20),name="bias_strips")(w)

def fwd_kernel(n,act_ref,blk_ref,qkv_ref,fq_ref,fk_ref,bias_ref,o_ref,lse_ref,qx,kx,vx,s_scr,m_scr,o_scr):
    lane=lax.broadcasted_iota(jnp.int32,(1,128),1)
    q=qkv_ref[:,0:128]; k=qkv_ref[:,128:256]; v=qkv_ref[:,256:384]
    vt=v.T
    for h in range(2):
        own=(lane<HD) if h==0 else (lane>=HD)
        qx[h]=jnp.where(own,q,fq_ref[...])
        kx[h]=jnp.where(own,k,fk_ref[...])
        vx[h]=jnp.concatenate([vt[h*HD:(h+1)*HD],jnp.ones((16,vt.shape[1]),BF)],axis=0)
    def row(qi,_):
        qs=pl.ds(pl.multiple_of(qi*B,B),B)
        m_scr[...]=jnp.full_like(m_scr,-3e38)
        o_scr[...]=jnp.zeros_like(o_scr)
        def p1(kb,_):
            @pl.when(act_ref[qi*n+kb]!=0)
            def _():
                ks=pl.ds(pl.multiple_of(kb*B,B),B)
                bs=pl.ds(pl.multiple_of((blk_ref[kb]-blk_ref[qi]+n-1)*B,B),B)
                for h in range(2):
                    s=nt(kx[h,ks,:],qx[h,qs,:])+bias_ref[h,bs,:]
                    s_scr[h,ks,:]=s
                    m_scr[h]=jnp.maximum(m_scr[h],jnp.max(s.reshape(B//8,8,B),axis=0))
            return 0
        lax.fori_loop(0,n,p1,0)
        ms=[jnp.max(m_scr[h],axis=0,keepdims=True) for h in range(2)]
        def p2(kb,_):
            @pl.when(act_ref[qi*n+kb]!=0)
            def _():
                ks=pl.ds(pl.multiple_of(kb*B,B),B)
                for h in range(2):
                    p=jnp.exp(s_scr[h,ks,:]-ms[h]).astype(BF)
                    o_scr[h]+=nn(vx[h,:,ks],p)
            return 0
        lax.fori_loop(0,n,p2,0)
        outs=[]
        for h in range(2):
            tot=o_scr[h,HD:HD+1,:]
            outs.append(o_scr[h,0:HD,:]/tot)
            lse_ref[0,pl.ds(h,1),qs]=ms[h]+jnp.log(tot)
        o_ref[qs,:]=jnp.concatenate(outs,axis=0).T.astype(BF)
        return 0
    lax.fori_loop(0,n,row,0)

def attend_fwd(qkv,fq,fk,bias,act,blk):
    L,w3=qkv.shape; n=L//B; np_=w3//384
    H2=2
    return pl.pallas_call(functools.partial(fwd_kernel,n),
        grid_spec=pltpu.PrefetchScalarGridSpec(num_scalar_prefetch=2,grid=(np_,),
          in_specs=[pl.BlockSpec((L,384),lambda p,*_:(0,p)),
                    pl.BlockSpec((L,128),lambda p,*_:(0,0)),
                    pl.BlockSpec((L,128),lambda p,*_:(0,0)),
                    pl.BlockSpec((2,(2*n-1)*B,B),lambda p,*_:(p,0,0))],
          out_specs=[pl.BlockSpec((L,128),lambda p,*_:(0,p)),
                     pl.BlockSpec((1,2,L),lambda p,*_:(p,0,0))],
          scratch_shapes=[pltpu.VMEM((2,L,128),BF),pltpu.VMEM((2,L,128),BF),pltpu.VMEM((2,HD+16,L),BF),
                          pltpu.VMEM((2,L,B),F32),pltpu.VMEM((2,8,B),F32),pltpu.VMEM((2,HD+16,B),F32)]),
        out_shape=[jax.ShapeDtypeStruct((L,np_*128),BF),jax.ShapeDtypeStruct((np_,2,L),F32)],
        compiler_params=pltpu.CompilerParams(vmem_limit_bytes=40<<20),
        cost_estimate=pl.CostEstimate(flops=int(np_*2*L*L*128*2*2),bytes_accessed=int(L*w3*2+np_*2*(2*n-1)*B*B*4),transcendentals=np_*2*L*L),
        name="attend_forward")(act,blk,qkv,fq,fk,bias)

def bwd_kernel(n,act_ref,blk_ref,qkv_ref,fq_ref,fk_ref,bias_ref,lse_ref,o_ref,do_ref,g_ref,fold_ref,qx,kx,v0,kt,delta,dk,dv,dqt,diag):
    lane=lax.broadcasted_iota(jnp.int32,(1,128),1)
    q=qkv_ref[:,0:128]; k=qkv_ref[:,128:256]; v=qkv_ref[:,256:384]
    for h in range(2):
        own=(lane<HD) if h==0 else (lane>=HD)
        qx[h]=jnp.where(own,q,fq_ref[...])
        kx[h]=jnp.where(own,k,fk_ref[...])
        v0[h]=jnp.where(own,v,jnp.zeros_like(v))
    kt[...]=k.T
    prod=(o_ref[...].astype(F32)*do_ref[...].astype(F32)).T
    for h in range(2):
        delta[h:h+1,:]=jnp.sum(prod[h*HD:(h+1)*HD],axis=0,keepdims=True)
    dk[...]=jnp.zeros_like(dk); dv[...]=jnp.zeros_like(dv); diag[...]=jnp.zeros_like(diag)
    def row(qi,_):
        qs=pl.ds(pl.multiple_of(qi*B,B),B)
        dqt[...]=jnp.zeros_like(dqt)
        lses=[lse_ref[0,pl.ds(h,1),qs] for h in range(2)]
        dels=[delta[pl.ds(h,1),qs] for h in range(2)]
        def inner(kb,_):
            @pl.when(act_ref[qi*n+kb]!=0)
            def _():
                ks=pl.ds(pl.multiple_of(kb*B,B),B)
                bs=pl.ds(pl.multiple_of((blk_ref[kb]-blk_ref[qi]+n-1)*B,B),B)
                dob=do_ref[qs,:]; qb=qkv_ref[qs,0:128]
                for h in range(2):
                    s=nt(kx[h,ks,:],qx[h,qs,:])+bias_ref[h,bs,:]
                    dp=nt(v0[h,ks,:],dob)
                    p=jnp.exp(s-lses[h])
                    ds=p*(dp-dels[h])
                    pb=p.astype(BF); dsb=ds.astype(BF)
                    diag[h,bs,:]+=ds
                    dv[h,ks,:]+=nn(pb,dob)
                    dk[h,ks,:]+=nn(dsb,qb)
                    dqt[h]+=nn(kt[h*HD:(h+1)*HD,ks],dsb)
            return 0
        lax.fori_loop(0,n,inner,0)
        g_ref[qs,0:128]=jnp.concatenate([dqt[0],dqt[1]],axis=0).T.astype(BF)
        return 0
    lax.fori_loop(0,n,row,0)
    first=lane<HD
    g_ref[:,128:256]=jnp.where(first,dk[0],dk[1]).astype(BF)
    g_ref[:,256:384]=jnp.where(first,dv[0],dv[1]).astype(BF)
    for h in range(2):
        def fold(i,_):
            a=diag[h,pl.ds(pl.multiple_of(i*B,B),B),:]
            zero=jnp.zeros((8,B),F32)
            acc=jnp.zeros((8,2*B),F32)
            for g in range(B//8):
                part=jnp.concatenate([a[8*g:8*g+8],zero],axis=1)
                acc=acc+(pltpu.roll(part,2*B-8*g,1) if g else part)
            tot=acc[0:1]
            for r in range(1,8):
                tot=tot+pltpu.roll(acc[r:r+1],2*B-r,1)
            fold_ref[0,h,pl.ds(i,1),:]=tot
            return 0
        lax.fori_loop(0,2*n-1,fold,0)

def attend_bwd(qkv,fq,fk,bias,lse,o,do,act,blk):
    L,w3=qkv.shape; n=L//B; np_=w3//384
    return pl.pallas_call(functools.partial(bwd_kernel,n),
        grid_spec=pltpu.PrefetchScalarGridSpec(num_scalar_prefetch=2,grid=(np_,),
          in_specs=[pl.BlockSpec((L,384),lambda p,*_:(0,p)),
                    pl.BlockSpec((L,128),lambda p,*_:(0,0)),
                    pl.BlockSpec((L,128),lambda p,*_:(0,0)),
                    pl.BlockSpec((2,(2*n-1)*B,B),lambda p,*_:(p,0,0)),
                    pl.BlockSpec((1,2,L),lambda p,*_:(p,0,0)),
                    pl.BlockSpec((L,128),lambda p,*_:(0,p)),
                    pl.BlockSpec((L,128),lambda p,*_:(0,p))],
          out_specs=[pl.BlockSpec((L,384),lambda p,*_:(0,p)),
                     pl.BlockSpec((1,2,2*n-1,2*B),lambda p,*_:(p,0,0,0))],
          scratch_shapes=[pltpu.VMEM((2,L,128),BF),pltpu.VMEM((2,L,128),BF),pltpu.VMEM((2,L,128),BF),
                          pltpu.VMEM((128,L),BF),pltpu.VMEM((2,L),F32),
                          pltpu.VMEM((2,L,128),F32),pltpu.VMEM((2,L,128),F32),pltpu.VMEM((2,HD,B),F32),
                          pltpu.VMEM((2,(2*n-1)*B,B),F32)]),
        out_shape=[jax.ShapeDtypeStruct((L,w3),BF),jax.ShapeDtypeStruct((np_,2,2*n-1,2*B),F32)],
        compiler_params=pltpu.CompilerParams(vmem_limit_bytes=48<<20),
        cost_estimate=pl.CostEstimate(flops=int(np_*2*L*L*128*2*5),bytes_accessed=int(L*w3*4+np_*2*(2*n-1)*B*B*4),transcendentals=np_*2*L*L),
        name="attend_backward")(act,blk,qkv,fq,fk,bias,lse,o,do)

EPSILON = 1e-06
MICRO = 2


def norm_scale(rows):
    return lax.rsqrt(jnp.mean(rows * rows, axis=-1, keepdims=True) + EPSILON)


def norm_back(rows, scale, gain, grad_normed):
    scaled = gain * grad_normed
    inner = jnp.mean(scaled * rows, axis=-1, keepdims=True)
    grad_rows = scale * scaled - rows * scale * scale * scale * inner
    return grad_rows, jnp.sum(grad_normed * rows * scale, axis=0)


def tn(left, right):
    return lax.dot_general(left, right, (((0,), (0,)), ((), ())), preferred_element_type=F32)


def hop(part, bit, count):
    return lax.ppermute(part, "tensor", [(i, i ^ bit) for i in range(count)])


def gather_rows(part, count):
    if count != 4:
        return lax.all_gather(part, "tensor", axis=0, tiled=True)
    half = part.shape[0] // 2
    from_x = hop(part, 1, count)
    from_y = hop(part, 2, count)
    diag_low = hop(from_y[:half], 1, count)
    diag_high = hop(from_x[half:], 2, count)
    return jnp.concatenate([part, from_x, from_y, diag_low, diag_high], axis=0)


def reduce_rows(partial, count):
    if count != 4:
        return lax.psum_scatter(partial, "tensor", scatter_dimension=0, tiled=True).astype(F32)
    size = partial.shape[0] // 4
    half = size // 2
    own, to_x, to_y, to_d = (partial[i * size : (i + 1) * size] for i in range(4))
    x_first = hop(jnp.concatenate([to_x[:half], to_d[:half]], axis=0), 1, count)
    y_first = hop(jnp.concatenate([to_y[half:], to_d[half:]], axis=0), 2, count)
    x_second = hop((to_x[half:].astype(F32) + y_first[half:].astype(F32)).astype(BF), 1, count)
    y_second = hop((to_y[:half].astype(F32) + x_first[half:].astype(F32)).astype(BF), 2, count)
    low = own[:half].astype(F32) + x_first[:half].astype(F32) + y_second.astype(F32)
    high = own[half:].astype(F32) + y_first[:half].astype(F32) + x_second.astype(F32)
    return jnp.concatenate([low, high], axis=0)


def gelu_parts(gate):
    c = 0.7978845608028654
    square = gate * gate
    th = jnp.tanh(c * gate * (1.0 + 0.044715 * square))
    value = 0.5 * gate * (1.0 + th)
    slope = 0.5 * (1.0 + th) + 0.5 * gate * (1.0 - th * th) * c * (1.0 + 3 * 0.044715 * square)
    return value, slope


def local(
    count_dp,
    count,
    tokens,
    cotangent,
    doc_lengths,
    rel_bucket,
    gain_attn,
    w_query,
    w_key,
    w_value,
    w_out,
    rel_table,
    gain_ff,
    w_gate,
    w_up,
    w_down,
):
    slots = tokens.shape[0]
    length = slots * count
    blocks = length // B
    rows_w, width = w_query.shape
    width_ff = w_gate.shape[1]
    pairs = width // 128
    heads = width // HD
    buckets_local = rel_table.shape[0]
    buckets = buckets_local * count_dp
    docs = doc_lengths.shape[1]

    def spread(part):
        return lax.all_gather(part, "dp", axis=0, tiled=True)

    local_qkv = jnp.stack(
        [w.reshape(rows_w, pairs, 128) for w in (w_query, w_key, w_value)], axis=2
    ).reshape(rows_w, 3 * width)
    small = spread(jnp.concatenate([gain_attn, gain_ff, rel_table.reshape(-1)])[None])
    full_qkv = spread(local_qkv)
    full_out = spread(w_out.T)
    full_ff = spread(jnp.concatenate([w_gate, w_up], axis=1))
    full_down = spread(w_down.T)
    gain_one = small[:, :rows_w].reshape(1, -1).astype(F32)
    gain_two = small[:, rows_w : 2 * rows_w].reshape(1, -1).astype(F32)
    table = small[:, 2 * rows_w :].reshape(buckets, heads)

    reverse = jnp.concatenate([jnp.full((1,), -1, jnp.int32), rel_bucket[::-1]])
    onehot = reverse[None, :] == jnp.arange(buckets, dtype=jnp.int32)[:, None]
    offsets = lax.dot_general(
        table, onehot.astype(BF), (((0,), (0,)), ((), ())), preferred_element_type=F32
    ).reshape(heads, 2 * blocks, B)
    tiles = 2 * blocks - 1
    ahead = offsets[:, ::-1]
    bias = strips_call(jnp.concatenate([ahead[:, :tiles], ahead[:, 1:]], axis=2), blocks)

    order = jnp.arange(blocks, dtype=jnp.int32)
    if count == 4:
        order = order ^ lax.axis_index("tensor").astype(jnp.int32)
    positions = (order[:, None] * B + jnp.arange(B, dtype=jnp.int32)[None]).reshape(-1)
    ends = jnp.cumsum(doc_lengths, axis=1)
    lane = jnp.arange(128, dtype=jnp.int32) % HD

    xs, scales, wholes, cots, attends = [], [], [], [], []
    for m in range(MICRO):
        rows = tokens[:, m].astype(F32)
        scale = norm_scale(rows)
        xs.append(rows)
        scales.append(scale)
        wholes.append(gather_rows((rows * scale * gain_one).astype(BF), count))
    for m in range(MICRO):
        cots.append(gather_rows(cotangent[:, m], count))

    saved = []
    for m in range(MICRO):
        number = jnp.sum((positions[:, None] >= ends[m][None, :]).astype(jnp.int32), axis=1)
        by_block = number.reshape(blocks, B)
        least, most = by_block.min(axis=1), by_block.max(axis=1)
        active = (least[:, None] <= most[None, :]) & (least[None, :] <= most[:, None])
        active = active.astype(jnp.int32).reshape(-1)
        same = number[:, None] == lane[None, :]
        feat_q = same.astype(BF)
        feat_k = jnp.where(same | (lane >= docs)[None, :], 0.0, -BIG).astype(BF)
        qkv = nn(wholes[m], full_qkv).astype(BF)
        mixed, logsum = attend_fwd(qkv, feat_q, feat_k, bias, active, order)
        middle = xs[m] + reduce_rows(nt(mixed, full_out).astype(BF), count)
        scale_two = norm_scale(middle)
        whole_two = gather_rows((middle * scale_two * gain_two).astype(BF), count)
        saved.append((qkv, feat_q, feat_k, active, mixed, logsum, middle, scale_two, whole_two))

    ff_saved, outputs, mid_saved = [], [], []
    for m in range(MICRO):
        middle, scale_two, whole_two = saved[m][6:]
        gate_up = nn(whole_two, full_ff).astype(BF)
        gate = gate_up[:, :width_ff].astype(F32)
        up = gate_up[:, width_ff:].astype(F32)
        value, slope = gelu_parts(gate)
        hidden = (value * up).astype(BF)
        grad_hidden = nn(cots[m], full_down)
        grad_ff = jnp.concatenate([grad_hidden * up * slope, grad_hidden * value], axis=1).astype(BF)
        grad_normed = reduce_rows(nt(grad_ff, full_ff).astype(BF), count)
        grad_norm, grad_gain_two = norm_back(middle, scale_two, gain_two, grad_normed)
        grad_middle = cotangent[:, m].astype(F32) + grad_norm
        whole_mid = gather_rows(grad_middle.astype(BF), count)
        mid_saved.append((grad_middle, whole_mid, grad_gain_two))
        ff_saved.append((hidden, grad_ff))
    for m in range(MICRO):
        ff_rows = reduce_rows(nt(ff_saved[m][0], full_down).astype(BF), count)
        outputs.append((saved[m][6] + ff_rows).astype(BF))

    def over_both(lefts, rights):
        total = tn(lefts[0], rights[0])
        for left, right in zip(lefts[1:], rights[1:]):
            total = total + tn(left, right)
        return lax.psum_scatter(total.astype(BF), "dp", scatter_dimension=0, tiled=True).astype(F32)

    grad_ff_weight = over_both([s[8] for s in saved], [f[1] for f in ff_saved])
    grad_down = over_both(cots, [f[0] for f in ff_saved])

    projects, folds, grad_inputs, gains_one = [], [], [], []
    for m in range(MICRO):
        qkv, feat_q, feat_k, active, mixed, logsum = saved[m][:6]
        grad_middle, whole_mid, _ = mid_saved[m]
        grad_mixed = nn(whole_mid, full_out).astype(BF)
        project, fold = attend_bwd(
            qkv, feat_q, feat_k, bias, logsum, mixed, grad_mixed, active, order
        )
        projects.append(project)
        folds.append(fold)
        grad_normed = reduce_rows(nt(project, full_qkv).astype(BF), count)
        grad_norm, grad_gain_one = norm_back(xs[m], scales[m], gain_one, grad_normed)
        grad_inputs.append((grad_middle + grad_norm).astype(BF))
        gains_one.append(grad_gain_one)
    grad_out = over_both([s[1] for s in mid_saved], [s[4] for s in saved])
    grad_qkv = over_both(wholes, projects)

    fold = sum(folds).reshape(heads, tiles, 2 * B)
    zero = jnp.zeros((heads, 1, B), F32)
    by_offset = (
        jnp.concatenate([fold[:, :, :B], zero], axis=1)
        + jnp.concatenate([zero, fold[:, :, B:]], axis=1)
    )[:, ::-1].reshape(heads, 2 * length)
    grad_table = lax.dot_general(
        onehot.astype(F32), by_offset, (((1,), (1,)), ((), ())), precision=lax.Precision.HIGHEST
    )
    gain_grads = jnp.concatenate(
        [
            sum(gains_one).reshape(count_dp, rows_w),
            sum(s[2] for s in mid_saved).reshape(count_dp, rows_w),
            grad_table.reshape(count_dp, buckets_local * heads),
        ],
        axis=1,
    )
    gain_grads = lax.psum_scatter(gain_grads, "dp", scatter_dimension=0, tiled=True)[0]
    both_gains = lax.psum(gain_grads[: 2 * rows_w], "tensor")
    grad_qkv = grad_qkv.reshape(rows_w, pairs, 3, 128)
    return (
        jnp.stack(outputs, axis=1),
        jnp.stack(grad_inputs, axis=1),
        both_gains[:rows_w],
        grad_qkv[:, :, 0].reshape(rows_w, width),
        grad_qkv[:, :, 1].reshape(rows_w, width),
        grad_qkv[:, :, 2].reshape(rows_w, width),
        grad_out.T,
        gain_grads[2 * rows_w :].reshape(buckets_local, heads),
        both_gains[rows_w:],
        grad_ff_weight[:, :width_ff],
        grad_ff_weight[:, width_ff:],
        grad_down.T,
    )


def solution(mesh):
    row, col = P("dp", "tensor"), P("tensor", "dp")
    acts = P("tensor", "dp", None)
    in_specs = (
        acts, acts, P("dp", None), P(), P("dp"), row, row, row, col, row, P("dp"), row, row, col
    )
    out_specs = (acts, acts, P("dp"), row, row, row, col, row, P("dp"), row, row, col)
    body = functools.partial(local, mesh.shape["dp"], mesh.shape["tensor"])
    return jax.shard_map(body, mesh=mesh, in_specs=in_specs, out_specs=out_specs, check_vma=False)
```

time: 3290 us -> 1130 us (0.34); the launches traced: 3220 us -> 1130 us
  local copies, waits for them, and re-layouts: 1490 us -> 85.1 us
  waiting for transfers between devices: 899 us -> 370 us
  matrix products: 513 us -> 246 us
  Pallas kernels: 0 us -> 194 us
  other arithmetic: 190 us -> 60.8 us
  starting transfers between devices: 2.16 us -> 65.3 us
  loops' own time: 35.5 us -> 0 us
    rev x4 -> x1, local copies, waits for them, and re-layouts: 484 us -> 0.07 us  [local(): (jnp.concatenate([fold[:, :, :B], zero], axis=1) + jnp.concatenate([zero,...]
    all_gather x15 -> x4, waiting for transfers between devices: 457 us -> 0.01 us  [spread(): return lax.all_gather(part, 'dp', axis=0, tiled=True)]
    reduce_scatter x16 -> x4, waiting for transfers between devices: 437 us -> 0.01 us  [over_both(): lax.psum_scatter(total.astype(BF), 'dp', scatter_dimension=0, tiled=True)]
    ppermute x0 -> x64, waiting for transfers between devices: none -> 369 us  [hop(): return lax.ppermute(part, 'tensor', [(i, i ^ bit) for i in range(count)])]
    while x72 -> x0, local copies, waits for them, and re-layouts: 280 us -> none
    dot_general x54 -> x26, matrix products: 513 us -> 246 us  [the longest x8 87.9 us: tn(): lax.dot_general(left, right, (((0,), (0,)), ((), ())), preferred_element_...]
    reshape x5 -> x7, local copies, waits for them, and re-layouts: 255 us -> 2.36 us  [the longest x1 1.4 us: local(): grad_qkv = grad_qkv.reshape(rows_w, pairs, 3, 128)]
    unnamed x167 -> x273, local copies, waits for them, and re-layouts: 265 us -> 54.4 us
  transfers between devices with their start and end apart: 31 -> 72, of which waited for: 20 -> 37; matrix products, arithmetic and copies ran while one was open for 41% -> 28% of each run, Pallas kernels for 0% -> 17%
where the time goes in v1:
time: 1130 us
  waiting for transfers between devices  370 us (33%)
  matrix products  246 us (22%)
  Pallas kernels  194 us (17%)
  blocking collectives  95.4 us (8%)
  local copies, waits for them, and re-layouts  85.1 us (8%)
  starting transfers between devices  65.3 us (6%)
  other arithmetic  60.8 us (5%)
  between operations  17.5 us (2%)
    ppermute x64, waiting for transfers between devices, hop(): return lax.ppermute(part, 'tensor', [(i, i ^ bit) for i in range(count)])  369 us
    pallas_call x2, Pallas kernels, attend_bwd(): pl.pallas_call(functools.partial(bwd_kernel, n), grid_spec=pltpu.Prefetch...  120 us
    dot_general x8, matrix products, tn(): lax.dot_general(left, right, (((0,), (0,)), ((), ())), preferred_element_...  87.9 us
    unnamed x2, blocking collectives  86.8 us
    dot_general x8, matrix products, nn(): lax.dot_general(a, b, (((1,), (0,)), ((), ())), preferred_element_type=F32)  82.2 us
    dot_general x8, matrix products, nt(): lax.dot_general(a, b, (((1,), (1,)), ((), ())), preferred_element_type=F32)  75.1 us
    pallas_call x2, Pallas kernels, attend_fwd(): pl.pallas_call(functools.partial(fwd_kernel, n), grid_spec=pltpu.Prefetch...  66.3 us
    ppermute x64, starting transfers between devices, hop(): return lax.ppermute(part, 'tensor', [(i, i ^ bit) for i in range(count)])  65 us
  transfers between devices with their start and end apart: 72, of which 37 were waited for; matrix products, arithmetic and copies ran while one was open for 28% of the time, Pallas kernels for 17%

profile of v1, /device:TPU:0, one launch (start us, length us, event | category | flops | bytes accessed | tf_op | source)
XLA Modules:
  0.0 1134.4 jit_solution(14786991735585418712)
XLA Ops:
  16.5 31.7 %all-reduce.2 = bf16[4352]{0:T(1024)(128)(2,1)S(1)} all-reduce(bf16[4352]{0:T(1024)(128)(2,1)S(1)} %dynamic-update-slice), channel_id=2, replica_groups=mesh['dp'=8,'tensor'=4] {'dp'}, use_global_device_ids=true, to_apply=%add.2 | all-reduce | flops 4352 | bytes 17408
  70.4 7.7 bias_strips.1.bias_ref
  91.0 14.7 %collective-permute-done.33 = bf16[256,2048]{1,0:T(8,128)(2,1)} collective-permute-done((bf16[256,2048]{1,0:T(8,128)(2,1)S(1)}, bf16[256,2048]{1,0:T(8,128)(2,1)}, u32[]{:S(2)}, u32[]{:S(2)}) %collective-permute-start.33) | collective-permute-done | bytes 1048608 | tf_op jit(solution)/shard_map/ppermute | solution.py:194
  113.9 14.1 %collective-permute-done.17 = bf16[256,2048]{1,0:T(8,128)(2,1)S(1)} collective-permute-done((bf16[256,2048]{1,0:T(8,128)(2,1)}, bf16[256,2048]{1,0:T(8,128)(2,1)S(1)}, u32[]{:S(2)}, u32[]{:S(2)}) %collective-permute-start.17) | collective-permute-done | bytes 1048608 | tf_op jit(solution)/shard_map/ppermute | solution.py:194
  141.1 10.2 convolution_convert_fusion.7.qkv_ref
  151.3 29.4 %attend_forward.2 = (bf16[1024,512]{1,0:T(8,128)(2,1)S(1)}, f32[4,2,1024]{2,1,0:T(2,128)S(1)}) custom-call(s32[16]{0:T(128)S(1)} %reshape.612.act_ref, s32[4]{0:T(128)S(1)} %iota_xor_fusion.blk_ref, bf16[1024,1536]{1,0:T(8,128)(2,1)S(1)} %convolution_convert_fusion.7.qkv_ref, bf16[1024,128]{1,0:T(8,128)(2,1)S(1)} %get-tuple-element.195.fq_ref, ...), custom_call_target="tpu_custom_call" | custom-call | flops 4294967296 | bytes 17825792 | tf_op jit(solution)/shard_map/attend_forward/pallas_call | solution.py:80
  195.1 11.4 %collective-permute-done.4 = bf16[256,2048]{1,0:T(8,128)(2,1)S(1)} collective-permute-done((bf16[256,2048]{1,0:T(8,128)(2,1)S(1)}, bf16[256,2048]{1,0:T(8,128)(2,1)S(1)}, u32[]{:S(2)}, u32[]{:S(2)}) %collective-permute-start.4) | collective-permute-done | bytes 1048608 | tf_op jit(solution)/shard_map/ppermute | solution.py:194
  211.4 7.9 collective-permute-done.6
  226.3 7.1 convolution_convert_fusion.6.qkv_ref
  233.5 36.9 %attend_forward.3 = (bf16[1024,512]{1,0:T(8,128)(2,1)S(1)}, f32[4,2,1024]{2,1,0:T(2,128)S(1)}) custom-call(s32[16]{0:T(128)S(1)} %reshape.616.act_ref, s32[4]{0:T(128)S(1)} %iota_xor_fusion.blk_ref, bf16[1024,1536]{1,0:T(8,128)(2,1)S(1)} %convolution_convert_fusion.6.qkv_ref, bf16[1024,128]{1,0:T(8,128)(2,1)S(1)} %get-tuple-element.196.fq_ref, ...), custom_call_target="tpu_custom_call" | custom-call | flops 4294967296 | bytes 17825792 | tf_op jit(solution)/shard_map/attend_forward/pallas_call | solution.py:80
  279.0 16.0 %collective-permute-done.9 = bf16[256,2048]{1,0:T(8,128)(2,1)S(1)} collective-permute-done((bf16[256,2048]{1,0:T(8,128)(2,1)S(1)}, bf16[256,2048]{1,0:T(8,128)(2,1)S(1)}, u32[]{:S(2)}, u32[]{:S(2)}) %collective-permute-start.9) | collective-permute-done | bytes 1048608 | tf_op jit(solution)/shard_map/ppermute | solution.py:194
  301.5 22.3 %collective-permute-done.10 = bf16[128,2048]{1,0:T(8,128)(2,1)S(1)} collective-permute-done((bf16[128,2048]{1,0:T(8,128)(2,1)S(1)}, bf16[128,2048]{1,0:T(8,128)(2,1)S(1)}, u32[]{:S(2)}, u32[]{:S(2)}) %collective-permute-start.10) | collective-permute-done | bytes 524320 | tf_op jit(solution)/shard_map/ppermute | solution.py:194
  325.5 16.5 %convolution_convert_fusion.1 = bf16[1024,2560]{1,0:T(8,128)(2,1)} fusion(bf16[1024,2048]{1,0:T(8,128)(2,1)} %constant_dynamic-update-slice_fusion.5, bf16[2048,2560]{1,0:T(8,128)(2,1)} %all-gather.10.cloned.1.call-done), kind=kOutput, calls=%fused_computation.22 | convolution fusion | flops 10740039680 | bytes 19922944 | tf_op jit(solution)/shard_map/dot_general | solution.py:15
  342.0 13.4 %fusion.24 = (bf16[1024,1280]{1,0:T(8,128)(2,1)S(1)}, bf16[1024,1280]{1,0:T(8,128)(2,1)S(1)}) fusion(bf16[1024,2560]{1,0:T(8,128)(2,1)} %convolution_convert_fusion.1, bf16[1024,2048]{1,0:T(8,128)(2,1)} %constant_dynamic-update-slice_fusion.20, bf16[2048,1280]{0,1:T(8,128)(2,1)} %all-gather.12.cloned.1.call-done), kind=kOutput, calls=%fused_computation.39 | convolution fusion | flops 5400166400 | bytes 19922944 | tf_op jit(solution)/shard_map/dot_general | solution.py:15
  355.4 15.6 %convolution_convert_fusion.3 = bf16[1024,2048]{1,0:T(8,128)(2,1)S(1)} fusion(bf16[2048,2560]{1,0:T(8,128)(2,1)} %all-gather.10.cloned.1.call-done, bf16[1024,1280]{1,0:T(8,128)(2,1)S(1)} %get-tuple-element.111, bf16[1024,1280]{1,0:T(8,128)(2,1)S(1)} %get-tuple-element.110), kind=kOutput, calls=%fused_computation.49 | convolution fusion | flops 10750001152 | bytes 19922944 | tf_op jit(solution)/shard_map/dot_general | solution.py:14
  378.5 19.0 %collective-permute-done.36 = bf16[256,2048]{1,0:T(8,128)(2,1)S(1)} collective-permute-done((bf16[256,2048]{1,0:T(8,128)(2,1)S(1)}, bf16[256,2048]{1,0:T(8,128)(2,1)S(1)}, u32[]{:S(2)}, u32[]{:S(2)}) %collective-permute-start.36) | collective-permute-done | bytes 1048608 | tf_op jit(solution)/shard_map/ppermute | solution.py:194
  402.7 9.2 collective-permute-done.38
  411.8 24.4 %collective-permute-done.37 = bf16[128,2048]{1,0:T(8,128)(2,1)S(1)} collective-permute-done((bf16[128,2048]{1,0:T(8,128)(2,1)S(1)}, bf16[128,2048]{1,0:T(8,128)(2,1)S(1)}, u32[]{:S(2)}, u32[]{:S(2)}) %collective-permute-start.37) | collective-permute-done | bytes 524320 | tf_op jit(solution)/shard_map/ppermute | solution.py:194
  439.7 8.3 collective-permute-done.39
  456.7 28.5 %collective-permute-done.50 = bf16[128,2048]{1,0:T(8,128)(2,1)S(1)} collective-permute-done((bf16[128,2048]{1,0:T(8,128)(2,1)S(1)}, bf16[128,2048]{1,0:T(8,128)(2,1)S(1)}, u32[]{:S(2)}, u32[]{:S(2)}) %collective-permute-start.50) | collective-permute-done | bytes 524320 | tf_op jit(solution)/shard_map/ppermute | solution.py:194
  498.1 15.4 %convolution_convert_fusion = bf16[1024,2560]{1,0:T(8,128)(2,1)} fusion(bf16[1024,2048]{1,0:T(8,128)(2,1)S(1)} %constant_dynamic-update-slice_fusion.15, bf16[2048,2560]{1,0:T(8,128)(2,1)} %all-gather.10.cloned.1.call-done), kind=kOutput, calls=%fused_computation.21 | convolution fusion | flops 10740039680 | bytes 19922944 | tf_op jit(solution)/shard_map/dot_general | solution.py:15
  513.5 12.1 %fusion.15 = (bf16[1024,1280]{1,0:T(8,128)(2,1)}, bf16[1024,1280]{1,0:T(8,128)(2,1)}) fusion(bf16[1024,2560]{1,0:T(8,128)(2,1)} %convolution_convert_fusion, bf16[1024,2048]{1,0:T(8,128)(2,1)S(1)} %constant_dynamic-update-slice_fusion.30, bf16[2048,1280]{0,1:T(8,128)(2,1)S(1)} %bitcast.225), kind=kOutput, calls=%fused_computation.30 | convolution fusion | flops 5400166400 | bytes 19922944 | tf_op jit(solution)/shard_map/dot_general | solution.py:15
  525.5 15.5 %convolution_convert_fusion.2 = bf16[1024,2048]{1,0:T(8,128)(2,1)S(1)} fusion(bf16[2048,2560]{1,0:T(8,128)(2,1)} %all-gather.10.cloned.1.call-done, bf16[1024,1280]{1,0:T(8,128)(2,1)} %get-tuple-element.113, bf16[1024,1280]{1,0:T(8,128)(2,1)} %get-tuple-element.112), kind=kOutput, calls=%fused_computation.48 | convolution fusion | flops 10750001152 | bytes 19922944 | tf_op jit(solution)/shard_map/dot_general | solution.py:14
  543.4 12.9 %collective-permute-done.52 = bf16[256,2048]{1,0:T(8,128)(2,1)S(1)} collective-permute-done((bf16[256,2048]{1,0:T(8,128)(2,1)S(1)}, bf16[256,2048]{1,0:T(8,128)(2,1)S(1)}, u32[]{:S(2)}, u32[]{:S(2)}) %collective-permute-start.52) | collective-permute-done | bytes 1048608 | tf_op jit(solution)/shard_map/ppermute | solution.py:194
  563.1 11.2 collective-permute-done.53
  578.5 11.2 collective-permute-done.55
  594.3 8.6 collective-permute-done.41
  611.1 20.5 %collective-permute-done.42 = bf16[128,2048]{1,0:T(8,128)(2,1)S(1)} collective-permute-done((bf16[128,2048]{1,0:T(8,128)(2,1)S(1)}, bf16[128,2048]{1,0:T(8,128)(2,1)S(1)}, u32[]{:S(2)}, u32[]{:S(2)}) %collective-permute-start.42) | collective-permute-done | bytes 524320 | tf_op jit(solution)/shard_map/ppermute | solution.py:194
  633.9 7.1 collective-permute-done.58
  649.3 12.2 %fusion.84 = f32[2048,1280]{1,0:T(8,128)} fusion(bf16[1024,2048]{1,0:T(8,128)(2,1)} %copy-done.70, bf16[1024,2560]{1,0:T(8,128)(2,1)} %convolution_convert_fusion), kind=kOutput, calls=%fused_computation.273 | convolution fusion | flops 5384437760 | bytes 19922944 | tf_op jit(solution)/shard_map/dot_general | solution.py:190
  661.5 12.4 %add_convert_fusion.2 = bf16[2048,1280]{1,0:T(8,128)(2,1)} fusion(f32[2048,1280]{1,0:T(8,128)} %fusion.84, bf16[1024,2048]{1,0:T(8,128)(2,1)S(1)} %copy-done.69, bf16[1024,2560]{1,0:T(8,128)(2,1)} %convolution_convert_fusion.1), kind=kOutput, calls=%fused_computation.2 | convolution fusion | flops 5389680640 | bytes 25165824 | tf_op jit(solution)/shard_map/dot_general | solution.py:190
  679.3 55.4 %attend_backward.2 = (bf16[1024,1536]{1,0:T(8,128)(2,1)S(1)}, f32[4,2,7,512]{3,2,1,0:T(8,128)S(1)}) custom-call(s32[16]{0:T(128)S(1)} %copy-done.8, s32[4]{0:T(128)S(1)} %copy-done.4, bf16[1024,1536]{1,0:T(8,128)(2,1)} %copy-done.1, bf16[1024,128]{1,0:T(8,128)(2,1)S(1)} %get-tuple-element.195.fq_ref, bf16[1024,128]{1,0:T(8,128)(2,1)S(1)} %get-tuple-element.189.fk_ref, ...), custom_call_target="tpu_custom_call" | custom-call | flops 10737418240 | bytes 20971520 | tf_op jit(solution)/shard_map/attend_backward/pallas_call | solution.py:154
  737.1 65.1 %attend_backward.3 = (bf16[1024,1536]{1,0:T(8,128)(2,1)S(1)}, f32[4,2,7,512]{3,2,1,0:T(8,128)S(1)}) custom-call(s32[16]{0:T(128)S(1)} %copy-done.6, s32[4]{0:T(128)S(1)} %copy-done.4, bf16[1024,1536]{1,0:T(8,128)(2,1)} %copy-done.2, bf16[1024,128]{1,0:T(8,128)(2,1)S(1)} %get-tuple-element.196.fq_ref, bf16[1024,128]{1,0:T(8,128)(2,1)S(1)} %get-tuple-element.190.fk_ref, ...), custom_call_target="tpu_custom_call" | custom-call | flops 10737418240 | bytes 20971520 | tf_op jit(solution)/shard_map/attend_backward/pallas_call | solution.py:154
  802.2 9.3 fusion.109
  811.6 12.9 %add_convert_fusion.1 = bf16[2048,1536]{1,0:T(8,128)(2,1)} fusion(f32[2048,1536]{1,0:T(8,128)} %fusion.109, bf16[1024,2048]{1,0:T(8,128)(2,1)} %constant_dynamic-update-slice_fusion, bf16[1024,1536]{1,0:T(8,128)(2,1)S(1)} %get-tuple-element.23), kind=kOutput, calls=%fused_computation.1 | convolution fusion | flops 6448742400 | bytes 26214400 | tf_op jit(solution)/shard_map/dot_general | solution.py:190
  824.6 10.2 convolution_convert_fusion.10
  839.0 14.7 %fusion.28 = f32[2048,2560]{1,0:T(8,128)} fusion(bf16[1024,2048]{1,0:T(8,128)(2,1)S(1)} %copy-done.74, bf16[1024,1280]{1,0:T(8,128)(2,1)S(1)} %copy-done.104, bf16[1024,1280]{1,0:T(8,128)(2,1)S(1)} %copy-done.103), kind=kOutput, calls=%fused_computation.58 | convolution fusion | flops 10747904000 | bytes 30408704 | tf_op jit(solution)/shard_map/dot_general | solution.py:190
  853.7 20.1 %add_convert_fusion = bf16[2048,2560]{1,0:T(8,128)(2,1)} fusion(f32[2048,2560]{1,0:T(8,128)} %fusion.28, bf16[1024,2048]{1,0:T(8,128)(2,1)} %constant_dynamic-update-slice_fusion.5, bf16[1024,1280]{1,0:T(8,128)(2,1)} %copy-done.106, bf16[1024,1280]{1,0:T(8,128)(2,1)} %copy-done.105), kind=kOutput, calls=%fused_computation | convolution fusion | flops 10758389760 | bytes 40894464 | tf_op jit(solution)/shard_map/dot_general | solution.py:190
  875.0 21.4 %collective-permute-done.12 = bf16[256,2048]{1,0:T(8,128)(2,1)S(1)} collective-permute-done((bf16[256,2048]{1,0:T(8,128)(2,1)S(1)}, bf16[256,2048]{1,0:T(8,128)(2,1)S(1)}, u32[]{:S(2)}, u32[]{:S(2)}) %collective-permute-start.12) | collective-permute-done | bytes 1048608 | tf_op jit(solution)/shard_map/ppermute | solution.py:194
  898.7 10.0 collective-permute-done.13
  911.7 10.0 convolution_convert_fusion.5
  924.0 9.9 convolution_convert_fusion.8
  944.7 22.3 %collective-permute-done.28 = bf16[256,2048]{1,0:T(8,128)(2,1)S(1)} collective-permute-done((bf16[256,2048]{1,0:T(8,128)(2,1)S(1)}, bf16[256,2048]{1,0:T(8,128)(2,1)S(1)}, u32[]{:S(2)}, u32[]{:S(2)}) %collective-permute-start.28) | collective-permute-done | bytes 1048608 | tf_op jit(solution)/shard_map/ppermute | solution.py:194
  967.2 7.3 convolution_convert_fusion.4
  977.2 9.4 collective-permute-done.45
  1020.9 7.9 collective-permute-done.63
  1049.2 55.0 %all-reduce.3 = f32[8,544]{1,0:T(8,128)S(1)} all-reduce(f32[8,544]{1,0:T(8,128)S(1)} %pad_maximum_fusion.31), channel_id=3, replica_groups=mesh['dp'=8,'tensor'=4] {'dp'}, use_global_device_ids=true, to_apply=%region_19.20.clone | all-reduce | flops 4352 | bytes 34816
  1106.1 8.6 psum.7
  (560 shorter events, 284.1 us)
Async XLA Ops:
  7.2 133.8 %all-gather.6.cloned.1.call-start = ((), (), s32[]{:S(2)}) async-start(), calls=%async_computation.4 | async-start | bytes 7077888 | tf_op jit(solution)/shard_map/all_gather | solution.py:262
  11.7 170.7 %all-gather.8.cloned.1.call-start = ((), (), s32[]{:S(2)}) async-start(), calls=%async_computation.5 | async-start | bytes 2359296 | tf_op jit(solution)/shard_map/all_gather | solution.py:262
  12.5 313.1 %all-gather.10.cloned.1.call-start = ((), (), s32[]{:S(2)}) async-start(), calls=%async_computation.6 | async-start | bytes 11796480 | tf_op jit(solution)/shard_map/all_gather | solution.py:262
  14.8 327.2 %all-gather.12.cloned.1.call-start = ((), (), s32[]{:S(2)}) async-start(), calls=%async_computation.7 | async-start | bytes 5898240 | tf_op jit(solution)/shard_map/all_gather | solution.py:262
  55.4 31.4 %collective-permute-start = (bf16[256,2048]{1,0:T(8,128)(2,1)}, bf16[256,2048]{1,0:T(8,128)(2,1)}, u32[]{:S(2)}, u32[]{:S(2)}) collective-permute-start(bf16[256,2048]{1,0:T(8,128)(2,1)} %get-tuple-element.101), channel_id=1, source_target_pairs={{0,1},{1,0},{2,3},{3,2},{4,5},{5,4},{6,7},{7,6},{8,9},{9,8},{10,11... | collective-permute-start | bytes 3145736 | tf_op jit(solution)/shard_map/ppermute | solution.py:194
  56.8 26.5 %collective-permute-start.1 = (bf16[256,2048]{1,0:T(8,128)(2,1)}, bf16[256,2048]{1,0:T(8,128)(2,1)}, u32[]{:S(2)}, u32[]{:S(2)}) collective-permute-start(bf16[256,2048]{1,0:T(8,128)(2,1)} %get-tuple-element.101), channel_id=1, source_target_pairs={{0,2},{1,3},{2,0},{3,1},{4,6},{5,7},{6,4},{7,5},{8,10},{9,11},{10,... | collective-permute-start | bytes 3145736 | tf_op jit(solution)/shard_map/ppermute | solution.py:194
  65.2 46.4 %collective-permute-start.32 = (bf16[256,2048]{1,0:T(8,128)(2,1)S(1)}, bf16[256,2048]{1,0:T(8,128)(2,1)}, u32[]{:S(2)}, u32[]{:S(2)}) collective-permute-start(bf16[256,2048]{1,0:T(8,128)(2,1)S(1)} %get-tuple-element.93), channel_id=1, source_target_pairs={{0,1},{1,0},{2,3},{3,2},{4,5},{5,4},{6,7},{7,6},{8,9},{9,8},{10,11... | collective-permute-start | bytes 3145736 | tf_op jit(solution)/shard_map/ppermute | solution.py:194
  65.7 40.0 %collective-permute-start.33 = (bf16[256,2048]{1,0:T(8,128)(2,1)S(1)}, bf16[256,2048]{1,0:T(8,128)(2,1)}, u32[]{:S(2)}, u32[]{:S(2)}) collective-permute-start(bf16[256,2048]{1,0:T(8,128)(2,1)S(1)} %get-tuple-element.93), channel_id=1, source_target_pairs={{0,2},{1,3},{2,0},{3,1},{4,6},{5,7},{6,4},{7,5},{8,10},{9,11},{10,... | collective-permute-start | bytes 3145736 | tf_op jit(solution)/shard_map/ppermute | solution.py:194
  66.2 64.3 %collective-permute-start.16 = (bf16[256,2048]{1,0:T(8,128)(2,1)}, bf16[256,2048]{1,0:T(8,128)(2,1)}, u32[]{:S(2)}, u32[]{:S(2)}) collective-permute-start(bf16[256,2048]{1,0:T(8,128)(2,1)} %get-tuple-element.186), channel_id=1, source_target_pairs={{0,1},{1,0},{2,3},{3,2},{4,5},{5,4},{6,7},{7,6},{8,9},{9,8},{10,11... | collective-permute-start | bytes 3145736 | tf_op jit(solution)/shard_map/ppermute | solution.py:194
  67.6 1047.7 %reduce-scatter.7.cloned.1.call-start = ((), (), s32[]{:S(2)}) async-start(), calls=%async_computation.9 | async-start | bytes 2359296 | tf_op jit(solution)/shard_map/reduce_scatter | solution.py:343
  83.4 44.7 %collective-permute-start.17 = (bf16[256,2048]{1,0:T(8,128)(2,1)}, bf16[256,2048]{1,0:T(8,128)(2,1)S(1)}, u32[]{:S(2)}, u32[]{:S(2)}) collective-permute-start(bf16[256,2048]{1,0:T(8,128)(2,1)} %get-tuple-element.186), channel_id=1, source_target_pairs={{0,2},{1,3},{2,0},{3,1},{4,6},{5,7},{6,4},{7,5},{8,10},{9,11},{10,... | collective-permute-start | bytes 3145736 | tf_op jit(solution)/shard_map/ppermute | solution.py:194
  86.9 51.0 %collective-permute-start.2 = (bf16[128,2048]{1,0:T(8,128)(2,1)S(1)}, bf16[128,2048]{1,0:T(8,128)(2,1)S(1)}, u32[]{:S(2)}, u32[]{:S(2)}) collective-permute-start(bf16[128,2048]{1,0:T(8,128)(2,1)S(1)} %slice.664), channel_id=1, source_target_pairs={{0,1},{1,0},{2,3},{3,2},{4,5},{5,4},{6,7},{7,6},{8,9},{9,8},{10,11... | collective-permute-start | bytes 1572872 | tf_op jit(solution)/shard_map/ppermute | solution.py:194
  105.7 34.6 %collective-permute-start.3 = (bf16[128,2048]{1,0:T(8,128)(2,1)S(1)}, bf16[128,2048]{1,0:T(8,128)(2,1)S(1)}, u32[]{:S(2)}, u32[]{:S(2)}) collective-permute-start(bf16[128,2048]{1,0:T(8,128)(2,1)S(1)} %slice.665), channel_id=1, source_target_pairs={{0,2},{1,3},{2,0},{3,1},{4,6},{5,7},{6,4},{7,5},{8,10},{9,11},{10,... | collective-permute-start | bytes 1572872 | tf_op jit(solution)/shard_map/ppermute | solution.py:194
  111.5 81.1 %collective-permute-start.34 = (bf16[128,2048]{1,0:T(8,128)(2,1)}, bf16[128,2048]{1,0:T(8,128)(2,1)}, u32[]{:S(2)}, u32[]{:S(2)}) collective-permute-start(bf16[128,2048]{1,0:T(8,128)(2,1)} %slice.728), channel_id=1, source_target_pairs={{0,1},{1,0},{2,3},{3,2},{4,5},{5,4},{6,7},{7,6},{8,9},{9,8},{10,11... | collective-permute-start | bytes 1572872 | tf_op jit(solution)/shard_map/ppermute | solution.py:194
  128.0 79.2 %collective-permute-start.35 = (bf16[128,2048]{1,0:T(8,128)(2,1)}, bf16[128,2048]{1,0:T(8,128)(2,1)}, u32[]{:S(2)}, u32[]{:S(2)}) collective-permute-start(bf16[128,2048]{1,0:T(8,128)(2,1)} %slice.729), channel_id=1, source_target_pairs={{0,2},{1,3},{2,0},{3,1},{4,6},{5,7},{6,4},{7,5},{8,10},{9,11},{10,... | collective-permute-start | bytes 1572872 | tf_op jit(solution)/shard_map/ppermute | solution.py:194
  130.5 78.6 %collective-permute-start.18 = (bf16[128,2048]{1,0:T(8,128)(2,1)}, bf16[128,2048]{1,0:T(8,128)(2,1)}, u32[]{:S(2)}, u32[]{:S(2)}) collective-permute-start(bf16[128,2048]{1,0:T(8,128)(2,1)} %slice.698), channel_id=1, source_target_pairs={{0,1},{1,0},{2,3},{3,2},{4,5},{5,4},{6,7},{7,6},{8,9},{9,8},{10,11... | collective-permute-start | bytes 1572872 | tf_op jit(solution)/shard_map/ppermute | solution.py:194
  137.9 72.4 %collective-permute-start.19 = (bf16[128,2048]{1,0:T(8,128)(2,1)}, bf16[128,2048]{1,0:T(8,128)(2,1)}, u32[]{:S(2)}, u32[]{:S(2)}) collective-permute-start(bf16[128,2048]{1,0:T(8,128)(2,1)} %slice.699), channel_id=1, source_target_pairs={{0,2},{1,3},{2,0},{3,1},{4,6},{5,7},{6,4},{7,5},{8,10},{9,11},{10,... | collective-permute-start | bytes 1572872 | tf_op jit(solution)/shard_map/ppermute | solution.py:194
  194.6 24.6 %collective-permute-start.6 = (bf16[256,2048]{1,0:T(8,128)(2,1)S(1)}, bf16[256,2048]{1,0:T(8,128)(2,1)S(1)}, u32[]{:S(2)}, u32[]{:S(2)}) collective-permute-start(bf16[256,2048]{1,0:T(8,128)(2,1)S(1)} %pad_maximum_fusion.14), channel_id=1, source_target_pairs={{0,2},{1,3},{2,0},{3,1},{4,6},{5,7},{6,4},{7,5},{8,10},{9,11},{10,... | collective-permute-start | bytes 3145736 | tf_op jit(solution)/shard_map/ppermute | solution.py:194
  225.3 45.0 %collective-permute-start.7 = (bf16[128,2048]{1,0:T(8,128)(2,1)S(1)}, bf16[128,2048]{1,0:T(8,128)(2,1)S(1)}, u32[]{:S(2)}, u32[]{:S(2)}) collective-permute-start(bf16[128,2048]{1,0:T(8,128)(2,1)S(1)} %get-tuple-element.145), channel_id=1, source_target_pairs={{0,1},{1,0},{2,3},{3,2},{4,5},{5,4},{6,7},{7,6},{8,9},{9,8},{10,11... | collective-permute-start | bytes 1572872 | tf_op jit(solution)/shard_map/ppermute | solution.py:194
  272.4 26.1 %collective-permute-start.8 = (bf16[256,2048]{1,0:T(8,128)(2,1)S(1)}, bf16[256,2048]{1,0:T(8,128)(2,1)S(1)}, u32[]{:S(2)}, u32[]{:S(2)}) collective-permute-start(bf16[256,2048]{1,0:T(8,128)(2,1)S(1)} %get-tuple-element.99), channel_id=1, source_target_pairs={{0,1},{1,0},{2,3},{3,2},{4,5},{5,4},{6,7},{7,6},{8,9},{9,8},{10,11... | collective-permute-start | bytes 3145736 | tf_op jit(solution)/shard_map/ppermute | solution.py:194
  278.0 94.7 %collective-permute-start.20 = (bf16[256,2048]{1,0:T(8,128)(2,1)}, bf16[256,2048]{1,0:T(8,128)(2,1)}, u32[]{:S(2)}, u32[]{:S(2)}) collective-permute-start(bf16[256,2048]{1,0:T(8,128)(2,1)} %pad_maximum_fusion.17), channel_id=1, source_target_pairs={{0,1},{1,0},{2,3},{3,2},{4,5},{5,4},{6,7},{7,6},{8,9},{9,8},{10,11... | collective-permute-start | bytes 3145736 | tf_op jit(solution)/shard_map/ppermute | solution.py:194
  295.1 28.7 %collective-permute-start.10 = (bf16[128,2048]{1,0:T(8,128)(2,1)S(1)}, bf16[128,2048]{1,0:T(8,128)(2,1)S(1)}, u32[]{:S(2)}, u32[]{:S(2)}) collective-permute-start(bf16[128,2048]{1,0:T(8,128)(2,1)S(1)} %slice.682), channel_id=1, source_target_pairs={{0,1},{1,0},{2,3},{3,2},{4,5},{5,4},{6,7},{7,6},{8,9},{9,8},{10,11... | collective-permute-start | bytes 1572872 | tf_op jit(solution)/shard_map/ppermute | solution.py:194
  296.5 102.0 %collective-permute-start.22 = (bf16[256,2048]{1,0:T(8,128)(2,1)}, bf16[256,2048]{1,0:T(8,128)(2,1)}, u32[]{:S(2)}, u32[]{:S(2)}) collective-permute-start(bf16[256,2048]{1,0:T(8,128)(2,1)} %pad_maximum_fusion.18), channel_id=1, source_target_pairs={{0,2},{1,3},{2,0},{3,1},{4,6},{5,7},{6,4},{7,5},{8,10},{9,11},{10,... | collective-permute-start | bytes 3145736 | tf_op jit(solution)/shard_map/ppermute | solution.py:194
  298.5 26.2 %collective-permute-start.11 = (bf16[128,2048]{1,0:T(8,128)(2,1)S(1)}, bf16[128,2048]{1,0:T(8,128)(2,1)S(1)}, u32[]{:S(2)}, u32[]{:S(2)}) collective-permute-start(bf16[128,2048]{1,0:T(8,128)(2,1)S(1)} %slice.683), channel_id=1, source_target_pairs={{0,2},{1,3},{2,0},{3,1},{4,6},{5,7},{6,4},{7,5},{8,10},{9,11},{10,... | collective-permute-start | bytes 1572872 | tf_op jit(solution)/shard_map/ppermute | solution.py:194
  371.4 26.2 %collective-permute-start.36 = (bf16[256,2048]{1,0:T(8,128)(2,1)S(1)}, bf16[256,2048]{1,0:T(8,128)(2,1)S(1)}, u32[]{:S(2)}, u32[]{:S(2)}) collective-permute-start(bf16[256,2048]{1,0:T(8,128)(2,1)S(1)} %pad_maximum_fusion.21), channel_id=1, source_target_pairs={{0,1},{1,0},{2,3},{3,2},{4,5},{5,4},{6,7},{7,6},{8,9},{9,8},{10,11... | collective-permute-start | bytes 3145736 | tf_op jit(solution)/shard_map/ppermute | solution.py:194
  374.4 25.4 %collective-permute-start.21 = (bf16[128,2048]{1,0:T(8,128)(2,1)S(1)}, bf16[128,2048]{1,0:T(8,128)(2,1)S(1)}, u32[]{:S(2)}, u32[]{:S(2)}) collective-permute-start(bf16[128,2048]{1,0:T(8,128)(2,1)S(1)} %add_convert_fusion.17), channel_id=1, source_target_pairs={{0,2},{1,3},{2,0},{3,1},{4,6},{5,7},{6,4},{7,5},{8,10},{9,11},{10,... | collective-permute-start | bytes 1572872 | tf_op jit(solution)/shard_map/ppermute | solution.py:194
  375.4 36.4 %collective-permute-start.38 = (bf16[256,2048]{1,0:T(8,128)(2,1)S(1)}, bf16[256,2048]{1,0:T(8,128)(2,1)S(1)}, u32[]{:S(2)}, u32[]{:S(2)}) collective-permute-start(bf16[256,2048]{1,0:T(8,128)(2,1)S(1)} %pad_maximum_fusion.22), channel_id=1, source_target_pairs={{0,2},{1,3},{2,0},{3,1},{4,6},{5,7},{6,4},{7,5},{8,10},{9,11},{10,... | collective-permute-start | bytes 3145736 | tf_op jit(solution)/shard_map/ppermute | solution.py:194
  377.3 78.5 %collective-permute-start.48 = (bf16[256,2048]{1,0:T(8,128)(2,1)S(1)}, bf16[256,2048]{1,0:T(8,128)(2,1)S(1)}, u32[]{:S(2)}, u32[]{:S(2)}) collective-permute-start(bf16[256,2048]{1,0:T(8,128)(2,1)S(1)} %get-tuple-element.97), channel_id=1, source_target_pairs={{0,1},{1,0},{2,3},{3,2},{4,5},{5,4},{6,7},{7,6},{8,9},{9,8},{10,11... | collective-permute-start | bytes 3145736 | tf_op jit(solution)/shard_map/ppermute | solution.py:194
  397.6 56.5 %collective-permute-start.49 = (bf16[256,2048]{1,0:T(8,128)(2,1)S(1)}, bf16[256,2048]{1,0:T(8,128)(2,1)S(1)}, u32[]{:S(2)}, u32[]{:S(2)}) collective-permute-start(bf16[256,2048]{1,0:T(8,128)(2,1)S(1)} %get-tuple-element.97), channel_id=1, source_target_pairs={{0,2},{1,3},{2,0},{3,1},{4,6},{5,7},{6,4},{7,5},{8,10},{9,11},{10,... | collective-permute-start | bytes 3145736 | tf_op jit(solution)/shard_map/ppermute | solution.py:194
  398.5 37.7 %collective-permute-start.37 = (bf16[128,2048]{1,0:T(8,128)(2,1)S(1)}, bf16[128,2048]{1,0:T(8,128)(2,1)S(1)}, u32[]{:S(2)}, u32[]{:S(2)}) collective-permute-start(bf16[128,2048]{1,0:T(8,128)(2,1)S(1)} %add_convert_fusion.13), channel_id=1, source_target_pairs={{0,2},{1,3},{2,0},{3,1},{4,6},{5,7},{6,4},{7,5},{8,10},{9,11},{10,... | collective-permute-start | bytes 1572872 | tf_op jit(solution)/shard_map/ppermute | solution.py:194
  401.5 36.5 %collective-permute-start.23 = (bf16[128,2048]{1,0:T(8,128)(2,1)S(1)}, bf16[128,2048]{1,0:T(8,128)(2,1)S(1)}, u32[]{:S(2)}, u32[]{:S(2)}) collective-permute-start(bf16[128,2048]{1,0:T(8,128)(2,1)S(1)} %get-tuple-element.157), channel_id=1, source_target_pairs={{0,1},{1,0},{2,3},{3,2},{4,5},{5,4},{6,7},{7,6},{8,9},{9,8},{10,11... | collective-permute-start | bytes 1572872 | tf_op jit(solution)/shard_map/ppermute | solution.py:194
  452.2 33.0 %collective-permute-start.25 = (bf16[256,2048]{1,0:T(8,128)(2,1)S(1)}, bf16[256,2048]{1,0:T(8,128)(2,1)S(1)}, u32[]{:S(2)}, u32[]{:S(2)}) collective-permute-start(bf16[256,2048]{1,0:T(8,128)(2,1)S(1)} %get-tuple-element.184), channel_id=1, source_target_pairs={{0,2},{1,3},{2,0},{3,1},{4,6},{5,7},{6,4},{7,5},{8,10},{9,11},{10,... | collective-permute-start | bytes 3145736 | tf_op jit(solution)/shard_map/ppermute | solution.py:194
  453.7 33.1 %collective-permute-start.24 = (bf16[256,2048]{1,0:T(8,128)(2,1)S(1)}, bf16[256,2048]{1,0:T(8,128)(2,1)S(1)}, u32[]{:S(2)}, u32[]{:S(2)}) collective-permute-start(bf16[256,2048]{1,0:T(8,128)(2,1)S(1)} %get-tuple-element.184), channel_id=1, source_target_pairs={{0,1},{1,0},{2,3},{3,2},{4,5},{5,4},{6,7},{7,6},{8,9},{9,8},{10,11... | collective-permute-start | bytes 3145736 | tf_op jit(solution)/shard_map/ppermute | solution.py:194
  454.2 31.1 %collective-permute-start.50 = (bf16[128,2048]{1,0:T(8,128)(2,1)S(1)}, bf16[128,2048]{1,0:T(8,128)(2,1)S(1)}, u32[]{:S(2)}, u32[]{:S(2)}) collective-permute-start(bf16[128,2048]{1,0:T(8,128)(2,1)S(1)} %slice.756), channel_id=1, source_target_pairs={{0,1},{1,0},{2,3},{3,2},{4,5},{5,4},{6,7},{7,6},{8,9},{9,8},{10,11... | collective-permute-start | bytes 1572872 | tf_op jit(solution)/shard_map/ppermute | solution.py:194
  455.8 30.8 %collective-permute-start.51 = (bf16[128,2048]{1,0:T(8,128)(2,1)S(1)}, bf16[128,2048]{1,0:T(8,128)(2,1)S(1)}, u32[]{:S(2)}, u32[]{:S(2)}) collective-permute-start(bf16[128,2048]{1,0:T(8,128)(2,1)S(1)} %slice.757), channel_id=1, source_target_pairs={{0,2},{1,3},{2,0},{3,1},{4,6},{5,7},{6,4},{7,5},{8,10},{9,11},{10,... | collective-permute-start | bytes 1572872 | tf_op jit(solution)/shard_map/ppermute | solution.py:194
  576.6 32.6 %collective-permute-start.40 = (bf16[256,2048]{1,0:T(8,128)(2,1)S(1)}, bf16[256,2048]{1,0:T(8,128)(2,1)S(1)}, u32[]{:S(2)}, u32[]{:S(2)}) collective-permute-start(bf16[256,2048]{1,0:T(8,128)(2,1)S(1)} %copy-done.62), channel_id=1, source_target_pairs={{0,1},{1,0},{2,3},{3,2},{4,5},{5,4},{6,7},{7,6},{8,9},{9,8},{10,11... | collective-permute-start | bytes 3145736 | tf_op jit(solution)/shard_map/ppermute | solution.py:194
  576.8 26.1 %collective-permute-start.41 = (bf16[256,2048]{1,0:T(8,128)(2,1)S(1)}, bf16[256,2048]{1,0:T(8,128)(2,1)S(1)}, u32[]{:S(2)}, u32[]{:S(2)}) collective-permute-start(bf16[256,2048]{1,0:T(8,128)(2,1)S(1)} %copy-done.62), channel_id=1, source_target_pairs={{0,2},{1,3},{2,0},{3,1},{4,6},{5,7},{6,4},{7,5},{8,10},{9,11},{10,... | collective-permute-start | bytes 3145736 | tf_op jit(solution)/shard_map/ppermute | solution.py:194
  592.2 39.5 %collective-permute-start.57 = (bf16[256,2048]{1,0:T(8,128)(2,1)S(1)}, bf16[256,2048]{1,0:T(8,128)(2,1)S(1)}, u32[]{:S(2)}, u32[]{:S(2)}) collective-permute-start(bf16[256,2048]{1,0:T(8,128)(2,1)S(1)} %get-tuple-element.95), channel_id=1, source_target_pairs={{0,2},{1,3},{2,0},{3,1},{4,6},{5,7},{6,4},{7,5},{8,10},{9,11},{10,... | collective-permute-start | bytes 3145736 | tf_op jit(solution)/shard_map/ppermute | solution.py:194
  593.8 39.8 %collective-permute-start.56 = (bf16[256,2048]{1,0:T(8,128)(2,1)S(1)}, bf16[256,2048]{1,0:T(8,128)(2,1)S(1)}, u32[]{:S(2)}, u32[]{:S(2)}) collective-permute-start(bf16[256,2048]{1,0:T(8,128)(2,1)S(1)} %get-tuple-element.95), channel_id=1, source_target_pairs={{0,1},{1,0},{2,3},{3,2},{4,5},{5,4},{6,7},{7,6},{8,9},{9,8},{10,11... | collective-permute-start | bytes 3145736 | tf_op jit(solution)/shard_map/ppermute | solution.py:194
  603.0 28.7 %collective-permute-start.42 = (bf16[128,2048]{1,0:T(8,128)(2,1)S(1)}, bf16[128,2048]{1,0:T(8,128)(2,1)S(1)}, u32[]{:S(2)}, u32[]{:S(2)}) collective-permute-start(bf16[128,2048]{1,0:T(8,128)(2,1)S(1)} %slice.742), channel_id=1, source_target_pairs={{0,1},{1,0},{2,3},{3,2},{4,5},{5,4},{6,7},{7,6},{8,9},{9,8},{10,11... | collective-permute-start | bytes 1572872 | tf_op jit(solution)/shard_map/ppermute | solution.py:194
  649.3 468.0 %reduce-scatter.11.cloned.1.call-start = ((), (), s32[]{:S(2)}) async-start(), calls=%async_computation.11 | async-start | bytes 5898240 | tf_op jit(solution)/shard_map/reduce_scatter | solution.py:343
  674.0 445.9 %reduce-scatter.5.cloned.1.call-start = ((), (), s32[]{:S(2)}) async-start(), calls=%async_computation.8 | async-start | bytes 7077888 | tf_op jit(solution)/shard_map/reduce_scatter | solution.py:343
  824.5 299.9 %reduce-scatter.9.cloned.1.call-start = ((), (), s32[]{:S(2)}) async-start(), calls=%async_computation.10 | async-start | bytes 11796480 | tf_op jit(solution)/shard_map/reduce_scatter | solution.py:343
  934.3 32.6 %collective-permute-start.28 = (bf16[256,2048]{1,0:T(8,128)(2,1)S(1)}, bf16[256,2048]{1,0:T(8,128)(2,1)S(1)}, u32[]{:S(2)}, u32[]{:S(2)}) collective-permute-start(bf16[256,2048]{1,0:T(8,128)(2,1)S(1)} %pad_maximum_fusion.19), channel_id=1, source_target_pairs={{0,1},{1,0},{2,3},{3,2},{4,5},{5,4},{6,7},{7,6},{8,9},{9,8},{10,11... | collective-permute-start | bytes 3145736 | tf_op jit(solution)/shard_map/ppermute | solution.py:194
  938.0 39.2 %collective-permute-start.46 = (bf16[256,2048]{1,0:T(8,128)(2,1)S(1)}, bf16[256,2048]{1,0:T(8,128)(2,1)S(1)}, u32[]{:S(2)}, u32[]{:S(2)}) collective-permute-start(bf16[256,2048]{1,0:T(8,128)(2,1)S(1)} %pad_maximum_fusion.24), channel_id=1, source_target_pairs={{0,2},{1,3},{2,0},{3,1},{4,6},{5,7},{6,4},{7,5},{8,10},{9,11},{10,... | collective-permute-start | bytes 3145736 | tf_op jit(solution)/shard_map/ppermute | solution.py:194
  938.7 50.2 %collective-permute-start.30 = (bf16[256,2048]{1,0:T(8,128)(2,1)S(1)}, bf16[256,2048]{1,0:T(8,128)(2,1)S(1)}, u32[]{:S(2)}, u32[]{:S(2)}) collective-permute-start(bf16[256,2048]{1,0:T(8,128)(2,1)S(1)} %pad_maximum_fusion.20), channel_id=1, source_target_pairs={{0,2},{1,3},{2,0},{3,1},{4,6},{5,7},{6,4},{7,5},{8,10},{9,11},{10,... | collective-permute-start | bytes 3145736 | tf_op jit(solution)/shard_map/ppermute | solution.py:194
  944.6 42.0 %collective-permute-start.45 = (bf16[128,2048]{1,0:T(8,128)(2,1)S(1)}, bf16[128,2048]{1,0:T(8,128)(2,1)S(1)}, u32[]{:S(2)}, u32[]{:S(2)}) collective-permute-start(bf16[128,2048]{1,0:T(8,128)(2,1)S(1)} %add_convert_fusion.11), channel_id=1, source_target_pairs={{0,2},{1,3},{2,0},{3,1},{4,6},{5,7},{6,4},{7,5},{8,10},{9,11},{10,... | collective-permute-start | bytes 1572872 | tf_op jit(solution)/shard_map/ppermute | solution.py:194
  967.1 25.1 %collective-permute-start.29 = (bf16[128,2048]{1,0:T(8,128)(2,1)S(1)}, bf16[128,2048]{1,0:T(8,128)(2,1)S(1)}, u32[]{:S(2)}, u32[]{:S(2)}) collective-permute-start(bf16[128,2048]{1,0:T(8,128)(2,1)S(1)} %add_convert_fusion.15), channel_id=1, source_target_pairs={{0,2},{1,3},{2,0},{3,1},{4,6},{5,7},{6,4},{7,5},{8,10},{9,11},{10,... | collective-permute-start | bytes 1572872 | tf_op jit(solution)/shard_map/ppermute | solution.py:194
  (137 other events, 3870.2 us)
Sparse Core Ops, SparseCore 0:
  11.8 68.2 all-gather.5
  81.8 29.0 all-gather.7
  113.0 98.4 all-gather.9
  213.0 54.9 all-gather.11
  649.4 51.1 reduce-scatter.6
  702.7 58.5 reduce-scatter.10
  824.6 80.1 reduce-scatter.4
  907.1 107.7 reduce-scatter.8

commit v2 on v1

v2 whole, which is shorter than its diff:
```python
import functools
import jax
import jax.numpy as jnp
from jax import lax
from jax.experimental import pallas as pl
from jax.experimental.pallas import tpu as pltpu
from jax.sharding import PartitionSpec as P

HD=64
B=256
BIG=1e30
F32=jnp.float32; BF=jnp.bfloat16

def nt(a,b): return lax.dot_general(a,b,(((1,),(1,)),((),())),preferred_element_type=F32)
def nn(a,b): return lax.dot_general(a,b,(((1,),(0,)),((),())),preferred_element_type=F32)


EPSILON = 1e-06
MICRO = 2
HBM = pl.BlockSpec(memory_space=pltpu.HBM)
MIB = 1 << 20
CHEAP = pl.CostEstimate(flops=1, bytes_accessed=1, transcendentals=0)


def tn(left, right):
    return lax.dot_general(left, right, (((0,), (0,)), ((), ())), preferred_element_type=F32)


def pick(size, *tiles, start=0):
    return next(tile for tile in (*tiles, 128, size) if size % tile == 0 and start % tile == 0)


def strips_kernel(w_ref, out_ref):
    def body(i, _):
        wide = jnp.broadcast_to(w_ref[0, pl.ds(i, 1), :], (B, 2 * B))
        rolled = pltpu.roll(wide, 0, 1, stride=1, stride_axis=0)
        out_ref[0, pl.ds(pl.multiple_of(i * B, B), B), :] = rolled[:, :B]
        return 0

    lax.fori_loop(0, w_ref.shape[1], body, 0)


def bias_strips(w):
    heads, tiles, _ = w.shape
    return pl.pallas_call(
        strips_kernel,
        grid=(heads,),
        in_specs=[pl.BlockSpec((1, tiles, 2 * B), lambda h: (h, 0, 0))],
        out_specs=pl.BlockSpec((1, tiles * B, B), lambda h: (h, 0, 0)),
        out_shape=jax.ShapeDtypeStruct((heads, tiles * B, B), F32),
        compiler_params=pltpu.CompilerParams(vmem_limit_bytes=60 * MIB),
        cost_estimate=CHEAP,
        name="bias_strips",
    )(w)


def attend_forward_kernel(n, extra, *refs):
    act_ref, blk_ref, qkv_ref, fq_ref, fk_ref, bias_ref = refs[:6]
    o_ref, lse_ref, qx, kx, vx, s_scr, m_scr, o_scr = refs[6 + extra :]
    lane = lax.broadcasted_iota(jnp.int32, (1, 128), 1)
    q, k, v = qkv_ref[:, 0:128], qkv_ref[:, 128:256], qkv_ref[:, 256:384]
    vt = v.T
    for h in range(2):
        own = (lane < HD) if h == 0 else (lane >= HD)
        qx[h] = jnp.where(own, q, fq_ref[...])
        kx[h] = jnp.where(own, k, fk_ref[...])
        vx[h] = jnp.concatenate([vt[h * HD : (h + 1) * HD], jnp.ones((16, vt.shape[1]), BF)], axis=0)

    def row(qi, _):
        qs = pl.ds(pl.multiple_of(qi * B, B), B)
        m_scr[...] = jnp.full_like(m_scr, -3e38)
        o_scr[...] = jnp.zeros_like(o_scr)

        def score(kb, _):
            @pl.when(act_ref[qi * n + kb] != 0)
            def _():
                ks = pl.ds(pl.multiple_of(kb * B, B), B)
                bs = pl.ds(pl.multiple_of((blk_ref[kb] - blk_ref[qi] + n - 1) * B, B), B)
                for h in range(2):
                    s = nt(kx[h, ks, :], qx[h, qs, :]) + bias_ref[h, bs, :]
                    s_scr[h, ks, :] = s
                    m_scr[h] = jnp.maximum(m_scr[h], jnp.max(s.reshape(B // 8, 8, B), axis=0))

            return 0

        lax.fori_loop(0, n, score, 0)
        peaks = [jnp.max(m_scr[h], axis=0, keepdims=True) for h in range(2)]

        def share(kb, _):
            @pl.when(act_ref[qi * n + kb] != 0)
            def _():
                ks = pl.ds(pl.multiple_of(kb * B, B), B)
                for h in range(2):
                    p = jnp.exp(s_scr[h, ks, :] - peaks[h]).astype(BF)
                    o_scr[h] += nn(vx[h, :, ks], p)

            return 0

        lax.fori_loop(0, n, share, 0)
        outs = []
        for h in range(2):
            total = o_scr[h, HD : HD + 1, :]
            outs.append(o_scr[h, 0:HD, :] / total)
            lse_ref[0, pl.ds(h, 1), qs] = peaks[h] + jnp.log(total)
        o_ref[qs, :] = jnp.concatenate(outs, axis=0).T.astype(BF)
        return 0

    lax.fori_loop(0, n, row, 0)


def attend_forward(qkv, feat_q, feat_k, bias, active, order, first, into=(), deps=()):
    length, width3 = qkv.shape
    n, number, pairs = length // B, width3 // 384, bias.shape[0] // 2
    rows = (2 * n - 1) * B
    extra = len(into) + len(deps)
    whole = pl.BlockSpec((length, 128), lambda p, *_: (0, 0))
    return pl.pallas_call(
        functools.partial(attend_forward_kernel, n, extra),
        grid_spec=pltpu.PrefetchScalarGridSpec(
            num_scalar_prefetch=2,
            grid=(number,),
            in_specs=[
                pl.BlockSpec((length, 384), lambda p, *_: (0, p)),
                whole,
                whole,
                pl.BlockSpec((2, rows, B), lambda p, *_: (p + first, 0, 0)),
            ]
            + [HBM] * extra,
            out_specs=[
                pl.BlockSpec((length, 128), lambda p, *_: (0, p + first)),
                pl.BlockSpec((1, 2, length), lambda p, *_: (p + first, 0, 0)),
            ],
            scratch_shapes=[
                pltpu.VMEM((2, length, 128), BF),
                pltpu.VMEM((2, length, 128), BF),
                pltpu.VMEM((2, HD + 16, length), BF),
                pltpu.VMEM((2, length, B), F32),
                pltpu.VMEM((2, 8, B), F32),
                pltpu.VMEM((2, HD + 16, B), F32),
            ],
        ),
        out_shape=[
            jax.ShapeDtypeStruct((length, pairs * 128), BF),
            jax.ShapeDtypeStruct((pairs, 2, length), F32),
        ],
        input_output_aliases={6 + i: i for i in range(len(into))},
        compiler_params=pltpu.CompilerParams(vmem_limit_bytes=60 * MIB),
        cost_estimate=CHEAP,
        name="attend_forward",
    )(active, order, qkv, feat_q, feat_k, bias, *into, *deps)


def attend_backward_kernel(n, extra, *refs):
    act_ref, blk_ref, qkv_ref, fq_ref, fk_ref, bias_ref, lse_ref, o_ref, do_ref, sc_ref = refs[:10]
    g_ref, fold_ref, qx, kx, v0, kt, delta, dk, dv, dqt, diag = refs[10 + extra :]
    lane = lax.broadcasted_iota(jnp.int32, (1, 128), 1)
    q, k, v = qkv_ref[:, 0:128], qkv_ref[:, 128:256], qkv_ref[:, 256:384]
    for h in range(2):
        own = (lane < HD) if h == 0 else (lane >= HD)
        qx[h] = jnp.where(own, q, fq_ref[...])
        kx[h] = jnp.where(own, k, fk_ref[...])
        v0[h] = jnp.where(own, v, jnp.zeros_like(v))
    kt[...] = k.T
    prod = (o_ref[...].astype(F32) * do_ref[...].astype(F32)).T
    for h in range(2):
        delta[h : h + 1, :] = jnp.sum(prod[h * HD : (h + 1) * HD], axis=0, keepdims=True)
    dk[...] = jnp.zeros_like(dk)
    dv[...] = jnp.zeros_like(dv)
    diag[...] = jnp.zeros_like(diag)

    def row(qi, _):
        qs = pl.ds(pl.multiple_of(qi * B, B), B)
        dqt[...] = jnp.zeros_like(dqt)
        lses = [lse_ref[0, pl.ds(h, 1), qs] for h in range(2)]
        dels = [delta[pl.ds(h, 1), qs] for h in range(2)]

        def inner(kb, _):
            @pl.when(act_ref[qi * n + kb] != 0)
            def _():
                ks = pl.ds(pl.multiple_of(kb * B, B), B)
                bs = pl.ds(pl.multiple_of((blk_ref[kb] - blk_ref[qi] + n - 1) * B, B), B)
                dob = do_ref[qs, :]
                qb = qkv_ref[qs, 0:128]
                for h in range(2):
                    s = nt(kx[h, ks, :], qx[h, qs, :]) + bias_ref[h, bs, :]
                    dp = nt(v0[h, ks, :], dob)
                    p = jnp.exp(s - lses[h])
                    ds = p * (dp - dels[h])
                    pb, dsb = p.astype(BF), ds.astype(BF)
                    diag[h, bs, :] += ds
                    dv[h, ks, :] += nn(pb, dob)
                    dk[h, ks, :] += nn(dsb, qb)
                    dqt[h] += nn(kt[h * HD : (h + 1) * HD, ks], dsb)

            return 0

        lax.fori_loop(0, n, inner, 0)
        g_ref[qs, 0:128] = (jnp.concatenate([dqt[0], dqt[1]], axis=0).T * sc_ref[qs, :]).astype(BF)
        return 0

    lax.fori_loop(0, n, row, 0)
    left = lane < HD
    g_ref[:, 128:256] = (jnp.where(left, dk[0], dk[1]) * sc_ref[...]).astype(BF)
    g_ref[:, 256:384] = (jnp.where(left, dv[0], dv[1]) * sc_ref[...]).astype(BF)
    for h in range(2):

        def fold(i, _):
            a = diag[h, pl.ds(pl.multiple_of(i * B, B), B), :]
            zero = jnp.zeros((8, B), F32)
            acc = jnp.zeros((8, 2 * B), F32)
            for g in range(B // 8):
                part = jnp.concatenate([a[8 * g : 8 * g + 8], zero], axis=1)
                acc = acc + (pltpu.roll(part, 2 * B - 8 * g, 1) if g else part)
            total = acc[0:1]
            for r in range(1, 8):
                total = total + pltpu.roll(acc[r : r + 1], 2 * B - r, 1)
            fold_ref[0, h, pl.ds(i, 1), :] = total
            return 0

        lax.fori_loop(0, 2 * n - 1, fold, 0)


def attend_backward(
    qkv, feat_q, feat_k, bias, lse, mixed, grad, scale, active, order, first, into=(), deps=()
):
    length, width3 = qkv.shape
    n, number, pairs = length // B, width3 // 384, bias.shape[0] // 2
    tiles = 2 * n - 1
    rows = tiles * B
    extra = len(into) + len(deps)
    whole = pl.BlockSpec((length, 128), lambda p, *_: (0, 0))
    one = pl.BlockSpec((length, 128), lambda p, *_: (0, p + first))
    three = pl.BlockSpec((length, 384), lambda p, *_: (0, p))
    return pl.pallas_call(
        functools.partial(attend_backward_kernel, n, extra),
        grid_spec=pltpu.PrefetchScalarGridSpec(
            num_scalar_prefetch=2,
            grid=(number,),
            in_specs=[
                three,
                whole,
                whole,
                pl.BlockSpec((2, rows, B), lambda p, *_: (p + first, 0, 0)),
                pl.BlockSpec((1, 2, length), lambda p, *_: (p + first, 0, 0)),
                one,
                one,
                whole,
            ]
            + [HBM] * extra,
            out_specs=[three, pl.BlockSpec((1, 2, tiles, 2 * B), lambda p, *_: (p + first, 0, 0, 0))],
            scratch_shapes=[
                pltpu.VMEM((2, length, 128), BF),
                pltpu.VMEM((2, length, 128), BF),
                pltpu.VMEM((2, length, 128), BF),
                pltpu.VMEM((128, length), BF),
                pltpu.VMEM((2, length), F32),
                pltpu.VMEM((2, length, 128), F32),
                pltpu.VMEM((2, length, 128), F32),
                pltpu.VMEM((2, HD, B), F32),
                pltpu.VMEM((2, rows, B), F32),
            ],
        ),
        out_shape=[
            jax.ShapeDtypeStruct((length, width3), BF),
            jax.ShapeDtypeStruct((pairs, 2, tiles, 2 * B), F32),
        ],
        input_output_aliases={10: 1} if into else {},
        compiler_params=pltpu.CompilerParams(vmem_limit_bytes=60 * MIB),
        cost_estimate=CHEAP,
        name="attend_backward",
    )(active, order, qkv, feat_q, feat_k, bias, lse, mixed, grad, scale, *into, *deps)


def load(pieces, rows, sems):
    copies, start = [], 0
    for i, piece in enumerate(pieces):
        size = piece.shape[0]
        copies.append(pltpu.make_async_copy(piece, rows.at[pl.ds(start, size)], sems.at[i]))
        start += size

    @pl.when(pl.program_id(0) == 0)
    def _():
        for copy in copies:
            copy.start()
        for copy in copies:
            copy.wait()


def product_kernel(mode, count, extra, carried, *refs):
    pieces, w_ref = refs[:count], refs[count]
    refs = refs[count + 1 :]
    if mode == "take":
        sc_ref, refs = refs[0], refs[1:]
    refs = refs[extra:]
    o_ref, refs = refs[0], refs[1:]
    if mode == "make":
        sc_ref, refs = refs[0], refs[1:]
    rows, sems = refs[carried:]
    load(pieces, rows, sems)
    if mode == "make":

        @pl.when(pl.program_id(0) == 0)
        def _():
            step = pick(rows.shape[0], 256)

            def body(i, _):
                part = pl.ds(pl.multiple_of(i * step, step), step)
                x = rows[part, :].astype(F32)
                scale = norm_scale(x)
                sc_ref[part, :] = jnp.broadcast_to(scale, (step, 128))
                return 0

            lax.fori_loop(0, rows.shape[0] // step, body, 0)

    value = nn(rows[...], w_ref[...])
    if mode != "plain":
        value = value * sc_ref[:, 0:1]
    o_ref[...] = value.astype(BF)


def product(pieces, w, start, width, mode="plain", scale=(), deps=(), carry=()):
    length, depth = sum(p.shape[0] for p in pieces), w.shape[0]
    tile = pick(width, 512, 256, start=start)
    by_row = pl.BlockSpec((length, 128), lambda j: (0, 0))
    make = mode == "make"
    return pl.pallas_call(
        functools.partial(product_kernel, mode, len(pieces), len(deps) + len(carry), len(carry)),
        grid=(width // tile,),
        in_specs=[HBM] * len(pieces)
        + [pl.BlockSpec((depth, tile), lambda j: (0, start // tile + j))]
        + [by_row] * len(scale)
        + [HBM] * (len(deps) + len(carry)),
        out_specs=[pl.BlockSpec((length, tile), lambda j: (0, j))] + [by_row] * make + [HBM] * len(carry),
        out_shape=[jax.ShapeDtypeStruct((length, width), BF)]
        + [jax.ShapeDtypeStruct((length, 128), F32)] * make
        + [jax.ShapeDtypeStruct(c.shape, c.dtype) for c in carry],
        input_output_aliases={
            len(pieces) + 1 + len(scale) + len(deps) + i: 1 + make + i for i in range(len(carry))
        },
        scratch_shapes=[pltpu.VMEM((length, depth), BF), pltpu.SemaphoreType.DMA((len(pieces),))],
        compiler_params=pltpu.CompilerParams(vmem_limit_bytes=60 * MIB),
        cost_estimate=CHEAP,
        name="rows_product",
    )(*pieces, w, *scale, *deps, *carry)


def outer_kernel(counts, extra, *refs):
    total = sum(counts)
    groups, start = [], 0
    for count in counts:
        groups.append(refs[start : start + count])
        start += count
    rights = refs[total : total + len(counts)]
    out_ref, rows, sems = refs[total + len(counts) + extra :]
    first = 0
    for m, group in enumerate(groups):
        load(group, rows.at[m], sems.at[pl.ds(first, len(group))])
        first += len(group)
    value = tn(rights[0][...], rows[0])
    for m in range(1, len(counts)):
        value = value + tn(rights[m][...], rows[m])
    out_ref[...] = value.astype(BF).T


def outer(lefts, rights, deps=(), first=0, width=None):
    length = rights[0].shape[0]
    width = width or rights[0].shape[1]
    depth = lefts[0][0].shape[1]
    tile = pick(width, 512, 640, 384, 256, start=first)
    counts = tuple(len(group) for group in lefts)
    flat = [piece for group in lefts for piece in group]
    return pl.pallas_call(
        functools.partial(outer_kernel, counts, len(deps)),
        grid=(width // tile,),
        in_specs=[HBM] * len(flat)
        + [pl.BlockSpec((length, tile), lambda j: (0, first // tile + j))] * len(rights)
        + [HBM] * len(deps),
        out_specs=pl.BlockSpec((depth, tile), lambda j: (0, j)),
        out_shape=jax.ShapeDtypeStruct((depth, width), BF),
        scratch_shapes=[
            pltpu.VMEM((len(lefts), length, depth), BF),
            pltpu.SemaphoreType.DMA((len(flat),)),
        ],
        compiler_params=pltpu.CompilerParams(vmem_limit_bytes=60 * MIB),
        cost_estimate=CHEAP,
        name="weight_gradient",
    )(*flat, *rights, *deps)


def partial_kernel(form, layouts, against, extra, *refs):
    number = len(layouts)
    rows = refs[2 * number : 2 * number + against]
    outs = refs[2 * number + against + extra :]
    value = None
    for a_ref, w_ref, (size, pitch, start) in zip(refs[:number], refs[number:], layouts):
        for i in range(a_ref.shape[1] // size):
            cols = slice(i * pitch + start, i * pitch + start + size)
            part = nt(a_ref[:, i * size : (i + 1) * size], w_ref[:, cols])
            value = part if value is None else value + part
    if against:
        total, at = 0.0, 0
        for piece in rows:
            size = piece.shape[0]
            total = total + jnp.sum(value[at : at + size] * piece[...].astype(F32), axis=0, keepdims=True)
            at += size
        outs[-1][...] = total
        outs = outs[:-1]
    value = value.astype(BF)
    if form is None:
        outs[0][...] = value
        return
    size = outs[0].shape[0]
    half = size // 2
    blocks = [value[i * size : (i + 1) * size] for i in range(4)]
    if form != "both":
        own, pair, late = outs
        first, second = (1, 2) if form == "x" else (2, 1)
        own[...] = blocks[0]
        pair[:size] = blocks[first]
        pair[size:] = blocks[3]
        late[...] = blocks[second]
        return
    own, send_x, send_y, late_x, late_y = outs
    own[...] = blocks[0]
    send_x[:half] = blocks[1][:half]
    send_x[half:] = blocks[3][:half]
    send_y[:half] = blocks[2][half:]
    send_y[half:] = blocks[3][half:]
    late_x[...] = blocks[1][half:]
    late_y[...] = blocks[2][:half]


def partial_rows(lefts, weights, widths, ats, layouts, form, deps=(), pieces=()):
    length = lefts[0].shape[0]
    depth = weights[0].shape[0]
    tile = pick(depth, 512, 256)
    size = length // 4
    heights = {
        None: [length],
        "both": [size, size, size, size // 2, size // 2],
        "x": [size, 2 * size, size],
        "y": [size, 2 * size, size],
    }[form]
    sums = [jax.ShapeDtypeStruct((1, depth), F32)] if pieces else []
    return pl.pallas_call(
        functools.partial(partial_kernel, form, layouts, len(pieces), len(deps)),
        grid=(depth // tile,),
        in_specs=[pl.BlockSpec(a.shape, lambda j: (0, 0)) for a in lefts]
        + [pl.BlockSpec((tile, width), lambda j, at=at: (j, at)) for width, at in zip(widths, ats)]
        + [pl.BlockSpec((p.shape[0], tile), lambda j: (0, j)) for p in pieces]
        + [HBM] * len(deps),
        out_specs=[pl.BlockSpec((height, tile), lambda j: (0, j)) for height in heights]
        + [pl.BlockSpec((1, tile), lambda j: (0, j))] * len(sums),
        out_shape=[jax.ShapeDtypeStruct((height, depth), BF) for height in heights] + sums,
        compiler_params=pltpu.CompilerParams(vmem_limit_bytes=60 * MIB),
        cost_estimate=CHEAP,
        name="partial_rows",
    )(*lefts, *weights, *pieces, *deps)


def ff_kernel(count, count_cot, extra, *refs):
    total = count + count_cot
    pieces, cots = refs[:count], refs[count:total]
    w_ref, d_ref = refs[total : total + 2]
    hid_ref, g_ref, rows, cot, sems = refs[total + 2 + extra :]
    load(pieces, rows, sems.at[pl.ds(0, count)])
    load(cots, cot, sems.at[pl.ds(count, count_cot)])
    tile = d_ref.shape[1]
    length = rows.shape[0]
    step = pick(length, 256)
    c = 0.7978845608028654
    for i in range(length // step):
        part = slice(i * step, (i + 1) * step)
        both = nn(rows[part], w_ref[...])
        grad = nn(cot[part], d_ref[...])
        gate, up = both[:, :tile], both[:, tile:]
        square = gate * gate
        th = jnp.tanh(c * gate * (1.0 + 0.044715 * square))
        half = 0.5 * (1.0 + th)
        value = gate * half
        slope = half + 0.5 * gate * (1.0 - th * th) * (c + 3 * 0.044715 * c * square)
        hid_ref[part] = (value * up).astype(BF)
        g_ref[part, :tile] = (grad * up * slope).astype(BF)
        g_ref[part, tile:] = (grad * value).astype(BF)


def ff_tile(width):
    return pick(width, 256)


def feed_forward(pieces, cots, w, first, number, into=(), deps=()):
    length, depth, width = sum(p.shape[0] for p in pieces), w.shape[0], w.shape[1] // 3
    tile = ff_tile(width)
    count = len(pieces) + len(cots)
    extra = len(deps) + len(into)
    return pl.pallas_call(
        functools.partial(ff_kernel, len(pieces), len(cots), extra),
        grid=(number,),
        in_specs=[HBM] * count
        + [
            pl.BlockSpec((depth, 2 * tile), lambda j: (0, j + first)),
            pl.BlockSpec((depth, tile), lambda j: (0, j + first + 2 * width // tile)),
        ]
        + [HBM] * extra,
        out_specs=[
            pl.BlockSpec((length, tile), lambda j: (0, j + first)),
            pl.BlockSpec((length, 2 * tile), lambda j: (0, j + first)),
        ],
        out_shape=[
            jax.ShapeDtypeStruct((length, width), BF),
            jax.ShapeDtypeStruct((length, 2 * width), BF),
        ],
        input_output_aliases={count + 2 + i: i for i in range(len(into))},
        scratch_shapes=[
            pltpu.VMEM((length, depth), BF),
            pltpu.VMEM((length, depth), BF),
            pltpu.SemaphoreType.DMA((count,)),
        ],
        compiler_params=pltpu.CompilerParams(vmem_limit_bytes=60 * MIB),
        cost_estimate=CHEAP,
        name="feed_forward",
    )(*pieces, *cots, w, w, *into, *deps)


def hop(part, bit, count, axis="tensor"):
    return lax.ppermute(part, axis, [(i, i ^ bit) for i in range(count)])


class Gather:
    def __init__(self, part, via, count, then=()):
        self.own = part
        if count != 4:
            self.first = self.sent = (lax.all_gather(part, "tensor", axis=0, tiled=True),)
            self.pieces = list(self.first)
            return
        from_x, from_y = hop(part, 1, count), hop(part, 2, count)
        self.first = (from_x, from_y)
        half = part.shape[0] // 2
        self.pieces = [part, from_x, from_y]
        if then:
            from_x, from_y = lax.optimization_barrier((from_x, from_y, *then))[:2]
        if via == "x":
            self.pieces.append(hop(from_y, 1, count))
        elif via == "y":
            self.pieces.append(hop(from_x, 2, count))
        else:
            self.sent = (from_y[:half], from_x[half:])
            self.pieces += [hop(self.sent[0], 1, count), hop(self.sent[1], 2, count)]


def add_kernel(number, carried, *refs):
    ins, outs = refs[: 2 * number], refs[len(refs) - number - carried :][:number]
    for i, out in enumerate(outs):
        out[...] = (ins[2 * i][...].astype(F32) + ins[2 * i + 1][...].astype(F32)).astype(BF)


def add_arrived(pairs, deps, carry):
    depth = pairs[0][0].shape[1]
    tile = pick(depth, 1024)
    specs, args, outs = [], [], []
    for late, arrived in pairs:
        height = late.shape[0]
        specs += [pl.BlockSpec((height, tile), lambda j: (0, j)), pl.BlockSpec((height, tile), lambda j: (1, j))]
        args += [late, arrived]
        outs.append(late)
    return pl.pallas_call(
        functools.partial(add_kernel, len(pairs), len(carry)),
        grid=(depth // tile,),
        in_specs=specs + [HBM] * (len(deps) + len(carry)),
        out_specs=[pl.BlockSpec((o.shape[0], tile), lambda j: (0, j)) for o in outs] + [HBM] * len(carry),
        out_shape=[jax.ShapeDtypeStruct(o.shape, o.dtype) for o in (*outs, *carry)],
        input_output_aliases={len(args) + len(deps) + i: len(outs) + i for i in range(len(carry))},
        compiler_params=pltpu.CompilerParams(vmem_limit_bytes=60 * MIB),
        cost_estimate=CHEAP,
        name="add_arrived",
    )(*args, *deps, *carry)


class Reduce:
    def __init__(self, parts, form, count, then=()):
        if then:
            parts = lax.optimization_barrier((*parts, *then))[: len(parts)]
        self.form, self.count, self.parts = form, count, parts
        if count != 4:
            self.total = lax.psum_scatter(parts[0], "tensor", scatter_dimension=0, tiled=True).astype(F32)
        elif form == "both":
            self.arrived = (hop(parts[1], 1, count), hop(parts[2], 2, count))
        else:
            self.arrived = (hop(parts[1], 1 if form == "x" else 2, count),)

    def first(self, deps=(), carry=()):
        if self.count != 4:
            return (self.total, *carry)
        if self.form == "both":
            x_first, y_first = self.arrived
            late = add_arrived([(self.parts[3], y_first), (self.parts[4], x_first)], deps, carry)
            self.second = (hop(late[0], 1, self.count), hop(late[1], 2, self.count))
        else:
            late = add_arrived([(self.parts[2], self.arrived[0])], deps, carry)
            self.second = (hop(late[0], 2 if self.form == "x" else 1, self.count),)
        return tuple(late)

    def settle(self, function, rows, kinds, deps=(), carry=()):
        if self.count != 4:
            return (*function(self.total, *rows), *carry)
        return settle_rows(
            self.form, self.parts[0], self.arrived, self.second, function, rows, kinds, deps, carry
        )


def settle_kernel(form, function, number, extra, kinds, *refs):
    own = refs[0][...].astype(F32)
    if form == "both":
        x_first, y_first, x_second, y_second = refs[1:5]
        refs = refs[5:]
        low = pl.program_id(0) == 0
        total = own + jnp.where(
            low,
            x_first[...].astype(F32) + y_second[...].astype(F32),
            y_first[...].astype(F32) + x_second[...].astype(F32),
        )
    else:
        total = own + refs[1][...].astype(F32) + refs[2][...].astype(F32)
        refs = refs[3:]
    values = function(total, *(ref[...] for ref in refs[:number]))
    for out, kind, value in zip(refs[number + extra :], kinds, values):
        if kind != "sum":
            out[...] = value
            continue

        @pl.when(pl.program_id(0) == 0)
        def _(out=out):
            out[...] = jnp.zeros_like(out)

        out[...] += value


def settle_rows(form, own, arrived, second, function, rows, kinds, deps, carry):
    size, depth = own.shape
    half = size // 2
    block = pl.BlockSpec((half, depth), lambda i: (i, 0))
    top = pl.BlockSpec((half, depth), lambda i: (0, 0))
    others = [top] * 4 if form == "both" else [block] * 2
    out_specs, out_shape = [], []
    for kind in kinds:
        out_specs.append(pl.BlockSpec((1, depth), lambda i: (0, 0)) if kind == "sum" else block)
        out_shape.append(
            jax.ShapeDtypeStruct((1, depth), F32) if kind == "sum" else jax.ShapeDtypeStruct((size, depth), kind)
        )
    return pl.pallas_call(
        functools.partial(settle_kernel, form, function, len(rows), len(deps) + len(carry), kinds),
        grid=(2,),
        in_specs=[block] + others + [block] * len(rows) + [HBM] * (len(deps) + len(carry)),
        out_specs=out_specs + [HBM] * len(carry),
        out_shape=out_shape + [jax.ShapeDtypeStruct(c.shape, c.dtype) for c in carry],
        input_output_aliases={
            1 + len(others) + len(rows) + len(deps) + i: len(kinds) + i for i in range(len(carry))
        },
        compiler_params=pltpu.CompilerParams(vmem_limit_bytes=60 * MIB),
        cost_estimate=CHEAP,
        name="settle_rows",
    )(own, *arrived, *second, *rows, *deps, *carry)


def bits(count):
    assert count & (count - 1) == 0
    return [1 << i for i in range(count.bit_length() - 1)]


def sum_over(value, axis, count):
    for bit in bits(count):
        value = value + hop(value, bit, count, axis)
    return value


def norm_scale(rows):
    return lax.rsqrt(jnp.mean(rows * rows, axis=-1, keepdims=True) + EPSILON)


def add_branch(total, rows):
    middle = rows.astype(F32) + total
    return middle, (middle * norm_scale(middle)).astype(BF)


def add_last(total, middle):
    return ((middle + total).astype(BF),)


def turn_back(total, middle, cotangent):
    scale = norm_scale(middle)
    inner = jnp.mean(total * middle, axis=-1, keepdims=True)
    grad = cotangent.astype(F32) + scale * total - middle * (scale * scale * scale * inner)
    return grad, grad.astype(BF), jnp.sum(total * middle * scale, axis=0, keepdims=True)


def finish_back(total, rows, grad_middle):
    rows = rows.astype(F32)
    scale = norm_scale(rows)
    inner = jnp.mean(total * rows, axis=-1, keepdims=True)
    grad = grad_middle + total - rows * (scale * scale * inner)
    return (grad.astype(BF),)


def unpack_kernel(groups, pitch, *refs):
    parts, gain_ref, outs = refs[: len(groups)], refs[len(groups)], refs[len(groups) + 1 :]
    at = 0
    for part, number in zip(parts, groups):
        size = part.shape[1] // (number * pitch)
        for i in range(number):
            for k, out in enumerate(outs):
                start = (i * pitch + k) * size
                out[:, at : at + size] = part[:, start : start + size].astype(F32) * gain_ref[...]
            at += size


def turn_kernel(number, *refs):
    for part, out in zip(refs[:number], refs[number:]):
        out[...] = part[...].astype(F32).T


def turned(parts):
    return pl.pallas_call(
        functools.partial(turn_kernel, len(parts)),
        out_shape=[jax.ShapeDtypeStruct(p.shape[::-1], F32) for p in parts],
        compiler_params=pltpu.CompilerParams(vmem_limit_bytes=60 * MIB),
        cost_estimate=CHEAP,
        name="turned",
    )(*parts)


def unpack(parts, groups, pitch, gain):
    rows_w = gain.shape[0]
    width = sum(p.shape[1] for p in parts) // pitch
    return pl.pallas_call(
        functools.partial(unpack_kernel, groups, pitch),
        out_shape=[jax.ShapeDtypeStruct((rows_w, width), F32)] * pitch,
        compiler_params=pltpu.CompilerParams(vmem_limit_bytes=60 * MIB),
        cost_estimate=CHEAP,
        name="unpack",
    )(*parts, gain)


def local(
    count_dp,
    count,
    tokens,
    cotangent,
    doc_lengths,
    rel_bucket,
    gain_attn,
    w_query,
    w_key,
    w_value,
    w_out,
    rel_table,
    gain_ff,
    w_gate,
    w_up,
    w_down,
):
    slots = tokens.shape[0]
    length = slots * count
    blocks = length // B
    rows_w, width = w_query.shape
    width_ff = w_gate.shape[1]
    pairs = width // 128
    heads = width // HD
    buckets_local = rel_table.shape[0]
    buckets = buckets_local * count_dp
    docs = doc_lengths.shape[1]
    tile = ff_tile(width_ff)
    me = lax.axis_index("dp").astype(jnp.int32)

    def spread(part):
        return lax.all_gather(part, "dp", axis=0, tiled=True)

    def after(value, *others):
        return lax.optimization_barrier((value, *others))[0]

    xs = [tokens[:, m] for m in range(MICRO)]
    gain_one = gain_attn.astype(F32)[:, None]
    gain_two = gain_ff.astype(F32)[:, None]
    cuts = 2
    each = pairs // cuts
    part_w = each * 384

    def grouped(weights, size):
        number = weights[0].shape[1] // size
        return jnp.stack([w.reshape(rows_w, number, size) for w in weights], axis=2).reshape(rows_w, -1)

    def scaled(w, gain):
        return (w.astype(F32) * gain).astype(BF)

    local_qkv = grouped([scaled(w, gain_one) for w in (w_query, w_key, w_value)], 128)
    halves = [local_qkv[:, cut * part_w : (cut + 1) * part_w] for cut in range(cuts)]
    halves[-1] = jnp.concatenate([halves[-1], w_out.T], axis=1)
    full_qkv = [spread(half) for half in halves]
    full_out, out_at = full_qkv[-1], part_w
    local_ff = grouped([scaled(after(w_gate, xs[0]), gain_two), scaled(w_up, gain_two)], tile)
    full_ff = spread(jnp.concatenate([local_ff, w_down.T], axis=1))

    table = rel_table.reshape(1, buckets_local * heads)
    for bit in bits(count_dp):
        table = jnp.concatenate([table, hop(table, bit, count_dp, "dp")], axis=0)
    table = jnp.take(table, jnp.arange(count_dp, dtype=jnp.int32) ^ me, axis=0).reshape(buckets, heads)
    reverse = jnp.concatenate([jnp.full((1,), -1, jnp.int32), rel_bucket[::-1]])
    onehot = reverse[None, :] == jnp.arange(buckets, dtype=jnp.int32)[:, None]
    offsets = tn(table, onehot.astype(BF)).reshape(heads, 2 * blocks, B)
    tiles = 2 * blocks - 1
    ahead = offsets[:, ::-1]
    bias = bias_strips(jnp.concatenate([ahead[:, :tiles], ahead[:, 1:]], axis=2))

    order = jnp.arange(blocks, dtype=jnp.int32)
    if count == 4:
        order = order ^ lax.axis_index("tensor").astype(jnp.int32)
    positions = (order[:, None] * B + jnp.arange(B, dtype=jnp.int32)[None]).reshape(-1)
    ends = jnp.cumsum(doc_lengths, axis=1)
    lane = jnp.arange(128, dtype=jnp.int32) % HD

    cs, masks = [], []
    for m in range(MICRO):
        cs.append(cotangent[:, m])
        number = jnp.sum((positions[:, None] >= ends[m][None, :]).astype(jnp.int32), axis=1)
        by_block = number.reshape(blocks, B)
        least, most = by_block.min(axis=1), by_block.max(axis=1)
        active = (least[:, None] <= most[None, :]) & (least[None, :] <= most[:, None])
        same = number[:, None] == lane[None, :]
        feat_q = same.astype(BF)
        feat_k = jnp.where(same | (lane >= docs)[None, :], 0.0, -BIG).astype(BF)
        masks.append((feat_q, feat_k, active.astype(jnp.int32).reshape(-1)))
    form = "both" if count == 4 else None
    ones = [Gather(xs[0], "both", count, (bias,))]
    ones.append(Gather(after(xs[1], *ones[0].pieces), "x", count))

    def project(m, cut, scale, deps):
        mode = "take" if scale else "make"
        return product(ones[m].pieces, full_qkv[cut], 0, part_w, mode, scale, deps)

    def forward(m, cut, qkv, into, deps):
        feat_q, feat_k, active = masks[m]
        return attend_forward(qkv, feat_q, feat_k, bias, active, order, cut * each, into, deps)

    def out_rows(mixed, deps):
        return partial_rows([mixed], [full_out], [full_out.shape[1]], [0], [(width, width, out_at)], form, deps)

    def ff_rows(left, inner, way, deps):
        size = 2 * width_ff if inner else width_ff
        return partial_rows([left], [full_ff], [size], [0 if inner else 2], [(size, size, 0)], way, deps)

    def qkv_rows(projects, m, deps):
        return partial_rows(
            projects, full_qkv, [part_w] * cuts, [0] * cuts, [(part_w, part_w, 0)] * cuts, form, deps, ones[m].pieces
        )

    def scatter(value):
        return lax.psum_scatter(value, "dp", scatter_dimension=0, tiled=True)

    qkv_0a, scale_0 = project(0, 0, (), ())
    cots = [Gather(after(cs[0], qkv_0a), "y", count)]
    into = forward(0, 0, qkv_0a, (), ())
    (qkv_0b,) = project(0, 1, (scale_0,), (into[0], *ones[1].first))
    cots.append(Gather(after(cs[1], qkv_0b), "x", count))
    mixed_0, lse_0 = forward(0, 1, qkv_0b, into, ones[1].first)
    parts = out_rows(mixed_0, cots[0].first)
    sum_0 = Reduce(parts, form, count)
    qkv_1a, scale_1 = project(1, 0, (), (parts[0],))
    into = forward(1, 0, qkv_1a, (), (*cots[0].pieces, *cots[1].first))
    late = sum_0.first((into[0],))
    (qkv_1b,) = project(1, 1, (scale_1,), (late[0],))
    middle_0, normed = sum_0.settle(add_branch, [xs[0]], (F32, BF), (qkv_1b, *cots[1].pieces))
    twos = [Gather(normed, "both", count)]
    mixed_1, lse_1 = forward(1, 1, qkv_1b, into, (normed,))
    parts = out_rows(mixed_1, twos[0].sent)
    sum_1 = Reduce(parts, form, count)

    steps = width_ff // tile
    early = (steps + 1) // 2
    into = feed_forward(twos[0].pieces, cots[0].pieces, full_ff, 0, early, (), (parts[0],))
    late = sum_1.first((into[0],))
    hidden_0, grad_ff_0 = feed_forward(
        twos[0].pieces, cots[0].pieces, full_ff, early, steps - early, into, (late[0],)
    )
    middle_1, normed = sum_1.settle(add_branch, [xs[1]], (F32, BF), (hidden_0,))
    twos.append(Gather(normed, "both", count))
    parts = ff_rows(grad_ff_0, True, form, (normed,))
    sum_0 = Reduce(parts, form, count, twos[1].pieces)
    hidden_1, grad_ff_1 = feed_forward(
        twos[1].pieces, cots[1].pieces, full_ff, 0, steps, (), (parts[0],)
    )
    late = sum_0.first((hidden_1,))
    parts = ff_rows(grad_ff_1, True, form, (late[0],))
    sum_1 = Reduce(parts, form, count)
    grad_middle_0, rounded, gain_two_0 = sum_0.settle(
        turn_back, [middle_0, cs[0]], (F32, BF, "sum"), (parts[0],)
    )
    mids = [Gather(rounded, "both", count)]
    weight = outer([c.pieces for c in cots], [hidden_0, hidden_1], (rounded,))
    late = sum_1.first((), (weight,))
    grad_down = scatter(late[-1])
    two_pieces, grad_ffs = [g.pieces for g in twos], [grad_ff_0, grad_ff_1]
    ff_half = early * 2 * tile
    weight = outer(two_pieces, grad_ffs, (late[0], *mids[0].sent), 0, ff_half)
    grad_middle_1, rounded, gain_two_1, weight = sum_1.settle(
        turn_back, [middle_1, cs[1]], (F32, BF, "sum"), tuple(mids[0].pieces), (weight,)
    )
    grad_ff_a = scatter(weight)
    mids.append(Gather(rounded, "both", count))

    def backward(m, qkv, lse, mixed, grad, scale, cut, into, deps):
        feat_q, feat_k, active = masks[m]
        return attend_backward(
            qkv, feat_q, feat_k, bias, lse, mixed, grad, scale, active, order, cut * each, into, deps
        )

    way = ("x", "y") if form else (None, None)
    (grad,) = product(mids[0].pieces, full_out, out_at, width, deps=(rounded,))
    grad_0a, fold = backward(0, qkv_0a, lse_0, mixed_0, grad, scale_0, 0, (), ())
    parts = ff_rows(hidden_0, False, way[0], (grad_0a,))
    down_0 = Reduce(parts, way[0], count)
    grad_0b, fold_0 = backward(0, qkv_0b, lse_0, mixed_0, grad, scale_0, 1, (fold,), (parts[0],))
    *parts, gain_one_0 = qkv_rows([grad_0a, grad_0b], 0, (*mids[1].sent, grad_down))
    sum_0 = Reduce(parts, form, count)
    weight = outer(two_pieces, grad_ffs, (parts[0],), ff_half, 2 * width_ff - ff_half)
    late = down_0.first((grad_ff_a, weight))
    (grad,) = product(mids[1].pieces, full_out, out_at, width, deps=(late[0],))
    late = sum_0.first((grad,), (weight,))
    grad_ff_b = scatter(late[-1])
    grad_1a, fold = backward(1, qkv_1a, lse_1, mixed_1, grad, scale_1, 0, (), (late[0],))
    (output_0,) = down_0.settle(add_last, [middle_0], (BF,), (grad_1a,))
    weight = outer([g.pieces for g in mids], [mixed_0, mixed_1], (output_0,))
    token_0, weight = sum_0.settle(finish_back, [xs[0], grad_middle_0], (BF,), (), (weight,))
    grad_out = scatter(weight)
    weight = outer([g.pieces for g in ones], [grad_0a, grad_1a], (token_0,))
    parts = ff_rows(hidden_1, False, way[1], (weight, grad_ff_b))
    down_1 = Reduce(parts, way[1], count)
    grad_1b, fold_1 = backward(1, qkv_1b, lse_1, mixed_1, grad, scale_1, 1, (fold,), (parts[0],))
    late = down_1.first((grad_1b,), (weight,))
    grad_qkv_a = scatter(late[-1])
    *parts, gain_one_1 = qkv_rows([grad_1a, grad_1b], 1, (late[0], grad_out))
    sum_1 = Reduce(parts, form, count)
    weight = outer([g.pieces for g in ones], [grad_0b, grad_1b], (parts[0],))
    late = sum_1.first((), (weight,))
    grad_qkv_b = scatter(late[-1])
    (output_1,) = down_1.settle(add_last, [middle_1], (BF,), (late[0],))
    grad_gate, grad_up = unpack(
        [grad_ff_a, grad_ff_b], (early, steps - early), 2, gain_two
    )
    grad_out, grad_down = turned([grad_out, grad_down])
    fold = (fold_0 + fold_1).reshape(heads, tiles, 2 * B)
    zero = jnp.zeros((heads, 1, B), F32)
    by_offset = (
        jnp.concatenate([fold[:, :, :B], zero], axis=1)
        + jnp.concatenate([zero, fold[:, :, B:]], axis=1)
    )[:, ::-1].reshape(heads, 2 * length)
    grad_table = lax.dot_general(
        onehot.astype(F32), by_offset, (((1,), (1,)), ((), ())), precision=lax.Precision.HIGHEST
    )
    small = jnp.concatenate(
        [
            (gain_one_0 + gain_one_1).reshape(count_dp, rows_w),
            (gain_two_0 + gain_two_1).reshape(count_dp, rows_w),
            grad_table.reshape(count_dp, buckets_local * heads),
        ],
        axis=1,
    )
    small = lax.dynamic_index_in_dim(sum_over(small, "dp", count_dp), me, 0, keepdims=False)
    both_gains = sum_over(small[: 2 * rows_w], "tensor", count)
    (token_1,) = sum_1.settle(
        finish_back,
        [xs[1], grad_middle_1],
        (BF,),
        (output_1, grad_qkv_a, grad_gate, grad_out, grad_down, both_gains),
    )
    return (
        jnp.stack([output_0, output_1], axis=1),
        jnp.stack([token_0, token_1], axis=1),
        both_gains[:rows_w] / gain_one[:, 0],
        *unpack([grad_qkv_a, grad_qkv_b], (each, each), 3, gain_one),
        grad_out,
        small[2 * rows_w :].reshape(buckets_local, heads),
        both_gains[rows_w:] / gain_two[:, 0],
        grad_gate,
        grad_up,
        grad_down,
    )


def solution(mesh):
    row, col = P("dp", "tensor"), P("tensor", "dp")
    acts = P("tensor", "dp", None)
    in_specs = (
        acts, acts, P("dp", None), P(), P("dp"), row, row, row, col, row, P("dp"), row, row, col
    )
    out_specs = (acts, acts, P("dp"), row, row, row, col, row, P("dp"), row, row, col)
    body = functools.partial(local, mesh.shape["dp"], mesh.shape["tensor"])
    return jax.shard_map(body, mesh=mesh, in_specs=in_specs, out_specs=out_specs, check_vma=False)
```

time: 1130 us -> 933 us (0.83); the launches traced: 1130 us -> 926 us
  Pallas kernels: 194 us -> 583 us
  matrix products: 246 us -> 0.39 us
  waiting for transfers between devices: 370 us -> 146 us
  blocking collectives: 95.4 us -> 0 us
  other arithmetic: 60.8 us -> 12.6 us
  starting transfers between devices: 65.3 us -> 92.7 us
    pallas_call x5 -> x51, Pallas kernels: 194 us -> 583 us  [the longest x4 136 us: attend_backward(): pl.pallas_call(functools.partial(attend_backward_kernel, n, extra), grid_...]
    ppermute x64 -> x65, waiting for transfers between devices: 369 us -> 146 us  [hop(): return lax.ppermute(part, axis, [(i, i ^ bit) for i in range(count)])]
    dot_general x17 -> x0, matrix products: 158 us -> none  [the longest x8 82.2 us: nn(): lax.dot_general(a, b, (((1,), (0,)), ((), ())), preferred_element_type=F32)]
    dot_general x8 -> x1, matrix products: 87.9 us -> 0.2 us  [tn(): lax.dot_general(left, right, (((0,), (0,)), ((), ())), preferred_element_...]
    unnamed x2 -> x0, blocking collectives: 86.8 us -> none
    ppermute x64 -> x65, starting transfers between devices: 65 us -> 92.4 us  [hop(): return lax.ppermute(part, axis, [(i, i ^ bit) for i in range(count)])]
    concatenate x23 -> x5, other arithmetic: 16.6 us -> 2.33 us  [the longest x1 1.39 us: local(): full_ff = spread(jnp.concatenate([local_ff, w_down.T], axis=1))]
    add x15 -> x8, other arithmetic: 11.9 us -> 0.1 us  [the longest x1 0.03 us: local(): gain_one_0 + gain_one_1]
  transfers between devices with their start and end apart: 72 -> 74, of which waited for: 37 -> 25; matrix products, arithmetic and copies ran while one was open for 28% -> 7% of each run, Pallas kernels for 17% -> 59%
where the time goes in v2:
time: 933 us; the launch traced here: 926 us
  Pallas kernels  583 us (62%)
  waiting for transfers between devices  146 us (16%)
  starting transfers between devices  92.7 us (10%)
  local copies, waits for them, and re-layouts  76.3 us (8%)
  between operations  15.3 us (2%)
  other arithmetic  12.6 us (1%)
    ppermute x65, waiting for transfers between devices, hop(): return lax.ppermute(part, axis, [(i, i ^ bit) for i in range(count)])  146 us
    pallas_call x4, Pallas kernels, attend_backward(): pl.pallas_call(functools.partial(attend_backward_kernel, n, extra), grid_...  136 us
    pallas_call x6, Pallas kernels, outer(): pl.pallas_call(functools.partial(outer_kernel, counts, len(deps)), grid=(...  98.2 us
    ppermute x65, starting transfers between devices, hop(): return lax.ppermute(part, axis, [(i, i ^ bit) for i in range(count)])  92.4 us
    pallas_call x8, Pallas kernels, partial_rows(): pl.pallas_call(functools.partial(partial_kernel, form, layouts, len(piece...  87.1 us
    pallas_call x4, Pallas kernels, attend_forward(): pl.pallas_call(functools.partial(attend_forward_kernel, n, extra), grid_s...  75.4 us
    pallas_call x3, Pallas kernels, feed_forward(): pl.pallas_call(functools.partial(ff_kernel, len(pieces), len(cots), extra...  60.9 us
    pallas_call x6, Pallas kernels, product(): pl.pallas_call(functools.partial(product_kernel, mode, len(pieces), len(d...  50 us
  transfers between devices with their start and end apart: 74, of which 25 were waited for; matrix products, arithmetic and copies ran while one was open for 7% of the time, Pallas kernels for 59%

profile of v2, /device:TPU:0, one launch (start us, length us, event | category | flops | bytes accessed | tf_op | source)
XLA Modules:
  0.0 926.1 jit_solution(10414273627219477339)
XLA Ops:
  44.2 10.6 %bias_strips.1.refs_5_ = f32[8,1792,256]{2,1,0:T(8,128)} custom-call(f32[8,7,512]{2,1,0:T(8,128)} %pad_maximum_fusion.6.w_ref), custom_call_target="tpu_custom_call" | custom-call | flops 1 | bytes 1 | tf_op jit(solution)/shard_map/bias_strips/pallas_call | solution.py:45
  60.3 9.5 %collective-permute-done.6.refs_4_.refs_8_ = bf16[128,2048]{1,0:T(8,128)(2,1)S(1)} collective-permute-done((bf16[128,2048]{1,0:T(8,128)(2,1)}, bf16[128,2048]{1,0:T(8,128)(2,1)S(1)}, u32[]{:S(2)}, u32[]{:S(2)}) %collective-permute-start.6) | collective-permute-done | bytes 524320 | tf_op jit(solution)/shard_map/ppermute | solution.py:526
  72.4 6.9 fusion.10
  84.8 9.5 %collective-permute-done.8.refs_9_.refs_2_.refs_7_.refs_6_ = bf16[256,2048]{1,0:T(8,128)(2,1)S(1)} collective-permute-done((bf16[256,2048]{1,0:T(8,128)(2,1)S(1)}, bf16[256,2048]{1,0:T(8,128)(2,1)S(1)}, u32[]{:S(2)}, u32[]{:S(2)}) %collective-permute-start.8) | collective-permute-done | bytes 1048608 | tf_op jit(solution)/shard_map/ppermute | solution.py:526
  95.9 9.4 %rows_product.6 = (bf16[1024,768]{1,0:T(8,128)(2,1)}, f32[1024,128]{1,0:T(8,128)}) custom-call(bf16[256,2048]{1,0:T(8,128)(2,1)} %bitcast.49, bf16[256,2048]{1,0:T(8,128)(2,1)} %copy-done.5, bf16[256,2048]{1,0:T(8,128)(2,1)} %copy-done.4, bf16[128,2048]{1,0:T(8,128)(2,1)} %copy-done.12, bf16[128,2048]{1,0:T(8,128)(2,1)} %copy-done.11, ...), custom_call_target="tpu_custom_call" | custom-call | flops 1 | bytes 1 | tf_op jit(solution)/shard_map/rows_product/pallas_call | solution.py:326
  112.9 20.9 %attend_forward.4 = (bf16[1024,512]{1,0:T(8,128)(2,1)}, f32[4,2,1024]{2,1,0:T(2,128)}) custom-call(s32[16]{0:T(128)} %reshape.200.refs_0_, s32[4]{0:T(128)} %iota_xor_fusion.refs_1_, bf16[1024,768]{1,0:T(8,128)(2,1)} %get-tuple-element.127.refs_2_, bf16[1024,128]{1,0:T(8,128)(2,1)} %get-tuple-element.300.refs_3_, ...), custom_call_target="tpu_custom_call" | custom-call | flops 1 | bytes 1 | tf_op jit(solution)/shard_map/attend_forward/pallas_call | solution.py:117
  134.7 8.6 rows_product.7.refs_2_
  150.1 20.6 %attend_forward.5 = (bf16[1024,512]{1,0:T(8,128)(2,1)}, f32[4,2,1024]{2,1,0:T(2,128)}) custom-call(s32[16]{0:T(128)} %reshape.200.refs_0_, s32[4]{0:T(128)} %iota_xor_fusion.refs_1_, bf16[1024,768]{1,0:T(8,128)(2,1)} %rows_product.7.refs_2_, bf16[1024,128]{1,0:T(8,128)(2,1)} %get-tuple-element.300.refs_3_, ...), custom_call_target="tpu_custom_call", output_to_operand_aliasing={{0}: (6, {}), {1}: (7, {})} | custom-call | flops 1 | bytes 1 | tf_op jit(solution)/shard_map/attend_forward/pallas_call | solution.py:117
  170.6 6.4 partial_rows.8
  180.0 9.5 %rows_product.8 = (bf16[1024,768]{1,0:T(8,128)(2,1)}, f32[1024,128]{1,0:T(8,128)}) custom-call(bf16[256,2048]{1,0:T(8,128)(2,1)} %bitcast.58, bf16[256,2048]{1,0:T(8,128)(2,1)} %copy-done.3, bf16[256,2048]{1,0:T(8,128)(2,1)} %copy-done.2, bf16[256,2048]{1,0:T(8,128)(2,1)} %collective-permute-done.13.refs_3_.refs_8_.refs_7_, ...), custom_call_target="tpu_custom_call" | custom-call | flops 1 | bytes 1 | tf_op jit(solution)/shard_map/rows_product/pallas_call | solution.py:326
  192.9 17.0 %attend_forward.6 = (bf16[1024,512]{1,0:T(8,128)(2,1)}, f32[4,2,1024]{2,1,0:T(2,128)}) custom-call(s32[16]{0:T(128)} %reshape.201.refs_0_, s32[4]{0:T(128)} %iota_xor_fusion.refs_1_, bf16[1024,768]{1,0:T(8,128)(2,1)} %get-tuple-element.138.refs_2_, bf16[1024,128]{1,0:T(8,128)(2,1)} %get-tuple-element.299.refs_3_, ...), custom_call_target="tpu_custom_call" | custom-call | flops 1 | bytes 1 | tf_op jit(solution)/shard_map/attend_forward/pallas_call | solution.py:117
  214.7 8.6 rows_product.9.refs_6_.refs_2_
  223.3 8.4 collective-permute-done.17.refs_3_
  233.5 4.2 settle_rows.8
  239.1 17.1 %attend_forward.7 = (bf16[1024,512]{1,0:T(8,128)(2,1)}, f32[4,2,1024]{2,1,0:T(2,128)}) custom-call(s32[16]{0:T(128)} %reshape.201.refs_0_, s32[4]{0:T(128)} %iota_xor_fusion.refs_1_, bf16[1024,768]{1,0:T(8,128)(2,1)} %rows_product.9.refs_6_.refs_2_, bf16[1024,128]{1,0:T(8,128)(2,1)} %get-tuple-element.299.refs_3_, ...), custom_call_target="tpu_custom_call", output_to_operand_aliasing={{0}: (6, {}), {1}: (7, {})} | custom-call | flops 1 | bytes 1 | tf_op jit(solution)/shard_map/attend_forward/pallas_call | solution.py:117
  259.8 6.4 partial_rows.9
  270.3 26.7 %collective-permute-done.22.refs_3_ = bf16[128,2048]{1,0:T(8,128)(2,1)S(1)} collective-permute-done((bf16[128,2048]{1,0:T(8,128)(2,1)}, bf16[128,2048]{1,0:T(8,128)(2,1)S(1)}, u32[]{:S(2)}, u32[]{:S(2)}) %collective-permute-start.22) | collective-permute-done | bytes 524320 | tf_op jit(solution)/shard_map/ppermute | solution.py:526
  298.0 19.0 %feed_forward.3 = (bf16[1024,1280]{1,0:T(8,128)(2,1)}, bf16[1024,2560]{1,0:T(8,128)(2,1)}) custom-call(bf16[256,2048]{1,0:T(8,128)(2,1)} %get-tuple-element.144.refs_8_.refs_0_, bf16[256,2048]{1,0:T(8,128)(2,1)} %copy-done.8, bf16[256,2048]{1,0:T(8,128)(2,1)} %copy-done.7, bf16[128,2048]{1,0:T(8,128)(2,1)} %copy-done.20, bf16[128,2048]{1,0:T(8,128)(2,1)} %copy-done.21, ...), custom_call_target="tpu_custom_call" | custom-call | flops 1 | bytes 1 | tf_op jit(solution)/shard_map/feed_forward/pallas_call | solution.py:496
  323.6 15.3 %feed_forward.4 = (bf16[1024,1280]{1,0:T(8,128)(2,1)}, bf16[1024,2560]{1,0:T(8,128)(2,1)}) custom-call(bf16[256,2048]{1,0:T(8,128)(2,1)} %get-tuple-element.144.refs_8_.refs_0_, bf16[256,2048]{1,0:T(8,128)(2,1)} %copy-done.8, bf16[256,2048]{1,0:T(8,128)(2,1)} %copy-done.7, ...), custom_call_target="tpu_custom_call", output_to_operand_aliasing={{0}: (11, {}), {1}: (12, {})} | custom-call | flops 1 | bytes 1 | tf_op jit(solution)/shard_map/feed_forward/pallas_call | solution.py:496
  345.4 20.8 %collective-permute-done.29.refs_2_.refs_7_ = bf16[256,2048]{1,0:T(8,128)(2,1)S(1)} collective-permute-done((bf16[256,2048]{1,0:T(8,128)(2,1)}, bf16[256,2048]{1,0:T(8,128)(2,1)S(1)}, u32[]{:S(2)}, u32[]{:S(2)}) %collective-permute-start.29) | collective-permute-done | bytes 1048608 | tf_op jit(solution)/shard_map/ppermute | solution.py:526
  370.3 16.1 %partial_rows.10 = (bf16[256,2048]{1,0:T(8,128)(2,1)}, bf16[256,2048]{1,0:T(8,128)(2,1)}, bf16[256,2048]{1,0:T(8,128)(2,1)}, bf16[128,2048]{1,0:T(8,128)(2,1)}, bf16[128,2048]{1,0:T(8,128)(2,1)}) custom-call(bf16[1024,2560]{1,0:T(8,128)(2,1)} %get-tuple-element.158.refs_0_.refs_10_, bf16[2048,3840]{1,0:T(8,128)(2,1)} %all-gather.8.cloned.1.call-done.refs_9_.refs_10_.refs_1_, ...), custom_call_target="tpu_custom_call" | custom-call | flops 1 | bytes 1 | tf_op jit(solution)/shard_map/partial_rows/pallas_call | solution.py:445
  387.5 26.6 %feed_forward.5 = (bf16[1024,1280]{1,0:T(8,128)(2,1)}, bf16[1024,2560]{1,0:T(8,128)(2,1)}) custom-call(bf16[256,2048]{1,0:T(8,128)(2,1)} %get-tuple-element.160.refs_2_.refs_0_.refs_5_, bf16[256,2048]{1,0:T(8,128)(2,1)} %copy-done.14, bf16[256,2048]{1,0:T(8,128)(2,1)} %copy-done.13, bf16[128,2048]{1,0:T(8,128)(2,1)} %copy-done.26, ...), custom_call_target="tpu_custom_call" | custom-call | flops 1 | bytes 1 | tf_op jit(solution)/shard_map/feed_forward/pallas_call | solution.py:496
  417.8 15.9 %partial_rows.11 = (bf16[256,2048]{1,0:T(8,128)(2,1)}, bf16[256,2048]{1,0:T(8,128)(2,1)}, bf16[256,2048]{1,0:T(8,128)(2,1)}, bf16[128,2048]{1,0:T(8,128)(2,1)}, bf16[128,2048]{1,0:T(8,128)(2,1)}) custom-call(bf16[1024,2560]{1,0:T(8,128)(2,1)} %get-tuple-element.175.refs_0_.refs_11_, bf16[2048,3840]{1,0:T(8,128)(2,1)} %all-gather.8.cloned.1.call-done.refs_9_.refs_10_.refs_1_, ...), custom_call_target="tpu_custom_call" | custom-call | flops 1 | bytes 1 | tf_op jit(solution)/shard_map/partial_rows/pallas_call | solution.py:445
  437.8 19.0 %collective-permute-done.35.refs_4_ = bf16[128,2048]{1,0:T(8,128)(2,1)S(1)} collective-permute-done((bf16[128,2048]{1,0:T(8,128)(2,1)}, bf16[128,2048]{1,0:T(8,128)(2,1)S(1)}, u32[]{:S(2)}, u32[]{:S(2)}) %collective-permute-start.35) | collective-permute-done | bytes 524320 | tf_op jit(solution)/shard_map/ppermute | solution.py:526
  457.9 5.7 settle_rows.10
  463.6 19.7 %weight_gradient.6.refs_4_ = bf16[2048,1280]{1,0:T(8,128)(2,1)} custom-call(bf16[256,2048]{1,0:T(8,128)(2,1)} %bitcast.71, bf16[256,2048]{1,0:T(8,128)(2,1)} %collective-permute-done.9.refs_2_.refs_7_.refs_6_.refs_1_, bf16[256,2048]{1,0:T(8,128)(2,1)} %collective-permute-done.10.refs_3_.refs_8_.refs_7_.refs_2_, bf16[256,2048]{1,0:T(8,128)(2,1)} %copy-done.9, ...), custom_call_target="tpu_custom_call" | custom-call | flops 1 | bytes 1 | tf_op jit(solution)/shard_map/weight_gradient/pallas_call | solution.py:372
  492.3 17.3 %collective-permute-done.37.refs_9_.refs_2_ = bf16[256,2048]{1,0:T(8,128)(2,1)S(1)} collective-permute-done((bf16[256,2048]{1,0:T(8,128)(2,1)S(1)}, bf16[256,2048]{1,0:T(8,128)(2,1)S(1)}, u32[]{:S(2)}, u32[]{:S(2)}) %collective-permute-start.37) | collective-permute-done | bytes 1048608 | tf_op jit(solution)/shard_map/ppermute | solution.py:526
  513.1 21.3 %weight_gradient.7.refs_12_ = bf16[2048,1536]{1,0:T(8,128)(2,1)} custom-call(bf16[256,2048]{1,0:T(8,128)(2,1)} %get-tuple-element.144.refs_8_.refs_0_, bf16[256,2048]{1,0:T(8,128)(2,1)} %copy-done.8, bf16[256,2048]{1,0:T(8,128)(2,1)} %copy-done.7, bf16[128,2048]{1,0:T(8,128)(2,1)} %copy-done.20, bf16[128,2048]{1,0:T(8,128)(2,1)} %copy-done.21, ...), custom_call_target="tpu_custom_call" | custom-call | flops 1 | bytes 1 | tf_op jit(solution)/shard_map/weight_gradient/pallas_call | solution.py:372
  535.5 5.7 settle_rows.11
  544.4 7.1 rows_product.10.refs_8_
  551.5 36.5 %attend_backward.4 = (bf16[1024,768]{1,0:T(8,128)(2,1)}, f32[4,2,7,512]{3,2,1,0:T(8,128)}) custom-call(s32[16]{0:T(128)} %reshape.200.refs_0_, s32[4]{0:T(128)} %iota_xor_fusion.refs_1_, bf16[1024,768]{1,0:T(8,128)(2,1)} %get-tuple-element.127.refs_2_, bf16[1024,128]{1,0:T(8,128)(2,1)} %get-tuple-element.300.refs_3_, ...), custom_call_target="tpu_custom_call" | custom-call | flops 1 | bytes 1 | tf_op jit(solution)/shard_map/attend_backward/pallas_call | solution.py:234
  588.1 9.4 %partial_rows.12 = (bf16[256,2048]{1,0:T(8,128)(2,1)}, bf16[512,2048]{1,0:T(8,128)(2,1)}, bf16[256,2048]{1,0:T(8,128)(2,1)}) custom-call(bf16[1024,1280]{1,0:T(8,128)(2,1)} %get-tuple-element.156.refs_6_.refs_8_.refs_0_, bf16[2048,3840]{1,0:T(8,128)(2,1)} %all-gather.8.cloned.1.call-done.refs_9_.refs_10_.refs_1_, ...), custom_call_target="tpu_custom_call" | custom-call | flops 1 | bytes 1 | tf_op jit(solution)/shard_map/partial_rows/pallas_call | solution.py:445
  598.8 36.6 %attend_backward.5 = (bf16[1024,768]{1,0:T(8,128)(2,1)}, f32[4,2,7,512]{3,2,1,0:T(8,128)}) custom-call(s32[16]{0:T(128)} %reshape.200.refs_0_, s32[4]{0:T(128)} %iota_xor_fusion.refs_1_, bf16[1024,768]{1,0:T(8,128)(2,1)} %rows_product.7.refs_2_, bf16[1024,128]{1,0:T(8,128)(2,1)} %get-tuple-element.300.refs_3_, ...), custom_call_target="tpu_custom_call", output_to_operand_aliasing={{1}: (10, {})} | custom-call | flops 1 | bytes 1 | tf_op jit(solution)/shard_map/attend_backward/pallas_call | solution.py:234
  639.2 11.7 %partial_rows.13 = (bf16[256,2048]{1,0:T(8,128)(2,1)}, bf16[256,2048]{1,0:T(8,128)(2,1)}, bf16[256,2048]{1,0:T(8,128)(2,1)}, bf16[128,2048]{1,0:T(8,128)(2,1)}, ...) custom-call(bf16[1024,768]{1,0:T(8,128)(2,1)} %get-tuple-element.186.refs_2_.refs_0_.refs_9_, ...), custom_call_target="tpu_custom_call" | custom-call | flops 1 | bytes 1 | tf_op jit(solution)/shard_map/partial_rows/pallas_call | solution.py:445
  655.0 16.7 %weight_gradient.8.refs_3_.refs_5_ = bf16[2048,1024]{1,0:T(8,128)(2,1)} custom-call(bf16[256,2048]{1,0:T(8,128)(2,1)} %get-tuple-element.144.refs_8_.refs_0_, bf16[256,2048]{1,0:T(8,128)(2,1)} %copy-done.8, bf16[256,2048]{1,0:T(8,128)(2,1)} %copy-done.7, bf16[128,2048]{1,0:T(8,128)(2,1)} %copy-done.20, bf16[128,2048]{1,0:T(8,128)(2,1)} %copy-done.21, ...), custom_call_target="tpu_custom_call" | custom-call | flops 1 | bytes 1 | tf_op jit(solution)/shard_map/weight_gradient/pallas_call | solution.py:372
  678.1 6.8 rows_product.11.refs_4_.refs_8_
  692.8 31.3 %attend_backward.6 = (bf16[1024,768]{1,0:T(8,128)(2,1)}, f32[4,2,7,512]{3,2,1,0:T(8,128)}) custom-call(s32[16]{0:T(128)} %reshape.201.refs_0_, s32[4]{0:T(128)} %iota_xor_fusion.refs_1_, bf16[1024,768]{1,0:T(8,128)(2,1)} %get-tuple-element.138.refs_2_, bf16[1024,128]{1,0:T(8,128)(2,1)} %get-tuple-element.299.refs_3_, ...), custom_call_target="tpu_custom_call" | custom-call | flops 1 | bytes 1 | tf_op jit(solution)/shard_map/attend_backward/pallas_call | solution.py:234
  728.7 12.0 %weight_gradient.9.refs_7_ = bf16[2048,512]{1,0:T(8,128)(2,1)} custom-call(bf16[256,2048]{1,0:T(8,128)(2,1)} %get-tuple-element.177.refs_10_.refs_7_.refs_0_, bf16[256,2048]{1,0:T(8,128)(2,1)} %copy-done.16, bf16[256,2048]{1,0:T(8,128)(2,1)} %copy-done.15, bf16[128,2048]{1,0:T(8,128)(2,1)} %copy-done.28, bf16[128,2048]{1,0:T(8,128)(2,1)} %copy-done.29, ...), custom_call_target="tpu_custom_call" | custom-call | flops 1 | bytes 1 | tf_op jit(solution)/shard_map/weight_gradient/pallas_call | solution.py:372
  741.6 4.7 settle_rows.13
  746.4 14.2 %weight_gradient.10.refs_2_.refs_3_ = bf16[2048,768]{1,0:T(8,128)(2,1)} custom-call(bf16[256,2048]{1,0:T(8,128)(2,1)} %bitcast.54, bf16[256,2048]{1,0:T(8,128)(2,1)} %copy-done.5, bf16[256,2048]{1,0:T(8,128)(2,1)} %copy-done.4, bf16[128,2048]{1,0:T(8,128)(2,1)} %copy-done.12, bf16[128,2048]{1,0:T(8,128)(2,1)} %copy-done.11, bf16[256,2048]{1,0:T(8,128)(2,1)} %bitcast.61, ...), custom_call_target="tpu_custom_call" | custom-call | flops 1 | bytes 1 | tf_op jit(solution)/shard_map/weight_gradient/pallas_call | solution.py:372
  760.7 9.4 %partial_rows.14 = (bf16[256,2048]{1,0:T(8,128)(2,1)}, bf16[512,2048]{1,0:T(8,128)(2,1)}, bf16[256,2048]{1,0:T(8,128)(2,1)}) custom-call(bf16[1024,1280]{1,0:T(8,128)(2,1)} %get-tuple-element.171.refs_4_.refs_9_.refs_0_, bf16[2048,3840]{1,0:T(8,128)(2,1)} %all-gather.8.cloned.1.call-done.refs_9_.refs_10_.refs_1_, ...), custom_call_target="tpu_custom_call" | custom-call | flops 1 | bytes 1 | tf_op jit(solution)/shard_map/partial_rows/pallas_call | solution.py:445
  771.0 31.5 %attend_backward.7 = (bf16[1024,768]{1,0:T(8,128)(2,1)}, f32[4,2,7,512]{3,2,1,0:T(8,128)}) custom-call(s32[16]{0:T(128)} %reshape.201.refs_0_, s32[4]{0:T(128)} %iota_xor_fusion.refs_1_, bf16[1024,768]{1,0:T(8,128)(2,1)} %rows_product.9.refs_6_.refs_2_, bf16[1024,128]{1,0:T(8,128)(2,1)} %get-tuple-element.299.refs_3_, ...), custom_call_target="tpu_custom_call", output_to_operand_aliasing={{1}: (10, {})} | custom-call | flops 1 | bytes 1 | tf_op jit(solution)/shard_map/attend_backward/pallas_call | solution.py:234
  802.4 8.4 collective-permute-done.54.refs_1_
  814.7 11.8 %partial_rows.15 = (bf16[256,2048]{1,0:T(8,128)(2,1)}, bf16[256,2048]{1,0:T(8,128)(2,1)}, bf16[256,2048]{1,0:T(8,128)(2,1)}, bf16[128,2048]{1,0:T(8,128)(2,1)}, ...) custom-call(bf16[1024,768]{1,0:T(8,128)(2,1)} %get-tuple-element.201.refs_4_.refs_10_.refs_0_, ...), custom_call_target="tpu_custom_call" | custom-call | flops 1 | bytes 1 | tf_op jit(solution)/shard_map/partial_rows/pallas_call | solution.py:445
  829.5 14.2 %weight_gradient.11.refs_4_ = bf16[2048,768]{1,0:T(8,128)(2,1)} custom-call(bf16[256,2048]{1,0:T(8,128)(2,1)} %bitcast.55, bf16[256,2048]{1,0:T(8,128)(2,1)} %copy-done.5, bf16[256,2048]{1,0:T(8,128)(2,1)} %copy-done.4, bf16[128,2048]{1,0:T(8,128)(2,1)} %copy-done.12, bf16[128,2048]{1,0:T(8,128)(2,1)} %copy-done.11, bf16[256,2048]{1,0:T(8,128)(2,1)} %bitcast.63, ...), custom_call_target="tpu_custom_call" | custom-call | flops 1 | bytes 1 | tf_op jit(solution)/shard_map/weight_gradient/pallas_call | solution.py:372
  854.7 7.5 collective-permute-start.61
  864.9 16.9 %collective-permute-start.62 = (f32[8,544]{1,0:T(8,128)S(1)}, f32[8,544]{1,0:T(8,128)S(1)}, u32[]{:S(2)}, u32[]{:S(2)}) collective-permute-start(f32[8,544]{1,0:T(8,128)S(1)} %add.113), channel_id=1, source_target_pairs={{0,16},{4,20},{8,24},{12,28},{16,0},{20,4},{24,8},{28,12},{1,17},{... | collective-permute-start | bytes 52232 | tf_op jit(solution)/shard_map/ppermute | solution.py:526
  906.4 5.0 settle_rows.15
  (418 shorter events, 216.4 us)
Async XLA Ops:
  7.2 88.7 %all-gather.6.cloned.1.call-start = ((), (), s32[]{:S(2)}) async-start(), calls=%async_computation.7 | async-start | bytes 3538944 | tf_op jit(solution)/shard_map/all_gather | solution.py:775
  10.8 123.0 %all-gather.4.cloned.1.call-start = ((), (), s32[]{:S(2)}) async-start(), calls=%async_computation.6 | async-start | bytes 5898240 | tf_op jit(solution)/shard_map/all_gather | solution.py:775
  12.1 285.0 %all-gather.8.cloned.1.call-start = ((), (), s32[]{:S(2)}) async-start(), calls=%async_computation.8 | async-start | bytes 17694720 | tf_op jit(solution)/shard_map/all_gather | solution.py:775
  27.8 611.4 %reduce-scatter.9.cloned.1.call-start = ((), (), s32[]{:S(2)}) async-start(), calls=%async_computation.10 | async-start | bytes 5898240 | tf_op jit(solution)/shard_map/reduce_scatter | solution.py:856
  27.8 27.0 %collective-permute-start.1 = (bf16[256,2048]{1,0:T(8,128)(2,1)S(1)}, bf16[256,2048]{1,0:T(8,128)(2,1)S(1)}, u32[]{:S(2)}, u32[]{:S(2)}) collective-permute-start(bf16[256,2048]{1,0:T(8,128)(2,1)S(1)} %bitcast.47), channel_id=1, source_target_pairs={{0,2},{1,3},{2,0},{3,1},{4,6},{5,7},{6,4},{7,5},{8,10},{9,11},{10,... | collective-permute-start | bytes 3145736 | tf_op jit(solution)/shard_map/ppermute | solution.py:526
  30.9 24.6 %collective-permute-start = (bf16[256,2048]{1,0:T(8,128)(2,1)S(1)}, bf16[256,2048]{1,0:T(8,128)(2,1)S(1)}, u32[]{:S(2)}, u32[]{:S(2)}) collective-permute-start(bf16[256,2048]{1,0:T(8,128)(2,1)S(1)} %bitcast.48), channel_id=1, source_target_pairs={{0,1},{1,0},{2,3},{3,2},{4,5},{5,4},{6,7},{7,6},{8,9},{9,8},{10,11... | collective-permute-start | bytes 3145736 | tf_op jit(solution)/shard_map/ppermute | solution.py:526
  71.4 22.9 %collective-permute-start.8 = (bf16[256,2048]{1,0:T(8,128)(2,1)S(1)}, bf16[256,2048]{1,0:T(8,128)(2,1)S(1)}, u32[]{:S(2)}, u32[]{:S(2)}) collective-permute-start(bf16[256,2048]{1,0:T(8,128)(2,1)S(1)} %bitcast.56), channel_id=1, source_target_pairs={{0,2},{1,3},{2,0},{3,1},{4,6},{5,7},{6,4},{7,5},{8,10},{9,11},{10,... | collective-permute-start | bytes 3145736 | tf_op jit(solution)/shard_map/ppermute | solution.py:526
  79.3 54.4 %collective-permute-start.7 = (bf16[256,2048]{1,0:T(8,128)(2,1)S(1)}, bf16[256,2048]{1,0:T(8,128)(2,1)S(1)}, u32[]{:S(2)}, u32[]{:S(2)}) collective-permute-start(bf16[256,2048]{1,0:T(8,128)(2,1)S(1)} %bitcast.57), channel_id=1, source_target_pairs={{0,1},{1,0},{2,3},{3,2},{4,5},{5,4},{6,7},{7,6},{8,9},{9,8},{10,11... | collective-permute-start | bytes 3145736 | tf_op jit(solution)/shard_map/ppermute | solution.py:526
  94.3 82.7 %collective-permute-start.13 = (bf16[256,2048]{1,0:T(8,128)(2,1)S(1)}, bf16[256,2048]{1,0:T(8,128)(2,1)}, u32[]{:S(2)}, u32[]{:S(2)}) collective-permute-start(bf16[256,2048]{1,0:T(8,128)(2,1)S(1)} %collective-permute-done.8.refs_9_.refs_2_.refs_7_.refs_6_), channel_id=1, source_target_pairs={{0,1},{1,0},{2,3},{3,2},{4,5},{5,4},{6,7},{7,6},{8,9},{9,8},{10,11... | collective-permute-start | bytes 3145736 | tf_op jit(solution)/shard_map/ppermute | solution.py:526
  105.3 65.3 %collective-permute-start.10 = (bf16[256,2048]{1,0:T(8,128)(2,1)}, bf16[256,2048]{1,0:T(8,128)(2,1)}, u32[]{:S(2)}, u32[]{:S(2)}) collective-permute-start(bf16[256,2048]{1,0:T(8,128)(2,1)} %bitcast.65), channel_id=1, source_target_pairs={{0,2},{1,3},{2,0},{3,1},{4,6},{5,7},{6,4},{7,5},{8,10},{9,11},{10,... | collective-permute-start | bytes 3145736 | tf_op jit(solution)/shard_map/ppermute | solution.py:526
  106.1 40.9 %collective-permute-start.9 = (bf16[256,2048]{1,0:T(8,128)(2,1)}, bf16[256,2048]{1,0:T(8,128)(2,1)}, u32[]{:S(2)}, u32[]{:S(2)}) collective-permute-start(bf16[256,2048]{1,0:T(8,128)(2,1)} %bitcast.66), channel_id=1, source_target_pairs={{0,1},{1,0},{2,3},{3,2},{4,5},{5,4},{6,7},{7,6},{8,9},{9,8},{10,11... | collective-permute-start | bytes 3145736 | tf_op jit(solution)/shard_map/ppermute | solution.py:526
  143.3 34.8 %collective-permute-start.16 = (bf16[256,2048]{1,0:T(8,128)(2,1)S(1)}, bf16[256,2048]{1,0:T(8,128)(2,1)}, u32[]{:S(2)}, u32[]{:S(2)}) collective-permute-start(bf16[256,2048]{1,0:T(8,128)(2,1)S(1)} %bitcast.76), channel_id=1, source_target_pairs={{0,2},{1,3},{2,0},{3,1},{4,6},{5,7},{6,4},{7,5},{8,10},{9,11},{10,... | collective-permute-start | bytes 3145736 | tf_op jit(solution)/shard_map/ppermute | solution.py:526
  147.0 45.0 %collective-permute-start.14 = (bf16[256,2048]{1,0:T(8,128)(2,1)}, bf16[256,2048]{1,0:T(8,128)(2,1)S(1)}, u32[]{:S(2)}, u32[]{:S(2)}) collective-permute-start(bf16[256,2048]{1,0:T(8,128)(2,1)} %collective-permute-done.9.refs_2_.refs_7_.refs_6_.refs_1_), channel_id=1, source_target_pairs={{0,2},{1,3},{2,0},{3,1},{4,6},{5,7},{6,4},{7,5},{8,10},{9,11},{10,... | collective-permute-start | bytes 3145736 | tf_op jit(solution)/shard_map/ppermute | solution.py:526
  148.0 43.9 %collective-permute-start.15 = (bf16[256,2048]{1,0:T(8,128)(2,1)S(1)}, bf16[256,2048]{1,0:T(8,128)(2,1)}, u32[]{:S(2)}, u32[]{:S(2)}) collective-permute-start(bf16[256,2048]{1,0:T(8,128)(2,1)S(1)} %bitcast.77), channel_id=1, source_target_pairs={{0,1},{1,0},{2,3},{3,2},{4,5},{5,4},{6,7},{7,6},{8,9},{9,8},{10,11... | collective-permute-start | bytes 3145736 | tf_op jit(solution)/shard_map/ppermute | solution.py:526
  177.0 32.8 %collective-permute-start.11 = (bf16[256,2048]{1,0:T(8,128)(2,1)}, bf16[256,2048]{1,0:T(8,128)(2,1)}, u32[]{:S(2)}, u32[]{:S(2)}) collective-permute-start(bf16[256,2048]{1,0:T(8,128)(2,1)} %get-tuple-element.134), channel_id=1, source_target_pairs={{0,1},{1,0},{2,3},{3,2},{4,5},{5,4},{6,7},{7,6},{8,9},{9,8},{10,11... | collective-permute-start | bytes 3145736 | tf_op jit(solution)/shard_map/ppermute | solution.py:526
  177.1 32.8 %collective-permute-start.12 = (bf16[256,2048]{1,0:T(8,128)(2,1)}, bf16[256,2048]{1,0:T(8,128)(2,1)}, u32[]{:S(2)}, u32[]{:S(2)}) collective-permute-start(bf16[256,2048]{1,0:T(8,128)(2,1)} %get-tuple-element.135), channel_id=1, source_target_pairs={{0,2},{1,3},{2,0},{3,1},{4,6},{5,7},{6,4},{7,5},{8,10},{9,11},{10,... | collective-permute-start | bytes 3145736 | tf_op jit(solution)/shard_map/ppermute | solution.py:526
  178.1 53.6 %collective-permute-start.19 = (bf16[256,2048]{1,0:T(8,128)(2,1)}, bf16[256,2048]{1,0:T(8,128)(2,1)S(1)}, u32[]{:S(2)}, u32[]{:S(2)}) collective-permute-start(bf16[256,2048]{1,0:T(8,128)(2,1)} %collective-permute-done.16.refs_11_.refs_9_.refs_7_.refs_6_), channel_id=1, source_target_pairs={{0,1},{1,0},{2,3},{3,2},{4,5},{5,4},{6,7},{7,6},{8,9},{9,8},{10,11... | collective-permute-start | bytes 3145736 | tf_op jit(solution)/shard_map/ppermute | solution.py:526
  266.2 50.9 %collective-permute-start.24 = (bf16[256,2048]{1,0:T(8,128)(2,1)}, bf16[256,2048]{1,0:T(8,128)(2,1)S(1)}, u32[]{:S(2)}, u32[]{:S(2)}) collective-permute-start(bf16[256,2048]{1,0:T(8,128)(2,1)} %get-tuple-element.152), channel_id=1, source_target_pairs={{0,2},{1,3},{2,0},{3,1},{4,6},{5,7},{6,4},{7,5},{8,10},{9,11},{10,... | collective-permute-start | bytes 3145736 | tf_op jit(solution)/shard_map/ppermute | solution.py:526
  267.1 50.0 %collective-permute-start.25 = (bf16[256,2048]{1,0:T(8,128)(2,1)}, bf16[256,2048]{1,0:T(8,128)(2,1)S(1)}, u32[]{:S(2)}, u32[]{:S(2)}) collective-permute-start(bf16[256,2048]{1,0:T(8,128)(2,1)} %get-tuple-element.154), channel_id=1, source_target_pairs={{0,1},{1,0},{2,3},{3,2},{4,5},{5,4},{6,7},{7,6},{8,9},{9,8},{10,11... | collective-permute-start | bytes 3145736 | tf_op jit(solution)/shard_map/ppermute | solution.py:526
  268.0 29.1 %collective-permute-start.22 = (bf16[128,2048]{1,0:T(8,128)(2,1)}, bf16[128,2048]{1,0:T(8,128)(2,1)S(1)}, u32[]{:S(2)}, u32[]{:S(2)}) collective-permute-start(bf16[128,2048]{1,0:T(8,128)(2,1)} %slice.123.refs_2_), channel_id=1, source_target_pairs={{0,1},{1,0},{2,3},{3,2},{4,5},{5,4},{6,7},{7,6},{8,9},{9,8},{10,11... | collective-permute-start | bytes 1572872 | tf_op jit(solution)/shard_map/ppermute | solution.py:526
  269.1 27.9 %collective-permute-start.23 = (bf16[128,2048]{1,0:T(8,128)(2,1)}, bf16[128,2048]{1,0:T(8,128)(2,1)S(1)}, u32[]{:S(2)}, u32[]{:S(2)}) collective-permute-start(bf16[128,2048]{1,0:T(8,128)(2,1)} %slice.124.refs_3_), channel_id=1, source_target_pairs={{0,2},{1,3},{2,0},{3,1},{4,6},{5,7},{6,4},{7,5},{8,10},{9,11},{10,... | collective-permute-start | bytes 1572872 | tf_op jit(solution)/shard_map/ppermute | solution.py:526
  344.6 23.1 %collective-permute-start.28 = (bf16[256,2048]{1,0:T(8,128)(2,1)}, bf16[256,2048]{1,0:T(8,128)(2,1)S(1)}, u32[]{:S(2)}, u32[]{:S(2)}) collective-permute-start(bf16[256,2048]{1,0:T(8,128)(2,1)} %get-tuple-element.160.refs_2_.refs_0_.refs_5_), channel_id=1, source_target_pairs={{0,1},{1,0},{2,3},{3,2},{4,5},{5,4},{6,7},{7,6},{8,9},{9,8},{10,11... | collective-permute-start | bytes 3145736 | tf_op jit(solution)/shard_map/ppermute | solution.py:526
  386.4 27.7 %collective-permute-start.32 = (bf16[256,2048]{1,0:T(8,128)(2,1)}, bf16[256,2048]{1,0:T(8,128)(2,1)S(1)}, u32[]{:S(2)}, u32[]{:S(2)}) collective-permute-start(bf16[256,2048]{1,0:T(8,128)(2,1)} %get-tuple-element.167), channel_id=1, source_target_pairs={{0,1},{1,0},{2,3},{3,2},{4,5},{5,4},{6,7},{7,6},{8,9},{9,8},{10,11... | collective-permute-start | bytes 3145736 | tf_op jit(solution)/shard_map/ppermute | solution.py:526
  386.8 27.3 %collective-permute-start.33 = (bf16[256,2048]{1,0:T(8,128)(2,1)}, bf16[256,2048]{1,0:T(8,128)(2,1)S(1)}, u32[]{:S(2)}, u32[]{:S(2)}) collective-permute-start(bf16[256,2048]{1,0:T(8,128)(2,1)} %get-tuple-element.168), channel_id=1, source_target_pairs={{0,2},{1,3},{2,0},{3,1},{4,6},{5,7},{6,4},{7,5},{8,10},{9,11},{10,... | collective-permute-start | bytes 3145736 | tf_op jit(solution)/shard_map/ppermute | solution.py:526
  433.7 49.6 %collective-permute-start.40 = (bf16[256,2048]{1,0:T(8,128)(2,1)}, bf16[256,2048]{1,0:T(8,128)(2,1)S(1)}, u32[]{:S(2)}, u32[]{:S(2)}) collective-permute-start(bf16[256,2048]{1,0:T(8,128)(2,1)} %get-tuple-element.178), channel_id=1, source_target_pairs={{0,1},{1,0},{2,3},{3,2},{4,5},{5,4},{6,7},{7,6},{8,9},{9,8},{10,11... | collective-permute-start | bytes 3145736 | tf_op jit(solution)/shard_map/ppermute | solution.py:526
  435.1 48.2 %collective-permute-start.41 = (bf16[256,2048]{1,0:T(8,128)(2,1)}, bf16[256,2048]{1,0:T(8,128)(2,1)S(1)}, u32[]{:S(2)}, u32[]{:S(2)}) collective-permute-start(bf16[256,2048]{1,0:T(8,128)(2,1)} %get-tuple-element.179), channel_id=1, source_target_pairs={{0,2},{1,3},{2,0},{3,1},{4,6},{5,7},{6,4},{7,5},{8,10},{9,11},{10,... | collective-permute-start | bytes 3145736 | tf_op jit(solution)/shard_map/ppermute | solution.py:526
  487.0 184.8 %reduce-scatter.7.cloned.1.call-start = ((), (), s32[]{:S(2)}) async-start(), calls=%async_computation.9 | async-start | bytes 7077888 | tf_op jit(solution)/shard_map/reduce_scatter | solution.py:856
  489.4 22.8 %collective-permute-start.36 = (bf16[256,2048]{1,0:T(8,128)(2,1)S(1)}, bf16[256,2048]{1,0:T(8,128)(2,1)S(1)}, u32[]{:S(2)}, u32[]{:S(2)}) collective-permute-start(bf16[256,2048]{1,0:T(8,128)(2,1)S(1)} %copy-done.10), channel_id=1, source_target_pairs={{0,1},{1,0},{2,3},{3,2},{4,5},{5,4},{6,7},{7,6},{8,9},{9,8},{10,11... | collective-permute-start | bytes 3145736 | tf_op jit(solution)/shard_map/ppermute | solution.py:526
  490.1 44.3 %collective-permute-start.43 = (bf16[128,2048]{1,0:T(8,128)(2,1)}, bf16[128,2048]{1,0:T(8,128)(2,1)}, u32[]{:S(2)}, u32[]{:S(2)}) collective-permute-start(bf16[128,2048]{1,0:T(8,128)(2,1)} %get-tuple-element.183), channel_id=1, source_target_pairs={{0,2},{1,3},{2,0},{3,1},{4,6},{5,7},{6,4},{7,5},{8,10},{9,11},{10,... | collective-permute-start | bytes 1572872 | tf_op jit(solution)/shard_map/ppermute | solution.py:526
  491.8 42.6 %collective-permute-start.42 = (bf16[128,2048]{1,0:T(8,128)(2,1)}, bf16[128,2048]{1,0:T(8,128)(2,1)}, u32[]{:S(2)}, u32[]{:S(2)}) collective-permute-start(bf16[128,2048]{1,0:T(8,128)(2,1)} %get-tuple-element.182.refs_12_), channel_id=1, source_target_pairs={{0,1},{1,0},{2,3},{3,2},{4,5},{5,4},{6,7},{7,6},{8,9},{9,8},{10,11... | collective-permute-start | bytes 1572872 | tf_op jit(solution)/shard_map/ppermute | solution.py:526
  510.5 24.0 %collective-permute-start.38 = (bf16[128,2048]{1,0:T(8,128)(2,1)}, bf16[128,2048]{1,0:T(8,128)(2,1)S(1)}, u32[]{:S(2)}, u32[]{:S(2)}) collective-permute-start(bf16[128,2048]{1,0:T(8,128)(2,1)} %slice.127.refs_13_), channel_id=1, source_target_pairs={{0,1},{1,0},{2,3},{3,2},{4,5},{5,4},{6,7},{7,6},{8,9},{9,8},{10,11... | collective-permute-start | bytes 1572872 | tf_op jit(solution)/shard_map/ppermute | solution.py:526
  512.2 22.3 %collective-permute-start.39 = (bf16[128,2048]{1,0:T(8,128)(2,1)S(1)}, bf16[128,2048]{1,0:T(8,128)(2,1)S(1)}, u32[]{:S(2)}, u32[]{:S(2)}) collective-permute-start(bf16[128,2048]{1,0:T(8,128)(2,1)S(1)} %slice.128.refs_14_), channel_id=1, source_target_pairs={{0,2},{1,3},{2,0},{3,1},{4,6},{5,7},{6,4},{7,5},{8,10},{9,11},{10,... | collective-permute-start | bytes 1572872 | tf_op jit(solution)/shard_map/ppermute | solution.py:526
  541.2 219.4 %reduce-scatter.11.cloned.1.call-start = ((), (), s32[]{:S(2)}) async-start(), calls=%async_computation.11 | async-start | bytes 4718592 | tf_op jit(solution)/shard_map/reduce_scatter | solution.py:856
  542.4 92.9 %collective-permute-start.46 = (bf16[256,2048]{1,0:T(8,128)(2,1)S(1)}, bf16[256,2048]{1,0:T(8,128)(2,1)}, u32[]{:S(2)}, u32[]{:S(2)}) collective-permute-start(bf16[256,2048]{1,0:T(8,128)(2,1)S(1)} %copy-done.19), channel_id=1, source_target_pairs={{0,1},{1,0},{2,3},{3,2},{4,5},{5,4},{6,7},{7,6},{8,9},{9,8},{10,11... | collective-permute-start | bytes 3145736 | tf_op jit(solution)/shard_map/ppermute | solution.py:526
  543.1 94.2 %collective-permute-start.45 = (bf16[256,2048]{1,0:T(8,128)(2,1)S(1)}, bf16[256,2048]{1,0:T(8,128)(2,1)}, u32[]{:S(2)}, u32[]{:S(2)}) collective-permute-start(bf16[256,2048]{1,0:T(8,128)(2,1)S(1)} %copy-done.19), channel_id=1, source_target_pairs={{0,2},{1,3},{2,0},{3,1},{4,6},{5,7},{6,4},{7,5},{8,10},{9,11},{10,... | collective-permute-start | bytes 3145736 | tf_op jit(solution)/shard_map/ppermute | solution.py:526
  597.5 74.3 %collective-permute-start.44 = (bf16[512,2048]{1,0:T(8,128)(2,1)}, bf16[512,2048]{1,0:T(8,128)(2,1)S(1)}, u32[]{:S(2)}, u32[]{:S(2)}) collective-permute-start(bf16[512,2048]{1,0:T(8,128)(2,1)} %get-tuple-element.188), channel_id=1, source_target_pairs={{0,1},{1,0},{2,3},{3,2},{4,5},{5,4},{6,7},{7,6},{8,9},{9,8},{10,11... | collective-permute-start | bytes 6291464 | tf_op jit(solution)/shard_map/ppermute | solution.py:526
  650.9 34.1 %collective-permute-start.50 = (bf16[256,2048]{1,0:T(8,128)(2,1)}, bf16[256,2048]{1,0:T(8,128)(2,1)S(1)}, u32[]{:S(2)}, u32[]{:S(2)}) collective-permute-start(bf16[256,2048]{1,0:T(8,128)(2,1)} %get-tuple-element.197), channel_id=1, source_target_pairs={{0,2},{1,3},{2,0},{3,1},{4,6},{5,7},{6,4},{7,5},{8,10},{9,11},{10,... | collective-permute-start | bytes 3145736 | tf_op jit(solution)/shard_map/ppermute | solution.py:526
  651.7 33.3 %collective-permute-start.51 = (bf16[256,2048]{1,0:T(8,128)(2,1)}, bf16[256,2048]{1,0:T(8,128)(2,1)}, u32[]{:S(2)}, u32[]{:S(2)}) collective-permute-start(bf16[256,2048]{1,0:T(8,128)(2,1)} %get-tuple-element.199), channel_id=1, source_target_pairs={{0,1},{1,0},{2,3},{3,2},{4,5},{5,4},{6,7},{7,6},{8,9},{9,8},{10,11... | collective-permute-start | bytes 3145736 | tf_op jit(solution)/shard_map/ppermute | solution.py:526
  652.5 25.7 %collective-permute-start.49 = (bf16[128,2048]{1,0:T(8,128)(2,1)}, bf16[128,2048]{1,0:T(8,128)(2,1)}, u32[]{:S(2)}, u32[]{:S(2)}) collective-permute-start(bf16[128,2048]{1,0:T(8,128)(2,1)} %slice.130.refs_10_), channel_id=1, source_target_pairs={{0,2},{1,3},{2,0},{3,1},{4,6},{5,7},{6,4},{7,5},{8,10},{9,11},{10,... | collective-permute-start | bytes 1572872 | tf_op jit(solution)/shard_map/ppermute | solution.py:526
  653.7 24.4 %collective-permute-start.48 = (bf16[128,2048]{1,0:T(8,128)(2,1)}, bf16[128,2048]{1,0:T(8,128)(2,1)}, u32[]{:S(2)}, u32[]{:S(2)}) collective-permute-start(bf16[128,2048]{1,0:T(8,128)(2,1)} %slice.129.refs_9_), channel_id=1, source_target_pairs={{0,1},{1,0},{2,3},{3,2},{4,5},{5,4},{6,7},{7,6},{8,9},{9,8},{10,11... | collective-permute-start | bytes 1572872 | tf_op jit(solution)/shard_map/ppermute | solution.py:526
  688.6 126.2 %reduce-scatter.13.cloned.1.call-start = ((), (), s32[]{:S(2)}) async-start(), calls=%async_computation.12 | async-start | bytes 2359296 | tf_op jit(solution)/shard_map/reduce_scatter | solution.py:856
  689.8 34.3 %collective-permute-start.47 = (bf16[256,2048]{1,0:T(8,128)(2,1)S(1)}, bf16[256,2048]{1,0:T(8,128)(2,1)S(1)}, u32[]{:S(2)}, u32[]{:S(2)}) collective-permute-start(bf16[256,2048]{1,0:T(8,128)(2,1)S(1)} %copy-done.35), channel_id=1, source_target_pairs={{0,2},{1,3},{2,0},{3,1},{4,6},{5,7},{6,4},{7,5},{8,10},{9,11},{10,... | collective-permute-start | bytes 3145736 | tf_op jit(solution)/shard_map/ppermute | solution.py:526
  691.0 49.7 %collective-permute-start.53 = (bf16[128,2048]{1,0:T(8,128)(2,1)}, bf16[128,2048]{1,0:T(8,128)(2,1)S(1)}, u32[]{:S(2)}, u32[]{:S(2)}) collective-permute-start(bf16[128,2048]{1,0:T(8,128)(2,1)} %get-tuple-element.202), channel_id=1, source_target_pairs={{0,2},{1,3},{2,0},{3,1},{4,6},{5,7},{6,4},{7,5},{8,10},{9,11},{10,... | collective-permute-start | bytes 1572872 | tf_op jit(solution)/shard_map/ppermute | solution.py:526
  691.8 48.9 %collective-permute-start.52 = (bf16[128,2048]{1,0:T(8,128)(2,1)S(1)}, bf16[128,2048]{1,0:T(8,128)(2,1)S(1)}, u32[]{:S(2)}, u32[]{:S(2)}) collective-permute-start(bf16[128,2048]{1,0:T(8,128)(2,1)S(1)} %copy-done.46), channel_id=1, source_target_pairs={{0,1},{1,0},{2,3},{3,2},{4,5},{5,4},{6,7},{7,6},{8,9},{9,8},{10,11... | collective-permute-start | bytes 1572872 | tf_op jit(solution)/shard_map/ppermute | solution.py:526
  746.3 160.0 %reduce-scatter.15.cloned.1.call-start = ((), (), s32[]{:S(2)}) async-start(), calls=%async_computation.13 | async-start | bytes 3538944 | tf_op jit(solution)/shard_map/reduce_scatter | solution.py:856
  770.1 40.8 %collective-permute-start.54 = (bf16[512,2048]{1,0:T(8,128)(2,1)}, bf16[512,2048]{1,0:T(8,128)(2,1)S(1)}, u32[]{:S(2)}, u32[]{:S(2)}) collective-permute-start(bf16[512,2048]{1,0:T(8,128)(2,1)} %get-tuple-element.207), channel_id=1, source_target_pairs={{0,2},{1,3},{2,0},{3,1},{4,6},{5,7},{6,4},{7,5},{8,10},{9,11},{10,... | collective-permute-start | bytes 6291464 | tf_op jit(solution)/shard_map/ppermute | solution.py:526
  814.6 102.0 %reduce-scatter.17.cloned.1.call-start = ((), (), s32[]{:S(2)}) async-start(), calls=%async_computation.14 | async-start | bytes 3538944 | tf_op jit(solution)/shard_map/reduce_scatter | solution.py:856
  851.5 45.4 %collective-permute-start.55 = (bf16[256,2048]{1,0:T(8,128)(2,1)S(1)}, bf16[256,2048]{1,0:T(8,128)(2,1)S(1)}, u32[]{:S(2)}, u32[]{:S(2)}) collective-permute-start(bf16[256,2048]{1,0:T(8,128)(2,1)S(1)} %copy-done.42), channel_id=1, source_target_pairs={{0,1},{1,0},{2,3},{3,2},{4,5},{5,4},{6,7},{7,6},{8,9},{9,8},{10,11... | collective-permute-start | bytes 3145736 | tf_op jit(solution)/shard_map/ppermute | solution.py:526
  (103 other events, 876.6 us)
Sparse Core Ops, SparseCore 0:
  10.9 41.0 all-gather.5
  53.6 54.8 all-gather.3
  110.2 141.3 all-gather.7
  487.1 79.1 reduce-scatter.8
  568.5 68.1 reduce-scatter.6
  688.7 67.3 reduce-scatter.10
  758.9 45.8 reduce-scatter.12
  814.8 59.7 reduce-scatter.14
  876.8 39.7 reduce-scatter.16

commit v3 on v2

--- a/solution.py
+++ b/solution.py
@@ -19,7 +19,10 @@
 MICRO = 2
 HBM = pl.BlockSpec(memory_space=pltpu.HBM)
 MIB = 1 << 20
-CHEAP = pl.CostEstimate(flops=1, bytes_accessed=1, transcendentals=0)
+
+
+def cost(flops):
+    return pl.CostEstimate(flops=int(2 * flops), bytes_accessed=1, transcendentals=0)
 
 
 def tn(left, right):
@@ -49,9 +52,35 @@
         out_specs=pl.BlockSpec((1, tiles * B, B), lambda h: (h, 0, 0)),
         out_shape=jax.ShapeDtypeStruct((heads, tiles * B, B), F32),
         compiler_params=pltpu.CompilerParams(vmem_limit_bytes=60 * MIB),
-        cost_estimate=CHEAP,
+        cost_estimate=cost(6e9),
         name="bias_strips",
     )(w)
+
+
+def by_tile(act_ref, base, n, *functions):
+    count = act_ref[base]
+    for i in range(1, n):
+        count = count + act_ref[base + i]
+    most = count * 4 >= 3 * n
+
+    @pl.when(most)
+    def _():
+        for function in functions:
+            for i in range(n):
+                function(i)
+
+    @pl.when(jnp.logical_not(most))
+    def _():
+        for function in functions:
+
+            def step(i, _, function=function):
+                @pl.when(act_ref[base + i] != 0)
+                def _():
+                    function(i)
+
+                return 0
+
+            lax.fori_loop(0, n, step, 0)
 
 
 def attend_forward_kernel(n, extra, *refs):
@@ -62,7 +91,7 @@
     vt = v.T
     for h in range(2):
         own = (lane < HD) if h == 0 else (lane >= HD)
-        qx[h] = jnp.where(own, q, fq_ref[...])
+        qx[h] = jnp.where(own, q, fq_ref[...]).T
         kx[h] = jnp.where(own, k, fk_ref[...])
         vx[h] = jnp.concatenate([vt[h * HD : (h + 1) * HD], jnp.ones((16, vt.shape[1]), BF)], axis=0)
 
@@ -71,32 +100,22 @@
         m_scr[...] = jnp.full_like(m_scr, -3e38)
         o_scr[...] = jnp.zeros_like(o_scr)
 
-        def score(kb, _):
-            @pl.when(act_ref[qi * n + kb] != 0)
-            def _():
-                ks = pl.ds(pl.multiple_of(kb * B, B), B)
-                bs = pl.ds(pl.multiple_of((blk_ref[kb] - blk_ref[qi] + n - 1) * B, B), B)
-                for h in range(2):
-                    s = nt(kx[h, ks, :], qx[h, qs, :]) + bias_ref[h, bs, :]
-                    s_scr[h, ks, :] = s
-                    m_scr[h] = jnp.maximum(m_scr[h], jnp.max(s.reshape(B // 8, 8, B), axis=0))
-
-            return 0
-
-        lax.fori_loop(0, n, score, 0)
+        def score(kb):
+            ks = pl.ds(pl.multiple_of(kb * B, B), B)
+            bs = pl.ds(pl.multiple_of((blk_ref[kb] - blk_ref[qi] + n - 1) * B, B), B)
+            for h in range(2):
+                s = nn(kx[h, ks, :], qx[h, :, qs]) + bias_ref[h, bs, :]
+                s_scr[h, ks, :] = s
+                m_scr[h] = jnp.maximum(m_scr[h], jnp.max(s.reshape(B // 8, 8, B), axis=0))
+
+        def share(kb):
+            ks = pl.ds(pl.multiple_of(kb * B, B), B)
+            for h in range(2):
+                p = jnp.exp(s_scr[h, ks, :] - jnp.max(m_scr[h], axis=0, keepdims=True)).astype(BF)
+                o_scr[h] += nn(vx[h, :, ks], p)
+
+        by_tile(act_ref, qi * n, n, score, share)
         peaks = [jnp.max(m_scr[h], axis=0, keepdims=True) for h in range(2)]
-
-        def share(kb, _):
-            @pl.when(act_ref[qi * n + kb] != 0)
-            def _():
-                ks = pl.ds(pl.multiple_of(kb * B, B), B)
-                for h in range(2):
-                    p = jnp.exp(s_scr[h, ks, :] - peaks[h]).astype(BF)
-                    o_scr[h] += nn(vx[h, :, ks], p)
-
-            return 0
-
-        lax.fori_loop(0, n, share, 0)
         outs = []
         for h in range(2):
             total = o_scr[h, HD : HD + 1, :]
@@ -131,7 +150,7 @@
                 pl.BlockSpec((1, 2, length), lambda p, *_: (p + first, 0, 0)),
             ],
             scratch_shapes=[
-                pltpu.VMEM((2, length, 128), BF),
+                pltpu.VMEM((2, 128, length), BF),
                 pltpu.VMEM((2, length, 128), BF),
                 pltpu.VMEM((2, HD + 16, length), BF),
                 pltpu.VMEM((2, length, B), F32),
@@ -145,79 +164,78 @@
         ],
         input_output_aliases={6 + i: i for i in range(len(into))},
         compiler_params=pltpu.CompilerParams(vmem_limit_bytes=60 * MIB),
-        cost_estimate=CHEAP,
+        cost_estimate=cost(3.7e9 * number),
         name="attend_forward",
     )(active, order, qkv, feat_q, feat_k, bias, *into, *deps)
 
 
 def attend_backward_kernel(n, extra, *refs):
     act_ref, blk_ref, qkv_ref, fq_ref, fk_ref, bias_ref, lse_ref, o_ref, do_ref, sc_ref = refs[:10]
-    g_ref, fold_ref, qx, kx, v0, kt, delta, dk, dv, dqt, diag = refs[10 + extra :]
+    g_ref, fold_ref, qx, kx, v0, kt, delta, dk, dv, dqt, diag, p_scr, ds_scr, dot_ = refs[10 + extra :]
     lane = lax.broadcasted_iota(jnp.int32, (1, 128), 1)
     q, k, v = qkv_ref[:, 0:128], qkv_ref[:, 128:256], qkv_ref[:, 256:384]
     for h in range(2):
         own = (lane < HD) if h == 0 else (lane >= HD)
-        qx[h] = jnp.where(own, q, fq_ref[...])
+        qx[h] = jnp.where(own, q, fq_ref[...]).T
         kx[h] = jnp.where(own, k, fk_ref[...])
         v0[h] = jnp.where(own, v, jnp.zeros_like(v))
     kt[...] = k.T
+    dot_[...] = do_ref[...].T
     prod = (o_ref[...].astype(F32) * do_ref[...].astype(F32)).T
     for h in range(2):
         delta[h : h + 1, :] = jnp.sum(prod[h * HD : (h + 1) * HD], axis=0, keepdims=True)
-    dk[...] = jnp.zeros_like(dk)
-    dv[...] = jnp.zeros_like(dv)
     diag[...] = jnp.zeros_like(diag)
-
-    def row(qi, _):
-        qs = pl.ds(pl.multiple_of(qi * B, B), B)
-        dqt[...] = jnp.zeros_like(dqt)
-        lses = [lse_ref[0, pl.ds(h, 1), qs] for h in range(2)]
-        dels = [delta[pl.ds(h, 1), qs] for h in range(2)]
-
-        def inner(kb, _):
-            @pl.when(act_ref[qi * n + kb] != 0)
-            def _():
-                ks = pl.ds(pl.multiple_of(kb * B, B), B)
-                bs = pl.ds(pl.multiple_of((blk_ref[kb] - blk_ref[qi] + n - 1) * B, B), B)
-                dob = do_ref[qs, :]
-                qb = qkv_ref[qs, 0:128]
-                for h in range(2):
-                    s = nt(kx[h, ks, :], qx[h, qs, :]) + bias_ref[h, bs, :]
-                    dp = nt(v0[h, ks, :], dob)
-                    p = jnp.exp(s - lses[h])
-                    ds = p * (dp - dels[h])
-                    pb, dsb = p.astype(BF), ds.astype(BF)
-                    diag[h, bs, :] += ds
-                    dv[h, ks, :] += nn(pb, dob)
-                    dk[h, ks, :] += nn(dsb, qb)
-                    dqt[h] += nn(kt[h * HD : (h + 1) * HD, ks], dsb)
-
-            return 0
-
-        lax.fori_loop(0, n, inner, 0)
-        g_ref[qs, 0:128] = (jnp.concatenate([dqt[0], dqt[1]], axis=0).T * sc_ref[qs, :]).astype(BF)
+    dqt[...] = jnp.zeros_like(dqt)
+
+    def column(kb, _):
+        ks = pl.ds(pl.multiple_of(kb * B, B), B)
+
+        def tile(qi):
+            qs = pl.ds(pl.multiple_of(qi * B, B), B)
+            bs = pl.ds(pl.multiple_of((blk_ref[kb] - blk_ref[qi] + n - 1) * B, B), B)
+            for h in range(2):
+                s = nn(kx[h, ks, :], qx[h, :, qs]) + bias_ref[h, bs, :]
+                dp = nn(v0[h, ks, :], dot_[:, qs])
+                p = jnp.exp(s - lse_ref[0, pl.ds(h, 1), qs])
+                ds = p * (dp - delta[pl.ds(h, 1), qs])
+                p_scr[h, :, qs] = p.astype(BF)
+                ds_scr[h, :, qs] = ds.astype(BF)
+                diag[h, bs, :] += ds
+
+        count = act_ref[kb * n]
+        for i in range(1, n):
+            count = count + act_ref[kb * n + i]
+
+        @pl.when(count * 4 < 3 * n)
+        def _():
+            p_scr[...] = jnp.zeros_like(p_scr)
+            ds_scr[...] = jnp.zeros_like(ds_scr)
+
+        by_tile(act_ref, kb * n, n, tile)
+        for h in range(2):
+            dv[h, ks, :] = nn(p_scr[h], do_ref[...])
+            dk[h, ks, :] = nn(ds_scr[h], qkv_ref[:, 0:128])
+            dqt[h * HD : (h + 1) * HD, :] += nn(kt[h * HD : (h + 1) * HD, ks], ds_scr[h])
         return 0
 
-    lax.fori_loop(0, n, row, 0)
+    lax.fori_loop(0, n, column, 0)
+    g_ref[:, 0:128] = (dqt[...].T * sc_ref[...]).astype(BF)
     left = lane < HD
     g_ref[:, 128:256] = (jnp.where(left, dk[0], dk[1]) * sc_ref[...]).astype(BF)
     g_ref[:, 256:384] = (jnp.where(left, dv[0], dv[1]) * sc_ref[...]).astype(BF)
+    row = lax.broadcasted_iota(jnp.int32, (B, B), 0)
+    below = row >= lax.broadcasted_iota(jnp.int32, (B, B), 1)
+    half = B // 2
+    flip = lax.broadcasted_iota(jnp.int32, (half, half), 0) + lax.broadcasted_iota(jnp.int32, (half, half), 1)
+    flip = (flip == half - 1).astype(BF)
     for h in range(2):
-
-        def fold(i, _):
-            a = diag[h, pl.ds(pl.multiple_of(i * B, B), B), :]
-            zero = jnp.zeros((8, B), F32)
-            acc = jnp.zeros((8, 2 * B), F32)
-            for g in range(B // 8):
-                part = jnp.concatenate([a[8 * g : 8 * g + 8], zero], axis=1)
-                acc = acc + (pltpu.roll(part, 2 * B - 8 * g, 1) if g else part)
-            total = acc[0:1]
-            for r in range(1, 8):
-                total = total + pltpu.roll(acc[r : r + 1], 2 * B - r, 1)
-            fold_ref[0, h, pl.ds(i, 1), :] = total
-            return 0
-
-        lax.fori_loop(0, 2 * n - 1, fold, 0)
+        for j in range(2 * n):
+            low = diag[h, (j - 1) * B : j * B, :] if j > 0 else 0.0
+            high = diag[h, j * B : (j + 1) * B, :] if j < 2 * n - 1 else 0.0
+            part = jnp.where(below, low, high)
+            part = part[:half] + jnp.concatenate([part[half:, half:], part[half:, :half]], axis=1)
+            part = pltpu.roll(nn(flip, part.astype(BF)), half + 1, 1, stride=1, stride_axis=0)
+            fold_ref[0, h, j : j + 1, :] = jnp.sum(part, axis=0, keepdims=True)
 
 
 def attend_backward(
@@ -247,26 +265,29 @@
                 whole,
             ]
             + [HBM] * extra,
-            out_specs=[three, pl.BlockSpec((1, 2, tiles, 2 * B), lambda p, *_: (p + first, 0, 0, 0))],
+            out_specs=[three, pl.BlockSpec((1, 2, 2 * n, B), lambda p, *_: (p + first, 0, 0, 0))],
             scratch_shapes=[
-                pltpu.VMEM((2, length, 128), BF),
+                pltpu.VMEM((2, 128, length), BF),
                 pltpu.VMEM((2, length, 128), BF),
                 pltpu.VMEM((2, length, 128), BF),
                 pltpu.VMEM((128, length), BF),
                 pltpu.VMEM((2, length), F32),
                 pltpu.VMEM((2, length, 128), F32),
                 pltpu.VMEM((2, length, 128), F32),
-                pltpu.VMEM((2, HD, B), F32),
+                pltpu.VMEM((2 * HD, length), F32),
                 pltpu.VMEM((2, rows, B), F32),
+                pltpu.VMEM((2, B, length), BF),
+                pltpu.VMEM((2, B, length), BF),
+                pltpu.VMEM((128, length), BF),
             ],
         ),
         out_shape=[
             jax.ShapeDtypeStruct((length, width3), BF),
-            jax.ShapeDtypeStruct((pairs, 2, tiles, 2 * B), F32),
+            jax.ShapeDtypeStruct((pairs, 2, 2 * n, B), F32),
         ],
         input_output_aliases={10: 1} if into else {},
         compiler_params=pltpu.CompilerParams(vmem_limit_bytes=60 * MIB),
-        cost_estimate=CHEAP,
+        cost_estimate=cost(6.5e9 * number),
         name="attend_backward",
     )(active, order, qkv, feat_q, feat_k, bias, lse, mixed, grad, scale, *into, *deps)
 
@@ -339,7 +360,7 @@
         },
         scratch_shapes=[pltpu.VMEM((length, depth), BF), pltpu.SemaphoreType.DMA((len(pieces),))],
         compiler_params=pltpu.CompilerParams(vmem_limit_bytes=60 * MIB),
-        cost_estimate=CHEAP,
+        cost_estimate=cost(2 * length * depth * width + 2e9),
         name="rows_product",
     )(*pieces, w, *scale, *deps, *carry)
 
@@ -382,15 +403,15 @@
             pltpu.SemaphoreType.DMA((len(flat),)),
         ],
         compiler_params=pltpu.CompilerParams(vmem_limit_bytes=60 * MIB),
-        cost_estimate=CHEAP,
+        cost_estimate=cost(2 * len(lefts) * length * depth * width),
         name="weight_gradient",
     )(*flat, *rights, *deps)
 
 
-def partial_kernel(form, layouts, against, extra, *refs):
+def partial_kernel(form, layouts, against, extra, carried, *refs):
     number = len(layouts)
     rows = refs[2 * number : 2 * number + against]
-    outs = refs[2 * number + against + extra :]
+    outs = refs[2 * number + against + extra : len(refs) - carried]
     value = None
     for a_ref, w_ref, (size, pitch, start) in zip(refs[:number], refs[number:], layouts):
         for i in range(a_ref.shape[1] // size):
@@ -430,7 +451,7 @@
     late_y[...] = blocks[2][:half]
 
 
-def partial_rows(lefts, weights, widths, ats, layouts, form, deps=(), pieces=()):
+def partial_rows(lefts, weights, widths, ats, layouts, form, deps=(), pieces=(), carry=()):
     length = lefts[0].shape[0]
     depth = weights[0].shape[0]
     tile = pick(depth, 512, 256)
@@ -443,19 +464,26 @@
     }[form]
     sums = [jax.ShapeDtypeStruct((1, depth), F32)] if pieces else []
     return pl.pallas_call(
-        functools.partial(partial_kernel, form, layouts, len(pieces), len(deps)),
+        functools.partial(partial_kernel, form, layouts, len(pieces), len(deps) + len(carry), len(carry)),
         grid=(depth // tile,),
         in_specs=[pl.BlockSpec(a.shape, lambda j: (0, 0)) for a in lefts]
         + [pl.BlockSpec((tile, width), lambda j, at=at: (j, at)) for width, at in zip(widths, ats)]
         + [pl.BlockSpec((p.shape[0], tile), lambda j: (0, j)) for p in pieces]
-        + [HBM] * len(deps),
+        + [HBM] * (len(deps) + len(carry)),
         out_specs=[pl.BlockSpec((height, tile), lambda j: (0, j)) for height in heights]
-        + [pl.BlockSpec((1, tile), lambda j: (0, j))] * len(sums),
-        out_shape=[jax.ShapeDtypeStruct((height, depth), BF) for height in heights] + sums,
-        compiler_params=pltpu.CompilerParams(vmem_limit_bytes=60 * MIB),
-        cost_estimate=CHEAP,
+        + [pl.BlockSpec((1, tile), lambda j: (0, j))] * len(sums)
+        + [HBM] * len(carry),
+        out_shape=[jax.ShapeDtypeStruct((height, depth), BF) for height in heights]
+        + sums
+        + [jax.ShapeDtypeStruct(c.shape, c.dtype) for c in carry],
+        input_output_aliases={
+            len(lefts) + len(weights) + len(pieces) + len(deps) + i: len(heights) + len(sums) + i
+            for i in range(len(carry))
+        },
+        compiler_params=pltpu.CompilerParams(vmem_limit_bytes=60 * MIB),
+        cost_estimate=cost(2 * length * depth * sum(a.shape[1] for a in lefts)),
         name="partial_rows",
-    )(*lefts, *weights, *pieces, *deps)
+    )(*lefts, *weights, *pieces, *deps, *carry)
 
 
 def ff_kernel(count, count_cot, extra, *refs):
@@ -517,7 +545,7 @@
             pltpu.SemaphoreType.DMA((count,)),
         ],
         compiler_params=pltpu.CompilerParams(vmem_limit_bytes=60 * MIB),
-        cost_estimate=CHEAP,
+        cost_estimate=cost(6 * length * depth * tile * number),
         name="feed_forward",
     )(*pieces, *cots, w, w, *into, *deps)
 
@@ -529,6 +557,7 @@
 class Gather:
     def __init__(self, part, via, count, then=()):
         self.own = part
+        self.sent = ()
         if count != 4:
             self.first = self.sent = (lax.all_gather(part, "tensor", axis=0, tiled=True),)
             self.pieces = list(self.first)
@@ -571,7 +600,7 @@
         out_shape=[jax.ShapeDtypeStruct(o.shape, o.dtype) for o in (*outs, *carry)],
         input_output_aliases={len(args) + len(deps) + i: len(outs) + i for i in range(len(carry))},
         compiler_params=pltpu.CompilerParams(vmem_limit_bytes=60 * MIB),
-        cost_estimate=CHEAP,
+        cost_estimate=cost(1.4e9),
         name="add_arrived",
     )(*args, *deps, *carry)
 
@@ -583,6 +612,7 @@
         self.form, self.count, self.parts = form, count, parts
         if count != 4:
             self.total = lax.psum_scatter(parts[0], "tensor", scatter_dimension=0, tiled=True).astype(F32)
+            self.arrived = (self.total,)
         elif form == "both":
             self.arrived = (hop(parts[1], 1, count), hop(parts[2], 2, count))
         else:
@@ -657,7 +687,7 @@
             1 + len(others) + len(rows) + len(deps) + i: len(kinds) + i for i in range(len(carry))
         },
         compiler_params=pltpu.CompilerParams(vmem_limit_bytes=60 * MIB),
-        cost_estimate=CHEAP,
+        cost_estimate=cost(3e9),
         name="settle_rows",
     )(own, *arrived, *second, *rows, *deps, *carry)
 
@@ -699,6 +729,41 @@
     inner = jnp.mean(total * rows, axis=-1, keepdims=True)
     grad = grad_middle + total - rows * (scale * scale * inner)
     return (grad.astype(BF),)
+
+
+def pack_kernel(size, number, turned_count, cuts, extra, *refs):
+    weights, gain_ref = refs[:number], refs[number]
+    others = refs[number + 1 : number + 1 + turned_count]
+    outs = refs[number + 1 + turned_count + extra :]
+    gain = gain_ref[...]
+    groups = weights[0].shape[1] // size
+    at = 0
+    for i in range(groups):
+        out = outs[i * cuts // groups]
+        if i * cuts % groups == 0:
+            at = 0
+        for weight in weights:
+            out[:, at : at + size] = (weight[:, i * size : (i + 1) * size].astype(F32) * gain).astype(BF)
+            at += size
+    for other in others:
+        outs[-1][:, at : at + other.shape[0]] = other[...].T
+        at += other.shape[0]
+
+
+def pack(weights, gain, others, size, cuts, deps=()):
+    rows_w, width = weights[0].shape
+    widths = [len(weights) * width // cuts] * cuts
+    widths[-1] += sum(other.shape[0] for other in others)
+    whole = pl.BlockSpec(memory_space=pltpu.VMEM)
+    return pl.pallas_call(
+        functools.partial(pack_kernel, size, len(weights), len(others), cuts, len(deps)),
+        in_specs=[whole] * (len(weights) + 1 + len(others)) + [HBM] * len(deps),
+        out_specs=[whole] * cuts,
+        out_shape=[jax.ShapeDtypeStruct((rows_w, w), BF) for w in widths],
+        compiler_params=pltpu.CompilerParams(vmem_limit_bytes=60 * MIB),
+        cost_estimate=cost(2e9),
+        name="pack",
+    )(*weights, gain, *others, *deps)
 
 
 def unpack_kernel(groups, pitch, *refs):
@@ -723,7 +788,7 @@
         functools.partial(turn_kernel, len(parts)),
         out_shape=[jax.ShapeDtypeStruct(p.shape[::-1], F32) for p in parts],
         compiler_params=pltpu.CompilerParams(vmem_limit_bytes=60 * MIB),
-        cost_estimate=CHEAP,
+        cost_estimate=cost(2e9),
         name="turned",
     )(*parts)
 
@@ -735,7 +800,7 @@
         functools.partial(unpack_kernel, groups, pitch),
         out_shape=[jax.ShapeDtypeStruct((rows_w, width), F32)] * pitch,
         compiler_params=pltpu.CompilerParams(vmem_limit_bytes=60 * MIB),
-        cost_estimate=CHEAP,
+        cost_estimate=cost(2e9),
         name="unpack",
     )(*parts, gain)
 
@@ -784,20 +849,11 @@
     each = pairs // cuts
     part_w = each * 384
 
-    def grouped(weights, size):
-        number = weights[0].shape[1] // size
-        return jnp.stack([w.reshape(rows_w, number, size) for w in weights], axis=2).reshape(rows_w, -1)
-
-    def scaled(w, gain):
-        return (w.astype(F32) * gain).astype(BF)
-
-    local_qkv = grouped([scaled(w, gain_one) for w in (w_query, w_key, w_value)], 128)
-    halves = [local_qkv[:, cut * part_w : (cut + 1) * part_w] for cut in range(cuts)]
-    halves[-1] = jnp.concatenate([halves[-1], w_out.T], axis=1)
+    halves = pack([w_query, w_key, w_value], gain_one, [w_out], 128, cuts)
     full_qkv = [spread(half) for half in halves]
     full_out, out_at = full_qkv[-1], part_w
-    local_ff = grouped([scaled(after(w_gate, xs[0]), gain_two), scaled(w_up, gain_two)], tile)
-    full_ff = spread(jnp.concatenate([local_ff, w_down.T], axis=1))
+    form = "both" if count == 4 else None
+    way = ("x", "y") if form else (None, None)
 
     table = rel_table.reshape(1, buckets_local * heads)
     for bit in bits(count_dp):
@@ -817,9 +873,8 @@
     ends = jnp.cumsum(doc_lengths, axis=1)
     lane = jnp.arange(128, dtype=jnp.int32) % HD
 
-    cs, masks = [], []
+    masks = []
     for m in range(MICRO):
-        cs.append(cotangent[:, m])
         number = jnp.sum((positions[:, None] >= ends[m][None, :]).astype(jnp.int32), axis=1)
         by_block = number.reshape(blocks, B)
         least, most = by_block.min(axis=1), by_block.max(axis=1)
@@ -828,9 +883,9 @@
         feat_q = same.astype(BF)
         feat_k = jnp.where(same | (lane >= docs)[None, :], 0.0, -BIG).astype(BF)
         masks.append((feat_q, feat_k, active.astype(jnp.int32).reshape(-1)))
-    form = "both" if count == 4 else None
     ones = [Gather(xs[0], "both", count, (bias,))]
-    ones.append(Gather(after(xs[1], *ones[0].pieces), "x", count))
+    (packed,) = pack([w_gate, w_up], gain_two, [w_down], tile, 1, (bias, *ones[0].sent))
+    full_ff = spread(packed)
 
     def project(m, cut, scale, deps):
         mode = "take" if scale else "make"
@@ -843,68 +898,66 @@
     def out_rows(mixed, deps):
         return partial_rows([mixed], [full_out], [full_out.shape[1]], [0], [(width, width, out_at)], form, deps)
 
-    def ff_rows(left, inner, way, deps):
+    def ff_rows(left, inner, way, deps, carry=()):
         size = 2 * width_ff if inner else width_ff
-        return partial_rows([left], [full_ff], [size], [0 if inner else 2], [(size, size, 0)], way, deps)
-
-    def qkv_rows(projects, m, deps):
         return partial_rows(
-            projects, full_qkv, [part_w] * cuts, [0] * cuts, [(part_w, part_w, 0)] * cuts, form, deps, ones[m].pieces
+            [left], [full_ff], [size], [0 if inner else 2], [(size, size, 0)], way, deps, (), carry
+        )
+
+    def qkv_rows(projects, m, deps, carry=()):
+        return partial_rows(
+            projects, full_qkv, [part_w] * cuts, [0] * cuts, [(part_w, part_w, 0)] * cuts, form, deps, ones[m].pieces, carry
         )
 
     def scatter(value):
         return lax.psum_scatter(value, "dp", scatter_dimension=0, tiled=True)
 
-    qkv_0a, scale_0 = project(0, 0, (), ())
-    cots = [Gather(after(cs[0], qkv_0a), "y", count)]
+    qkv_0a, scale_0 = project(0, 0, (), (packed,))
+    ones.append(Gather(after(xs[1], *ones[0].pieces), "x", count, (qkv_0a,)))
     into = forward(0, 0, qkv_0a, (), ())
+    cs = [after(cotangent, qkv_0a)[:, m] for m in range(MICRO)]
     (qkv_0b,) = project(0, 1, (scale_0,), (into[0], *ones[1].first))
-    cots.append(Gather(after(cs[1], qkv_0b), "x", count))
-    mixed_0, lse_0 = forward(0, 1, qkv_0b, into, ones[1].first)
-    parts = out_rows(mixed_0, cots[0].first)
+    cots = [Gather(cs[0], "y", count, (qkv_0b,))]
+    mixed_0, lse_0 = forward(0, 1, qkv_0b, into, ())
+    parts = out_rows(mixed_0, (*ones[1].pieces, *cots[0].first))
     sum_0 = Reduce(parts, form, count)
+    cots.append(Gather(after(cs[1], qkv_0b), "x", count, (parts[0],)))
     qkv_1a, scale_1 = project(1, 0, (), (parts[0],))
-    into = forward(1, 0, qkv_1a, (), (*cots[0].pieces, *cots[1].first))
-    late = sum_0.first((into[0],))
+    into = forward(1, 0, qkv_1a, (), tuple(cots[0].pieces))
+    late = sum_0.first((into[0], *cots[1].first))
     (qkv_1b,) = project(1, 1, (scale_1,), (late[0],))
-    middle_0, normed = sum_0.settle(add_branch, [xs[0]], (F32, BF), (qkv_1b, *cots[1].pieces))
+    middle_0, normed = sum_0.settle(add_branch, [xs[0]], (F32, BF), (qkv_1b,))
     twos = [Gather(normed, "both", count)]
-    mixed_1, lse_1 = forward(1, 1, qkv_1b, into, (normed,))
+    mixed_1, lse_1 = forward(1, 1, qkv_1b, into, (normed, *cots[1].pieces))
     parts = out_rows(mixed_1, twos[0].sent)
     sum_1 = Reduce(parts, form, count)
+    late = sum_1.first((parts[0], *twos[0].pieces))
 
     steps = width_ff // tile
     early = (steps + 1) // 2
-    into = feed_forward(twos[0].pieces, cots[0].pieces, full_ff, 0, early, (), (parts[0],))
-    late = sum_1.first((into[0],))
-    hidden_0, grad_ff_0 = feed_forward(
-        twos[0].pieces, cots[0].pieces, full_ff, early, steps - early, into, (late[0],)
-    )
+    hidden_0, grad_ff_0 = feed_forward(twos[0].pieces, cots[0].pieces, full_ff, 0, steps, (), (late[0],))
     middle_1, normed = sum_1.settle(add_branch, [xs[1]], (F32, BF), (hidden_0,))
     twos.append(Gather(normed, "both", count))
     parts = ff_rows(grad_ff_0, True, form, (normed,))
     sum_0 = Reduce(parts, form, count, twos[1].pieces)
+    down = ff_rows(hidden_0, False, way[0], (parts[0], *twos[1].sent))
     hidden_1, grad_ff_1 = feed_forward(
-        twos[1].pieces, cots[1].pieces, full_ff, 0, steps, (), (parts[0],)
+        twos[1].pieces, cots[1].pieces, full_ff, 0, steps, (), (down[0],)
     )
     late = sum_0.first((hidden_1,))
-    parts = ff_rows(grad_ff_1, True, form, (late[0],))
+    weight = outer([c.pieces for c in cots], [hidden_0, hidden_1], (late[0],))
+    grad_middle_0, rounded, gain_two_0, weight = sum_0.settle(
+        turn_back, [middle_0, cs[0]], (F32, BF, "sum"), (), (weight,)
+    )
+    grad_down = scatter(weight)
+    mids = [Gather(rounded, "both", count)]
+    parts = ff_rows(grad_ff_1, True, form, (rounded,))
     sum_1 = Reduce(parts, form, count)
-    grad_middle_0, rounded, gain_two_0 = sum_0.settle(
-        turn_back, [middle_0, cs[0]], (F32, BF, "sum"), (parts[0],)
-    )
-    mids = [Gather(rounded, "both", count)]
-    weight = outer([c.pieces for c in cots], [hidden_0, hidden_1], (rounded,))
-    late = sum_1.first((), (weight,))
-    grad_down = scatter(late[-1])
     two_pieces, grad_ffs = [g.pieces for g in twos], [grad_ff_0, grad_ff_1]
     ff_half = early * 2 * tile
-    weight = outer(two_pieces, grad_ffs, (late[0], *mids[0].sent), 0, ff_half)
-    grad_middle_1, rounded, gain_two_1, weight = sum_1.settle(
-        turn_back, [middle_1, cs[1]], (F32, BF, "sum"), tuple(mids[0].pieces), (weight,)
-    )
-    grad_ff_a = scatter(weight)
-    mids.append(Gather(rounded, "both", count))
+    weight = outer(two_pieces, grad_ffs, (parts[0], *mids[0].sent), 0, ff_half)
+    late = sum_1.first(tuple(mids[0].pieces), (weight,))
+    grad_ff_a = scatter(late[-1])
 
     def backward(m, qkv, lse, mixed, grad, scale, cut, into, deps):
         feat_q, feat_k, active = masks[m]
@@ -912,46 +965,46 @@
             qkv, feat_q, feat_k, bias, lse, mixed, grad, scale, active, order, cut * each, into, deps
         )
 
-    way = ("x", "y") if form else (None, None)
-    (grad,) = product(mids[0].pieces, full_out, out_at, width, deps=(rounded,))
-    grad_0a, fold = backward(0, qkv_0a, lse_0, mixed_0, grad, scale_0, 0, (), ())
-    parts = ff_rows(hidden_0, False, way[0], (grad_0a,))
-    down_0 = Reduce(parts, way[0], count)
-    grad_0b, fold_0 = backward(0, qkv_0b, lse_0, mixed_0, grad, scale_0, 1, (fold,), (parts[0],))
-    *parts, gain_one_0 = qkv_rows([grad_0a, grad_0b], 0, (*mids[1].sent, grad_down))
+    (grad,) = product(mids[0].pieces, full_out, out_at, width, deps=(late[0],))
+    weight = outer(two_pieces, grad_ffs, (grad,), ff_half, 2 * width_ff - ff_half)
+    grad_middle_1, rounded, gain_two_1, weight = sum_1.settle(
+        turn_back, [middle_1, cs[1]], (F32, BF, "sum"), (), (weight,)
+    )
+    grad_ff_b = scatter(weight)
+    mids.append(Gather(rounded, "both", count))
+    grad_0a, fold = backward(0, qkv_0a, lse_0, mixed_0, grad, scale_0, 0, (), (rounded,))
+    down_0 = Reduce(down, way[0], count, mids[1].first)
+    grad_0b, fold_0 = backward(0, qkv_0b, lse_0, mixed_0, grad, scale_0, 1, (fold,), mids[1].sent)
+    *parts, gain_one_0 = qkv_rows([grad_0a, grad_0b], 0, (grad_down,))
     sum_0 = Reduce(parts, form, count)
-    weight = outer(two_pieces, grad_ffs, (parts[0],), ff_half, 2 * width_ff - ff_half)
-    late = down_0.first((grad_ff_a, weight))
-    (grad,) = product(mids[1].pieces, full_out, out_at, width, deps=(late[0],))
-    late = sum_0.first((grad,), (weight,))
-    grad_ff_b = scatter(late[-1])
+    (grad,) = product(mids[1].pieces, full_out, out_at, width, deps=(parts[0],))
+    late = down_0.first((grad,))
+    weight = outer([g.pieces for g in mids], [mixed_0, mixed_1], (late[0], grad_ff_a))
+    late = sum_0.first((), (weight,))
+    grad_out = scatter(late[-1])
     grad_1a, fold = backward(1, qkv_1a, lse_1, mixed_1, grad, scale_1, 0, (), (late[0],))
     (output_0,) = down_0.settle(add_last, [middle_0], (BF,), (grad_1a,))
-    weight = outer([g.pieces for g in mids], [mixed_0, mixed_1], (output_0,))
+    weight = outer([g.pieces for g in ones], [grad_0a, grad_1a], (output_0,))
     token_0, weight = sum_0.settle(finish_back, [xs[0], grad_middle_0], (BF,), (), (weight,))
-    grad_out = scatter(weight)
-    weight = outer([g.pieces for g in ones], [grad_0a, grad_1a], (token_0,))
-    parts = ff_rows(hidden_1, False, way[1], (weight, grad_ff_b))
-    down_1 = Reduce(parts, way[1], count)
-    grad_1b, fold_1 = backward(1, qkv_1b, lse_1, mixed_1, grad, scale_1, 1, (fold,), (parts[0],))
-    late = down_1.first((grad_1b,), (weight,))
-    grad_qkv_a = scatter(late[-1])
-    *parts, gain_one_1 = qkv_rows([grad_1a, grad_1b], 1, (late[0], grad_out))
+    grad_qkv_a = scatter(weight)
+    parts = ff_rows(hidden_1, False, form, (token_0,))
+    down_1 = Reduce(parts, form, count)
+    grad_1b, fold_1 = backward(1, qkv_1b, lse_1, mixed_1, grad, scale_1, 1, (fold,), (parts[0], grad_ff_b))
+    late = down_1.first((grad_1b,))
+    weight = outer([g.pieces for g in ones], [grad_0b, grad_1b], (late[0], grad_out))
+    *parts, gain_one_1, weight = qkv_rows([grad_1a, grad_1b], 1, down_1.arrived, (weight,))
+    grad_qkv_b = scatter(weight)
     sum_1 = Reduce(parts, form, count)
-    weight = outer([g.pieces for g in ones], [grad_0b, grad_1b], (parts[0],))
-    late = sum_1.first((), (weight,))
-    grad_qkv_b = scatter(late[-1])
-    (output_1,) = down_1.settle(add_last, [middle_1], (BF,), (late[0],))
+    (output_1,) = down_1.settle(add_last, [middle_1], (BF,), (parts[0],))
+    late = sum_1.first((output_1,))
     grad_gate, grad_up = unpack(
         [grad_ff_a, grad_ff_b], (early, steps - early), 2, gain_two
     )
     grad_out, grad_down = turned([grad_out, grad_down])
-    fold = (fold_0 + fold_1).reshape(heads, tiles, 2 * B)
-    zero = jnp.zeros((heads, 1, B), F32)
-    by_offset = (
-        jnp.concatenate([fold[:, :, :B], zero], axis=1)
-        + jnp.concatenate([zero, fold[:, :, B:]], axis=1)
-    )[:, ::-1].reshape(heads, 2 * length)
+
+    fold = (fold_0 + fold_1).reshape(heads, 2 * blocks, B)[:, ::-1]
+    before = jnp.concatenate([jnp.zeros((heads, 1, B), F32), fold[:, :-1]], axis=1)
+    by_offset = jnp.where(jnp.arange(B) == 0, before, fold).reshape(heads, 2 * length)
     grad_table = lax.dot_general(
         onehot.astype(F32), by_offset, (((1,), (1,)), ((), ())), precision=lax.Precision.HIGHEST
     )
@@ -969,7 +1022,7 @@
         finish_back,
         [xs[1], grad_middle_1],
         (BF,),
-        (output_1, grad_qkv_a, grad_gate, grad_out, grad_down, both_gains),
+        (late[0], grad_qkv_a, grad_gate, grad_out, grad_down, both_gains),
     )
     return (
         jnp.stack([output_0, output_1], axis=1),

time: 933 us -> 802 us (0.86)
  Pallas kernels: 583 us -> 514 us
  local copies, waits for them, and re-layouts: 76.3 us -> 41.2 us
  starting transfers between devices: 92.7 us -> 82.4 us
  waiting for transfers between devices: 146 us -> 136 us
    pallas_call x4, Pallas kernels: 136 us -> 90.3 us  [attend_backward(): pl.pallas_call(functools.partial(attend_backward_kernel, n, extra), grid_...]
    pallas_call x4, Pallas kernels: 75.4 us -> 52 us  [attend_forward(): pl.pallas_call(functools.partial(attend_forward_kernel, n, extra), grid_s...]
    unnamed x173 -> x172, local copies, waits for them, and re-layouts: 42.9 us -> 27.8 us
    ppermute x65 -> x67, waiting for transfers between devices: 146 us -> 132 us  [hop(): return lax.ppermute(part, axis, [(i, i ^ bit) for i in range(count)])]
    ppermute x65 -> x67, starting transfers between devices: 92.4 us -> 82 us  [hop(): return lax.ppermute(part, axis, [(i, i ^ bit) for i in range(count)])]
    pallas_call x3 -> x2, Pallas kernels: 60.9 us -> 53.4 us  [feed_forward(): pl.pallas_call(functools.partial(ff_kernel, len(pieces), len(cots), extra...]
  transfers between devices with their start and end apart: 74 -> 76, of which waited for: 25 -> 33; matrix products, arithmetic and copies ran while one was open for 7% -> 4% of each run, Pallas kernels for 59% -> 62%
where the time goes in v3:
time: 802 us; the launch traced here: 796 us
  Pallas kernels  514 us (64%)
  waiting for transfers between devices  136 us (17%)
  starting transfers between devices  82.4 us (10%)
  local copies, waits for them, and re-layouts  41.2 us (5%)
  between operations  15.2 us (2%)
    ppermute x67, waiting for transfers between devices, hop(): return lax.ppermute(part, axis, [(i, i ^ bit) for i in range(count)])  132 us
    pallas_call x6, Pallas kernels, outer(): pl.pallas_call(functools.partial(outer_kernel, counts, len(deps)), grid=(...  98.4 us
    pallas_call x4, Pallas kernels, attend_backward(): pl.pallas_call(functools.partial(attend_backward_kernel, n, extra), grid_...  90.3 us
    pallas_call x8, Pallas kernels, partial_rows(): pl.pallas_call(functools.partial(partial_kernel, form, layouts, len(piece...  87.9 us
    ppermute x67, starting transfers between devices, hop(): return lax.ppermute(part, axis, [(i, i ^ bit) for i in range(count)])  82 us
    pallas_call x2, Pallas kernels, feed_forward(): pl.pallas_call(functools.partial(ff_kernel, len(pieces), len(cots), extra...  53.4 us
    pallas_call x4, Pallas kernels, attend_forward(): pl.pallas_call(functools.partial(attend_forward_kernel, n, extra), grid_s...  52 us
    pallas_call x6, Pallas kernels, product(): pl.pallas_call(functools.partial(product_kernel, mode, len(pieces), len(d...  50.4 us
  transfers between devices with their start and end apart: 76, of which 33 were waited for; matrix products, arithmetic and copies ran while one was open for 4% of the time, Pallas kernels for 62%

profile of v3, /device:TPU:0, one launch (start us, length us, event | category | flops | bytes accessed | tf_op | source)
XLA Modules:
  0.0 796.2 jit_solution(15373677756830158575)
XLA Ops:
  33.3 10.6 %bias_strips.1.refs_4_.refs_5_ = f32[8,1792,256]{2,1,0:T(8,128)} custom-call(f32[8,7,512]{2,1,0:T(8,128)} %pad_maximum_fusion.2.w_ref), custom_call_target="tpu_custom_call" | custom-call | flops 12000000000 | bytes 1 | tf_op jit(solution)/shard_map/bias_strips/pallas_call | solution.py:48
  58.0 5.5 collective-permute-done.6.refs_4_.refs_8_
  66.7 10.1 %rows_product.6 = (bf16[1024,768]{1,0:T(8,128)(2,1)}, f32[1024,128]{1,0:T(8,128)}) custom-call(bf16[256,2048]{1,0:T(8,128)(2,1)} %bitcast.40, bf16[256,2048]{1,0:T(8,128)(2,1)} %copy-done.24, bf16[256,2048]{1,0:T(8,128)(2,1)} %copy-done.23, bf16[128,2048]{1,0:T(8,128)(2,1)} %collective-permute-done.5.refs_3_.refs_7_, ...), custom_call_target="tpu_custom_call" | custom-call | flops 10442450944 | bytes 1 | tf_op jit(solution)/shard_map/rows_product/pallas_call | solution.py:347
  79.5 11.1 %collective-permute-done.8.refs_9_.refs_4_.refs_2_.refs_7_.refs_6_ = bf16[256,2048]{1,0:T(8,128)(2,1)} collective-permute-done((bf16[256,2048]{1,0:T(8,128)(2,1)}, bf16[256,2048]{1,0:T(8,128)(2,1)}, u32[]{:S(2)}, u32[]{:S(2)}) %collective-permute-start.8) | collective-permute-done | bytes 1048608 | tf_op jit(solution)/shard_map/ppermute | solution.py:554
  93.1 13.1 %attend_forward.4 = (bf16[1024,512]{1,0:T(8,128)(2,1)}, f32[4,2,1024]{2,1,0:T(2,128)}) custom-call(s32[16]{0:T(128)} %reshape.190.refs_0_, s32[4]{0:T(128)} %iota_xor_fusion.refs_1_, bf16[1024,768]{1,0:T(8,128)(2,1)} %get-tuple-element.137.refs_2_, bf16[1024,128]{1,0:T(8,128)(2,1)} %get-tuple-element.307.refs_3_, ...), custom_call_target="tpu_custom_call" | custom-call | flops 14800000000 | bytes 1 | tf_op jit(solution)/shard_map/attend_forward/pallas_call | solution.py:136
  109.7 8.4 %rows_product.7.refs_2_ = bf16[1024,768]{1,0:T(8,128)(2,1)} custom-call(bf16[256,2048]{1,0:T(8,128)(2,1)} %bitcast.41, bf16[256,2048]{1,0:T(8,128)(2,1)} %copy-done.24, bf16[256,2048]{1,0:T(8,128)(2,1)} %copy-done.23, bf16[128,2048]{1,0:T(8,128)(2,1)} %collective-permute-done.5.refs_3_.refs_7_, bf16[128,2048]{1,0:T(8,128)(2,1)} %collective-permute-done.6.refs_4_.refs_8_, ...), custom_call_target="tpu_custom_call" | custom-call | flops 10442450944 | bytes 1 | tf_op jit(solution)/shard_map/rows_product/pallas_call | solution.py:347
  121.7 13.3 %attend_forward.5 = (bf16[1024,512]{1,0:T(8,128)(2,1)}, f32[4,2,1024]{2,1,0:T(2,128)}) custom-call(s32[16]{0:T(128)} %reshape.190.refs_0_, s32[4]{0:T(128)} %iota_xor_fusion.refs_1_, bf16[1024,768]{1,0:T(8,128)(2,1)} %rows_product.7.refs_2_, bf16[1024,128]{1,0:T(8,128)(2,1)} %get-tuple-element.307.refs_3_, ...), custom_call_target="tpu_custom_call", output_to_operand_aliasing={{0}: (6, {}), {1}: (7, {})} | custom-call | flops 14800000000 | bytes 1 | tf_op jit(solution)/shard_map/attend_forward/pallas_call | solution.py:136
  137.5 6.4 partial_rows.8
  146.4 9.6 %rows_product.8 = (bf16[1024,768]{1,0:T(8,128)(2,1)}, f32[1024,128]{1,0:T(8,128)}) custom-call(bf16[256,2048]{1,0:T(8,128)(2,1)} %bitcast.36.refs_2_.refs_0_.refs_5_.refs_4_, bf16[256,2048]{1,0:T(8,128)(2,1)} %collective-permute-done.7.refs_8_.refs_3_.refs_1_.refs_6_.refs_5_, ...), custom_call_target="tpu_custom_call" | custom-call | flops 10442450944 | bytes 1 | tf_op jit(solution)/shard_map/rows_product/pallas_call | solution.py:347
  160.6 6.1 collective-permute-done.14.refs_9_.refs_8_.refs_3_
  167.7 12.7 %attend_forward.6 = (bf16[1024,512]{1,0:T(8,128)(2,1)}, f32[4,2,1024]{2,1,0:T(2,128)}) custom-call(s32[16]{0:T(128)} %reshape.191.refs_0_, s32[4]{0:T(128)} %iota_xor_fusion.refs_1_, bf16[1024,768]{1,0:T(8,128)(2,1)} %get-tuple-element.149.refs_2_, bf16[1024,128]{1,0:T(8,128)(2,1)} %get-tuple-element.306.refs_3_, ...), custom_call_target="tpu_custom_call" | custom-call | flops 14800000000 | bytes 1 | tf_op jit(solution)/shard_map/attend_forward/pallas_call | solution.py:136
  181.4 7.1 collective-permute-done.13.refs_1_.refs_2_
  194.0 8.5 %rows_product.9.refs_6_.refs_2_ = bf16[1024,768]{1,0:T(8,128)(2,1)} custom-call(bf16[256,2048]{1,0:T(8,128)(2,1)} %bitcast.36.refs_2_.refs_0_.refs_5_.refs_4_, bf16[256,2048]{1,0:T(8,128)(2,1)} %collective-permute-done.7.refs_8_.refs_3_.refs_1_.refs_6_.refs_5_, bf16[256,2048]{1,0:T(8,128)(2,1)} %collective-permute-done.8.refs_9_.refs_4_.refs_2_.refs_7_.refs_6_, ...), custom_call_target="tpu_custom_call" | custom-call | flops 10442450944 | bytes 1 | tf_op jit(solution)/shard_map/rows_product/pallas_call | solution.py:347
  204.4 6.9 collective-permute-done.17.refs_3_
  212.1 4.4 settle_rows.8
  219.4 12.8 %attend_forward.7 = (bf16[1024,512]{1,0:T(8,128)(2,1)}, f32[4,2,1024]{2,1,0:T(2,128)}) custom-call(s32[16]{0:T(128)} %reshape.191.refs_0_, s32[4]{0:T(128)} %iota_xor_fusion.refs_1_, bf16[1024,768]{1,0:T(8,128)(2,1)} %rows_product.9.refs_6_.refs_2_, bf16[1024,128]{1,0:T(8,128)(2,1)} %get-tuple-element.306.refs_3_, ...), custom_call_target="tpu_custom_call", output_to_operand_aliasing={{0}: (6, {}), {1}: (7, {})} | custom-call | flops 14800000000 | bytes 1 | tf_op jit(solution)/shard_map/attend_forward/pallas_call | solution.py:136
  232.2 6.0 collective-permute-done.20.refs_7_.refs_2_
  240.5 6.5 partial_rows.9
  251.2 29.3 %collective-permute-done.21.refs_8_.refs_3_ = bf16[128,2048]{1,0:T(8,128)(2,1)S(1)} collective-permute-done((bf16[128,2048]{1,0:T(8,128)(2,1)S(1)}, bf16[128,2048]{1,0:T(8,128)(2,1)S(1)}, u32[]{:S(2)}, u32[]{:S(2)}) %collective-permute-start.21) | collective-permute-done | bytes 524320 | tf_op jit(solution)/shard_map/ppermute | solution.py:554
  286.8 26.6 %feed_forward.2 = (bf16[1024,1280]{1,0:T(8,128)(2,1)}, bf16[1024,2560]{1,0:T(8,128)(2,1)}) custom-call(bf16[256,2048]{1,0:T(8,128)(2,1)} %get-tuple-element.156.refs_8_.refs_5_.refs_0_, bf16[256,2048]{1,0:T(8,128)(2,1)} %copy-done.26, bf16[256,2048]{1,0:T(8,128)(2,1)} %copy-done.25, bf16[128,2048]{1,0:T(8,128)(2,1)} %copy-done.59, ...), custom_call_target="tpu_custom_call" | custom-call | flops 32212254720 | bytes 1 | tf_op jit(solution)/shard_map/feed_forward/pallas_call | solution.py:524
  314.4 4.2 settle_rows.9
  320.6 15.9 %partial_rows.10 = (bf16[256,2048]{1,0:T(8,128)(2,1)}, bf16[256,2048]{1,0:T(8,128)(2,1)}, bf16[256,2048]{1,0:T(8,128)(2,1)}, bf16[128,2048]{1,0:T(8,128)(2,1)}, bf16[128,2048]{1,0:T(8,128)(2,1)}) custom-call(bf16[1024,2560]{1,0:T(8,128)(2,1)} %get-tuple-element.167.refs_0_.refs_10_, bf16[2048,3840]{1,0:T(8,128)(2,1)} %all-gather.8.cloned.1.call-done.refs_9_.refs_10_.refs_1_, ...), custom_call_target="tpu_custom_call" | custom-call | flops 21474836480 | bytes 1 | tf_op jit(solution)/shard_map/partial_rows/pallas_call | solution.py:466
  336.4 4.1 collective-permute-done.29.refs_1_.refs_6_
  345.1 9.4 %partial_rows.11 = (bf16[256,2048]{1,0:T(8,128)(2,1)}, bf16[512,2048]{1,0:T(8,128)(2,1)}, bf16[256,2048]{1,0:T(8,128)(2,1)}) custom-call(bf16[1024,1280]{1,0:T(8,128)(2,1)} %get-tuple-element.166.refs_6_.refs_0_.refs_8_, bf16[2048,3840]{1,0:T(8,128)(2,1)} %all-gather.8.cloned.1.call-done.refs_9_.refs_10_.refs_1_, ...), custom_call_target="tpu_custom_call" | custom-call | flops 10737418240 | bytes 1 | tf_op jit(solution)/shard_map/partial_rows/pallas_call | solution.py:466
  361.5 26.8 %feed_forward.3 = (bf16[1024,1280]{1,0:T(8,128)(2,1)}, bf16[1024,2560]{1,0:T(8,128)(2,1)}) custom-call(bf16[256,2048]{1,0:T(8,128)(2,1)} %get-tuple-element.169.refs_2_.refs_0_.refs_5_, bf16[256,2048]{1,0:T(8,128)(2,1)} %copy-done.27, bf16[256,2048]{1,0:T(8,128)(2,1)} %copy-done.28, bf16[128,2048]{1,0:T(8,128)(2,1)} %collective-permute-done.30.refs_3_.refs_8_, ...), custom_call_target="tpu_custom_call" | custom-call | flops 32212254720 | bytes 1 | tf_op jit(solution)/shard_map/feed_forward/pallas_call | solution.py:524
  392.9 19.3 %weight_gradient.6.refs_7_ = bf16[2048,1280]{1,0:T(8,128)(2,1)} custom-call(bf16[256,2048]{1,0:T(8,128)(2,1)} %copy-done.9, bf16[256,2048]{1,0:T(8,128)(2,1)} %collective-permute-done.10.refs_6_.refs_7_.refs_1_, bf16[256,2048]{1,0:T(8,128)(2,1)} %collective-permute-done.11.refs_7_.refs_8_.refs_2_, bf16[256,2048]{1,0:T(8,128)(2,1)} %copy-done.46, ...), custom_call_target="tpu_custom_call" | custom-call | flops 21474836480 | bytes 1 | tf_op jit(solution)/shard_map/weight_gradient/pallas_call | solution.py:393
  413.2 5.7 settle_rows.10
  423.3 16.7 %partial_rows.12 = (bf16[256,2048]{1,0:T(8,128)(2,1)}, bf16[256,2048]{1,0:T(8,128)(2,1)}, bf16[256,2048]{1,0:T(8,128)(2,1)}, bf16[128,2048]{1,0:T(8,128)(2,1)}, bf16[128,2048]{1,0:T(8,128)(2,1)}) custom-call(bf16[1024,2560]{1,0:T(8,128)(2,1)} %get-tuple-element.174.refs_0_.refs_11_, bf16[2048,3840]{1,0:T(8,128)(2,1)} %all-gather.8.cloned.1.call-done.refs_9_.refs_10_.refs_1_, ...), custom_call_target="tpu_custom_call" | custom-call | flops 21474836480 | bytes 1 | tf_op jit(solution)/shard_map/partial_rows/pallas_call | solution.py:466
  447.7 21.5 %weight_gradient.7.refs_9_ = bf16[2048,1536]{1,0:T(8,128)(2,1)} custom-call(bf16[256,2048]{1,0:T(8,128)(2,1)} %get-tuple-element.156.refs_8_.refs_5_.refs_0_, bf16[256,2048]{1,0:T(8,128)(2,1)} %copy-done.26, bf16[256,2048]{1,0:T(8,128)(2,1)} %copy-done.25, bf16[128,2048]{1,0:T(8,128)(2,1)} %copy-done.59, bf16[128,2048]{1,0:T(8,128)(2,1)} %copy-done.60, ...), custom_call_target="tpu_custom_call" | custom-call | flops 25769803776 | bytes 1 | tf_op jit(solution)/shard_map/weight_gradient/pallas_call | solution.py:393
  479.0 6.9 rows_product.10.refs_12_.refs_8_
  485.8 17.2 %weight_gradient.8.refs_7_ = bf16[2048,1024]{1,0:T(8,128)(2,1)} custom-call(bf16[256,2048]{1,0:T(8,128)(2,1)} %get-tuple-element.156.refs_8_.refs_5_.refs_0_, bf16[256,2048]{1,0:T(8,128)(2,1)} %copy-done.26, bf16[256,2048]{1,0:T(8,128)(2,1)} %copy-done.25, bf16[128,2048]{1,0:T(8,128)(2,1)} %copy-done.59, bf16[128,2048]{1,0:T(8,128)(2,1)} %copy-done.60, ...), custom_call_target="tpu_custom_call" | custom-call | flops 17179869184 | bytes 1 | tf_op jit(solution)/shard_map/weight_gradient/pallas_call | solution.py:393
  504.0 5.7 settle_rows.11
  510.9 22.7 %attend_backward.4 = (bf16[1024,768]{1,0:T(8,128)(2,1)}, f32[4,2,8,256]{3,2,1,0:T(8,128)}) custom-call(s32[16]{0:T(128)} %reshape.190.refs_0_, s32[4]{0:T(128)} %iota_xor_fusion.refs_1_, bf16[1024,768]{1,0:T(8,128)(2,1)} %get-tuple-element.137.refs_2_, bf16[1024,128]{1,0:T(8,128)(2,1)} %get-tuple-element.307.refs_3_, ...), custom_call_target="tpu_custom_call" | custom-call | flops 25999998976 | bytes 1 | tf_op jit(solution)/shard_map/attend_backward/pallas_call | solution.py:252
  537.1 22.6 %attend_backward.5 = (bf16[1024,768]{1,0:T(8,128)(2,1)}, f32[4,2,8,256]{3,2,1,0:T(8,128)}) custom-call(s32[16]{0:T(128)} %reshape.190.refs_0_, s32[4]{0:T(128)} %iota_xor_fusion.refs_1_, bf16[1024,768]{1,0:T(8,128)(2,1)} %rows_product.7.refs_2_, bf16[1024,128]{1,0:T(8,128)(2,1)} %get-tuple-element.307.refs_3_, ...), custom_call_target="tpu_custom_call", output_to_operand_aliasing={{1}: (10, {})} | custom-call | flops 25999998976 | bytes 1 | tf_op jit(solution)/shard_map/attend_backward/pallas_call | solution.py:252
  559.7 11.7 %partial_rows.13 = (bf16[256,2048]{1,0:T(8,128)(2,1)}, bf16[256,2048]{1,0:T(8,128)(2,1)}, bf16[256,2048]{1,0:T(8,128)(2,1)}, bf16[128,2048]{1,0:T(8,128)(2,1)}, ...) custom-call(bf16[1024,768]{1,0:T(8,128)(2,1)} %get-tuple-element.202.refs_0_.refs_9_, ...), custom_call_target="tpu_custom_call" | custom-call | flops 12884901888 | bytes 1 | tf_op jit(solution)/shard_map/partial_rows/pallas_call | solution.py:466
  574.2 6.9 rows_product.11.refs_2_.refs_8_
  581.1 12.1 %collective-permute-done.46.refs_1_ = bf16[512,2048]{1,0:T(8,128)(2,1)} collective-permute-done((bf16[512,2048]{1,0:T(8,128)(2,1)}, bf16[512,2048]{1,0:T(8,128)(2,1)}, u32[]{:S(2)}, u32[]{:S(2)}) %collective-permute-start.46) | collective-permute-done | bytes 2097184 | tf_op jit(solution)/shard_map/ppermute | solution.py:554
  597.2 11.9 %weight_gradient.9.refs_4_ = bf16[2048,512]{1,0:T(8,128)(2,1)} custom-call(bf16[256,2048]{1,0:T(8,128)(2,1)} %get-tuple-element.188.refs_2_.refs_4_.refs_0_, bf16[256,2048]{1,0:T(8,128)(2,1)} %copy-done.3, bf16[256,2048]{1,0:T(8,128)(2,1)} %copy-done.2, bf16[128,2048]{1,0:T(8,128)(2,1)} %collective-permute-done.40.refs_7_.refs_3_, ...), custom_call_target="tpu_custom_call" | custom-call | flops 8589934592 | bytes 1 | tf_op jit(solution)/shard_map/weight_gradient/pallas_call | solution.py:393
  613.3 22.5 %attend_backward.6 = (bf16[1024,768]{1,0:T(8,128)(2,1)}, f32[4,2,8,256]{3,2,1,0:T(8,128)}) custom-call(s32[16]{0:T(128)} %reshape.191.refs_0_, s32[4]{0:T(128)} %iota_xor_fusion.refs_1_, bf16[1024,768]{1,0:T(8,128)(2,1)} %get-tuple-element.149.refs_2_, bf16[1024,128]{1,0:T(8,128)(2,1)} %get-tuple-element.306.refs_3_, ...), custom_call_target="tpu_custom_call" | custom-call | flops 25999998976 | bytes 1 | tf_op jit(solution)/shard_map/attend_backward/pallas_call | solution.py:252
  641.4 14.2 %weight_gradient.10.refs_7_ = bf16[2048,768]{1,0:T(8,128)(2,1)} custom-call(bf16[256,2048]{1,0:T(8,128)(2,1)} %bitcast.44, bf16[256,2048]{1,0:T(8,128)(2,1)} %copy-done.24, bf16[256,2048]{1,0:T(8,128)(2,1)} %copy-done.23, bf16[128,2048]{1,0:T(8,128)(2,1)} %collective-permute-done.5.refs_3_.refs_7_, bf16[128,2048]{1,0:T(8,128)(2,1)} %collective-permute-done.6.refs_4_.refs_8_, ...), custom_call_target="tpu_custom_call" | custom-call | flops 12884901888 | bytes 1 | tf_op jit(solution)/shard_map/weight_gradient/pallas_call | solution.py:393
  656.6 4.6 settle_rows.13
  661.3 9.8 %partial_rows.14 = (bf16[256,2048]{1,0:T(8,128)(2,1)}, bf16[256,2048]{1,0:T(8,128)(2,1)}, bf16[256,2048]{1,0:T(8,128)(2,1)}, bf16[128,2048]{1,0:T(8,128)(2,1)}, bf16[128,2048]{1,0:T(8,128)(2,1)}) custom-call(bf16[1024,1280]{1,0:T(8,128)(2,1)} %get-tuple-element.184.refs_4_.refs_9_.refs_0_, ...), custom_call_target="tpu_custom_call" | custom-call | flops 10737418240 | bytes 1 | tf_op jit(solution)/shard_map/partial_rows/pallas_call | solution.py:466
  673.9 22.4 %attend_backward.7 = (bf16[1024,768]{1,0:T(8,128)(2,1)}, f32[4,2,8,256]{3,2,1,0:T(8,128)}) custom-call(s32[16]{0:T(128)} %reshape.191.refs_0_, s32[4]{0:T(128)} %iota_xor_fusion.refs_1_, bf16[1024,768]{1,0:T(8,128)(2,1)} %rows_product.9.refs_6_.refs_2_, bf16[1024,128]{1,0:T(8,128)(2,1)} %get-tuple-element.306.refs_3_, ...), custom_call_target="tpu_custom_call", output_to_operand_aliasing={{1}: (10, {})} | custom-call | flops 25999998976 | bytes 1 | tf_op jit(solution)/shard_map/attend_backward/pallas_call | solution.py:252
  700.1 14.3 %weight_gradient.11.refs_10_ = bf16[2048,768]{1,0:T(8,128)(2,1)} custom-call(bf16[256,2048]{1,0:T(8,128)(2,1)} %bitcast.46, bf16[256,2048]{1,0:T(8,128)(2,1)} %copy-done.24, bf16[256,2048]{1,0:T(8,128)(2,1)} %copy-done.23, bf16[128,2048]{1,0:T(8,128)(2,1)} %collective-permute-done.5.refs_3_.refs_7_, ...), custom_call_target="tpu_custom_call" | custom-call | flops 12884901888 | bytes 1 | tf_op jit(solution)/shard_map/weight_gradient/pallas_call | solution.py:393
  714.4 11.4 %partial_rows.15 = (bf16[256,2048]{1,0:T(8,128)(2,1)}, bf16[256,2048]{1,0:T(8,128)(2,1)}, bf16[256,2048]{1,0:T(8,128)(2,1)}, bf16[128,2048]{1,0:T(8,128)(2,1)}, ...) custom-call(bf16[1024,768]{1,0:T(8,128)(2,1)} %get-tuple-element.214, ...), custom_call_target="tpu_custom_call", output_to_operand_aliasing={{6}: (10, {})} | custom-call | flops 12884901888 | bytes 1 | tf_op jit(solution)/shard_map/partial_rows/pallas_call | solution.py:466
  749.4 9.6 %collective-permute-done.58.refs_3_.refs_1_ = bf16[256,2048]{1,0:T(8,128)(2,1)} collective-permute-done((bf16[256,2048]{1,0:T(8,128)(2,1)S(1)}, bf16[256,2048]{1,0:T(8,128)(2,1)}, u32[]{:S(2)}, u32[]{:S(2)}) %collective-permute-start.58) | collective-permute-done | bytes 1048608 | tf_op jit(solution)/shard_map/ppermute | solution.py:554
  770.3 5.3 collective-permute-done.66
  777.2 4.7 settle_rows.15
  (412 shorter events, 205.8 us)
Async XLA Ops:
  7.2 59.6 %all-gather.6.cloned.1.call-start = ((), (), s32[]{:S(2)}) async-start(), calls=%async_computation.7 | async-start | bytes 3538944 | tf_op jit(solution)/shard_map/all_gather | solution.py:840
  11.3 98.4 %all-gather.4.cloned.1.call-start = ((), (), s32[]{:S(2)}) async-start(), calls=%async_computation.6 | async-start | bytes 5898240 | tf_op jit(solution)/shard_map/all_gather | solution.py:840
  12.0 274.8 %all-gather.8.cloned.1.call-start = ((), (), s32[]{:S(2)}) async-start(), calls=%async_computation.8 | async-start | bytes 17694720 | tf_op jit(solution)/shard_map/all_gather | solution.py:840
  16.5 27.4 %collective-permute-start.1 = (bf16[256,2048]{1,0:T(8,128)(2,1)S(1)}, bf16[256,2048]{1,0:T(8,128)(2,1)S(1)}, u32[]{:S(2)}, u32[]{:S(2)}) collective-permute-start(bf16[256,2048]{1,0:T(8,128)(2,1)S(1)} %bitcast.38), channel_id=1, source_target_pairs={{0,2},{1,3},{2,0},{3,1},{4,6},{5,7},{6,4},{7,5},{8,10},{9,11},{10,... | collective-permute-start | bytes 3145736 | tf_op jit(solution)/shard_map/ppermute | solution.py:554
  19.6 24.6 %collective-permute-start = (bf16[256,2048]{1,0:T(8,128)(2,1)S(1)}, bf16[256,2048]{1,0:T(8,128)(2,1)S(1)}, u32[]{:S(2)}, u32[]{:S(2)}) collective-permute-start(bf16[256,2048]{1,0:T(8,128)(2,1)S(1)} %bitcast.39), channel_id=1, source_target_pairs={{0,1},{1,0},{2,3},{3,2},{4,5},{5,4},{6,7},{7,6},{8,9},{9,8},{10,11... | collective-permute-start | bytes 3145736 | tf_op jit(solution)/shard_map/ppermute | solution.py:554
  49.6 510.0 %reduce-scatter.7.cloned.1.call-start = ((), (), s32[]{:S(2)}) async-start(), calls=%async_computation.9 | async-start | bytes 5898240 | tf_op jit(solution)/shard_map/reduce_scatter | solution.py:913
  64.2 26.4 %collective-permute-start.8 = (bf16[256,2048]{1,0:T(8,128)(2,1)}, bf16[256,2048]{1,0:T(8,128)(2,1)}, u32[]{:S(2)}, u32[]{:S(2)}) collective-permute-start(bf16[256,2048]{1,0:T(8,128)(2,1)} %bitcast.36.refs_2_.refs_0_.refs_5_.refs_4_), channel_id=1, source_target_pairs={{0,2},{1,3},{2,0},{3,1},{4,6},{5,7},{6,4},{7,5},{8,10},{9,11},{10,... | collective-permute-start | bytes 3145736 | tf_op jit(solution)/shard_map/ppermute | solution.py:554
  65.2 26.4 %collective-permute-start.7 = (bf16[256,2048]{1,0:T(8,128)(2,1)}, bf16[256,2048]{1,0:T(8,128)(2,1)}, u32[]{:S(2)}, u32[]{:S(2)}) collective-permute-start(bf16[256,2048]{1,0:T(8,128)(2,1)} %bitcast.36.refs_2_.refs_0_.refs_5_.refs_4_), channel_id=1, source_target_pairs={{0,1},{1,0},{2,3},{3,2},{4,5},{5,4},{6,7},{7,6},{8,9},{9,8},{10,11... | collective-permute-start | bytes 3145736 | tf_op jit(solution)/shard_map/ppermute | solution.py:554
  77.9 43.2 %collective-permute-start.11 = (bf16[256,2048]{1,0:T(8,128)(2,1)S(1)}, bf16[256,2048]{1,0:T(8,128)(2,1)}, u32[]{:S(2)}, u32[]{:S(2)}) collective-permute-start(bf16[256,2048]{1,0:T(8,128)(2,1)S(1)} %get-tuple-element.295.refs_6_.refs_5_.refs_0_), channel_id=1, source_target_pairs={{0,2},{1,3},{2,0},{3,1},{4,6},{5,7},{6,4},{7,5},{8,10},{9,11},{10,... | collective-permute-start | bytes 3145736 | tf_op jit(solution)/shard_map/ppermute | solution.py:554
  78.9 42.2 %collective-permute-start.10 = (bf16[256,2048]{1,0:T(8,128)(2,1)S(1)}, bf16[256,2048]{1,0:T(8,128)(2,1)}, u32[]{:S(2)}, u32[]{:S(2)}) collective-permute-start(bf16[256,2048]{1,0:T(8,128)(2,1)S(1)} %get-tuple-element.295.refs_6_.refs_5_.refs_0_), channel_id=1, source_target_pairs={{0,1},{1,0},{2,3},{3,2},{4,5},{5,4},{6,7},{7,6},{8,9},{9,8},{10,11... | collective-permute-start | bytes 3145736 | tf_op jit(solution)/shard_map/ppermute | solution.py:554
  91.6 44.8 %collective-permute-start.9 = (bf16[256,2048]{1,0:T(8,128)(2,1)}, bf16[256,2048]{1,0:T(8,128)(2,1)S(1)}, u32[]{:S(2)}, u32[]{:S(2)}) collective-permute-start(bf16[256,2048]{1,0:T(8,128)(2,1)} %collective-permute-done.8.refs_9_.refs_4_.refs_2_.refs_7_.refs_6_), channel_id=1, source_target_pairs={{0,1},{1,0},{2,3},{3,2},{4,5},{5,4},{6,7},{7,6},{8,9},{9,8},{10,11... | collective-permute-start | bytes 3145736 | tf_op jit(solution)/shard_map/ppermute | solution.py:554
  118.1 37.9 %collective-permute-start.16 = (bf16[256,2048]{1,0:T(8,128)(2,1)S(1)}, bf16[256,2048]{1,0:T(8,128)(2,1)}, u32[]{:S(2)}, u32[]{:S(2)}) collective-permute-start(bf16[256,2048]{1,0:T(8,128)(2,1)S(1)} %get-tuple-element.152.refs_9_.refs_5_.refs_4_.refs_6_), channel_id=1, source_target_pairs={{0,2},{1,3},{2,0},{3,1},{4,6},{5,7},{6,4},{7,5},{8,10},{9,11},{10,... | collective-permute-start | bytes 3145736 | tf_op jit(solution)/shard_map/ppermute | solution.py:554
  119.6 39.4 %collective-permute-start.15 = (bf16[256,2048]{1,0:T(8,128)(2,1)S(1)}, bf16[256,2048]{1,0:T(8,128)(2,1)}, u32[]{:S(2)}, u32[]{:S(2)}) collective-permute-start(bf16[256,2048]{1,0:T(8,128)(2,1)S(1)} %get-tuple-element.152.refs_9_.refs_5_.refs_4_.refs_6_), channel_id=1, source_target_pairs={{0,1},{1,0},{2,3},{3,2},{4,5},{5,4},{6,7},{7,6},{8,9},{9,8},{10,11... | collective-permute-start | bytes 3145736 | tf_op jit(solution)/shard_map/ppermute | solution.py:554
  121.1 45.5 %collective-permute-start.14 = (bf16[256,2048]{1,0:T(8,128)(2,1)}, bf16[256,2048]{1,0:T(8,128)(2,1)S(1)}, u32[]{:S(2)}, u32[]{:S(2)}) collective-permute-start(bf16[256,2048]{1,0:T(8,128)(2,1)} %collective-permute-done.10.refs_6_.refs_7_.refs_1_), channel_id=1, source_target_pairs={{0,2},{1,3},{2,0},{3,1},{4,6},{5,7},{6,4},{7,5},{8,10},{9,11},{10,... | collective-permute-start | bytes 3145736 | tf_op jit(solution)/shard_map/ppermute | solution.py:554
  143.9 37.5 %collective-permute-start.12 = (bf16[256,2048]{1,0:T(8,128)(2,1)}, bf16[256,2048]{1,0:T(8,128)(2,1)S(1)}, u32[]{:S(2)}, u32[]{:S(2)}) collective-permute-start(bf16[256,2048]{1,0:T(8,128)(2,1)} %get-tuple-element.145), channel_id=1, source_target_pairs={{0,1},{1,0},{2,3},{3,2},{4,5},{5,4},{6,7},{7,6},{8,9},{9,8},{10,11... | collective-permute-start | bytes 3145736 | tf_op jit(solution)/shard_map/ppermute | solution.py:554
  145.4 43.1 %collective-permute-start.13 = (bf16[256,2048]{1,0:T(8,128)(2,1)}, bf16[256,2048]{1,0:T(8,128)(2,1)}, u32[]{:S(2)}, u32[]{:S(2)}) collective-permute-start(bf16[256,2048]{1,0:T(8,128)(2,1)} %get-tuple-element.146), channel_id=1, source_target_pairs={{0,2},{1,3},{2,0},{3,1},{4,6},{5,7},{6,4},{7,5},{8,10},{9,11},{10,... | collective-permute-start | bytes 3145736 | tf_op jit(solution)/shard_map/ppermute | solution.py:554
  159.1 60.3 %collective-permute-start.23 = (bf16[256,2048]{1,0:T(8,128)(2,1)}, bf16[256,2048]{1,0:T(8,128)(2,1)}, u32[]{:S(2)}, u32[]{:S(2)}) collective-permute-start(bf16[256,2048]{1,0:T(8,128)(2,1)} %collective-permute-done.16.refs_6_.refs_11_.refs_7_), channel_id=1, source_target_pairs={{0,1},{1,0},{2,3},{3,2},{4,5},{5,4},{6,7},{7,6},{8,9},{9,8},{10,11... | collective-permute-start | bytes 3145736 | tf_op jit(solution)/shard_map/ppermute | solution.py:554
  247.1 33.4 %collective-permute-start.24 = (bf16[256,2048]{1,0:T(8,128)(2,1)}, bf16[256,2048]{1,0:T(8,128)(2,1)S(1)}, u32[]{:S(2)}, u32[]{:S(2)}) collective-permute-start(bf16[256,2048]{1,0:T(8,128)(2,1)} %get-tuple-element.161), channel_id=1, source_target_pairs={{0,2},{1,3},{2,0},{3,1},{4,6},{5,7},{6,4},{7,5},{8,10},{9,11},{10,... | collective-permute-start | bytes 3145736 | tf_op jit(solution)/shard_map/ppermute | solution.py:554
  248.3 32.2 %collective-permute-start.25 = (bf16[256,2048]{1,0:T(8,128)(2,1)}, bf16[256,2048]{1,0:T(8,128)(2,1)S(1)}, u32[]{:S(2)}, u32[]{:S(2)}) collective-permute-start(bf16[256,2048]{1,0:T(8,128)(2,1)} %get-tuple-element.163), channel_id=1, source_target_pairs={{0,1},{1,0},{2,3},{3,2},{4,5},{5,4},{6,7},{7,6},{8,9},{9,8},{10,11... | collective-permute-start | bytes 3145736 | tf_op jit(solution)/shard_map/ppermute | solution.py:554
  249.8 30.7 %collective-permute-start.21 = (bf16[128,2048]{1,0:T(8,128)(2,1)S(1)}, bf16[128,2048]{1,0:T(8,128)(2,1)S(1)}, u32[]{:S(2)}, u32[]{:S(2)}) collective-permute-start(bf16[128,2048]{1,0:T(8,128)(2,1)S(1)} %copy-done.16), channel_id=1, source_target_pairs={{0,1},{1,0},{2,3},{3,2},{4,5},{5,4},{6,7},{7,6},{8,9},{9,8},{10,11... | collective-permute-start | bytes 1572872 | tf_op jit(solution)/shard_map/ppermute | solution.py:554
  250.4 30.1 %collective-permute-start.22 = (bf16[128,2048]{1,0:T(8,128)(2,1)S(1)}, bf16[128,2048]{1,0:T(8,128)(2,1)S(1)}, u32[]{:S(2)}, u32[]{:S(2)}) collective-permute-start(bf16[128,2048]{1,0:T(8,128)(2,1)S(1)} %copy-done.17), channel_id=1, source_target_pairs={{0,2},{1,3},{2,0},{3,1},{4,6},{5,7},{6,4},{7,5},{8,10},{9,11},{10,... | collective-permute-start | bytes 1572872 | tf_op jit(solution)/shard_map/ppermute | solution.py:554
  284.8 28.6 %collective-permute-start.27 = (bf16[128,2048]{1,0:T(8,128)(2,1)}, bf16[128,2048]{1,0:T(8,128)(2,1)S(1)}, u32[]{:S(2)}, u32[]{:S(2)}) collective-permute-start(bf16[128,2048]{1,0:T(8,128)(2,1)} %get-tuple-element.168), channel_id=1, source_target_pairs={{0,2},{1,3},{2,0},{3,1},{4,6},{5,7},{6,4},{7,5},{8,10},{9,11},{10,... | collective-permute-start | bytes 1572872 | tf_op jit(solution)/shard_map/ppermute | solution.py:554
  285.3 28.1 %collective-permute-start.26 = (bf16[128,2048]{1,0:T(8,128)(2,1)}, bf16[128,2048]{1,0:T(8,128)(2,1)S(1)}, u32[]{:S(2)}, u32[]{:S(2)}) collective-permute-start(bf16[128,2048]{1,0:T(8,128)(2,1)} %get-tuple-element.165.refs_11_), channel_id=1, source_target_pairs={{0,1},{1,0},{2,3},{3,2},{4,5},{5,4},{6,7},{7,6},{8,9},{9,8},{10,11... | collective-permute-start | bytes 1572872 | tf_op jit(solution)/shard_map/ppermute | solution.py:554
  358.3 30.0 %collective-permute-start.32 = (bf16[256,2048]{1,0:T(8,128)(2,1)}, bf16[256,2048]{1,0:T(8,128)(2,1)S(1)}, u32[]{:S(2)}, u32[]{:S(2)}) collective-permute-start(bf16[256,2048]{1,0:T(8,128)(2,1)} %get-tuple-element.180), channel_id=1, source_target_pairs={{0,1},{1,0},{2,3},{3,2},{4,5},{5,4},{6,7},{7,6},{8,9},{9,8},{10,11... | collective-permute-start | bytes 3145736 | tf_op jit(solution)/shard_map/ppermute | solution.py:554
  359.9 28.4 %collective-permute-start.33 = (bf16[256,2048]{1,0:T(8,128)(2,1)}, bf16[256,2048]{1,0:T(8,128)(2,1)S(1)}, u32[]{:S(2)}, u32[]{:S(2)}) collective-permute-start(bf16[256,2048]{1,0:T(8,128)(2,1)} %get-tuple-element.181), channel_id=1, source_target_pairs={{0,2},{1,3},{2,0},{3,1},{4,6},{5,7},{6,4},{7,5},{8,10},{9,11},{10,... | collective-permute-start | bytes 3145736 | tf_op jit(solution)/shard_map/ppermute | solution.py:554
  418.9 178.2 %reduce-scatter.9.cloned.1.call-start = ((), (), s32[]{:S(2)}) async-start(), calls=%async_computation.10 | async-start | bytes 7077888 | tf_op jit(solution)/shard_map/reduce_scatter | solution.py:913
  421.3 25.6 %collective-permute-start.38 = (bf16[256,2048]{1,0:T(8,128)(2,1)S(1)}, bf16[256,2048]{1,0:T(8,128)(2,1)S(1)}, u32[]{:S(2)}, u32[]{:S(2)}) collective-permute-start(bf16[256,2048]{1,0:T(8,128)(2,1)S(1)} %copy-done.13), channel_id=1, source_target_pairs={{0,1},{1,0},{2,3},{3,2},{4,5},{5,4},{6,7},{7,6},{8,9},{9,8},{10,11... | collective-permute-start | bytes 3145736 | tf_op jit(solution)/shard_map/ppermute | solution.py:554
  440.0 29.3 %collective-permute-start.36 = (bf16[256,2048]{1,0:T(8,128)(2,1)}, bf16[256,2048]{1,0:T(8,128)(2,1)}, u32[]{:S(2)}, u32[]{:S(2)}) collective-permute-start(bf16[256,2048]{1,0:T(8,128)(2,1)} %get-tuple-element.190), channel_id=1, source_target_pairs={{0,1},{1,0},{2,3},{3,2},{4,5},{5,4},{6,7},{7,6},{8,9},{9,8},{10,11... | collective-permute-start | bytes 3145736 | tf_op jit(solution)/shard_map/ppermute | solution.py:554
  440.0 29.3 %collective-permute-start.37 = (bf16[256,2048]{1,0:T(8,128)(2,1)}, bf16[256,2048]{1,0:T(8,128)(2,1)}, u32[]{:S(2)}, u32[]{:S(2)}) collective-permute-start(bf16[256,2048]{1,0:T(8,128)(2,1)} %get-tuple-element.191), channel_id=1, source_target_pairs={{0,2},{1,3},{2,0},{3,1},{4,6},{5,7},{6,4},{7,5},{8,10},{9,11},{10,... | collective-permute-start | bytes 3145736 | tf_op jit(solution)/shard_map/ppermute | solution.py:554
  443.5 28.2 %collective-permute-start.40 = (bf16[128,2048]{1,0:T(8,128)(2,1)S(1)}, bf16[128,2048]{1,0:T(8,128)(2,1)}, u32[]{:S(2)}, u32[]{:S(2)}) collective-permute-start(bf16[128,2048]{1,0:T(8,128)(2,1)S(1)} %slice.119.refs_13_), channel_id=1, source_target_pairs={{0,1},{1,0},{2,3},{3,2},{4,5},{5,4},{6,7},{7,6},{8,9},{9,8},{10,11... | collective-permute-start | bytes 1572872 | tf_op jit(solution)/shard_map/ppermute | solution.py:554
  446.9 24.8 %collective-permute-start.41 = (bf16[128,2048]{1,0:T(8,128)(2,1)S(1)}, bf16[128,2048]{1,0:T(8,128)(2,1)S(1)}, u32[]{:S(2)}, u32[]{:S(2)}) collective-permute-start(bf16[128,2048]{1,0:T(8,128)(2,1)S(1)} %slice.120.refs_14_), channel_id=1, source_target_pairs={{0,2},{1,3},{2,0},{3,1},{4,6},{5,7},{6,4},{7,5},{8,10},{9,11},{10,... | collective-permute-start | bytes 1572872 | tf_op jit(solution)/shard_map/ppermute | solution.py:554
  474.9 199.0 %reduce-scatter.11.cloned.1.call-start = ((), (), s32[]{:S(2)}) async-start(), calls=%async_computation.11 | async-start | bytes 4718592 | tf_op jit(solution)/shard_map/reduce_scatter | solution.py:913
  475.9 27.1 %collective-permute-start.43 = (bf16[128,2048]{1,0:T(8,128)(2,1)S(1)}, bf16[128,2048]{1,0:T(8,128)(2,1)S(1)}, u32[]{:S(2)}, u32[]{:S(2)}) collective-permute-start(bf16[128,2048]{1,0:T(8,128)(2,1)S(1)} %copy-done.69), channel_id=1, source_target_pairs={{0,2},{1,3},{2,0},{3,1},{4,6},{5,7},{6,4},{7,5},{8,10},{9,11},{10,... | collective-permute-start | bytes 1572872 | tf_op jit(solution)/shard_map/ppermute | solution.py:554
  476.7 26.3 %collective-permute-start.42 = (bf16[128,2048]{1,0:T(8,128)(2,1)S(1)}, bf16[128,2048]{1,0:T(8,128)(2,1)S(1)}, u32[]{:S(2)}, u32[]{:S(2)}) collective-permute-start(bf16[128,2048]{1,0:T(8,128)(2,1)S(1)} %copy-done.67), channel_id=1, source_target_pairs={{0,1},{1,0},{2,3},{3,2},{4,5},{5,4},{6,7},{7,6},{8,9},{9,8},{10,11... | collective-permute-start | bytes 1572872 | tf_op jit(solution)/shard_map/ppermute | solution.py:554
  509.7 190.4 %reduce-scatter.13.cloned.1.call-start = ((), (), s32[]{:S(2)}) async-start(), calls=%async_computation.12 | async-start | bytes 2359296 | tf_op jit(solution)/shard_map/reduce_scatter | solution.py:913
  510.7 24.9 %collective-permute-start.44 = (bf16[256,2048]{1,0:T(8,128)(2,1)}, bf16[256,2048]{1,0:T(8,128)(2,1)S(1)}, u32[]{:S(2)}, u32[]{:S(2)}) collective-permute-start(bf16[256,2048]{1,0:T(8,128)(2,1)} %get-tuple-element.197.refs_10_.refs_0_.refs_5_), channel_id=1, source_target_pairs={{0,1},{1,0},{2,3},{3,2},{4,5},{5,4},{6,7},{7,6},{8,9},{9,8},{10,11... | collective-permute-start | bytes 3145736 | tf_op jit(solution)/shard_map/ppermute | solution.py:554
  533.7 40.5 %collective-permute-start.47 = (bf16[128,2048]{1,0:T(8,128)(2,1)S(1)}, bf16[128,2048]{1,0:T(8,128)(2,1)}, u32[]{:S(2)}, u32[]{:S(2)}) collective-permute-start(bf16[128,2048]{1,0:T(8,128)(2,1)S(1)} %slice.121.refs_11_), channel_id=1, source_target_pairs={{0,1},{1,0},{2,3},{3,2},{4,5},{5,4},{6,7},{7,6},{8,9},{9,8},{10,11... | collective-permute-start | bytes 1572872 | tf_op jit(solution)/shard_map/ppermute | solution.py:554
  535.7 38.5 %collective-permute-start.48 = (bf16[128,2048]{1,0:T(8,128)(2,1)S(1)}, bf16[128,2048]{1,0:T(8,128)(2,1)}, u32[]{:S(2)}, u32[]{:S(2)}) collective-permute-start(bf16[128,2048]{1,0:T(8,128)(2,1)S(1)} %slice.122.refs_12_), channel_id=1, source_target_pairs={{0,2},{1,3},{2,0},{3,1},{4,6},{5,7},{6,4},{7,5},{8,10},{9,11},{10,... | collective-permute-start | bytes 1572872 | tf_op jit(solution)/shard_map/ppermute | solution.py:554
  536.9 56.4 %collective-permute-start.46 = (bf16[512,2048]{1,0:T(8,128)(2,1)}, bf16[512,2048]{1,0:T(8,128)(2,1)}, u32[]{:S(2)}, u32[]{:S(2)}) collective-permute-start(bf16[512,2048]{1,0:T(8,128)(2,1)} %get-tuple-element.199), channel_id=1, source_target_pairs={{0,1},{1,0},{2,3},{3,2},{4,5},{5,4},{6,7},{7,6},{8,9},{9,8},{10,11... | collective-permute-start | bytes 6291464 | tf_op jit(solution)/shard_map/ppermute | solution.py:554
  571.4 37.7 %collective-permute-start.50 = (bf16[256,2048]{1,0:T(8,128)(2,1)}, bf16[256,2048]{1,0:T(8,128)(2,1)S(1)}, u32[]{:S(2)}, u32[]{:S(2)}) collective-permute-start(bf16[256,2048]{1,0:T(8,128)(2,1)} %get-tuple-element.209), channel_id=1, source_target_pairs={{0,2},{1,3},{2,0},{3,1},{4,6},{5,7},{6,4},{7,5},{8,10},{9,11},{10,... | collective-permute-start | bytes 3145736 | tf_op jit(solution)/shard_map/ppermute | solution.py:554
  572.4 37.1 %collective-permute-start.51 = (bf16[256,2048]{1,0:T(8,128)(2,1)}, bf16[256,2048]{1,0:T(8,128)(2,1)S(1)}, u32[]{:S(2)}, u32[]{:S(2)}) collective-permute-start(bf16[256,2048]{1,0:T(8,128)(2,1)} %get-tuple-element.211), channel_id=1, source_target_pairs={{0,1},{1,0},{2,3},{3,2},{4,5},{5,4},{6,7},{7,6},{8,9},{9,8},{10,11... | collective-permute-start | bytes 3145736 | tf_op jit(solution)/shard_map/ppermute | solution.py:554
  596.0 40.9 %collective-permute-start.49 = (bf16[256,2048]{1,0:T(8,128)(2,1)}, bf16[256,2048]{1,0:T(8,128)(2,1)S(1)}, u32[]{:S(2)}, u32[]{:S(2)}) collective-permute-start(bf16[256,2048]{1,0:T(8,128)(2,1)} %add_arrived.12.refs_12_), channel_id=1, source_target_pairs={{0,2},{1,3},{2,0},{3,1},{4,6},{5,7},{6,4},{7,5},{8,10},{9,11},{10,... | collective-permute-start | bytes 3145736 | tf_op jit(solution)/shard_map/ppermute | solution.py:554
  613.0 42.6 %collective-permute-start.52 = (bf16[128,2048]{1,0:T(8,128)(2,1)}, bf16[128,2048]{1,0:T(8,128)(2,1)S(1)}, u32[]{:S(2)}, u32[]{:S(2)}) collective-permute-start(bf16[128,2048]{1,0:T(8,128)(2,1)} %get-tuple-element.213.refs_10_), channel_id=1, source_target_pairs={{0,1},{1,0},{2,3},{3,2},{4,5},{5,4},{6,7},{7,6},{8,9},{9,8},{10,11... | collective-permute-start | bytes 1572872 | tf_op jit(solution)/shard_map/ppermute | solution.py:554
  613.3 163.1 %reduce-scatter.15.cloned.1.call-start = ((), (), s32[]{:S(2)}) async-start(), calls=%async_computation.13 | async-start | bytes 3538944 | tf_op jit(solution)/shard_map/reduce_scatter | solution.py:913
  661.2 125.6 %reduce-scatter.17.cloned.1.call-start = ((), (), s32[]{:S(2)}) async-start(), calls=%async_computation.14 | async-start | bytes 3538944 | tf_op jit(solution)/shard_map/reduce_scatter | solution.py:913
  671.1 25.2 %collective-permute-start.54 = (bf16[256,2048]{1,0:T(8,128)(2,1)}, bf16[256,2048]{1,0:T(8,128)(2,1)S(1)}, u32[]{:S(2)}, u32[]{:S(2)}) collective-permute-start(bf16[256,2048]{1,0:T(8,128)(2,1)} %get-tuple-element.219), channel_id=1, source_target_pairs={{0,1},{1,0},{2,3},{3,2},{4,5},{5,4},{6,7},{7,6},{8,9},{9,8},{10,11... | collective-permute-start | bytes 3145736 | tf_op jit(solution)/shard_map/ppermute | solution.py:554
  732.1 27.0 %collective-permute-start.58 = (bf16[256,2048]{1,0:T(8,128)(2,1)S(1)}, bf16[256,2048]{1,0:T(8,128)(2,1)}, u32[]{:S(2)}, u32[]{:S(2)}) collective-permute-start(bf16[256,2048]{1,0:T(8,128)(2,1)S(1)} %copy-done.50), channel_id=1, source_target_pairs={{0,1},{1,0},{2,3},{3,2},{4,5},{5,4},{6,7},{7,6},{8,9},{9,8},{10,11... | collective-permute-start | bytes 3145736 | tf_op jit(solution)/shard_map/ppermute | solution.py:554
  734.0 25.3 %collective-permute-start.59 = (bf16[256,2048]{1,0:T(8,128)(2,1)S(1)}, bf16[256,2048]{1,0:T(8,128)(2,1)}, u32[]{:S(2)}, u32[]{:S(2)}) collective-permute-start(bf16[256,2048]{1,0:T(8,128)(2,1)S(1)} %copy-done.49), channel_id=1, source_target_pairs={{0,2},{1,3},{2,0},{3,1},{4,6},{5,7},{6,4},{7,5},{8,10},{9,11},{10,... | collective-permute-start | bytes 3145736 | tf_op jit(solution)/shard_map/ppermute | solution.py:554
  (108 other events, 884.3 us)
Sparse Core Ops, SparseCore 0:
  11.4 41.0 all-gather.5
  54.7 54.9 all-gather.3
  111.9 141.2 all-gather.7
  419.1 61.2 reduce-scatter.6
  482.5 68.1 reduce-scatter.8
  552.8 48.3 reduce-scatter.10
  613.4 36.6 reduce-scatter.12
  661.3 41.3 reduce-scatter.14
  726.0 41.2 reduce-scatter.16

commit v4 on v3

--- a/solution.py
+++ b/solution.py
@@ -296,15 +296,26 @@
     copies, start = [], 0
     for i, piece in enumerate(pieces):
         size = piece.shape[0]
-        copies.append(pltpu.make_async_copy(piece, rows.at[pl.ds(start, size)], sems.at[i]))
+        copies.append((start, pltpu.make_async_copy(piece, rows.at[pl.ds(start, size)], sems.at[i])))
         start += size
-
-    @pl.when(pl.program_id(0) == 0)
+    first = pl.program_id(0) == 0
+
+    @pl.when(first)
     def _():
-        for copy in copies:
+        for _, copy in copies:
             copy.start()
-        for copy in copies:
-            copy.wait()
+
+    def ready(end):
+        due = [copy for at, copy in copies if at < end]
+        del copies[: len(due)]
+        if due:
+
+            @pl.when(first)
+            def _():
+                for copy in due:
+                    copy.wait()
+
+    return ready
 
 
 def product_kernel(mode, count, extra, carried, *refs):
@@ -317,7 +328,7 @@
     if mode == "make":
         sc_ref, refs = refs[0], refs[1:]
     rows, sems = refs[carried:]
-    load(pieces, rows, sems)
+    load(pieces, rows, sems)(rows.shape[0])
     if mode == "make":
 
         @pl.when(pl.program_id(0) == 0)
@@ -365,25 +376,30 @@
     )(*pieces, w, *scale, *deps, *carry)
 
 
-def outer_kernel(counts, extra, *refs):
+def outer_kernel(counts, based, extra, *refs):
     total = sum(counts)
     groups, start = [], 0
     for count in counts:
         groups.append(refs[start : start + count])
         start += count
     rights = refs[total : total + len(counts)]
-    out_ref, rows, sems = refs[total + len(counts) + extra :]
+    out_ref, rows, sems = refs[total + len(counts) + based + extra :]
     first = 0
+    loads = []
     for m, group in enumerate(groups):
-        load(group, rows.at[m], sems.at[pl.ds(first, len(group))])
+        loads.append(load(group, rows.at[m], sems.at[pl.ds(first, len(group))]))
         first += len(group)
-    value = tn(rights[0][...], rows[0])
-    for m in range(1, len(counts)):
+    value = 0.0
+    for m, ready in enumerate(loads):
+        ready(rows.shape[1])
         value = value + tn(rights[m][...], rows[m])
-    out_ref[...] = value.astype(BF).T
-
-
-def outer(lefts, rights, deps=(), first=0, width=None):
+    value = value.astype(BF).T
+    if based:
+        value = (value.astype(F32) + refs[total + len(counts)][...].astype(F32)).astype(BF)
+    out_ref[...] = value
+
+
+def outer(lefts, rights, deps=(), first=0, width=None, base=()):
     length = rights[0].shape[0]
     width = width or rights[0].shape[1]
     depth = lefts[0][0].shape[1]
@@ -391,10 +407,11 @@
     counts = tuple(len(group) for group in lefts)
     flat = [piece for group in lefts for piece in group]
     return pl.pallas_call(
-        functools.partial(outer_kernel, counts, len(deps)),
+        functools.partial(outer_kernel, counts, len(base), len(deps)),
         grid=(width // tile,),
         in_specs=[HBM] * len(flat)
         + [pl.BlockSpec((length, tile), lambda j: (0, first // tile + j))] * len(rights)
+        + [pl.BlockSpec((depth, tile), lambda j: (0, j))] * len(base)
         + [HBM] * len(deps),
         out_specs=pl.BlockSpec((depth, tile), lambda j: (0, j)),
         out_shape=jax.ShapeDtypeStruct((depth, width), BF),
@@ -405,7 +422,7 @@
         compiler_params=pltpu.CompilerParams(vmem_limit_bytes=60 * MIB),
         cost_estimate=cost(2 * len(lefts) * length * depth * width),
         name="weight_gradient",
-    )(*flat, *rights, *deps)
+    )(*flat, *rights, *base, *deps)
 
 
 def partial_kernel(form, layouts, against, extra, carried, *refs):
@@ -491,8 +508,9 @@
     pieces, cots = refs[:count], refs[count:total]
     w_ref, d_ref = refs[total : total + 2]
     hid_ref, g_ref, rows, cot, sems = refs[total + 2 + extra :]
-    load(pieces, rows, sems.at[pl.ds(0, count)])
-    load(cots, cot, sems.at[pl.ds(count, count_cot)])
+    ready = load(pieces, rows, sems.at[pl.ds(0, count)])
+    load(cots, cot, sems.at[pl.ds(count, count_cot)])(cot.shape[0])
+    ready(rows.shape[0])
     tile = d_ref.shape[1]
     length = rows.shape[0]
     step = pick(length, 256)
@@ -913,39 +931,43 @@
         return lax.psum_scatter(value, "dp", scatter_dimension=0, tiled=True)
 
     qkv_0a, scale_0 = project(0, 0, (), (packed,))
-    ones.append(Gather(after(xs[1], *ones[0].pieces), "x", count, (qkv_0a,)))
+    ones.append(Gather(after(xs[1], *ones[0].pieces), "both", count, (qkv_0a,)))
     into = forward(0, 0, qkv_0a, (), ())
     cs = [after(cotangent, qkv_0a)[:, m] for m in range(MICRO)]
     (qkv_0b,) = project(0, 1, (scale_0,), (into[0], *ones[1].first))
-    cots = [Gather(cs[0], "y", count, (qkv_0b,))]
+    cots = [Gather(cs[0], "both", count, (qkv_0b,))]
     mixed_0, lse_0 = forward(0, 1, qkv_0b, into, ())
     parts = out_rows(mixed_0, (*ones[1].pieces, *cots[0].first))
     sum_0 = Reduce(parts, form, count)
-    cots.append(Gather(after(cs[1], qkv_0b), "x", count, (parts[0],)))
     qkv_1a, scale_1 = project(1, 0, (), (parts[0],))
     into = forward(1, 0, qkv_1a, (), tuple(cots[0].pieces))
-    late = sum_0.first((into[0], *cots[1].first))
+    late = sum_0.first((into[0],))
     (qkv_1b,) = project(1, 1, (scale_1,), (late[0],))
     middle_0, normed = sum_0.settle(add_branch, [xs[0]], (F32, BF), (qkv_1b,))
-    twos = [Gather(normed, "both", count)]
-    mixed_1, lse_1 = forward(1, 1, qkv_1b, into, (normed, *cots[1].pieces))
+    mixed_1, lse_1 = forward(1, 1, qkv_1b, into, (normed,))
+    twos = [Gather(normed, "both", count, (mixed_1,))]
     parts = out_rows(mixed_1, twos[0].sent)
-    sum_1 = Reduce(parts, form, count)
-    late = sum_1.first((parts[0], *twos[0].pieces))
+    sum_1 = Reduce(parts, form, count, twos[0].pieces)
 
     steps = width_ff // tile
-    early = (steps + 1) // 2
-    hidden_0, grad_ff_0 = feed_forward(twos[0].pieces, cots[0].pieces, full_ff, 0, steps, (), (late[0],))
-    middle_1, normed = sum_1.settle(add_branch, [xs[1]], (F32, BF), (hidden_0,))
+    ff_half = (steps + 1) // 2 * 2 * tile
+    hidden_0, grad_ff_0 = feed_forward(twos[0].pieces, cots[0].pieces, full_ff, 0, steps, (), (parts[0],))
+    late = sum_1.first((hidden_0,))
+    cots.append(Gather(after(cs[1], *twos[0].pieces), "both", count, (hidden_0,)))
+    parts = ff_rows(grad_ff_0, True, form, (late[0],))
+    middle_1, normed = sum_1.settle(add_branch, [xs[1]], (F32, BF), (parts[0],))
     twos.append(Gather(normed, "both", count))
-    parts = ff_rows(grad_ff_0, True, form, (normed,))
-    sum_0 = Reduce(parts, form, count, twos[1].pieces)
-    down = ff_rows(hidden_0, False, way[0], (parts[0], *twos[1].sent))
+    sum_0 = Reduce(parts, form, count, (*twos[1].pieces, *cots[1].pieces))
+    down_part = outer([cots[0].pieces], [hidden_0], (normed,))
+    ff_part_a = outer([twos[0].pieces], [grad_ff_0], (down_part,), 0, ff_half)
+    ff_part_b = outer(
+        [twos[0].pieces], [grad_ff_0], (ff_part_a, *twos[1].sent), ff_half, 2 * width_ff - ff_half
+    )
     hidden_1, grad_ff_1 = feed_forward(
-        twos[1].pieces, cots[1].pieces, full_ff, 0, steps, (), (down[0],)
+        twos[1].pieces, cots[1].pieces, full_ff, 0, steps, (), (ff_part_b,)
     )
     late = sum_0.first((hidden_1,))
-    weight = outer([c.pieces for c in cots], [hidden_0, hidden_1], (late[0],))
+    weight = outer([cots[1].pieces], [hidden_1], (late[0],), base=(down_part,))
     grad_middle_0, rounded, gain_two_0, weight = sum_0.settle(
         turn_back, [middle_0, cs[0]], (F32, BF, "sum"), (), (weight,)
     )
@@ -953,10 +975,11 @@
     mids = [Gather(rounded, "both", count)]
     parts = ff_rows(grad_ff_1, True, form, (rounded,))
     sum_1 = Reduce(parts, form, count)
-    two_pieces, grad_ffs = [g.pieces for g in twos], [grad_ff_0, grad_ff_1]
-    ff_half = early * 2 * tile
-    weight = outer(two_pieces, grad_ffs, (parts[0], *mids[0].sent), 0, ff_half)
-    late = sum_1.first(tuple(mids[0].pieces), (weight,))
+    weight = outer(
+        [twos[1].pieces], [grad_ff_1], (parts[0], *mids[0].sent), 0, ff_half, base=(ff_part_a,)
+    )
+    down = ff_rows(hidden_0, False, way[0], (weight,))
+    late = sum_1.first((down[0], *mids[0].pieces), (weight,))
     grad_ff_a = scatter(late[-1])
 
     def backward(m, qkv, lse, mixed, grad, scale, cut, into, deps):
@@ -966,7 +989,9 @@
         )
 
     (grad,) = product(mids[0].pieces, full_out, out_at, width, deps=(late[0],))
-    weight = outer(two_pieces, grad_ffs, (grad,), ff_half, 2 * width_ff - ff_half)
+    weight = outer(
+        [twos[1].pieces], [grad_ff_1], (grad,), ff_half, 2 * width_ff - ff_half, base=(ff_part_b,)
+    )
     grad_middle_1, rounded, gain_two_1, weight = sum_1.settle(
         turn_back, [middle_1, cs[1]], (F32, BF, "sum"), (), (weight,)
     )
@@ -978,10 +1003,10 @@
     *parts, gain_one_0 = qkv_rows([grad_0a, grad_0b], 0, (grad_down,))
     sum_0 = Reduce(parts, form, count)
     (grad,) = product(mids[1].pieces, full_out, out_at, width, deps=(parts[0],))
-    late = down_0.first((grad,))
-    weight = outer([g.pieces for g in mids], [mixed_0, mixed_1], (late[0], grad_ff_a))
+    weight = outer([g.pieces for g in mids], [mixed_0, mixed_1], (grad, grad_ff_a))
     late = sum_0.first((), (weight,))
     grad_out = scatter(late[-1])
+    late = down_0.first((late[0],))
     grad_1a, fold = backward(1, qkv_1a, lse_1, mixed_1, grad, scale_1, 0, (), (late[0],))
     (output_0,) = down_0.settle(add_last, [middle_0], (BF,), (grad_1a,))
     weight = outer([g.pieces for g in ones], [grad_0a, grad_1a], (output_0,))
@@ -992,13 +1017,12 @@
     grad_1b, fold_1 = backward(1, qkv_1b, lse_1, mixed_1, grad, scale_1, 1, (fold,), (parts[0], grad_ff_b))
     late = down_1.first((grad_1b,))
     weight = outer([g.pieces for g in ones], [grad_0b, grad_1b], (late[0], grad_out))
-    *parts, gain_one_1, weight = qkv_rows([grad_1a, grad_1b], 1, down_1.arrived, (weight,))
+    output_1, weight = down_1.settle(add_last, [middle_1], (BF,), (), (weight,))
     grad_qkv_b = scatter(weight)
+    *parts, gain_one_1 = qkv_rows([grad_1a, grad_1b], 1, (output_1,))
     sum_1 = Reduce(parts, form, count)
-    (output_1,) = down_1.settle(add_last, [middle_1], (BF,), (parts[0],))
-    late = sum_1.first((output_1,))
     grad_gate, grad_up = unpack(
-        [grad_ff_a, grad_ff_b], (early, steps - early), 2, gain_two
+        [grad_ff_a, grad_ff_b], ((steps + 1) // 2, steps // 2), 2, gain_two
     )
     grad_out, grad_down = turned([grad_out, grad_down])
 
@@ -1016,19 +1040,23 @@
         ],
         axis=1,
     )
-    small = lax.dynamic_index_in_dim(sum_over(small, "dp", count_dp), me, 0, keepdims=False)
+    small = sum_over(small, "dp", count_dp)
+    late = sum_1.first((small, grad_gate, grad_out, grad_down))
+    grad_qkv = unpack([grad_qkv_a, grad_qkv_b], (each, each), 3, gain_one)
+    small, output_0, output_1 = lax.optimization_barrier((small, output_0, output_1, grad_qkv[0]))[:3]
+    small = lax.dynamic_index_in_dim(small, me, 0, keepdims=False)
     both_gains = sum_over(small[: 2 * rows_w], "tensor", count)
     (token_1,) = sum_1.settle(
         finish_back,
         [xs[1], grad_middle_1],
         (BF,),
-        (late[0], grad_qkv_a, grad_gate, grad_out, grad_down, both_gains),
+        (late[0], grad_qkv[0]),
     )
     return (
         jnp.stack([output_0, output_1], axis=1),
         jnp.stack([token_0, token_1], axis=1),
         both_gains[:rows_w] / gain_one[:, 0],
-        *unpack([grad_qkv_a, grad_qkv_b], (each, each), 3, gain_one),
+        *grad_qkv,
         grad_out,
         small[2 * rows_w :].reshape(buckets_local, heads),
         both_gains[rows_w:] / gain_two[:, 0],

time: 802 us -> 783 us (0.976)
  waiting for transfers between devices: 136 us -> 107 us
  local copies, waits for them, and re-layouts: 41.2 us -> 49.6 us
    ppermute x67 -> x70, waiting for transfers between devices: 132 us -> 84.4 us  [hop(): return lax.ppermute(part, axis, [(i, i ^ bit) for i in range(count)])]
    all_gather x3, waiting for transfers between devices: 3.44 us -> 18.6 us  [spread(): return lax.all_gather(part, 'dp', axis=0, tiled=True)]
    pallas_call x6 -> x9, Pallas kernels: 98.4 us -> 108 us  [outer(): pl.pallas_call(functools.partial(outer_kernel, counts, len(base), len(dep...]
    ppermute x67 -> x70, starting transfers between devices: 82 us -> 74.9 us  [hop(): return lax.ppermute(part, axis, [(i, i ^ bit) for i in range(count)])]
    unnamed x172 -> x164, local copies, waits for them, and re-layouts: 27.8 us -> 30.1 us
  transfers between devices with their start and end apart: 76 -> 79, of which waited for: 33 -> 30; matrix products, arithmetic and copies ran while one was open for 4% -> 4% of each run, Pallas kernels for 62% -> 66%
where the time goes in v4:
time: 783 us; the launch traced here: 776 us
  Pallas kernels  522 us (67%)
  waiting for transfers between devices  107 us (14%)
  starting transfers between devices  75.2 us (10%)
  local copies, waits for them, and re-layouts  49.6 us (6%)
  between operations  15.5 us (2%)
    pallas_call x9, Pallas kernels, outer(): pl.pallas_call(functools.partial(outer_kernel, counts, len(base), len(dep...  108 us
    pallas_call x4, Pallas kernels, attend_backward(): pl.pallas_call(functools.partial(attend_backward_kernel, n, extra), grid_...  90.5 us
    pallas_call x8, Pallas kernels, partial_rows(): pl.pallas_call(functools.partial(partial_kernel, form, layouts, len(piece...  87.8 us
    ppermute x70, waiting for transfers between devices, hop(): return lax.ppermute(part, axis, [(i, i ^ bit) for i in range(count)])  84.4 us
    ppermute x70, starting transfers between devices, hop(): return lax.ppermute(part, axis, [(i, i ^ bit) for i in range(count)])  74.9 us
    pallas_call x4, Pallas kernels, attend_forward(): pl.pallas_call(functools.partial(attend_forward_kernel, n, extra), grid_s...  52.3 us
    pallas_call x2, Pallas kernels, feed_forward(): pl.pallas_call(functools.partial(ff_kernel, len(pieces), len(cots), extra...  51.3 us
    pallas_call x6, Pallas kernels, product(): pl.pallas_call(functools.partial(product_kernel, mode, len(pieces), len(d...  50.2 us
  transfers between devices with their start and end apart: 79, of which 30 were waited for; matrix products, arithmetic and copies ran while one was open for 4% of the time, Pallas kernels for 66%

profile of v4, /device:TPU:0, one launch (start us, length us, event | category | flops | bytes accessed | tf_op | source)
XLA Modules:
  0.0 776.2 jit_solution(7270382877769033098)
XLA Ops:
  12.2 3.8 fusion.10
  33.4 10.6 %bias_strips.1.refs_4_.refs_5_ = f32[8,1792,256]{2,1,0:T(8,128)} custom-call(f32[8,7,512]{2,1,0:T(8,128)} %pad_maximum_fusion.2.w_ref), custom_call_target="tpu_custom_call" | custom-call | flops 12000000000 | bytes 1 | tf_op jit(solution)/shard_map/bias_strips/pallas_call | solution.py:48
  58.1 5.4 collective-permute-done.6.refs_4_.refs_8_
  66.8 9.6 %rows_product.6 = (bf16[1024,768]{1,0:T(8,128)(2,1)}, f32[1024,128]{1,0:T(8,128)}) custom-call(bf16[256,2048]{1,0:T(8,128)(2,1)} %bitcast.40, bf16[256,2048]{1,0:T(8,128)(2,1)} %copy-done.25, bf16[256,2048]{1,0:T(8,128)(2,1)} %copy-done.24, bf16[128,2048]{1,0:T(8,128)(2,1)} %collective-permute-done.5.refs_3_.refs_7_, ...), custom_call_target="tpu_custom_call" | custom-call | flops 10442450944 | bytes 1 | tf_op jit(solution)/shard_map/rows_product/pallas_call | solution.py:358
  79.1 11.5 %collective-permute-done.8.refs_9_.refs_4_.refs_2_.refs_7_.refs_6_ = bf16[256,2048]{1,0:T(8,128)(2,1)S(1)} collective-permute-done((bf16[256,2048]{1,0:T(8,128)(2,1)}, bf16[256,2048]{1,0:T(8,128)(2,1)S(1)}, u32[]{:S(2)}, u32[]{:S(2)}) %collective-permute-start.8) | collective-permute-done | bytes 1048608 | tf_op jit(solution)/shard_map/ppermute | solution.py:572
  96.5 13.1 %attend_forward.4 = (bf16[1024,512]{1,0:T(8,128)(2,1)}, f32[4,2,1024]{2,1,0:T(2,128)}) custom-call(s32[16]{0:T(128)} %reshape.190.refs_0_, s32[4]{0:T(128)} %iota_xor_fusion.refs_1_, bf16[1024,768]{1,0:T(8,128)(2,1)} %get-tuple-element.149.refs_2_, bf16[1024,128]{1,0:T(8,128)(2,1)} %get-tuple-element.335.refs_3_, ...), custom_call_target="tpu_custom_call" | custom-call | flops 14800000000 | bytes 1 | tf_op jit(solution)/shard_map/attend_forward/pallas_call | solution.py:136
  109.6 8.4 %rows_product.7.refs_2_ = bf16[1024,768]{1,0:T(8,128)(2,1)} custom-call(bf16[256,2048]{1,0:T(8,128)(2,1)} %bitcast.41, bf16[256,2048]{1,0:T(8,128)(2,1)} %copy-done.25, bf16[256,2048]{1,0:T(8,128)(2,1)} %copy-done.24, bf16[128,2048]{1,0:T(8,128)(2,1)} %collective-permute-done.5.refs_3_.refs_7_, bf16[128,2048]{1,0:T(8,128)(2,1)} %collective-permute-done.6.refs_4_.refs_8_, ...), custom_call_target="tpu_custom_call" | custom-call | flops 10442450944 | bytes 1 | tf_op jit(solution)/shard_map/rows_product/pallas_call | solution.py:358
  118.0 13.7 %attend_forward.5 = (bf16[1024,512]{1,0:T(8,128)(2,1)}, f32[4,2,1024]{2,1,0:T(2,128)}) custom-call(s32[16]{0:T(128)} %reshape.190.refs_0_, s32[4]{0:T(128)} %iota_xor_fusion.refs_1_, bf16[1024,768]{1,0:T(8,128)(2,1)} %rows_product.7.refs_2_, bf16[1024,128]{1,0:T(8,128)(2,1)} %get-tuple-element.335.refs_3_, ...), custom_call_target="tpu_custom_call", output_to_operand_aliasing={{0}: (6, {}), {1}: (7, {})} | custom-call | flops 14800000000 | bytes 1 | tf_op jit(solution)/shard_map/attend_forward/pallas_call | solution.py:136
  136.6 6.5 partial_rows.8
  144.6 9.6 %rows_product.8 = (bf16[1024,768]{1,0:T(8,128)(2,1)}, f32[1024,128]{1,0:T(8,128)}) custom-call(bf16[256,2048]{1,0:T(8,128)(2,1)} %bitcast.36.refs_2_.refs_0_.refs_5_.refs_4_, bf16[256,2048]{1,0:T(8,128)(2,1)} %collective-permute-done.7.refs_8_.refs_3_.refs_1_.refs_6_.refs_5_, bf16[256,2048]{1,0:T(8,128)(2,1)} %copy-done.26, ...), custom_call_target="tpu_custom_call" | custom-call | flops 10442450944 | bytes 1 | tf_op jit(solution)/shard_map/rows_product/pallas_call | solution.py:358
  154.2 12.7 %attend_forward.6 = (bf16[1024,512]{1,0:T(8,128)(2,1)}, f32[4,2,1024]{2,1,0:T(2,128)}) custom-call(s32[16]{0:T(128)} %reshape.191.refs_0_, s32[4]{0:T(128)} %iota_xor_fusion.refs_1_, bf16[1024,768]{1,0:T(8,128)(2,1)} %get-tuple-element.165.refs_2_, bf16[1024,128]{1,0:T(8,128)(2,1)} %get-tuple-element.334.refs_3_, ...), custom_call_target="tpu_custom_call" | custom-call | flops 14800000000 | bytes 1 | tf_op jit(solution)/shard_map/attend_forward/pallas_call | solution.py:136
  166.9 4.1 collective-permute-done.13.refs_3_.refs_1_
  176.5 8.5 %rows_product.9.refs_6_.refs_2_ = bf16[1024,768]{1,0:T(8,128)(2,1)} custom-call(bf16[256,2048]{1,0:T(8,128)(2,1)} %bitcast.36.refs_2_.refs_0_.refs_5_.refs_4_, bf16[256,2048]{1,0:T(8,128)(2,1)} %collective-permute-done.7.refs_8_.refs_3_.refs_1_.refs_6_.refs_5_, bf16[256,2048]{1,0:T(8,128)(2,1)} %copy-done.26, ...), custom_call_target="tpu_custom_call" | custom-call | flops 10442450944 | bytes 1 | tf_op jit(solution)/shard_map/rows_product/pallas_call | solution.py:358
  188.9 4.6 settle_rows.8
  195.9 12.7 %attend_forward.7 = (bf16[1024,512]{1,0:T(8,128)(2,1)}, f32[4,2,1024]{2,1,0:T(2,128)}) custom-call(s32[16]{0:T(128)} %reshape.191.refs_0_, s32[4]{0:T(128)} %iota_xor_fusion.refs_1_, bf16[1024,768]{1,0:T(8,128)(2,1)} %rows_product.9.refs_6_.refs_2_, bf16[1024,128]{1,0:T(8,128)(2,1)} %get-tuple-element.334.refs_3_, ...), custom_call_target="tpu_custom_call", output_to_operand_aliasing={{0}: (6, {}), {1}: (7, {})} | custom-call | flops 14800000000 | bytes 1 | tf_op jit(solution)/shard_map/attend_forward/pallas_call | solution.py:136
  208.7 8.2 %collective-permute-done.20.refs_2_ = bf16[256,2048]{1,0:T(8,128)(2,1)S(1)} collective-permute-done((bf16[256,2048]{1,0:T(8,128)(2,1)}, bf16[256,2048]{1,0:T(8,128)(2,1)S(1)}, u32[]{:S(2)}, u32[]{:S(2)}) %collective-permute-start.20) | collective-permute-done | bytes 1048608 | tf_op jit(solution)/shard_map/ppermute | solution.py:572
  220.2 6.6 partial_rows.9
  234.1 18.6 %all-gather.8.cloned.1.call-done.refs_10_.refs_11_.refs_1_ = bf16[2048,3840]{1,0:T(8,128)(2,1)} async-done(((bf16[256,3840]{1,0:T(8,128)(2,1)}), bf16[2048,3840]{1,0:T(8,128)(2,1)}) %all-gather.8.cloned.1.call-update) | async-done | bytes 15728656 | tf_op jit(solution)/shard_map/all_gather | solution.py:858
  252.7 25.7 %feed_forward.2 = (bf16[1024,1280]{1,0:T(8,128)(2,1)}, bf16[1024,2560]{1,0:T(8,128)(2,1)}) custom-call(bf16[256,2048]{1,0:T(8,128)(2,1)} %get-tuple-element.172.refs_8_.refs_0_, bf16[256,2048]{1,0:T(8,128)(2,1)} %copy-done.31, bf16[256,2048]{1,0:T(8,128)(2,1)} %copy-done.30, bf16[128,2048]{1,0:T(8,128)(2,1)} %collective-permute-done.21.refs_3_, ...), custom_call_target="tpu_custom_call" | custom-call | flops 32212254720 | bytes 1 | tf_op jit(solution)/shard_map/feed_forward/pallas_call | solution.py:542
  285.1 15.9 %partial_rows.10 = (bf16[256,2048]{1,0:T(8,128)(2,1)}, bf16[256,2048]{1,0:T(8,128)(2,1)}, bf16[256,2048]{1,0:T(8,128)(2,1)}, bf16[128,2048]{1,0:T(8,128)(2,1)}, bf16[128,2048]{1,0:T(8,128)(2,1)}) custom-call(bf16[1024,2560]{1,0:T(8,128)(2,1)} %get-tuple-element.178.refs_0_.refs_5_, bf16[2048,3840]{1,0:T(8,128)(2,1)} %all-gather.8.cloned.1.call-done.refs_10_.refs_11_.refs_1_, ...), custom_call_target="tpu_custom_call" | custom-call | flops 21474836480 | bytes 1 | tf_op jit(solution)/shard_map/partial_rows/pallas_call | solution.py:483
  305.9 4.2 settle_rows.9
  312.1 11.2 %weight_gradient.9.refs_6_ = bf16[2048,1280]{1,0:T(8,128)(2,1)} custom-call(bf16[256,2048]{1,0:T(8,128)(2,1)} %copy-done.10, bf16[256,2048]{1,0:T(8,128)(2,1)} %collective-permute-done.11.refs_7_.refs_6_.refs_1_, bf16[256,2048]{1,0:T(8,128)(2,1)} %collective-permute-done.12.refs_8_.refs_7_.refs_2_, ...), custom_call_target="tpu_custom_call" | custom-call | flops 10737418240 | bytes 1 | tf_op jit(solution)/shard_map/weight_gradient/pallas_call | solution.py:409
  323.3 12.4 %weight_gradient.10.refs_6_ = bf16[2048,1536]{1,0:T(8,128)(2,1)} custom-call(bf16[256,2048]{1,0:T(8,128)(2,1)} %get-tuple-element.172.refs_8_.refs_0_, bf16[256,2048]{1,0:T(8,128)(2,1)} %copy-done.31, bf16[256,2048]{1,0:T(8,128)(2,1)} %copy-done.30, bf16[128,2048]{1,0:T(8,128)(2,1)} %collective-permute-done.21.refs_3_, bf16[128,2048]{1,0:T(8,128)(2,1)} %copy-done.57, ...), custom_call_target="tpu_custom_call" | custom-call | flops 12884901888 | bytes 1 | tf_op jit(solution)/shard_map/weight_gradient/pallas_call | solution.py:409
  339.1 9.9 %weight_gradient.11.refs_12_.refs_6_ = bf16[2048,1024]{1,0:T(8,128)(2,1)} custom-call(bf16[256,2048]{1,0:T(8,128)(2,1)} %get-tuple-element.172.refs_8_.refs_0_, bf16[256,2048]{1,0:T(8,128)(2,1)} %copy-done.31, bf16[256,2048]{1,0:T(8,128)(2,1)} %copy-done.30, bf16[128,2048]{1,0:T(8,128)(2,1)} %collective-permute-done.21.refs_3_, ...), custom_call_target="tpu_custom_call" | custom-call | flops 8589934592 | bytes 1 | tf_op jit(solution)/shard_map/weight_gradient/pallas_call | solution.py:409
  352.8 25.6 %feed_forward.3 = (bf16[1024,1280]{1,0:T(8,128)(2,1)}, bf16[1024,2560]{1,0:T(8,128)(2,1)}) custom-call(bf16[256,2048]{1,0:T(8,128)(2,1)} %get-tuple-element.196.refs_6_.refs_0_, bf16[256,2048]{1,0:T(8,128)(2,1)} %collective-permute-done.27.refs_1_, bf16[256,2048]{1,0:T(8,128)(2,1)} %copy-done.27, bf16[128,2048]{1,0:T(8,128)(2,1)} %copy-done.56, ...), custom_call_target="tpu_custom_call" | custom-call | flops 32212254720 | bytes 1 | tf_op jit(solution)/shard_map/feed_forward/pallas_call | solution.py:542
  383.5 12.4 %weight_gradient.12.refs_7_ = bf16[2048,1280]{1,0:T(8,128)(2,1)} custom-call(bf16[256,2048]{1,0:T(8,128)(2,1)} %copy-done.9, bf16[256,2048]{1,0:T(8,128)(2,1)} %copy-done.29, bf16[256,2048]{1,0:T(8,128)(2,1)} %copy-done.28, bf16[128,2048]{1,0:T(8,128)(2,1)} %collective-permute-done.33.refs_8_.refs_3_, ...), custom_call_target="tpu_custom_call" | custom-call | flops 10737418240 | bytes 1 | tf_op jit(solution)/shard_map/weight_gradient/pallas_call | solution.py:409
  396.9 5.6 settle_rows.10
  406.4 16.1 %partial_rows.11 = (bf16[256,2048]{1,0:T(8,128)(2,1)}, bf16[256,2048]{1,0:T(8,128)(2,1)}, bf16[256,2048]{1,0:T(8,128)(2,1)}, bf16[128,2048]{1,0:T(8,128)(2,1)}, bf16[128,2048]{1,0:T(8,128)(2,1)}) custom-call(bf16[1024,2560]{1,0:T(8,128)(2,1)} %get-tuple-element.210.refs_0_.refs_5_, bf16[2048,3840]{1,0:T(8,128)(2,1)} %all-gather.8.cloned.1.call-done.refs_10_.refs_11_.refs_1_, ...), custom_call_target="tpu_custom_call" | custom-call | flops 21474836480 | bytes 1 | tf_op jit(solution)/shard_map/partial_rows/pallas_call | solution.py:483
  424.4 5.5 collective-permute-done.40.refs_7_.refs_2_
  433.5 13.4 %weight_gradient.13.refs_2_.refs_10_ = bf16[2048,1536]{1,0:T(8,128)(2,1)} custom-call(bf16[256,2048]{1,0:T(8,128)(2,1)} %get-tuple-element.196.refs_6_.refs_0_, bf16[256,2048]{1,0:T(8,128)(2,1)} %collective-permute-done.27.refs_1_, bf16[256,2048]{1,0:T(8,128)(2,1)} %copy-done.27, bf16[128,2048]{1,0:T(8,128)(2,1)} %copy-done.56, ...), custom_call_target="tpu_custom_call" | custom-call | flops 12884901888 | bytes 1 | tf_op jit(solution)/shard_map/weight_gradient/pallas_call | solution.py:409
  447.0 9.5 %partial_rows.12 = (bf16[256,2048]{1,0:T(8,128)(2,1)}, bf16[512,2048]{1,0:T(8,128)(2,1)}, bf16[256,2048]{1,0:T(8,128)(2,1)}) custom-call(bf16[1024,1280]{1,0:T(8,128)(2,1)} %get-tuple-element.187.refs_4_.refs_5_.refs_0_, bf16[2048,3840]{1,0:T(8,128)(2,1)} %all-gather.8.cloned.1.call-done.refs_10_.refs_11_.refs_1_, ...), custom_call_target="tpu_custom_call" | custom-call | flops 10737418240 | bytes 1 | tf_op jit(solution)/shard_map/partial_rows/pallas_call | solution.py:483
  466.6 7.0 rows_product.10.refs_7_.refs_8_
  473.6 10.8 %weight_gradient.14.refs_7_ = bf16[2048,1024]{1,0:T(8,128)(2,1)} custom-call(bf16[256,2048]{1,0:T(8,128)(2,1)} %get-tuple-element.196.refs_6_.refs_0_, bf16[256,2048]{1,0:T(8,128)(2,1)} %collective-permute-done.27.refs_1_, bf16[256,2048]{1,0:T(8,128)(2,1)} %copy-done.27, bf16[128,2048]{1,0:T(8,128)(2,1)} %copy-done.56, ...), custom_call_target="tpu_custom_call" | custom-call | flops 8589934592 | bytes 1 | tf_op jit(solution)/shard_map/weight_gradient/pallas_call | solution.py:409
  485.3 5.7 settle_rows.11
  493.2 22.9 %attend_backward.4 = (bf16[1024,768]{1,0:T(8,128)(2,1)}, f32[4,2,8,256]{3,2,1,0:T(8,128)}) custom-call(s32[16]{0:T(128)} %reshape.190.refs_0_, s32[4]{0:T(128)} %iota_xor_fusion.refs_1_, bf16[1024,768]{1,0:T(8,128)(2,1)} %get-tuple-element.149.refs_2_, bf16[1024,128]{1,0:T(8,128)(2,1)} %get-tuple-element.335.refs_3_, ...), custom_call_target="tpu_custom_call" | custom-call | flops 25999998976 | bytes 1 | tf_op jit(solution)/shard_map/attend_backward/pallas_call | solution.py:252
  519.3 22.4 %attend_backward.5 = (bf16[1024,768]{1,0:T(8,128)(2,1)}, f32[4,2,8,256]{3,2,1,0:T(8,128)}) custom-call(s32[16]{0:T(128)} %reshape.190.refs_0_, s32[4]{0:T(128)} %iota_xor_fusion.refs_1_, bf16[1024,768]{1,0:T(8,128)(2,1)} %rows_product.7.refs_2_, bf16[1024,128]{1,0:T(8,128)(2,1)} %get-tuple-element.335.refs_3_, ...), custom_call_target="tpu_custom_call", output_to_operand_aliasing={{1}: (10, {})} | custom-call | flops 25999998976 | bytes 1 | tf_op jit(solution)/shard_map/attend_backward/pallas_call | solution.py:252
  541.8 11.7 %partial_rows.13 = (bf16[256,2048]{1,0:T(8,128)(2,1)}, bf16[256,2048]{1,0:T(8,128)(2,1)}, bf16[256,2048]{1,0:T(8,128)(2,1)}, bf16[128,2048]{1,0:T(8,128)(2,1)}, ...) custom-call(bf16[1024,768]{1,0:T(8,128)(2,1)} %get-tuple-element.221.refs_0_.refs_10_, ...), custom_call_target="tpu_custom_call" | custom-call | flops 12884901888 | bytes 1 | tf_op jit(solution)/shard_map/partial_rows/pallas_call | solution.py:483
  555.9 7.1 rows_product.11.refs_12_.refs_8_
  563.0 11.0 %weight_gradient.15.refs_4_ = bf16[2048,512]{1,0:T(8,128)(2,1)} custom-call(bf16[256,2048]{1,0:T(8,128)(2,1)} %get-tuple-element.209.refs_2_.refs_5_.refs_0_, bf16[256,2048]{1,0:T(8,128)(2,1)} %copy-done.3, bf16[256,2048]{1,0:T(8,128)(2,1)} %copy-done.2, bf16[128,2048]{1,0:T(8,128)(2,1)} %copy-done.15, bf16[128,2048]{1,0:T(8,128)(2,1)} %copy-done.16, ...), custom_call_target="tpu_custom_call" | custom-call | flops 8589934592 | bytes 1 | tf_op jit(solution)/shard_map/weight_gradient/pallas_call | solution.py:409
  574.0 19.1 %collective-permute-done.53.refs_3_.refs_1_ = bf16[256,2048]{1,0:T(8,128)(2,1)S(1)} collective-permute-done((bf16[256,2048]{1,0:T(8,128)(2,1)}, bf16[256,2048]{1,0:T(8,128)(2,1)S(1)}, u32[]{:S(2)}, u32[]{:S(2)}) %collective-permute-start.53) | collective-permute-done | bytes 1048608 | tf_op jit(solution)/shard_map/ppermute | solution.py:572
  601.3 22.7 %attend_backward.6 = (bf16[1024,768]{1,0:T(8,128)(2,1)}, f32[4,2,8,256]{3,2,1,0:T(8,128)}) custom-call(s32[16]{0:T(128)} %reshape.191.refs_0_, s32[4]{0:T(128)} %iota_xor_fusion.refs_1_, bf16[1024,768]{1,0:T(8,128)(2,1)} %get-tuple-element.165.refs_2_, bf16[1024,128]{1,0:T(8,128)(2,1)} %get-tuple-element.334.refs_3_, ...), custom_call_target="tpu_custom_call" | custom-call | flops 25999998976 | bytes 1 | tf_op jit(solution)/shard_map/attend_backward/pallas_call | solution.py:252
  629.6 13.6 %weight_gradient.16.refs_7_ = bf16[2048,768]{1,0:T(8,128)(2,1)} custom-call(bf16[256,2048]{1,0:T(8,128)(2,1)} %bitcast.44, bf16[256,2048]{1,0:T(8,128)(2,1)} %copy-done.25, bf16[256,2048]{1,0:T(8,128)(2,1)} %copy-done.24, bf16[128,2048]{1,0:T(8,128)(2,1)} %collective-permute-done.5.refs_3_.refs_7_, bf16[128,2048]{1,0:T(8,128)(2,1)} %collective-permute-done.6.refs_4_.refs_8_, ...), custom_call_target="tpu_custom_call" | custom-call | flops 12884901888 | bytes 1 | tf_op jit(solution)/shard_map/weight_gradient/pallas_call | solution.py:409
  644.2 4.6 settle_rows.13
  648.9 9.5 %partial_rows.14 = (bf16[256,2048]{1,0:T(8,128)(2,1)}, bf16[256,2048]{1,0:T(8,128)(2,1)}, bf16[256,2048]{1,0:T(8,128)(2,1)}, bf16[128,2048]{1,0:T(8,128)(2,1)}, bf16[128,2048]{1,0:T(8,128)(2,1)}) custom-call(bf16[1024,1280]{1,0:T(8,128)(2,1)} %get-tuple-element.205.refs_4_.refs_5_.refs_0_, ...), custom_call_target="tpu_custom_call" | custom-call | flops 10737418240 | bytes 1 | tf_op jit(solution)/shard_map/partial_rows/pallas_call | solution.py:483
  660.6 22.4 %attend_backward.7 = (bf16[1024,768]{1,0:T(8,128)(2,1)}, f32[4,2,8,256]{3,2,1,0:T(8,128)}) custom-call(s32[16]{0:T(128)} %reshape.191.refs_0_, s32[4]{0:T(128)} %iota_xor_fusion.refs_1_, bf16[1024,768]{1,0:T(8,128)(2,1)} %rows_product.9.refs_6_.refs_2_, bf16[1024,128]{1,0:T(8,128)(2,1)} %get-tuple-element.334.refs_3_, ...), custom_call_target="tpu_custom_call", output_to_operand_aliasing={{1}: (10, {})} | custom-call | flops 25999998976 | bytes 1 | tf_op jit(solution)/shard_map/attend_backward/pallas_call | solution.py:252
  688.7 13.6 %weight_gradient.17.refs_6_ = bf16[2048,768]{1,0:T(8,128)(2,1)} custom-call(bf16[256,2048]{1,0:T(8,128)(2,1)} %bitcast.46, bf16[256,2048]{1,0:T(8,128)(2,1)} %copy-done.25, bf16[256,2048]{1,0:T(8,128)(2,1)} %copy-done.24, bf16[128,2048]{1,0:T(8,128)(2,1)} %collective-permute-done.5.refs_3_.refs_7_, bf16[128,2048]{1,0:T(8,128)(2,1)} %collective-permute-done.6.refs_4_.refs_8_, ...), custom_call_target="tpu_custom_call" | custom-call | flops 12884901888 | bytes 1 | tf_op jit(solution)/shard_map/weight_gradient/pallas_call | solution.py:409
  709.1 12.0 %partial_rows.15 = (bf16[256,2048]{1,0:T(8,128)(2,1)}, bf16[256,2048]{1,0:T(8,128)(2,1)}, bf16[256,2048]{1,0:T(8,128)(2,1)}, bf16[128,2048]{1,0:T(8,128)(2,1)}, ...) custom-call(bf16[1024,768]{1,0:T(8,128)(2,1)} %get-tuple-element.238.refs_4_.refs_11_.refs_0_, ...), custom_call_target="tpu_custom_call" | custom-call | flops 12884901888 | bytes 1 | tf_op jit(solution)/shard_map/partial_rows/pallas_call | solution.py:483
  753.7 4.8 settle_rows.15
  (419 shorter events, 203.9 us)
Async XLA Ops:
  7.2 59.6 %all-gather.4.cloned.1.call-start = ((), (), s32[]{:S(2)}) async-start(), calls=%async_computation.6 | async-start | bytes 3538944 | tf_op jit(solution)/shard_map/all_gather | solution.py:858
  11.4 98.2 %all-gather.6.cloned.1.call-start = ((), (), s32[]{:S(2)}) async-start(), calls=%async_computation.7 | async-start | bytes 5898240 | tf_op jit(solution)/shard_map/all_gather | solution.py:858
  12.1 240.6 %all-gather.8.cloned.1.call-start = ((), (), s32[]{:S(2)}) async-start(), calls=%async_computation.8 | async-start | bytes 17694720 | tf_op jit(solution)/shard_map/all_gather | solution.py:858
  16.6 27.4 %collective-permute-start.1 = (bf16[256,2048]{1,0:T(8,128)(2,1)S(1)}, bf16[256,2048]{1,0:T(8,128)(2,1)S(1)}, u32[]{:S(2)}, u32[]{:S(2)}) collective-permute-start(bf16[256,2048]{1,0:T(8,128)(2,1)S(1)} %bitcast.38), channel_id=1, source_target_pairs={{0,2},{1,3},{2,0},{3,1},{4,6},{5,7},{6,4},{7,5},{8,10},{9,11},{10,... | collective-permute-start | bytes 3145736 | tf_op jit(solution)/shard_map/ppermute | solution.py:572
  19.6 24.6 %collective-permute-start = (bf16[256,2048]{1,0:T(8,128)(2,1)S(1)}, bf16[256,2048]{1,0:T(8,128)(2,1)S(1)}, u32[]{:S(2)}, u32[]{:S(2)}) collective-permute-start(bf16[256,2048]{1,0:T(8,128)(2,1)S(1)} %bitcast.39), channel_id=1, source_target_pairs={{0,1},{1,0},{2,3},{3,2},{4,5},{5,4},{6,7},{7,6},{8,9},{9,8},{10,11... | collective-permute-start | bytes 3145736 | tf_op jit(solution)/shard_map/ppermute | solution.py:572
  49.7 492.1 %reduce-scatter.7.cloned.1.call-start = ((), (), s32[]{:S(2)}) async-start(), calls=%async_computation.9 | async-start | bytes 5898240 | tf_op jit(solution)/shard_map/reduce_scatter | solution.py:931
  64.3 26.3 %collective-permute-start.8 = (bf16[256,2048]{1,0:T(8,128)(2,1)}, bf16[256,2048]{1,0:T(8,128)(2,1)S(1)}, u32[]{:S(2)}, u32[]{:S(2)}) collective-permute-start(bf16[256,2048]{1,0:T(8,128)(2,1)} %bitcast.36.refs_2_.refs_0_.refs_5_.refs_4_), channel_id=1, source_target_pairs={{0,2},{1,3},{2,0},{3,1},{4,6},{5,7},{6,4},{7,5},{8,10},{9,11},{10,... | collective-permute-start | bytes 3145736 | tf_op jit(solution)/shard_map/ppermute | solution.py:572
  65.3 26.4 %collective-permute-start.7 = (bf16[256,2048]{1,0:T(8,128)(2,1)}, bf16[256,2048]{1,0:T(8,128)(2,1)}, u32[]{:S(2)}, u32[]{:S(2)}) collective-permute-start(bf16[256,2048]{1,0:T(8,128)(2,1)} %bitcast.36.refs_2_.refs_0_.refs_5_.refs_4_), channel_id=1, source_target_pairs={{0,1},{1,0},{2,3},{3,2},{4,5},{5,4},{6,7},{7,6},{8,9},{9,8},{10,11... | collective-permute-start | bytes 3145736 | tf_op jit(solution)/shard_map/ppermute | solution.py:572
  77.5 54.2 %collective-permute-start.12 = (bf16[256,2048]{1,0:T(8,128)(2,1)S(1)}, bf16[256,2048]{1,0:T(8,128)(2,1)}, u32[]{:S(2)}, u32[]{:S(2)}) collective-permute-start(bf16[256,2048]{1,0:T(8,128)(2,1)S(1)} %get-tuple-element.323.refs_6_.refs_5_.refs_0_), channel_id=1, source_target_pairs={{0,2},{1,3},{2,0},{3,1},{4,6},{5,7},{6,4},{7,5},{8,10},{9,11},{10,... | collective-permute-start | bytes 3145736 | tf_op jit(solution)/shard_map/ppermute | solution.py:572
  78.6 53.2 %collective-permute-start.11 = (bf16[256,2048]{1,0:T(8,128)(2,1)S(1)}, bf16[256,2048]{1,0:T(8,128)(2,1)}, u32[]{:S(2)}, u32[]{:S(2)}) collective-permute-start(bf16[256,2048]{1,0:T(8,128)(2,1)S(1)} %get-tuple-element.323.refs_6_.refs_5_.refs_0_), channel_id=1, source_target_pairs={{0,1},{1,0},{2,3},{3,2},{4,5},{5,4},{6,7},{7,6},{8,9},{9,8},{10,11... | collective-permute-start | bytes 3145736 | tf_op jit(solution)/shard_map/ppermute | solution.py:572
  93.9 42.7 %collective-permute-start.10 = (bf16[128,2048]{1,0:T(8,128)(2,1)S(1)}, bf16[128,2048]{1,0:T(8,128)(2,1)}, u32[]{:S(2)}, u32[]{:S(2)}) collective-permute-start(bf16[128,2048]{1,0:T(8,128)(2,1)S(1)} %slice.110), channel_id=1, source_target_pairs={{0,2},{1,3},{2,0},{3,1},{4,6},{5,7},{6,4},{7,5},{8,10},{9,11},{10,... | collective-permute-start | bytes 1572872 | tf_op jit(solution)/shard_map/ppermute | solution.py:572
  95.0 41.6 %collective-permute-start.9 = (bf16[128,2048]{1,0:T(8,128)(2,1)S(1)}, bf16[128,2048]{1,0:T(8,128)(2,1)}, u32[]{:S(2)}, u32[]{:S(2)}) collective-permute-start(bf16[128,2048]{1,0:T(8,128)(2,1)S(1)} %slice.109), channel_id=1, source_target_pairs={{0,1},{1,0},{2,3},{3,2},{4,5},{5,4},{6,7},{7,6},{8,9},{9,8},{10,11... | collective-permute-start | bytes 1572872 | tf_op jit(solution)/shard_map/ppermute | solution.py:572
  143.0 28.0 %collective-permute-start.13 = (bf16[256,2048]{1,0:T(8,128)(2,1)}, bf16[256,2048]{1,0:T(8,128)(2,1)S(1)}, u32[]{:S(2)}, u32[]{:S(2)}) collective-permute-start(bf16[256,2048]{1,0:T(8,128)(2,1)} %get-tuple-element.161), channel_id=1, source_target_pairs={{0,1},{1,0},{2,3},{3,2},{4,5},{5,4},{6,7},{7,6},{8,9},{9,8},{10,11... | collective-permute-start | bytes 3145736 | tf_op jit(solution)/shard_map/ppermute | solution.py:572
  143.6 27.5 %collective-permute-start.14 = (bf16[256,2048]{1,0:T(8,128)(2,1)}, bf16[256,2048]{1,0:T(8,128)(2,1)}, u32[]{:S(2)}, u32[]{:S(2)}) collective-permute-start(bf16[256,2048]{1,0:T(8,128)(2,1)} %get-tuple-element.162), channel_id=1, source_target_pairs={{0,2},{1,3},{2,0},{3,1},{4,6},{5,7},{6,4},{7,5},{8,10},{9,11},{10,... | collective-permute-start | bytes 3145736 | tf_op jit(solution)/shard_map/ppermute | solution.py:572
  193.5 23.3 %collective-permute-start.20 = (bf16[256,2048]{1,0:T(8,128)(2,1)}, bf16[256,2048]{1,0:T(8,128)(2,1)S(1)}, u32[]{:S(2)}, u32[]{:S(2)}) collective-permute-start(bf16[256,2048]{1,0:T(8,128)(2,1)} %get-tuple-element.172.refs_8_.refs_0_), channel_id=1, source_target_pairs={{0,2},{1,3},{2,0},{3,1},{4,6},{5,7},{6,4},{7,5},{8,10},{9,11},{10,... | collective-permute-start | bytes 3145736 | tf_op jit(solution)/shard_map/ppermute | solution.py:572
  194.5 22.7 %collective-permute-start.19 = (bf16[256,2048]{1,0:T(8,128)(2,1)}, bf16[256,2048]{1,0:T(8,128)(2,1)S(1)}, u32[]{:S(2)}, u32[]{:S(2)}) collective-permute-start(bf16[256,2048]{1,0:T(8,128)(2,1)} %get-tuple-element.172.refs_8_.refs_0_), channel_id=1, source_target_pairs={{0,1},{1,0},{2,3},{3,2},{4,5},{5,4},{6,7},{7,6},{8,9},{9,8},{10,11... | collective-permute-start | bytes 3145736 | tf_op jit(solution)/shard_map/ppermute | solution.py:572
  230.0 48.3 %collective-permute-start.32 = (bf16[256,2048]{1,0:T(8,128)(2,1)S(1)}, bf16[256,2048]{1,0:T(8,128)(2,1)S(1)}, u32[]{:S(2)}, u32[]{:S(2)}) collective-permute-start(bf16[256,2048]{1,0:T(8,128)(2,1)S(1)} %get-tuple-element.197.refs_5_.refs_0_.refs_6_), channel_id=1, source_target_pairs={{0,2},{1,3},{2,0},{3,1},{4,6},{5,7},{6,4},{7,5},{8,10},{9,11},{10,... | collective-permute-start | bytes 3145736 | tf_op jit(solution)/shard_map/ppermute | solution.py:572
  231.1 47.3 %collective-permute-start.31 = (bf16[256,2048]{1,0:T(8,128)(2,1)S(1)}, bf16[256,2048]{1,0:T(8,128)(2,1)S(1)}, u32[]{:S(2)}, u32[]{:S(2)}) collective-permute-start(bf16[256,2048]{1,0:T(8,128)(2,1)S(1)} %get-tuple-element.197.refs_5_.refs_0_.refs_6_), channel_id=1, source_target_pairs={{0,1},{1,0},{2,3},{3,2},{4,5},{5,4},{6,7},{7,6},{8,9},{9,8},{10,11... | collective-permute-start | bytes 3145736 | tf_op jit(solution)/shard_map/ppermute | solution.py:572
  232.5 49.0 %collective-permute-start.23 = (bf16[256,2048]{1,0:T(8,128)(2,1)}, bf16[256,2048]{1,0:T(8,128)(2,1)}, u32[]{:S(2)}, u32[]{:S(2)}) collective-permute-start(bf16[256,2048]{1,0:T(8,128)(2,1)} %get-tuple-element.184), channel_id=1, source_target_pairs={{0,2},{1,3},{2,0},{3,1},{4,6},{5,7},{6,4},{7,5},{8,10},{9,11},{10,... | collective-permute-start | bytes 3145736 | tf_op jit(solution)/shard_map/ppermute | solution.py:572
  233.5 48.0 %collective-permute-start.24 = (bf16[256,2048]{1,0:T(8,128)(2,1)}, bf16[256,2048]{1,0:T(8,128)(2,1)}, u32[]{:S(2)}, u32[]{:S(2)}) collective-permute-start(bf16[256,2048]{1,0:T(8,128)(2,1)} %get-tuple-element.186), channel_id=1, source_target_pairs={{0,1},{1,0},{2,3},{3,2},{4,5},{5,4},{6,7},{7,6},{8,9},{9,8},{10,11... | collective-permute-start | bytes 3145736 | tf_op jit(solution)/shard_map/ppermute | solution.py:572
  278.5 70.4 %collective-permute-start.34 = (bf16[128,2048]{1,0:T(8,128)(2,1)S(1)}, bf16[128,2048]{1,0:T(8,128)(2,1)}, u32[]{:S(2)}, u32[]{:S(2)}) collective-permute-start(bf16[128,2048]{1,0:T(8,128)(2,1)S(1)} %slice.121), channel_id=1, source_target_pairs={{0,2},{1,3},{2,0},{3,1},{4,6},{5,7},{6,4},{7,5},{8,10},{9,11},{10,... | collective-permute-start | bytes 1572872 | tf_op jit(solution)/shard_map/ppermute | solution.py:572
  280.0 68.9 %collective-permute-start.33 = (bf16[128,2048]{1,0:T(8,128)(2,1)S(1)}, bf16[128,2048]{1,0:T(8,128)(2,1)}, u32[]{:S(2)}, u32[]{:S(2)}) collective-permute-start(bf16[128,2048]{1,0:T(8,128)(2,1)S(1)} %slice.120), channel_id=1, source_target_pairs={{0,1},{1,0},{2,3},{3,2},{4,5},{5,4},{6,7},{7,6},{8,9},{9,8},{10,11... | collective-permute-start | bytes 1572872 | tf_op jit(solution)/shard_map/ppermute | solution.py:572
  284.5 20.6 %collective-permute-start.25 = (bf16[128,2048]{1,0:T(8,128)(2,1)}, bf16[128,2048]{1,0:T(8,128)(2,1)S(1)}, u32[]{:S(2)}, u32[]{:S(2)}) collective-permute-start(bf16[128,2048]{1,0:T(8,128)(2,1)} %get-tuple-element.188.refs_2_), channel_id=1, source_target_pairs={{0,1},{1,0},{2,3},{3,2},{4,5},{5,4},{6,7},{7,6},{8,9},{9,8},{10,11... | collective-permute-start | bytes 1572872 | tf_op jit(solution)/shard_map/ppermute | solution.py:572
  310.1 25.7 %collective-permute-start.28 = (bf16[256,2048]{1,0:T(8,128)(2,1)}, bf16[256,2048]{1,0:T(8,128)(2,1)S(1)}, u32[]{:S(2)}, u32[]{:S(2)}) collective-permute-start(bf16[256,2048]{1,0:T(8,128)(2,1)} %get-tuple-element.196.refs_6_.refs_0_), channel_id=1, source_target_pairs={{0,2},{1,3},{2,0},{3,1},{4,6},{5,7},{6,4},{7,5},{8,10},{9,11},{10,... | collective-permute-start | bytes 3145736 | tf_op jit(solution)/shard_map/ppermute | solution.py:572
  310.6 25.8 %collective-permute-start.27 = (bf16[256,2048]{1,0:T(8,128)(2,1)}, bf16[256,2048]{1,0:T(8,128)(2,1)}, u32[]{:S(2)}, u32[]{:S(2)}) collective-permute-start(bf16[256,2048]{1,0:T(8,128)(2,1)} %get-tuple-element.196.refs_6_.refs_0_), channel_id=1, source_target_pairs={{0,1},{1,0},{2,3},{3,2},{4,5},{5,4},{6,7},{7,6},{8,9},{9,8},{10,11... | collective-permute-start | bytes 3145736 | tf_op jit(solution)/shard_map/ppermute | solution.py:572
  350.2 28.2 %collective-permute-start.35 = (bf16[256,2048]{1,0:T(8,128)(2,1)}, bf16[256,2048]{1,0:T(8,128)(2,1)S(1)}, u32[]{:S(2)}, u32[]{:S(2)}) collective-permute-start(bf16[256,2048]{1,0:T(8,128)(2,1)} %get-tuple-element.201), channel_id=1, source_target_pairs={{0,1},{1,0},{2,3},{3,2},{4,5},{5,4},{6,7},{7,6},{8,9},{9,8},{10,11... | collective-permute-start | bytes 3145736 | tf_op jit(solution)/shard_map/ppermute | solution.py:572
  351.5 26.9 %collective-permute-start.36 = (bf16[256,2048]{1,0:T(8,128)(2,1)}, bf16[256,2048]{1,0:T(8,128)(2,1)S(1)}, u32[]{:S(2)}, u32[]{:S(2)}) collective-permute-start(bf16[256,2048]{1,0:T(8,128)(2,1)} %get-tuple-element.202), channel_id=1, source_target_pairs={{0,2},{1,3},{2,0},{3,1},{4,6},{5,7},{6,4},{7,5},{8,10},{9,11},{10,... | collective-permute-start | bytes 3145736 | tf_op jit(solution)/shard_map/ppermute | solution.py:572
  402.6 160.4 %reduce-scatter.9.cloned.1.call-start = ((), (), s32[]{:S(2)}) async-start(), calls=%async_computation.10 | async-start | bytes 7077888 | tf_op jit(solution)/shard_map/reduce_scatter | solution.py:931
  403.8 26.1 %collective-permute-start.40 = (bf16[256,2048]{1,0:T(8,128)(2,1)S(1)}, bf16[256,2048]{1,0:T(8,128)(2,1)S(1)}, u32[]{:S(2)}, u32[]{:S(2)}) collective-permute-start(bf16[256,2048]{1,0:T(8,128)(2,1)S(1)} %copy-done.7), channel_id=1, source_target_pairs={{0,2},{1,3},{2,0},{3,1},{4,6},{5,7},{6,4},{7,5},{8,10},{9,11},{10,... | collective-permute-start | bytes 3145736 | tf_op jit(solution)/shard_map/ppermute | solution.py:572
  405.1 27.1 %collective-permute-start.39 = (bf16[256,2048]{1,0:T(8,128)(2,1)S(1)}, bf16[256,2048]{1,0:T(8,128)(2,1)S(1)}, u32[]{:S(2)}, u32[]{:S(2)}) collective-permute-start(bf16[256,2048]{1,0:T(8,128)(2,1)S(1)} %copy-done.7), channel_id=1, source_target_pairs={{0,1},{1,0},{2,3},{3,2},{4,5},{5,4},{6,7},{7,6},{8,9},{9,8},{10,11... | collective-permute-start | bytes 3145736 | tf_op jit(solution)/shard_map/ppermute | solution.py:572
  422.5 34.0 %collective-permute-start.43 = (bf16[256,2048]{1,0:T(8,128)(2,1)}, bf16[256,2048]{1,0:T(8,128)(2,1)}, u32[]{:S(2)}, u32[]{:S(2)}) collective-permute-start(bf16[256,2048]{1,0:T(8,128)(2,1)} %get-tuple-element.212), channel_id=1, source_target_pairs={{0,2},{1,3},{2,0},{3,1},{4,6},{5,7},{6,4},{7,5},{8,10},{9,11},{10,... | collective-permute-start | bytes 3145736 | tf_op jit(solution)/shard_map/ppermute | solution.py:572
  423.7 32.8 %collective-permute-start.44 = (bf16[256,2048]{1,0:T(8,128)(2,1)}, bf16[256,2048]{1,0:T(8,128)(2,1)}, u32[]{:S(2)}, u32[]{:S(2)}) collective-permute-start(bf16[256,2048]{1,0:T(8,128)(2,1)} %get-tuple-element.214), channel_id=1, source_target_pairs={{0,1},{1,0},{2,3},{3,2},{4,5},{5,4},{6,7},{7,6},{8,9},{9,8},{10,11... | collective-permute-start | bytes 3145736 | tf_op jit(solution)/shard_map/ppermute | solution.py:572
  430.8 29.1 %collective-permute-start.41 = (bf16[128,2048]{1,0:T(8,128)(2,1)}, bf16[128,2048]{1,0:T(8,128)(2,1)S(1)}, u32[]{:S(2)}, u32[]{:S(2)}) collective-permute-start(bf16[128,2048]{1,0:T(8,128)(2,1)} %slice.141.refs_8_), channel_id=1, source_target_pairs={{0,1},{1,0},{2,3},{3,2},{4,5},{5,4},{6,7},{7,6},{8,9},{9,8},{10,11... | collective-permute-start | bytes 1572872 | tf_op jit(solution)/shard_map/ppermute | solution.py:572
  432.2 27.7 %collective-permute-start.42 = (bf16[128,2048]{1,0:T(8,128)(2,1)S(1)}, bf16[128,2048]{1,0:T(8,128)(2,1)S(1)}, u32[]{:S(2)}, u32[]{:S(2)}) collective-permute-start(bf16[128,2048]{1,0:T(8,128)(2,1)S(1)} %slice.142.refs_9_), channel_id=1, source_target_pairs={{0,2},{1,3},{2,0},{3,1},{4,6},{5,7},{6,4},{7,5},{8,10},{9,11},{10,... | collective-permute-start | bytes 1572872 | tf_op jit(solution)/shard_map/ppermute | solution.py:572
  463.3 197.3 %reduce-scatter.11.cloned.1.call-start = ((), (), s32[]{:S(2)}) async-start(), calls=%async_computation.11 | async-start | bytes 4718592 | tf_op jit(solution)/shard_map/reduce_scatter | solution.py:931
  491.1 197.6 %reduce-scatter.13.cloned.1.call-start = ((), (), s32[]{:S(2)}) async-start(), calls=%async_computation.12 | async-start | bytes 2359296 | tf_op jit(solution)/shard_map/reduce_scatter | solution.py:931
  491.1 25.1 %collective-permute-start.48 = (bf16[256,2048]{1,0:T(8,128)(2,1)}, bf16[256,2048]{1,0:T(8,128)(2,1)S(1)}, u32[]{:S(2)}, u32[]{:S(2)}) collective-permute-start(bf16[256,2048]{1,0:T(8,128)(2,1)} %get-tuple-element.220.refs_10_.refs_0_.refs_5_), channel_id=1, source_target_pairs={{0,1},{1,0},{2,3},{3,2},{4,5},{5,4},{6,7},{7,6},{8,9},{9,8},{10,11... | collective-permute-start | bytes 3145736 | tf_op jit(solution)/shard_map/ppermute | solution.py:572
  492.0 25.1 %collective-permute-start.47 = (bf16[256,2048]{1,0:T(8,128)(2,1)}, bf16[256,2048]{1,0:T(8,128)(2,1)S(1)}, u32[]{:S(2)}, u32[]{:S(2)}) collective-permute-start(bf16[256,2048]{1,0:T(8,128)(2,1)} %get-tuple-element.220.refs_10_.refs_0_.refs_5_), channel_id=1, source_target_pairs={{0,2},{1,3},{2,0},{3,1},{4,6},{5,7},{6,4},{7,5},{8,10},{9,11},{10,... | collective-permute-start | bytes 3145736 | tf_op jit(solution)/shard_map/ppermute | solution.py:572
  516.2 39.6 %collective-permute-start.50 = (bf16[128,2048]{1,0:T(8,128)(2,1)S(1)}, bf16[128,2048]{1,0:T(8,128)(2,1)}, u32[]{:S(2)}, u32[]{:S(2)}) collective-permute-start(bf16[128,2048]{1,0:T(8,128)(2,1)S(1)} %slice.144.refs_12_), channel_id=1, source_target_pairs={{0,2},{1,3},{2,0},{3,1},{4,6},{5,7},{6,4},{7,5},{8,10},{9,11},{10,... | collective-permute-start | bytes 1572872 | tf_op jit(solution)/shard_map/ppermute | solution.py:572
  517.2 38.7 %collective-permute-start.49 = (bf16[128,2048]{1,0:T(8,128)(2,1)S(1)}, bf16[128,2048]{1,0:T(8,128)(2,1)}, u32[]{:S(2)}, u32[]{:S(2)}) collective-permute-start(bf16[128,2048]{1,0:T(8,128)(2,1)S(1)} %slice.143.refs_11_), channel_id=1, source_target_pairs={{0,1},{1,0},{2,3},{3,2},{4,5},{5,4},{6,7},{7,6},{8,9},{9,8},{10,11... | collective-permute-start | bytes 1572872 | tf_op jit(solution)/shard_map/ppermute | solution.py:572
  518.4 79.3 %collective-permute-start.51 = (bf16[512,2048]{1,0:T(8,128)(2,1)}, bf16[512,2048]{1,0:T(8,128)(2,1)}, u32[]{:S(2)}, u32[]{:S(2)}) collective-permute-start(bf16[512,2048]{1,0:T(8,128)(2,1)} %get-tuple-element.231), channel_id=1, source_target_pairs={{0,1},{1,0},{2,3},{3,2},{4,5},{5,4},{6,7},{7,6},{8,9},{9,8},{10,11... | collective-permute-start | bytes 6291464 | tf_op jit(solution)/shard_map/ppermute | solution.py:572
  554.8 38.4 %collective-permute-start.53 = (bf16[256,2048]{1,0:T(8,128)(2,1)}, bf16[256,2048]{1,0:T(8,128)(2,1)S(1)}, u32[]{:S(2)}, u32[]{:S(2)}) collective-permute-start(bf16[256,2048]{1,0:T(8,128)(2,1)} %get-tuple-element.235), channel_id=1, source_target_pairs={{0,1},{1,0},{2,3},{3,2},{4,5},{5,4},{6,7},{7,6},{8,9},{9,8},{10,11... | collective-permute-start | bytes 3145736 | tf_op jit(solution)/shard_map/ppermute | solution.py:572
  596.5 46.7 %collective-permute-start.54 = (bf16[128,2048]{1,0:T(8,128)(2,1)}, bf16[128,2048]{1,0:T(8,128)(2,1)S(1)}, u32[]{:S(2)}, u32[]{:S(2)}) collective-permute-start(bf16[128,2048]{1,0:T(8,128)(2,1)} %get-tuple-element.237.refs_2_), channel_id=1, source_target_pairs={{0,1},{1,0},{2,3},{3,2},{4,5},{5,4},{6,7},{7,6},{8,9},{9,8},{10,11... | collective-permute-start | bytes 1572872 | tf_op jit(solution)/shard_map/ppermute | solution.py:572
  600.1 24.9 %collective-permute-start.56 = (bf16[256,2048]{1,0:T(8,128)(2,1)}, bf16[256,2048]{1,0:T(8,128)(2,1)S(1)}, u32[]{:S(2)}, u32[]{:S(2)}) collective-permute-start(bf16[256,2048]{1,0:T(8,128)(2,1)} %add_arrived.13.refs_10_), channel_id=1, source_target_pairs={{0,2},{1,3},{2,0},{3,1},{4,6},{5,7},{6,4},{7,5},{8,10},{9,11},{10,... | collective-permute-start | bytes 3145736 | tf_op jit(solution)/shard_map/ppermute | solution.py:572
  601.3 142.5 %reduce-scatter.15.cloned.1.call-start = ((), (), s32[]{:S(2)}) async-start(), calls=%async_computation.13 | async-start | bytes 3538944 | tf_op jit(solution)/shard_map/reduce_scatter | solution.py:931
  648.9 97.5 %reduce-scatter.17.cloned.1.call-start = ((), (), s32[]{:S(2)}) async-start(), calls=%async_computation.14 | async-start | bytes 3538944 | tf_op jit(solution)/shard_map/reduce_scatter | solution.py:931
  658.5 24.6 %collective-permute-start.57 = (bf16[256,2048]{1,0:T(8,128)(2,1)}, bf16[256,2048]{1,0:T(8,128)(2,1)S(1)}, u32[]{:S(2)}, u32[]{:S(2)}) collective-permute-start(bf16[256,2048]{1,0:T(8,128)(2,1)} %get-tuple-element.247), channel_id=1, source_target_pairs={{0,1},{1,0},{2,3},{3,2},{4,5},{5,4},{6,7},{7,6},{8,9},{9,8},{10,11... | collective-permute-start | bytes 3145736 | tf_op jit(solution)/shard_map/ppermute | solution.py:572
  659.3 23.8 %collective-permute-start.58 = (bf16[256,2048]{1,0:T(8,128)(2,1)}, bf16[256,2048]{1,0:T(8,128)(2,1)S(1)}, u32[]{:S(2)}, u32[]{:S(2)}) collective-permute-start(bf16[256,2048]{1,0:T(8,128)(2,1)} %get-tuple-element.248), channel_id=1, source_target_pairs={{0,2},{1,3},{2,0},{3,1},{4,6},{5,7},{6,4},{7,5},{8,10},{9,11},{10,... | collective-permute-start | bytes 3145736 | tf_op jit(solution)/shard_map/ppermute | solution.py:572
  (107 other events, 913.4 us)
Sparse Core Ops, SparseCore 0:
  11.5 41.0 all-gather.3
  54.2 54.9 all-gather.5
  111.4 141.2 all-gather.7
  402.7 57.7 reduce-scatter.6
  463.4 67.3 reduce-scatter.8
  533.0 48.3 reduce-scatter.10
  601.4 32.7 reduce-scatter.12
  649.0 37.6 reduce-scatter.14
  707.8 38.5 reduce-scatter.16

commit v5 on v4

--- a/solution.py
+++ b/solution.py
@@ -978,7 +978,7 @@
     weight = outer(
         [twos[1].pieces], [grad_ff_1], (parts[0], *mids[0].sent), 0, ff_half, base=(ff_part_a,)
     )
-    down = ff_rows(hidden_0, False, way[0], (weight,))
+    down = ff_rows(hidden_0, False, form, (weight,))
     late = sum_1.first((down[0], *mids[0].pieces), (weight,))
     grad_ff_a = scatter(late[-1])
 
@@ -998,7 +998,7 @@
     grad_ff_b = scatter(weight)
     mids.append(Gather(rounded, "both", count))
     grad_0a, fold = backward(0, qkv_0a, lse_0, mixed_0, grad, scale_0, 0, (), (rounded,))
-    down_0 = Reduce(down, way[0], count, mids[1].first)
+    down_0 = Reduce(down, form, count, mids[1].first)
     grad_0b, fold_0 = backward(0, qkv_0b, lse_0, mixed_0, grad, scale_0, 1, (fold,), mids[1].sent)
     *parts, gain_one_0 = qkv_rows([grad_0a, grad_0b], 0, (grad_down,))
     sum_0 = Reduce(parts, form, count)

time: 783 us -> 765 us (0.977)
  waiting for transfers between devices: 107 us -> 88 us
    ppermute x70 -> x72, waiting for transfers between devices: 84.4 us -> 67.7 us  [hop(): return lax.ppermute(part, axis, [(i, i ^ bit) for i in range(count)])]
    ppermute x70 -> x72, starting transfers between devices: 74.9 us -> 77 us  [hop(): return lax.ppermute(part, axis, [(i, i ^ bit) for i in range(count)])]
    unnamed x164 -> x166, local copies, waits for them, and re-layouts: 30.1 us -> 29.9 us
  transfers between devices with their start and end apart: 79 -> 81, of which waited for: 30 -> 29; matrix products, arithmetic and copies ran while one was open for 4% -> 5% of each run, Pallas kernels for 66% -> 67%
where the time goes in v5:
time: 765 us; the launch traced here: 759 us
  Pallas kernels  521 us (68%)
  waiting for transfers between devices  88 us (12%)
  starting transfers between devices  77.4 us (10%)
  local copies, waits for them, and re-layouts  49.2 us (6%)
  between operations  15.5 us (2%)
    pallas_call x9, Pallas kernels, outer(): pl.pallas_call(functools.partial(outer_kernel, counts, len(base), len(dep...  108 us
    pallas_call x4, Pallas kernels, attend_backward(): pl.pallas_call(functools.partial(attend_backward_kernel, n, extra), grid_...  90.5 us
    pallas_call x8, Pallas kernels, partial_rows(): pl.pallas_call(functools.partial(partial_kernel, form, layouts, len(piece...  87.5 us
    ppermute x72, starting transfers between devices, hop(): return lax.ppermute(part, axis, [(i, i ^ bit) for i in range(count)])  77 us
    ppermute x72, waiting for transfers between devices, hop(): return lax.ppermute(part, axis, [(i, i ^ bit) for i in range(count)])  67.7 us
    pallas_call x4, Pallas kernels, attend_forward(): pl.pallas_call(functools.partial(attend_forward_kernel, n, extra), grid_s...  51.9 us
    pallas_call x2, Pallas kernels, feed_forward(): pl.pallas_call(functools.partial(ff_kernel, len(pieces), len(cots), extra...  51.3 us
    pallas_call x6, Pallas kernels, product(): pl.pallas_call(functools.partial(product_kernel, mode, len(pieces), len(d...  50.3 us
  transfers between devices with their start and end apart: 81, of which 29 were waited for; matrix products, arithmetic and copies ran while one was open for 5% of the time, Pallas kernels for 67%

profile of v5, /device:TPU:0, one launch (start us, length us, event | category | flops | bytes accessed | tf_op | source)
XLA Modules:
  0.0 758.9 jit_solution(3919649542826891259)
XLA Ops:
  12.1 3.8 fusion.10
  33.4 10.6 %bias_strips.1.refs_4_.refs_5_ = f32[8,1792,256]{2,1,0:T(8,128)} custom-call(f32[8,7,512]{2,1,0:T(8,128)} %pad_maximum_fusion.2.w_ref), custom_call_target="tpu_custom_call" | custom-call | flops 12000000000 | bytes 1 | tf_op jit(solution)/shard_map/bias_strips/pallas_call | solution.py:48
  58.0 5.5 collective-permute-done.6.refs_4_.refs_8_
  66.8 9.8 %rows_product.6 = (bf16[1024,768]{1,0:T(8,128)(2,1)}, f32[1024,128]{1,0:T(8,128)}) custom-call(bf16[256,2048]{1,0:T(8,128)(2,1)} %bitcast.40, bf16[256,2048]{1,0:T(8,128)(2,1)} %copy-done.25, bf16[256,2048]{1,0:T(8,128)(2,1)} %copy-done.24, bf16[128,2048]{1,0:T(8,128)(2,1)} %collective-permute-done.5.refs_3_.refs_7_, ...), custom_call_target="tpu_custom_call" | custom-call | flops 10442450944 | bytes 1 | tf_op jit(solution)/shard_map/rows_product/pallas_call | solution.py:358
  79.2 11.4 %collective-permute-done.8.refs_9_.refs_4_.refs_2_.refs_7_.refs_6_ = bf16[256,2048]{1,0:T(8,128)(2,1)S(1)} collective-permute-done((bf16[256,2048]{1,0:T(8,128)(2,1)}, bf16[256,2048]{1,0:T(8,128)(2,1)S(1)}, u32[]{:S(2)}, u32[]{:S(2)}) %collective-permute-start.8) | collective-permute-done | bytes 1048608 | tf_op jit(solution)/shard_map/ppermute | solution.py:572
  96.4 12.8 %attend_forward.4 = (bf16[1024,512]{1,0:T(8,128)(2,1)}, f32[4,2,1024]{2,1,0:T(2,128)}) custom-call(s32[16]{0:T(128)} %reshape.190.refs_0_, s32[4]{0:T(128)} %iota_xor_fusion.refs_1_, bf16[1024,768]{1,0:T(8,128)(2,1)} %get-tuple-element.155.refs_2_, bf16[1024,128]{1,0:T(8,128)(2,1)} %get-tuple-element.347.refs_3_, ...), custom_call_target="tpu_custom_call" | custom-call | flops 14800000000 | bytes 1 | tf_op jit(solution)/shard_map/attend_forward/pallas_call | solution.py:136
  109.3 8.4 %rows_product.7.refs_2_ = bf16[1024,768]{1,0:T(8,128)(2,1)} custom-call(bf16[256,2048]{1,0:T(8,128)(2,1)} %bitcast.41, bf16[256,2048]{1,0:T(8,128)(2,1)} %copy-done.25, bf16[256,2048]{1,0:T(8,128)(2,1)} %copy-done.24, bf16[128,2048]{1,0:T(8,128)(2,1)} %collective-permute-done.5.refs_3_.refs_7_, bf16[128,2048]{1,0:T(8,128)(2,1)} %collective-permute-done.6.refs_4_.refs_8_, ...), custom_call_target="tpu_custom_call" | custom-call | flops 10442450944 | bytes 1 | tf_op jit(solution)/shard_map/rows_product/pallas_call | solution.py:358
  117.7 13.3 %attend_forward.5 = (bf16[1024,512]{1,0:T(8,128)(2,1)}, f32[4,2,1024]{2,1,0:T(2,128)}) custom-call(s32[16]{0:T(128)} %reshape.190.refs_0_, s32[4]{0:T(128)} %iota_xor_fusion.refs_1_, bf16[1024,768]{1,0:T(8,128)(2,1)} %rows_product.7.refs_2_, bf16[1024,128]{1,0:T(8,128)(2,1)} %get-tuple-element.347.refs_3_, ...), custom_call_target="tpu_custom_call", output_to_operand_aliasing={{0}: (6, {}), {1}: (7, {})} | custom-call | flops 14800000000 | bytes 1 | tf_op jit(solution)/shard_map/attend_forward/pallas_call | solution.py:136
  136.2 6.5 partial_rows.8
  143.8 9.6 %rows_product.8 = (bf16[1024,768]{1,0:T(8,128)(2,1)}, f32[1024,128]{1,0:T(8,128)}) custom-call(bf16[256,2048]{1,0:T(8,128)(2,1)} %bitcast.36.refs_2_.refs_0_.refs_5_.refs_4_, bf16[256,2048]{1,0:T(8,128)(2,1)} %collective-permute-done.7.refs_8_.refs_3_.refs_1_.refs_6_.refs_5_, bf16[256,2048]{1,0:T(8,128)(2,1)} %copy-done.26, ...), custom_call_target="tpu_custom_call" | custom-call | flops 10442450944 | bytes 1 | tf_op jit(solution)/shard_map/rows_product/pallas_call | solution.py:358
  153.4 12.9 %attend_forward.6 = (bf16[1024,512]{1,0:T(8,128)(2,1)}, f32[4,2,1024]{2,1,0:T(2,128)}) custom-call(s32[16]{0:T(128)} %reshape.191.refs_0_, s32[4]{0:T(128)} %iota_xor_fusion.refs_1_, bf16[1024,768]{1,0:T(8,128)(2,1)} %get-tuple-element.171.refs_2_, bf16[1024,128]{1,0:T(8,128)(2,1)} %get-tuple-element.346.refs_3_, ...), custom_call_target="tpu_custom_call" | custom-call | flops 14800000000 | bytes 1 | tf_op jit(solution)/shard_map/attend_forward/pallas_call | solution.py:136
  166.3 4.8 collective-permute-done.13.refs_3_.refs_1_
  176.6 8.5 %rows_product.9.refs_6_.refs_2_ = bf16[1024,768]{1,0:T(8,128)(2,1)} custom-call(bf16[256,2048]{1,0:T(8,128)(2,1)} %bitcast.36.refs_2_.refs_0_.refs_5_.refs_4_, bf16[256,2048]{1,0:T(8,128)(2,1)} %collective-permute-done.7.refs_8_.refs_3_.refs_1_.refs_6_.refs_5_, bf16[256,2048]{1,0:T(8,128)(2,1)} %copy-done.26, ...), custom_call_target="tpu_custom_call" | custom-call | flops 10442450944 | bytes 1 | tf_op jit(solution)/shard_map/rows_product/pallas_call | solution.py:358
  189.5 4.6 settle_rows.8
  196.5 12.9 %attend_forward.7 = (bf16[1024,512]{1,0:T(8,128)(2,1)}, f32[4,2,1024]{2,1,0:T(2,128)}) custom-call(s32[16]{0:T(128)} %reshape.191.refs_0_, s32[4]{0:T(128)} %iota_xor_fusion.refs_1_, bf16[1024,768]{1,0:T(8,128)(2,1)} %rows_product.9.refs_6_.refs_2_, bf16[1024,128]{1,0:T(8,128)(2,1)} %get-tuple-element.346.refs_3_, ...), custom_call_target="tpu_custom_call", output_to_operand_aliasing={{0}: (6, {}), {1}: (7, {})} | custom-call | flops 14800000000 | bytes 1 | tf_op jit(solution)/shard_map/attend_forward/pallas_call | solution.py:136
  209.4 8.5 %collective-permute-done.20.refs_2_ = bf16[256,2048]{1,0:T(8,128)(2,1)S(1)} collective-permute-done((bf16[256,2048]{1,0:T(8,128)(2,1)}, bf16[256,2048]{1,0:T(8,128)(2,1)S(1)}, u32[]{:S(2)}, u32[]{:S(2)}) %collective-permute-start.20) | collective-permute-done | bytes 1048608 | tf_op jit(solution)/shard_map/ppermute | solution.py:572
  221.3 6.4 partial_rows.9
  235.5 17.2 %all-gather.8.cloned.1.call-done.refs_10_.refs_11_.refs_1_ = bf16[2048,3840]{1,0:T(8,128)(2,1)} async-done(((bf16[256,3840]{1,0:T(8,128)(2,1)}), bf16[2048,3840]{1,0:T(8,128)(2,1)}) %all-gather.8.cloned.1.call-update) | async-done | bytes 15728656 | tf_op jit(solution)/shard_map/all_gather | solution.py:858
  252.7 25.7 %feed_forward.2 = (bf16[1024,1280]{1,0:T(8,128)(2,1)}, bf16[1024,2560]{1,0:T(8,128)(2,1)}) custom-call(bf16[256,2048]{1,0:T(8,128)(2,1)} %get-tuple-element.178.refs_8_.refs_0_, bf16[256,2048]{1,0:T(8,128)(2,1)} %copy-done.31, bf16[256,2048]{1,0:T(8,128)(2,1)} %copy-done.30, bf16[128,2048]{1,0:T(8,128)(2,1)} %collective-permute-done.21.refs_3_, ...), custom_call_target="tpu_custom_call" | custom-call | flops 32212254720 | bytes 1 | tf_op jit(solution)/shard_map/feed_forward/pallas_call | solution.py:542
  285.1 15.9 %partial_rows.10 = (bf16[256,2048]{1,0:T(8,128)(2,1)}, bf16[256,2048]{1,0:T(8,128)(2,1)}, bf16[256,2048]{1,0:T(8,128)(2,1)}, bf16[128,2048]{1,0:T(8,128)(2,1)}, bf16[128,2048]{1,0:T(8,128)(2,1)}) custom-call(bf16[1024,2560]{1,0:T(8,128)(2,1)} %get-tuple-element.184.refs_0_.refs_5_, bf16[2048,3840]{1,0:T(8,128)(2,1)} %all-gather.8.cloned.1.call-done.refs_10_.refs_11_.refs_1_, ...), custom_call_target="tpu_custom_call" | custom-call | flops 21474836480 | bytes 1 | tf_op jit(solution)/shard_map/partial_rows/pallas_call | solution.py:483
  305.9 4.2 settle_rows.9
  312.1 11.1 %weight_gradient.9.refs_6_ = bf16[2048,1280]{1,0:T(8,128)(2,1)} custom-call(bf16[256,2048]{1,0:T(8,128)(2,1)} %copy-done.10, bf16[256,2048]{1,0:T(8,128)(2,1)} %collective-permute-done.11.refs_7_.refs_6_.refs_1_, bf16[256,2048]{1,0:T(8,128)(2,1)} %collective-permute-done.12.refs_8_.refs_7_.refs_2_, ...), custom_call_target="tpu_custom_call" | custom-call | flops 10737418240 | bytes 1 | tf_op jit(solution)/shard_map/weight_gradient/pallas_call | solution.py:409
  323.2 12.4 %weight_gradient.10.refs_6_ = bf16[2048,1536]{1,0:T(8,128)(2,1)} custom-call(bf16[256,2048]{1,0:T(8,128)(2,1)} %get-tuple-element.178.refs_8_.refs_0_, bf16[256,2048]{1,0:T(8,128)(2,1)} %copy-done.31, bf16[256,2048]{1,0:T(8,128)(2,1)} %copy-done.30, bf16[128,2048]{1,0:T(8,128)(2,1)} %collective-permute-done.21.refs_3_, bf16[128,2048]{1,0:T(8,128)(2,1)} %copy-done.56, ...), custom_call_target="tpu_custom_call" | custom-call | flops 12884901888 | bytes 1 | tf_op jit(solution)/shard_map/weight_gradient/pallas_call | solution.py:409
  339.0 9.8 %weight_gradient.11.refs_12_.refs_6_ = bf16[2048,1024]{1,0:T(8,128)(2,1)} custom-call(bf16[256,2048]{1,0:T(8,128)(2,1)} %get-tuple-element.178.refs_8_.refs_0_, bf16[256,2048]{1,0:T(8,128)(2,1)} %copy-done.31, bf16[256,2048]{1,0:T(8,128)(2,1)} %copy-done.30, bf16[128,2048]{1,0:T(8,128)(2,1)} %collective-permute-done.21.refs_3_, ...), custom_call_target="tpu_custom_call" | custom-call | flops 8589934592 | bytes 1 | tf_op jit(solution)/shard_map/weight_gradient/pallas_call | solution.py:409
  352.7 25.6 %feed_forward.3 = (bf16[1024,1280]{1,0:T(8,128)(2,1)}, bf16[1024,2560]{1,0:T(8,128)(2,1)}) custom-call(bf16[256,2048]{1,0:T(8,128)(2,1)} %get-tuple-element.202.refs_6_.refs_0_, bf16[256,2048]{1,0:T(8,128)(2,1)} %collective-permute-done.27.refs_1_, bf16[256,2048]{1,0:T(8,128)(2,1)} %copy-done.27, bf16[128,2048]{1,0:T(8,128)(2,1)} %copy-done.55, ...), custom_call_target="tpu_custom_call" | custom-call | flops 32212254720 | bytes 1 | tf_op jit(solution)/shard_map/feed_forward/pallas_call | solution.py:542
  383.4 12.4 %weight_gradient.12.refs_7_ = bf16[2048,1280]{1,0:T(8,128)(2,1)} custom-call(bf16[256,2048]{1,0:T(8,128)(2,1)} %copy-done.9, bf16[256,2048]{1,0:T(8,128)(2,1)} %copy-done.29, bf16[256,2048]{1,0:T(8,128)(2,1)} %copy-done.28, bf16[128,2048]{1,0:T(8,128)(2,1)} %collective-permute-done.33.refs_8_.refs_3_, ...), custom_call_target="tpu_custom_call" | custom-call | flops 10737418240 | bytes 1 | tf_op jit(solution)/shard_map/weight_gradient/pallas_call | solution.py:409
  396.8 5.7 settle_rows.10
  406.3 16.1 %partial_rows.11 = (bf16[256,2048]{1,0:T(8,128)(2,1)}, bf16[256,2048]{1,0:T(8,128)(2,1)}, bf16[256,2048]{1,0:T(8,128)(2,1)}, bf16[128,2048]{1,0:T(8,128)(2,1)}, bf16[128,2048]{1,0:T(8,128)(2,1)}) custom-call(bf16[1024,2560]{1,0:T(8,128)(2,1)} %get-tuple-element.216.refs_0_.refs_5_, bf16[2048,3840]{1,0:T(8,128)(2,1)} %all-gather.8.cloned.1.call-done.refs_10_.refs_11_.refs_1_, ...), custom_call_target="tpu_custom_call" | custom-call | flops 21474836480 | bytes 1 | tf_op jit(solution)/shard_map/partial_rows/pallas_call | solution.py:483
  424.3 5.5 collective-permute-done.40.refs_7_.refs_2_
  433.4 13.5 %weight_gradient.13.refs_2_.refs_10_ = bf16[2048,1536]{1,0:T(8,128)(2,1)} custom-call(bf16[256,2048]{1,0:T(8,128)(2,1)} %get-tuple-element.202.refs_6_.refs_0_, bf16[256,2048]{1,0:T(8,128)(2,1)} %collective-permute-done.27.refs_1_, bf16[256,2048]{1,0:T(8,128)(2,1)} %copy-done.27, bf16[128,2048]{1,0:T(8,128)(2,1)} %copy-done.55, ...), custom_call_target="tpu_custom_call" | custom-call | flops 12884901888 | bytes 1 | tf_op jit(solution)/shard_map/weight_gradient/pallas_call | solution.py:409
  446.9 9.4 %partial_rows.12 = (bf16[256,2048]{1,0:T(8,128)(2,1)}, bf16[256,2048]{1,0:T(8,128)(2,1)}, bf16[256,2048]{1,0:T(8,128)(2,1)}, bf16[128,2048]{1,0:T(8,128)(2,1)}, bf16[128,2048]{1,0:T(8,128)(2,1)}) custom-call(bf16[1024,1280]{1,0:T(8,128)(2,1)} %get-tuple-element.193.refs_4_.refs_5_.refs_0_, ...), custom_call_target="tpu_custom_call" | custom-call | flops 10737418240 | bytes 1 | tf_op jit(solution)/shard_map/partial_rows/pallas_call | solution.py:483
  466.4 7.0 rows_product.10.refs_7_.refs_8_
  473.4 10.8 %weight_gradient.14.refs_7_ = bf16[2048,1024]{1,0:T(8,128)(2,1)} custom-call(bf16[256,2048]{1,0:T(8,128)(2,1)} %get-tuple-element.202.refs_6_.refs_0_, bf16[256,2048]{1,0:T(8,128)(2,1)} %collective-permute-done.27.refs_1_, bf16[256,2048]{1,0:T(8,128)(2,1)} %copy-done.27, bf16[128,2048]{1,0:T(8,128)(2,1)} %copy-done.55, ...), custom_call_target="tpu_custom_call" | custom-call | flops 8589934592 | bytes 1 | tf_op jit(solution)/shard_map/weight_gradient/pallas_call | solution.py:409
  485.1 5.7 settle_rows.11
  493.1 22.9 %attend_backward.4 = (bf16[1024,768]{1,0:T(8,128)(2,1)}, f32[4,2,8,256]{3,2,1,0:T(8,128)}) custom-call(s32[16]{0:T(128)} %reshape.190.refs_0_, s32[4]{0:T(128)} %iota_xor_fusion.refs_1_, bf16[1024,768]{1,0:T(8,128)(2,1)} %get-tuple-element.155.refs_2_, bf16[1024,128]{1,0:T(8,128)(2,1)} %get-tuple-element.347.refs_3_, ...), custom_call_target="tpu_custom_call" | custom-call | flops 25999998976 | bytes 1 | tf_op jit(solution)/shard_map/attend_backward/pallas_call | solution.py:252
  520.3 22.4 %attend_backward.5 = (bf16[1024,768]{1,0:T(8,128)(2,1)}, f32[4,2,8,256]{3,2,1,0:T(8,128)}) custom-call(s32[16]{0:T(128)} %reshape.190.refs_0_, s32[4]{0:T(128)} %iota_xor_fusion.refs_1_, bf16[1024,768]{1,0:T(8,128)(2,1)} %rows_product.7.refs_2_, bf16[1024,128]{1,0:T(8,128)(2,1)} %get-tuple-element.347.refs_3_, ...), custom_call_target="tpu_custom_call", output_to_operand_aliasing={{1}: (10, {})} | custom-call | flops 25999998976 | bytes 1 | tf_op jit(solution)/shard_map/attend_backward/pallas_call | solution.py:252
  542.8 11.7 %partial_rows.13 = (bf16[256,2048]{1,0:T(8,128)(2,1)}, bf16[256,2048]{1,0:T(8,128)(2,1)}, bf16[256,2048]{1,0:T(8,128)(2,1)}, bf16[128,2048]{1,0:T(8,128)(2,1)}, ...) custom-call(bf16[1024,768]{1,0:T(8,128)(2,1)} %get-tuple-element.227.refs_0_.refs_10_, ...), custom_call_target="tpu_custom_call" | custom-call | flops 12884901888 | bytes 1 | tf_op jit(solution)/shard_map/partial_rows/pallas_call | solution.py:483
  556.4 7.1 rows_product.11.refs_12_.refs_8_
  563.5 11.0 %weight_gradient.15.refs_4_ = bf16[2048,512]{1,0:T(8,128)(2,1)} custom-call(bf16[256,2048]{1,0:T(8,128)(2,1)} %get-tuple-element.215.refs_2_.refs_5_.refs_0_, bf16[256,2048]{1,0:T(8,128)(2,1)} %copy-done.3, bf16[256,2048]{1,0:T(8,128)(2,1)} %copy-done.2, bf16[128,2048]{1,0:T(8,128)(2,1)} %copy-done.15, bf16[128,2048]{1,0:T(8,128)(2,1)} %copy-done.16, ...), custom_call_target="tpu_custom_call" | custom-call | flops 8589934592 | bytes 1 | tf_op jit(solution)/shard_map/weight_gradient/pallas_call | solution.py:409
  583.9 22.7 %attend_backward.6 = (bf16[1024,768]{1,0:T(8,128)(2,1)}, f32[4,2,8,256]{3,2,1,0:T(8,128)}) custom-call(s32[16]{0:T(128)} %reshape.191.refs_0_, s32[4]{0:T(128)} %iota_xor_fusion.refs_1_, bf16[1024,768]{1,0:T(8,128)(2,1)} %get-tuple-element.171.refs_2_, bf16[1024,128]{1,0:T(8,128)(2,1)} %get-tuple-element.346.refs_3_, ...), custom_call_target="tpu_custom_call" | custom-call | flops 25999998976 | bytes 1 | tf_op jit(solution)/shard_map/attend_backward/pallas_call | solution.py:252
  608.5 3.7 settle_rows.12.refs_12_
  612.2 13.6 %weight_gradient.16.refs_7_ = bf16[2048,768]{1,0:T(8,128)(2,1)} custom-call(bf16[256,2048]{1,0:T(8,128)(2,1)} %bitcast.44, bf16[256,2048]{1,0:T(8,128)(2,1)} %copy-done.25, bf16[256,2048]{1,0:T(8,128)(2,1)} %copy-done.24, bf16[128,2048]{1,0:T(8,128)(2,1)} %collective-permute-done.5.refs_3_.refs_7_, bf16[128,2048]{1,0:T(8,128)(2,1)} %collective-permute-done.6.refs_4_.refs_8_, ...), custom_call_target="tpu_custom_call" | custom-call | flops 12884901888 | bytes 1 | tf_op jit(solution)/shard_map/weight_gradient/pallas_call | solution.py:409
  626.8 4.7 settle_rows.13
  631.5 9.5 %partial_rows.14 = (bf16[256,2048]{1,0:T(8,128)(2,1)}, bf16[256,2048]{1,0:T(8,128)(2,1)}, bf16[256,2048]{1,0:T(8,128)(2,1)}, bf16[128,2048]{1,0:T(8,128)(2,1)}, bf16[128,2048]{1,0:T(8,128)(2,1)}) custom-call(bf16[1024,1280]{1,0:T(8,128)(2,1)} %get-tuple-element.211.refs_4_.refs_5_.refs_0_, ...), custom_call_target="tpu_custom_call" | custom-call | flops 10737418240 | bytes 1 | tf_op jit(solution)/shard_map/partial_rows/pallas_call | solution.py:483
  643.3 22.5 %attend_backward.7 = (bf16[1024,768]{1,0:T(8,128)(2,1)}, f32[4,2,8,256]{3,2,1,0:T(8,128)}) custom-call(s32[16]{0:T(128)} %reshape.191.refs_0_, s32[4]{0:T(128)} %iota_xor_fusion.refs_1_, bf16[1024,768]{1,0:T(8,128)(2,1)} %rows_product.9.refs_6_.refs_2_, bf16[1024,128]{1,0:T(8,128)(2,1)} %get-tuple-element.346.refs_3_, ...), custom_call_target="tpu_custom_call", output_to_operand_aliasing={{1}: (10, {})} | custom-call | flops 25999998976 | bytes 1 | tf_op jit(solution)/shard_map/attend_backward/pallas_call | solution.py:252
  671.3 13.6 %weight_gradient.17.refs_6_ = bf16[2048,768]{1,0:T(8,128)(2,1)} custom-call(bf16[256,2048]{1,0:T(8,128)(2,1)} %bitcast.46, bf16[256,2048]{1,0:T(8,128)(2,1)} %copy-done.25, bf16[256,2048]{1,0:T(8,128)(2,1)} %copy-done.24, bf16[128,2048]{1,0:T(8,128)(2,1)} %collective-permute-done.5.refs_3_.refs_7_, bf16[128,2048]{1,0:T(8,128)(2,1)} %collective-permute-done.6.refs_4_.refs_8_, ...), custom_call_target="tpu_custom_call" | custom-call | flops 12884901888 | bytes 1 | tf_op jit(solution)/shard_map/weight_gradient/pallas_call | solution.py:409
  691.6 12.0 %partial_rows.15 = (bf16[256,2048]{1,0:T(8,128)(2,1)}, bf16[256,2048]{1,0:T(8,128)(2,1)}, bf16[256,2048]{1,0:T(8,128)(2,1)}, bf16[128,2048]{1,0:T(8,128)(2,1)}, ...) custom-call(bf16[1024,768]{1,0:T(8,128)(2,1)} %get-tuple-element.249.refs_6_.refs_11_.refs_0_, ...), custom_call_target="tpu_custom_call" | custom-call | flops 12884901888 | bytes 1 | tf_op jit(solution)/shard_map/partial_rows/pallas_call | solution.py:483
  736.2 4.8 settle_rows.15
  (425 shorter events, 203.1 us)
Async XLA Ops:
  7.2 59.6 %all-gather.4.cloned.1.call-start = ((), (), s32[]{:S(2)}) async-start(), calls=%async_computation.6 | async-start | bytes 3538944 | tf_op jit(solution)/shard_map/all_gather | solution.py:858
  11.3 97.9 %all-gather.6.cloned.1.call-start = ((), (), s32[]{:S(2)}) async-start(), calls=%async_computation.7 | async-start | bytes 5898240 | tf_op jit(solution)/shard_map/all_gather | solution.py:858
  12.1 240.6 %all-gather.8.cloned.1.call-start = ((), (), s32[]{:S(2)}) async-start(), calls=%async_computation.8 | async-start | bytes 17694720 | tf_op jit(solution)/shard_map/all_gather | solution.py:858
  16.5 27.4 %collective-permute-start.1 = (bf16[256,2048]{1,0:T(8,128)(2,1)S(1)}, bf16[256,2048]{1,0:T(8,128)(2,1)S(1)}, u32[]{:S(2)}, u32[]{:S(2)}) collective-permute-start(bf16[256,2048]{1,0:T(8,128)(2,1)S(1)} %bitcast.38), channel_id=1, source_target_pairs={{0,2},{1,3},{2,0},{3,1},{4,6},{5,7},{6,4},{7,5},{8,10},{9,11},{10,... | collective-permute-start | bytes 3145736 | tf_op jit(solution)/shard_map/ppermute | solution.py:572
  19.6 24.6 %collective-permute-start = (bf16[256,2048]{1,0:T(8,128)(2,1)S(1)}, bf16[256,2048]{1,0:T(8,128)(2,1)S(1)}, u32[]{:S(2)}, u32[]{:S(2)}) collective-permute-start(bf16[256,2048]{1,0:T(8,128)(2,1)S(1)} %bitcast.39), channel_id=1, source_target_pairs={{0,1},{1,0},{2,3},{3,2},{4,5},{5,4},{6,7},{7,6},{8,9},{9,8},{10,11... | collective-permute-start | bytes 3145736 | tf_op jit(solution)/shard_map/ppermute | solution.py:572
  49.6 493.1 %reduce-scatter.7.cloned.1.call-start = ((), (), s32[]{:S(2)}) async-start(), calls=%async_computation.9 | async-start | bytes 5898240 | tf_op jit(solution)/shard_map/reduce_scatter | solution.py:931
  64.2 26.3 %collective-permute-start.8 = (bf16[256,2048]{1,0:T(8,128)(2,1)}, bf16[256,2048]{1,0:T(8,128)(2,1)S(1)}, u32[]{:S(2)}, u32[]{:S(2)}) collective-permute-start(bf16[256,2048]{1,0:T(8,128)(2,1)} %bitcast.36.refs_2_.refs_0_.refs_5_.refs_4_), channel_id=1, source_target_pairs={{0,2},{1,3},{2,0},{3,1},{4,6},{5,7},{6,4},{7,5},{8,10},{9,11},{10,... | collective-permute-start | bytes 3145736 | tf_op jit(solution)/shard_map/ppermute | solution.py:572
  65.3 26.4 %collective-permute-start.7 = (bf16[256,2048]{1,0:T(8,128)(2,1)}, bf16[256,2048]{1,0:T(8,128)(2,1)}, u32[]{:S(2)}, u32[]{:S(2)}) collective-permute-start(bf16[256,2048]{1,0:T(8,128)(2,1)} %bitcast.36.refs_2_.refs_0_.refs_5_.refs_4_), channel_id=1, source_target_pairs={{0,1},{1,0},{2,3},{3,2},{4,5},{5,4},{6,7},{7,6},{8,9},{9,8},{10,11... | collective-permute-start | bytes 3145736 | tf_op jit(solution)/shard_map/ppermute | solution.py:572
  77.6 53.4 %collective-permute-start.12 = (bf16[256,2048]{1,0:T(8,128)(2,1)S(1)}, bf16[256,2048]{1,0:T(8,128)(2,1)}, u32[]{:S(2)}, u32[]{:S(2)}) collective-permute-start(bf16[256,2048]{1,0:T(8,128)(2,1)S(1)} %get-tuple-element.335.refs_6_.refs_5_.refs_0_), channel_id=1, source_target_pairs={{0,2},{1,3},{2,0},{3,1},{4,6},{5,7},{6,4},{7,5},{8,10},{9,11},{10,... | collective-permute-start | bytes 3145736 | tf_op jit(solution)/shard_map/ppermute | solution.py:572
  78.6 52.4 %collective-permute-start.11 = (bf16[256,2048]{1,0:T(8,128)(2,1)S(1)}, bf16[256,2048]{1,0:T(8,128)(2,1)}, u32[]{:S(2)}, u32[]{:S(2)}) collective-permute-start(bf16[256,2048]{1,0:T(8,128)(2,1)S(1)} %get-tuple-element.335.refs_6_.refs_5_.refs_0_), channel_id=1, source_target_pairs={{0,1},{1,0},{2,3},{3,2},{4,5},{5,4},{6,7},{7,6},{8,9},{9,8},{10,11... | collective-permute-start | bytes 3145736 | tf_op jit(solution)/shard_map/ppermute | solution.py:572
  93.8 42.4 %collective-permute-start.10 = (bf16[128,2048]{1,0:T(8,128)(2,1)S(1)}, bf16[128,2048]{1,0:T(8,128)(2,1)}, u32[]{:S(2)}, u32[]{:S(2)}) collective-permute-start(bf16[128,2048]{1,0:T(8,128)(2,1)S(1)} %slice.110), channel_id=1, source_target_pairs={{0,2},{1,3},{2,0},{3,1},{4,6},{5,7},{6,4},{7,5},{8,10},{9,11},{10,... | collective-permute-start | bytes 1572872 | tf_op jit(solution)/shard_map/ppermute | solution.py:572
  94.9 41.3 %collective-permute-start.9 = (bf16[128,2048]{1,0:T(8,128)(2,1)S(1)}, bf16[128,2048]{1,0:T(8,128)(2,1)}, u32[]{:S(2)}, u32[]{:S(2)}) collective-permute-start(bf16[128,2048]{1,0:T(8,128)(2,1)S(1)} %slice.109), channel_id=1, source_target_pairs={{0,1},{1,0},{2,3},{3,2},{4,5},{5,4},{6,7},{7,6},{8,9},{9,8},{10,11... | collective-permute-start | bytes 1572872 | tf_op jit(solution)/shard_map/ppermute | solution.py:572
  142.8 28.4 %collective-permute-start.13 = (bf16[256,2048]{1,0:T(8,128)(2,1)}, bf16[256,2048]{1,0:T(8,128)(2,1)S(1)}, u32[]{:S(2)}, u32[]{:S(2)}) collective-permute-start(bf16[256,2048]{1,0:T(8,128)(2,1)} %get-tuple-element.167), channel_id=1, source_target_pairs={{0,1},{1,0},{2,3},{3,2},{4,5},{5,4},{6,7},{7,6},{8,9},{9,8},{10,11... | collective-permute-start | bytes 3145736 | tf_op jit(solution)/shard_map/ppermute | solution.py:572
  143.4 27.7 %collective-permute-start.14 = (bf16[256,2048]{1,0:T(8,128)(2,1)}, bf16[256,2048]{1,0:T(8,128)(2,1)}, u32[]{:S(2)}, u32[]{:S(2)}) collective-permute-start(bf16[256,2048]{1,0:T(8,128)(2,1)} %get-tuple-element.168), channel_id=1, source_target_pairs={{0,2},{1,3},{2,0},{3,1},{4,6},{5,7},{6,4},{7,5},{8,10},{9,11},{10,... | collective-permute-start | bytes 3145736 | tf_op jit(solution)/shard_map/ppermute | solution.py:572
  194.1 23.8 %collective-permute-start.20 = (bf16[256,2048]{1,0:T(8,128)(2,1)}, bf16[256,2048]{1,0:T(8,128)(2,1)S(1)}, u32[]{:S(2)}, u32[]{:S(2)}) collective-permute-start(bf16[256,2048]{1,0:T(8,128)(2,1)} %get-tuple-element.178.refs_8_.refs_0_), channel_id=1, source_target_pairs={{0,2},{1,3},{2,0},{3,1},{4,6},{5,7},{6,4},{7,5},{8,10},{9,11},{10,... | collective-permute-start | bytes 3145736 | tf_op jit(solution)/shard_map/ppermute | solution.py:572
  195.0 23.3 %collective-permute-start.19 = (bf16[256,2048]{1,0:T(8,128)(2,1)}, bf16[256,2048]{1,0:T(8,128)(2,1)S(1)}, u32[]{:S(2)}, u32[]{:S(2)}) collective-permute-start(bf16[256,2048]{1,0:T(8,128)(2,1)} %get-tuple-element.178.refs_8_.refs_0_), channel_id=1, source_target_pairs={{0,1},{1,0},{2,3},{3,2},{4,5},{5,4},{6,7},{7,6},{8,9},{9,8},{10,11... | collective-permute-start | bytes 3145736 | tf_op jit(solution)/shard_map/ppermute | solution.py:572
  231.4 47.0 %collective-permute-start.32 = (bf16[256,2048]{1,0:T(8,128)(2,1)S(1)}, bf16[256,2048]{1,0:T(8,128)(2,1)S(1)}, u32[]{:S(2)}, u32[]{:S(2)}) collective-permute-start(bf16[256,2048]{1,0:T(8,128)(2,1)S(1)} %get-tuple-element.203.refs_5_.refs_0_.refs_6_), channel_id=1, source_target_pairs={{0,2},{1,3},{2,0},{3,1},{4,6},{5,7},{6,4},{7,5},{8,10},{9,11},{10,... | collective-permute-start | bytes 3145736 | tf_op jit(solution)/shard_map/ppermute | solution.py:572
  232.5 45.9 %collective-permute-start.31 = (bf16[256,2048]{1,0:T(8,128)(2,1)S(1)}, bf16[256,2048]{1,0:T(8,128)(2,1)S(1)}, u32[]{:S(2)}, u32[]{:S(2)}) collective-permute-start(bf16[256,2048]{1,0:T(8,128)(2,1)S(1)} %get-tuple-element.203.refs_5_.refs_0_.refs_6_), channel_id=1, source_target_pairs={{0,1},{1,0},{2,3},{3,2},{4,5},{5,4},{6,7},{7,6},{8,9},{9,8},{10,11... | collective-permute-start | bytes 3145736 | tf_op jit(solution)/shard_map/ppermute | solution.py:572
  233.9 47.6 %collective-permute-start.23 = (bf16[256,2048]{1,0:T(8,128)(2,1)}, bf16[256,2048]{1,0:T(8,128)(2,1)}, u32[]{:S(2)}, u32[]{:S(2)}) collective-permute-start(bf16[256,2048]{1,0:T(8,128)(2,1)} %get-tuple-element.190), channel_id=1, source_target_pairs={{0,2},{1,3},{2,0},{3,1},{4,6},{5,7},{6,4},{7,5},{8,10},{9,11},{10,... | collective-permute-start | bytes 3145736 | tf_op jit(solution)/shard_map/ppermute | solution.py:572
  234.9 46.6 %collective-permute-start.24 = (bf16[256,2048]{1,0:T(8,128)(2,1)}, bf16[256,2048]{1,0:T(8,128)(2,1)}, u32[]{:S(2)}, u32[]{:S(2)}) collective-permute-start(bf16[256,2048]{1,0:T(8,128)(2,1)} %get-tuple-element.192), channel_id=1, source_target_pairs={{0,1},{1,0},{2,3},{3,2},{4,5},{5,4},{6,7},{7,6},{8,9},{9,8},{10,11... | collective-permute-start | bytes 3145736 | tf_op jit(solution)/shard_map/ppermute | solution.py:572
  278.5 70.3 %collective-permute-start.34 = (bf16[128,2048]{1,0:T(8,128)(2,1)S(1)}, bf16[128,2048]{1,0:T(8,128)(2,1)}, u32[]{:S(2)}, u32[]{:S(2)}) collective-permute-start(bf16[128,2048]{1,0:T(8,128)(2,1)S(1)} %slice.121), channel_id=1, source_target_pairs={{0,2},{1,3},{2,0},{3,1},{4,6},{5,7},{6,4},{7,5},{8,10},{9,11},{10,... | collective-permute-start | bytes 1572872 | tf_op jit(solution)/shard_map/ppermute | solution.py:572
  280.1 68.8 %collective-permute-start.33 = (bf16[128,2048]{1,0:T(8,128)(2,1)S(1)}, bf16[128,2048]{1,0:T(8,128)(2,1)}, u32[]{:S(2)}, u32[]{:S(2)}) collective-permute-start(bf16[128,2048]{1,0:T(8,128)(2,1)S(1)} %slice.120), channel_id=1, source_target_pairs={{0,1},{1,0},{2,3},{3,2},{4,5},{5,4},{6,7},{7,6},{8,9},{9,8},{10,11... | collective-permute-start | bytes 1572872 | tf_op jit(solution)/shard_map/ppermute | solution.py:572
  310.1 25.5 %collective-permute-start.28 = (bf16[256,2048]{1,0:T(8,128)(2,1)}, bf16[256,2048]{1,0:T(8,128)(2,1)S(1)}, u32[]{:S(2)}, u32[]{:S(2)}) collective-permute-start(bf16[256,2048]{1,0:T(8,128)(2,1)} %get-tuple-element.202.refs_6_.refs_0_), channel_id=1, source_target_pairs={{0,2},{1,3},{2,0},{3,1},{4,6},{5,7},{6,4},{7,5},{8,10},{9,11},{10,... | collective-permute-start | bytes 3145736 | tf_op jit(solution)/shard_map/ppermute | solution.py:572
  310.6 25.7 %collective-permute-start.27 = (bf16[256,2048]{1,0:T(8,128)(2,1)}, bf16[256,2048]{1,0:T(8,128)(2,1)}, u32[]{:S(2)}, u32[]{:S(2)}) collective-permute-start(bf16[256,2048]{1,0:T(8,128)(2,1)} %get-tuple-element.202.refs_6_.refs_0_), channel_id=1, source_target_pairs={{0,1},{1,0},{2,3},{3,2},{4,5},{5,4},{6,7},{7,6},{8,9},{9,8},{10,11... | collective-permute-start | bytes 3145736 | tf_op jit(solution)/shard_map/ppermute | solution.py:572
  350.1 28.2 %collective-permute-start.35 = (bf16[256,2048]{1,0:T(8,128)(2,1)}, bf16[256,2048]{1,0:T(8,128)(2,1)S(1)}, u32[]{:S(2)}, u32[]{:S(2)}) collective-permute-start(bf16[256,2048]{1,0:T(8,128)(2,1)} %get-tuple-element.207), channel_id=1, source_target_pairs={{0,1},{1,0},{2,3},{3,2},{4,5},{5,4},{6,7},{7,6},{8,9},{9,8},{10,11... | collective-permute-start | bytes 3145736 | tf_op jit(solution)/shard_map/ppermute | solution.py:572
  351.4 26.9 %collective-permute-start.36 = (bf16[256,2048]{1,0:T(8,128)(2,1)}, bf16[256,2048]{1,0:T(8,128)(2,1)S(1)}, u32[]{:S(2)}, u32[]{:S(2)}) collective-permute-start(bf16[256,2048]{1,0:T(8,128)(2,1)} %get-tuple-element.208), channel_id=1, source_target_pairs={{0,2},{1,3},{2,0},{3,1},{4,6},{5,7},{6,4},{7,5},{8,10},{9,11},{10,... | collective-permute-start | bytes 3145736 | tf_op jit(solution)/shard_map/ppermute | solution.py:572
  402.5 161.0 %reduce-scatter.9.cloned.1.call-start = ((), (), s32[]{:S(2)}) async-start(), calls=%async_computation.10 | async-start | bytes 7077888 | tf_op jit(solution)/shard_map/reduce_scatter | solution.py:931
  403.7 26.1 %collective-permute-start.40 = (bf16[256,2048]{1,0:T(8,128)(2,1)S(1)}, bf16[256,2048]{1,0:T(8,128)(2,1)S(1)}, u32[]{:S(2)}, u32[]{:S(2)}) collective-permute-start(bf16[256,2048]{1,0:T(8,128)(2,1)S(1)} %copy-done.7), channel_id=1, source_target_pairs={{0,2},{1,3},{2,0},{3,1},{4,6},{5,7},{6,4},{7,5},{8,10},{9,11},{10,... | collective-permute-start | bytes 3145736 | tf_op jit(solution)/shard_map/ppermute | solution.py:572
  404.9 27.0 %collective-permute-start.39 = (bf16[256,2048]{1,0:T(8,128)(2,1)S(1)}, bf16[256,2048]{1,0:T(8,128)(2,1)S(1)}, u32[]{:S(2)}, u32[]{:S(2)}) collective-permute-start(bf16[256,2048]{1,0:T(8,128)(2,1)S(1)} %copy-done.7), channel_id=1, source_target_pairs={{0,1},{1,0},{2,3},{3,2},{4,5},{5,4},{6,7},{7,6},{8,9},{9,8},{10,11... | collective-permute-start | bytes 3145736 | tf_op jit(solution)/shard_map/ppermute | solution.py:572
  422.4 33.9 %collective-permute-start.43 = (bf16[256,2048]{1,0:T(8,128)(2,1)}, bf16[256,2048]{1,0:T(8,128)(2,1)}, u32[]{:S(2)}, u32[]{:S(2)}) collective-permute-start(bf16[256,2048]{1,0:T(8,128)(2,1)} %get-tuple-element.218), channel_id=1, source_target_pairs={{0,2},{1,3},{2,0},{3,1},{4,6},{5,7},{6,4},{7,5},{8,10},{9,11},{10,... | collective-permute-start | bytes 3145736 | tf_op jit(solution)/shard_map/ppermute | solution.py:572
  423.5 32.7 %collective-permute-start.44 = (bf16[256,2048]{1,0:T(8,128)(2,1)}, bf16[256,2048]{1,0:T(8,128)(2,1)}, u32[]{:S(2)}, u32[]{:S(2)}) collective-permute-start(bf16[256,2048]{1,0:T(8,128)(2,1)} %get-tuple-element.220), channel_id=1, source_target_pairs={{0,1},{1,0},{2,3},{3,2},{4,5},{5,4},{6,7},{7,6},{8,9},{9,8},{10,11... | collective-permute-start | bytes 3145736 | tf_op jit(solution)/shard_map/ppermute | solution.py:572
  430.6 29.2 %collective-permute-start.41 = (bf16[128,2048]{1,0:T(8,128)(2,1)}, bf16[128,2048]{1,0:T(8,128)(2,1)S(1)}, u32[]{:S(2)}, u32[]{:S(2)}) collective-permute-start(bf16[128,2048]{1,0:T(8,128)(2,1)} %slice.141.refs_8_), channel_id=1, source_target_pairs={{0,1},{1,0},{2,3},{3,2},{4,5},{5,4},{6,7},{7,6},{8,9},{9,8},{10,11... | collective-permute-start | bytes 1572872 | tf_op jit(solution)/shard_map/ppermute | solution.py:572
  432.0 27.8 %collective-permute-start.42 = (bf16[128,2048]{1,0:T(8,128)(2,1)S(1)}, bf16[128,2048]{1,0:T(8,128)(2,1)S(1)}, u32[]{:S(2)}, u32[]{:S(2)}) collective-permute-start(bf16[128,2048]{1,0:T(8,128)(2,1)S(1)} %slice.142.refs_9_), channel_id=1, source_target_pairs={{0,2},{1,3},{2,0},{3,1},{4,6},{5,7},{6,4},{7,5},{8,10},{9,11},{10,... | collective-permute-start | bytes 1572872 | tf_op jit(solution)/shard_map/ppermute | solution.py:572
  463.2 180.2 %reduce-scatter.11.cloned.1.call-start = ((), (), s32[]{:S(2)}) async-start(), calls=%async_computation.11 | async-start | bytes 4718592 | tf_op jit(solution)/shard_map/reduce_scatter | solution.py:931
  490.9 180.4 %reduce-scatter.13.cloned.1.call-start = ((), (), s32[]{:S(2)}) async-start(), calls=%async_computation.12 | async-start | bytes 2359296 | tf_op jit(solution)/shard_map/reduce_scatter | solution.py:931
  490.9 25.1 %collective-permute-start.48 = (bf16[256,2048]{1,0:T(8,128)(2,1)}, bf16[256,2048]{1,0:T(8,128)(2,1)S(1)}, u32[]{:S(2)}, u32[]{:S(2)}) collective-permute-start(bf16[256,2048]{1,0:T(8,128)(2,1)} %get-tuple-element.226.refs_10_.refs_0_.refs_5_), channel_id=1, source_target_pairs={{0,1},{1,0},{2,3},{3,2},{4,5},{5,4},{6,7},{7,6},{8,9},{9,8},{10,11... | collective-permute-start | bytes 3145736 | tf_op jit(solution)/shard_map/ppermute | solution.py:572
  491.8 25.0 %collective-permute-start.47 = (bf16[256,2048]{1,0:T(8,128)(2,1)}, bf16[256,2048]{1,0:T(8,128)(2,1)S(1)}, u32[]{:S(2)}, u32[]{:S(2)}) collective-permute-start(bf16[256,2048]{1,0:T(8,128)(2,1)} %get-tuple-element.226.refs_10_.refs_0_.refs_5_), channel_id=1, source_target_pairs={{0,2},{1,3},{2,0},{3,1},{4,6},{5,7},{6,4},{7,5},{8,10},{9,11},{10,... | collective-permute-start | bytes 3145736 | tf_op jit(solution)/shard_map/ppermute | solution.py:572
  516.0 39.2 %collective-permute-start.50 = (bf16[128,2048]{1,0:T(8,128)(2,1)S(1)}, bf16[128,2048]{1,0:T(8,128)(2,1)}, u32[]{:S(2)}, u32[]{:S(2)}) collective-permute-start(bf16[128,2048]{1,0:T(8,128)(2,1)S(1)} %slice.144.refs_12_), channel_id=1, source_target_pairs={{0,2},{1,3},{2,0},{3,1},{4,6},{5,7},{6,4},{7,5},{8,10},{9,11},{10,... | collective-permute-start | bytes 1572872 | tf_op jit(solution)/shard_map/ppermute | solution.py:572
  516.9 39.5 %collective-permute-start.49 = (bf16[128,2048]{1,0:T(8,128)(2,1)S(1)}, bf16[128,2048]{1,0:T(8,128)(2,1)}, u32[]{:S(2)}, u32[]{:S(2)}) collective-permute-start(bf16[128,2048]{1,0:T(8,128)(2,1)S(1)} %slice.143.refs_11_), channel_id=1, source_target_pairs={{0,1},{1,0},{2,3},{3,2},{4,5},{5,4},{6,7},{7,6},{8,9},{9,8},{10,11... | collective-permute-start | bytes 1572872 | tf_op jit(solution)/shard_map/ppermute | solution.py:572
  518.1 61.0 %collective-permute-start.51 = (bf16[256,2048]{1,0:T(8,128)(2,1)}, bf16[256,2048]{1,0:T(8,128)(2,1)}, u32[]{:S(2)}, u32[]{:S(2)}) collective-permute-start(bf16[256,2048]{1,0:T(8,128)(2,1)} %get-tuple-element.239), channel_id=1, source_target_pairs={{0,2},{1,3},{2,0},{3,1},{4,6},{5,7},{6,4},{7,5},{8,10},{9,11},{10,... | collective-permute-start | bytes 3145736 | tf_op jit(solution)/shard_map/ppermute | solution.py:572
  519.2 60.0 %collective-permute-start.52 = (bf16[256,2048]{1,0:T(8,128)(2,1)}, bf16[256,2048]{1,0:T(8,128)(2,1)}, u32[]{:S(2)}, u32[]{:S(2)}) collective-permute-start(bf16[256,2048]{1,0:T(8,128)(2,1)} %get-tuple-element.241), channel_id=1, source_target_pairs={{0,1},{1,0},{2,3},{3,2},{4,5},{5,4},{6,7},{7,6},{8,9},{9,8},{10,11... | collective-permute-start | bytes 3145736 | tf_op jit(solution)/shard_map/ppermute | solution.py:572
  578.3 47.5 %collective-permute-start.55 = (bf16[128,2048]{1,0:T(8,128)(2,1)}, bf16[128,2048]{1,0:T(8,128)(2,1)S(1)}, u32[]{:S(2)}, u32[]{:S(2)}) collective-permute-start(bf16[128,2048]{1,0:T(8,128)(2,1)} %get-tuple-element.247.refs_4_), channel_id=1, source_target_pairs={{0,1},{1,0},{2,3},{3,2},{4,5},{5,4},{6,7},{7,6},{8,9},{9,8},{10,11... | collective-permute-start | bytes 1572872 | tf_op jit(solution)/shard_map/ppermute | solution.py:572
  581.6 25.9 %collective-permute-start.58 = (bf16[128,2048]{1,0:T(8,128)(2,1)}, bf16[128,2048]{1,0:T(8,128)(2,1)S(1)}, u32[]{:S(2)}, u32[]{:S(2)}) collective-permute-start(bf16[128,2048]{1,0:T(8,128)(2,1)} %get-tuple-element.254), channel_id=1, source_target_pairs={{0,2},{1,3},{2,0},{3,1},{4,6},{5,7},{6,4},{7,5},{8,10},{9,11},{10,... | collective-permute-start | bytes 1572872 | tf_op jit(solution)/shard_map/ppermute | solution.py:572
  583.0 24.6 %collective-permute-start.57 = (bf16[128,2048]{1,0:T(8,128)(2,1)}, bf16[128,2048]{1,0:T(8,128)(2,1)S(1)}, u32[]{:S(2)}, u32[]{:S(2)}) collective-permute-start(bf16[128,2048]{1,0:T(8,128)(2,1)} %get-tuple-element.248.refs_10_), channel_id=1, source_target_pairs={{0,1},{1,0},{2,3},{3,2},{4,5},{5,4},{6,7},{7,6},{8,9},{9,8},{10,11... | collective-permute-start | bytes 1572872 | tf_op jit(solution)/shard_map/ppermute | solution.py:572
  583.8 143.1 %reduce-scatter.15.cloned.1.call-start = ((), (), s32[]{:S(2)}) async-start(), calls=%async_computation.13 | async-start | bytes 3538944 | tf_op jit(solution)/shard_map/reduce_scatter | solution.py:931
  631.5 97.6 %reduce-scatter.17.cloned.1.call-start = ((), (), s32[]{:S(2)}) async-start(), calls=%async_computation.14 | async-start | bytes 3538944 | tf_op jit(solution)/shard_map/reduce_scatter | solution.py:931
  641.0 24.8 %collective-permute-start.59 = (bf16[256,2048]{1,0:T(8,128)(2,1)}, bf16[256,2048]{1,0:T(8,128)(2,1)S(1)}, u32[]{:S(2)}, u32[]{:S(2)}) collective-permute-start(bf16[256,2048]{1,0:T(8,128)(2,1)} %get-tuple-element.259), channel_id=1, source_target_pairs={{0,1},{1,0},{2,3},{3,2},{4,5},{5,4},{6,7},{7,6},{8,9},{9,8},{10,11... | collective-permute-start | bytes 3145736 | tf_op jit(solution)/shard_map/ppermute | solution.py:572
  641.9 23.9 %collective-permute-start.60 = (bf16[256,2048]{1,0:T(8,128)(2,1)}, bf16[256,2048]{1,0:T(8,128)(2,1)S(1)}, u32[]{:S(2)}, u32[]{:S(2)}) collective-permute-start(bf16[256,2048]{1,0:T(8,128)(2,1)} %get-tuple-element.260), channel_id=1, source_target_pairs={{0,2},{1,3},{2,0},{3,1},{4,6},{5,7},{6,4},{7,5},{8,10},{9,11},{10,... | collective-permute-start | bytes 3145736 | tf_op jit(solution)/shard_map/ppermute | solution.py:572
  (110 other events, 943.2 us)
Sparse Core Ops, SparseCore 0:
  11.4 41.0 all-gather.3
  54.1 54.9 all-gather.5
  111.4 141.2 all-gather.7
  402.6 57.7 reduce-scatter.6
  463.3 67.4 reduce-scatter.8
  532.9 48.3 reduce-scatter.10
  584.0 33.4 reduce-scatter.12
  631.6 37.7 reduce-scatter.14
  690.3 38.7 reduce-scatter.16
